TPU v7x, 32 devices: a whole 2x2x4 slice. The times are simulated.
32 devices in a mesh: sec: 8 (over z, y), girth: 4 (over x, core).
Axes of the slice: x: 2, y: 2, z: 4, core: 2. Of those that a mesh axis runs over, the one named last changes fastest.
Arguments:
- displacement: float32 [5, 512, 2048], P(None, 'sec', 'girth'), may hold values from -6 to 6
- velocity: float32 [5, 512, 2048], P(None, 'sec', 'girth'), may hold values from -6 to 6
- stress: float32 [8, 512, 2048], P(None, 'sec', 'girth'), may hold values from -3 to 3
- thickness: int32 [512, 2048], P('sec', 'girth'), may hold values from 8 to 32
- pressure: float32 [512, 2048], P('sec', 'girth'), may hold values from 0.2 to 1
- weld_from: int32 [32, 32, 16], P(('sec', 'girth')), may hold values from -1 to 32767, as said below
- weld_to: int32 [32, 32, 16], P(('sec', 'girth')), may hold values from -1 to 32767, as said below
- weld_stiff: float32 [32, 32, 16], P(('sec', 'girth')), may hold values from 0.5 to 4
Outputs:
- displacement_out: float32 [5, 512, 2048], P(None, 'sec', 'girth')
- velocity_out: float32 [5, 512, 2048], P(None, 'sec', 'girth')
- stress_out: float32 [8, 512, 2048], P(None, 'sec', 'girth')
- section_moment: float32 [512], P('sec')
Inputs may be any that keep to these rules, and one draw needn't show every extreme that they name: weld_from[s, p, c] and weld_to[p, s, c] are the two nodes (numbered row by row within a device's 64 x 512 block) of one joint between devices s and p, or both -1 for an unused slot; in each pair (s, p) the used slots come first; each device s uses all 16 slots towards the next device along sec+girth (the last towards the first). `weld_to`: see weld_from.
All inputs are finite; a program needn't handle non-finite values.
Results may differ from a plain program's by a relative error of at most 0.00021.
Values sent between devices are 32-bit elements; how exact they have to be, the bound alone decides.
No kernel may reach another device: no remote copies, remote signals or barrier semaphores. Data moves between devices by JAX's collectives and lax.ppermute only.
A program may use at most 64 MiB of HBM per device.

v0:
```python
import jax
import jax.numpy as jnp
from jax import lax
from jax.sharding import PartitionSpec as P

STEPS = 3


young_modulus = 4.0
poisson_ratio = 0.3
plate_modulus = young_modulus / (1.0 - poisson_ratio * poisson_ratio)
shear_modulus = young_modulus / (2.0 * (1.0 + poisson_ratio))
shear_factor = 5.0 / 6.0
time_step = 0.2
spacing_mm = 50.0
rotary_share = 1.0 / 12.0


def extended(block, sides, width, periodic):
    for axis, dim in sides:
        count = lax.axis_size(axis)
        forward = [(i, i + 1) for i in range(count - 1)]
        if periodic:
            forward.append((count - 1, 0))
        backward = [(target, source) for source, target in forward]
        low = lax.ppermute(
            lax.slice_in_dim(block, block.shape[dim] - width, None, axis=dim), axis, forward
        )
        high = lax.ppermute(lax.slice_in_dim(block, 0, width, axis=dim), axis, backward)
        block = jnp.concatenate([low, block, high], axis=dim)
    return block


def along_length(values):
    padded = extended(values, (("sec", 1),), 1, False)
    return 0.5 * (padded[:, 2:, :] - padded[:, :-2, :])


def along_girth(values):
    padded = extended(values, (("girth", 2),), 1, True)
    return 0.5 * (padded[:, :, 2:] - padded[:, :, :-2])


def resultants(stress, plate_ratio):
    bending_arm = plate_ratio * plate_ratio / 6.0
    return jnp.concatenate(
        [
            plate_ratio * stress[0:3],
            bending_arm * stress[3:6],
            shear_factor * plate_ratio * stress[6:8],
        ]
    )


def lengthwise_set(result):
    return jnp.stack([result[0], result[2], result[6], result[3], result[5]])


def girthwise_set(result):
    return jnp.stack([result[2], result[1], result[7], result[5], result[4]])


def nodal_force(along_x, along_y, result):
    return jnp.stack(
        [
            along_x[0] + along_y[0],
            along_x[1] + along_y[1],
            along_x[2] + along_y[2],
            along_x[3] + along_y[3] - result[6],
            along_x[4] + along_y[4] - result[7],
        ]
    )


def radial_return(trial_state):
    normal_xx = trial_state[0]
    normal_yy = trial_state[1]
    shear_xy = trial_state[2]
    offset = normal_xx - 0.5 * normal_yy
    equivalent = jnp.sqrt(
        offset * offset + 0.75 * normal_yy * normal_yy + 3.0 * shear_xy * shear_xy
    )
    return trial_state / jnp.maximum(equivalent, 1.0)


def stress_update(stress, along_x, along_y, velocity, plate_ratio):
    strain_xx = along_x[0]
    strain_yy = along_y[1]
    strain_xy = along_y[0] + along_x[1]
    curve_xx = along_x[3]
    curve_yy = along_y[4]
    curve_xy = along_y[3] + along_x[4]
    membrane = stress[0:3] + time_step * jnp.stack(
        [
            plate_modulus * (strain_xx + poisson_ratio * strain_yy),
            plate_modulus * (strain_yy + poisson_ratio * strain_xx),
            shear_modulus * strain_xy,
        ]
    )
    fiber_half = 0.5 * plate_ratio
    bending = stress[3:6] + time_step * fiber_half * jnp.stack(
        [
            plate_modulus * (curve_xx + poisson_ratio * curve_yy),
            plate_modulus * (curve_yy + poisson_ratio * curve_xx),
            shear_modulus * curve_xy,
        ]
    )
    shear_part = stress[6:8] + time_step * shear_modulus * jnp.stack(
        [along_x[2] + velocity[3], along_y[2] + velocity[4]]
    )
    return jnp.concatenate([radial_return(membrane), radial_return(bending), shear_part])


def selectors(near_index, far_index, rows, cols):
    every = jnp.concatenate([near_index.reshape(-1), far_index.reshape(-1)])
    total = every.shape[0]
    column_select = (
        every[:, None] % cols == lax.broadcasted_iota(jnp.int32, (total, cols), 1)
    ).astype(jnp.float32)
    row_select = (
        every[None, :] // cols == lax.broadcasted_iota(jnp.int32, (rows, total), 0)
    ).astype(jnp.float32)
    return (column_select, row_select)


def weld_force(displacement, column_select, row_select, spring):
    fields, rows, cols = displacement.shape
    slot_shape = spring.shape
    slots = spring.size
    field_scale = jnp.array([1.0, 1.0, 1.0, rotary_share, rotary_share], jnp.float32).reshape(
        fields, 1, 1
    )
    by_column = lax.dot_general(
        displacement.reshape(fields * rows, cols),
        column_select,
        (((1,), (1,)), ((), ())),
        precision=lax.Precision.HIGHEST,
        preferred_element_type=jnp.float32,
    )
    picked = jnp.sum(by_column.reshape(fields, rows, 2 * slots) * row_select[None], axis=1)
    near_values = picked[:, :slots].reshape((fields,) + slot_shape)
    far_values = picked[:, slots:].reshape((fields,) + slot_shape)
    outgoing = jnp.concatenate([near_values, spring[None]], axis=0)
    received = lax.all_to_all(outgoing, ("sec", "girth"), split_axis=1, concat_axis=1, tiled=True)
    on_far = field_scale * received[5][None] * (received[0:5] - far_values)
    on_near = -lax.all_to_all(on_far, ("sec", "girth"), split_axis=1, concat_axis=1, tiled=True)
    pulls = jnp.concatenate([on_near.reshape(fields, slots), on_far.reshape(fields, slots)], axis=1)
    spread = (row_select[None] * pulls[:, None, :]).reshape(fields * rows, 2 * slots)
    summed = jnp.dot(
        spread, column_select, precision=lax.Precision.HIGHEST, preferred_element_type=jnp.float32
    )
    return summed.reshape(displacement.shape)


def local(displacement, velocity, stress, thickness, pressure, weld_from, weld_to, weld_stiff):
    plate_ratio = thickness.astype(jnp.float32) / spacing_mm
    rotary = plate_ratio * (1.0 + plate_ratio * plate_ratio) / 12.0
    inertia = jnp.stack([plate_ratio, plate_ratio, plate_ratio, rotary, rotary])
    near_index = jnp.maximum(weld_from[0], 0)
    far_index = jnp.maximum(weld_to[0], 0)
    spring = jnp.where(weld_from[0] >= 0, weld_stiff[0], 0.0)
    column_select, row_select = selectors(
        near_index, far_index, displacement.shape[1], displacement.shape[2]
    )
    for step_index in range(STEPS):
        joints = weld_force(displacement, column_select, row_select, spring)
        result = resultants(stress, plate_ratio)
        summed = nodal_force(
            along_length(lengthwise_set(result)), along_girth(girthwise_set(result)), result
        )
        summed = summed + joints
        summed = summed.at[2].add(pressure)
        velocity = velocity + time_step * summed / inertia
        displacement = displacement + time_step * velocity
        stress = stress_update(
            stress, along_length(velocity), along_girth(velocity), velocity, plate_ratio
        )
    girth_nodes = stress.shape[2]
    girth_total = girth_nodes * lax.axis_size("girth")
    column = (lax.axis_index("girth") * girth_nodes + lax.iota(jnp.int32, girth_nodes)).astype(
        jnp.float32
    )
    height = jnp.sin(2.0 * jnp.pi / girth_total * (column + 0.5))
    partial_value = jnp.sum(plate_ratio * stress[0] * height[None, :], axis=1)
    moment = lax.psum(partial_value, "girth") / girth_total
    return (displacement, velocity, stress, moment)


def solution(mesh):
    in_specs = (
        P(None, "sec", "girth"),
        P(None, "sec", "girth"),
        P(None, "sec", "girth"),
        P("sec", "girth"),
        P("sec", "girth"),
        P(("sec", "girth"), None, None),
        P(("sec", "girth"), None, None),
        P(("sec", "girth"), None, None),
    )
    out_specs = (
        P(None, "sec", "girth"),
        P(None, "sec", "girth"),
        P(None, "sec", "girth"),
        P("sec"),
    )
    return jax.shard_map(local, mesh=mesh, in_specs=in_specs, out_specs=out_specs, check_vma=False)
```

profile of v0, /device:TPU:0, one launch (start us, length us, event | category | flops | bytes accessed | tf_op | source)
XLA Modules:
  0.0 179.8 jit_solution(1885242708120321739)
XLA Ops:
  4.7 1.9 %collective-permute-start.2 = (f32[5,64,1]{2,1,0:T(8,128)}, f32[5,64,1]{2,1,0:T(8,128)}, u32[]{:S(2)}, u32[]{:S(2)}) collective-permute-start(f32[5,64,1]{2,1,0:T(8,128)} %get-tuple-element.98), channel_id=1, source_target_pairs={{1,0},{2,1},{3,2},{0,3},{5,4},{6,5},{7,6},{4,7},{9,8},{10,9},{11,1... | collective-permute-start | bytes 3848 | tf_op jit(solution)/shard_map/ppermute | solution.py:29
  6.7 4.2 %collective-permute-start.1 = (f32[5,1,512]{2,1,0:T(1,128)S(1)}, f32[5,1,512]{2,1,0:T(1,128)S(1)}, u32[]{:S(2)}, u32[]{:S(2)}) collective-permute-start(f32[5,1,512]{2,1,0:T(1,128)S(1)} %get-tuple-element.97), channel_id=1, source_target_pairs={{0,4},{4,8},{8,12},{12,16},{16,20},{20,24},{24,28},{1,5},{5,9},{9,... | collective-permute-start | bytes 30728 | tf_op jit(solution)/shard_map/ppermute | solution.py:26
  15.8 7.5 %all-to-all-start = ((f32[6,32,16]{2,0,1:T(8,128)}), f32[6,32,16]{2,0,1:T(8,128)S(1)}, u32[]{:S(2)}, u32[]{:S(2)}) async-start(f32[6,32,16]{2,0,1:T(8,128)} %copy.42), calls=%async_computation | async-start | bytes 262144 | tf_op jit(solution)/shard_map/all_to_all | solution.py:144
  29.7 1.9 %all-to-all-done = f32[6,32,16]{2,0,1:T(8,128)S(1)} async-done(((f32[6,32,16]{2,0,1:T(8,128)}), f32[6,32,16]{2,0,1:T(8,128)S(1)}, u32[]{:S(2)}, u32[]{:S(2)}) %all-to-all-start) | async-done | bytes 12320 | tf_op jit(solution)/shard_map/all_to_all | solution.py:144
  32.4 4.0 %all-to-all-start.1 = ((f32[5,32,16]{2,0,1:T(8,128)}), f32[5,32,16]{2,0,1:T(8,128)S(1)}, u32[]{:S(2)}, u32[]{:S(2)}) async-start(f32[5,32,16]{2,0,1:T(8,128)} %copy.44), calls=%async_computation.1 | async-start | bytes 262144 | tf_op jit(solution)/shard_map/all_to_all | solution.py:146
  38.0 6.5 %all-to-all-done.1 = f32[5,32,16]{2,0,1:T(8,128)S(1)} async-done(((f32[5,32,16]{2,0,1:T(8,128)}), f32[5,32,16]{2,0,1:T(8,128)S(1)}, u32[]{:S(2)}, u32[]{:S(2)}) %all-to-all-start.1) | async-done | bytes 10272 | tf_op jit(solution)/shard_map/all_to_all | solution.py:146
  44.9 2.7 %fusion.27 = f32[5,64,512]{2,1,0:T(8,128)S(1)} fusion(f32[5,64,512]{2,1,0:T(8,128)} %fusion.151, s32[1024]{0:T(1024)S(1)} %get-tuple-element.129, f32[5,1024]{1,0:T(8,128)S(1)} %pad_maximum_fusion.28, f32[64,1024]{1,0:T(8,128)S(1)} %fusion.87), kind=kOutput, calls=%fused_computation.16 | convolution fusion | flops 2014281728 | bytes 1597440 | tf_op jit(solution)/shard_map/dot_general | solution.py:149
  52.0 2.6 %collective-permute-start.5 = (f32[5,1,512]{2,1,0:T(1,128)S(1)}, f32[5,1,512]{2,1,0:T(1,128)S(1)}, u32[]{:S(2)}, u32[]{:S(2)}) collective-permute-start(f32[5,1,512]{2,1,0:T(1,128)S(1)} %get-tuple-element.95), channel_id=1, source_target_pairs={{0,4},{4,8},{8,12},{12,16},{16,20},{20,24},{24,28},{1,5},{5,9},{9,... | collective-permute-start | bytes 30728 | tf_op jit(solution)/shard_map/ppermute | solution.py:26
  57.5 4.7 %all-to-all-start.2 = ((f32[6,32,16]{2,0,1:T(8,128)}), f32[6,32,16]{2,0,1:T(8,128)}, u32[]{:S(2)}, u32[]{:S(2)}) async-start(f32[6,32,16]{2,0,1:T(8,128)} %copy.47), calls=%async_computation.2 | async-start | bytes 262144 | tf_op jit(solution)/shard_map/all_to_all | solution.py:144
  67.5 3.6 %collective-permute-start.9 = (f32[5,1,512]{2,1,0:T(1,128)S(1)}, f32[5,1,512]{2,1,0:T(1,128)S(1)}, u32[]{:S(2)}, u32[]{:S(2)}) collective-permute-start(f32[5,1,512]{2,1,0:T(1,128)S(1)} %get-tuple-element.85), channel_id=1, source_target_pairs={{0,4},{4,8},{8,12},{12,16},{16,20},{20,24},{24,28},{1,5},{5,9},{9,... | collective-permute-start | bytes 30728 | tf_op jit(solution)/shard_map/ppermute | solution.py:26
  73.0 3.8 %collective-permute-done.8 = f32[5,1,512]{2,1,0:T(1,128)S(1)} collective-permute-done((f32[5,1,512]{2,1,0:T(1,128)S(1)}, f32[5,1,512]{2,1,0:T(1,128)S(1)}, u32[]{:S(2)}, u32[]{:S(2)}) %collective-permute-start.8) | collective-permute-done | bytes 10272 | tf_op jit(solution)/shard_map/ppermute | solution.py:29
  82.3 5.8 %all-to-all-start.3 = ((f32[5,32,16]{2,0,1:T(8,128)}), f32[5,32,16]{2,0,1:T(8,128)}, u32[]{:S(2)}, u32[]{:S(2)}) async-start(f32[5,32,16]{2,0,1:T(8,128)} %copy.49), calls=%async_computation.3 | async-start | bytes 262144 | tf_op jit(solution)/shard_map/all_to_all | solution.py:146
  89.9 6.3 %all-to-all-done.3 = f32[5,32,16]{2,0,1:T(8,128)} async-done(((f32[5,32,16]{2,0,1:T(8,128)}), f32[5,32,16]{2,0,1:T(8,128)}, u32[]{:S(2)}, u32[]{:S(2)}) %all-to-all-start.3) | async-done | bytes 10272 | tf_op jit(solution)/shard_map/all_to_all | solution.py:146
  97.4 2.6 %fusion.32 = f32[5,64,512]{2,1,0:T(8,128)S(1)} fusion(f32[5,64,512]{2,1,0:T(8,128)} %fusion.139, s32[1024]{0:T(1024)} %copy-done.58, f32[5,1024]{1,0:T(8,128)S(1)} %pad_maximum_fusion.29, f32[64,1024]{1,0:T(8,128)S(1)} %copy-done.52), kind=kOutput, calls=%fused_computation.17 | convolution fusion | flops 2014281728 | bytes 1597440 | tf_op jit(solution)/shard_map/dot_general | solution.py:149
  105.1 2.6 %collective-permute-start.13 = (f32[5,1,512]{2,1,0:T(1,128)}, f32[5,1,512]{2,1,0:T(1,128)S(1)}, u32[]{:S(2)}, u32[]{:S(2)}) collective-permute-start(f32[5,1,512]{2,1,0:T(1,128)} %get-tuple-element.83), channel_id=1, source_target_pairs={{0,4},{4,8},{8,12},{12,16},{16,20},{20,24},{24,28},{1,5},{5,9},{9,... | collective-permute-start | bytes 30728 | tf_op jit(solution)/shard_map/ppermute | solution.py:26
  110.5 4.7 %all-to-all-start.4 = ((f32[6,32,16]{2,0,1:T(8,128)}), f32[6,32,16]{2,0,1:T(8,128)}, u32[]{:S(2)}, u32[]{:S(2)}) async-start(f32[6,32,16]{2,0,1:T(8,128)} %copy.52), calls=%async_computation.4 | async-start | bytes 262144 | tf_op jit(solution)/shard_map/all_to_all | solution.py:144
  122.7 3.6 %collective-permute-start.17 = (f32[5,1,512]{2,1,0:T(1,128)S(1)}, f32[5,1,512]{2,1,0:T(1,128)S(1)}, u32[]{:S(2)}, u32[]{:S(2)}) collective-permute-start(f32[5,1,512]{2,1,0:T(1,128)S(1)} %get-tuple-element.73), channel_id=1, source_target_pairs={{0,4},{4,8},{8,12},{12,16},{16,20},{20,24},{24,28},{1,5},{5,9},{9,... | collective-permute-start | bytes 30728 | tf_op jit(solution)/shard_map/ppermute | solution.py:26
  128.1 3.8 %collective-permute-done.16 = f32[5,1,512]{2,1,0:T(1,128)S(1)} collective-permute-done((f32[5,1,512]{2,1,0:T(1,128)S(1)}, f32[5,1,512]{2,1,0:T(1,128)S(1)}, u32[]{:S(2)}, u32[]{:S(2)}) %collective-permute-start.16) | collective-permute-done | bytes 10272 | tf_op jit(solution)/shard_map/ppermute | solution.py:29
  138.1 5.6 %all-to-all-start.5 = ((f32[5,32,16]{2,0,1:T(8,128)}), f32[5,32,16]{2,0,1:T(8,128)}, u32[]{:S(2)}, u32[]{:S(2)}) async-start(f32[5,32,16]{2,0,1:T(8,128)} %copy.54), calls=%async_computation.5 | async-start | bytes 262144 | tf_op jit(solution)/shard_map/all_to_all | solution.py:146
  146.3 5.6 %all-to-all-done.5 = f32[5,32,16]{2,0,1:T(8,128)} async-done(((f32[5,32,16]{2,0,1:T(8,128)}), f32[5,32,16]{2,0,1:T(8,128)}, u32[]{:S(2)}, u32[]{:S(2)}) %all-to-all-start.5) | async-done | bytes 10272 | tf_op jit(solution)/shard_map/all_to_all | solution.py:146
  153.1 2.8 %fusion.37 = f32[5,64,512]{2,1,0:T(8,128)S(1)} fusion(f32[5,64,512]{2,1,0:T(8,128)} %fusion.127, s32[1024]{0:T(1024)S(1)} %copy-done.60, f32[5,1024]{1,0:T(8,128)S(1)} %pad_maximum_fusion.30, f32[64,1024]{1,0:T(8,128)} %copy-done.51), kind=kOutput, calls=%fused_computation.18 | convolution fusion | flops 2014281728 | bytes 1597440 | tf_op jit(solution)/shard_map/dot_general | solution.py:149
  157.4 2.6 %collective-permute-start.21 = (f32[5,1,512]{2,1,0:T(1,128)S(1)}, f32[5,1,512]{2,1,0:T(1,128)S(1)}, u32[]{:S(2)}, u32[]{:S(2)}) collective-permute-start(f32[5,1,512]{2,1,0:T(1,128)S(1)} %get-tuple-element.69), channel_id=1, source_target_pairs={{0,4},{4,8},{8,12},{12,16},{16,20},{20,24},{24,28},{1,5},{5,9},{9,... | collective-permute-start | bytes 30728 | tf_op jit(solution)/shard_map/ppermute | solution.py:26
  163.1 3.6 %collective-permute-done.23 = f32[5,64,1]{2,1,0:T(8,128)S(1)} collective-permute-done((f32[5,64,1]{2,1,0:T(8,128)S(1)}, f32[5,64,1]{2,1,0:T(8,128)S(1)}, u32[]{:S(2)}, u32[]{:S(2)}) %collective-permute-start.23) | collective-permute-done | bytes 1312 | tf_op jit(solution)/shard_map/ppermute | solution.py:26
  170.1 6.9 %psum.7 = f32[64]{0:T(128)S(1)} all-reduce(f32[64]{0:T(128)S(1)} %fusion.120), channel_id=1, replica_groups=mesh['sec'=8,'girth'=4] {'girth'}, use_global_device_ids=true, to_apply=%region_4.5 | all-reduce | flops 64 | bytes 512 | tf_op jit(solution)/shard_map/psum | solution.py:185
  (330 shorter events, 77.5 us)
Async XLA Ops:
  4.3 19.3 %collective-permute-start.3 = (f32[5,64,1]{2,1,0:T(8,128)}, f32[5,64,1]{2,1,0:T(8,128)}, u32[]{:S(2)}, u32[]{:S(2)}) collective-permute-start(f32[5,64,1]{2,1,0:T(8,128)} %get-tuple-element.99), channel_id=1, source_target_pairs={{0,1},{1,2},{2,3},{3,0},{4,5},{5,6},{6,7},{7,4},{8,9},{9,10},{10,1... | collective-permute-start | bytes 3848 | tf_op jit(solution)/shard_map/ppermute | solution.py:26
  4.7 18.8 %collective-permute-start.2 = (f32[5,64,1]{2,1,0:T(8,128)}, f32[5,64,1]{2,1,0:T(8,128)}, u32[]{:S(2)}, u32[]{:S(2)}) collective-permute-start(f32[5,64,1]{2,1,0:T(8,128)} %get-tuple-element.98), channel_id=1, source_target_pairs={{1,0},{2,1},{3,2},{0,3},{5,4},{6,5},{7,6},{4,7},{9,8},{10,9},{11,1... | collective-permute-start | bytes 3848 | tf_op jit(solution)/shard_map/ppermute | solution.py:29
  6.7 18.7 %collective-permute-start.1 = (f32[5,1,512]{2,1,0:T(1,128)S(1)}, f32[5,1,512]{2,1,0:T(1,128)S(1)}, u32[]{:S(2)}, u32[]{:S(2)}) collective-permute-start(f32[5,1,512]{2,1,0:T(1,128)S(1)} %get-tuple-element.97), channel_id=1, source_target_pairs={{0,4},{4,8},{8,12},{12,16},{16,20},{20,24},{24,28},{1,5},{5,9},{9,... | collective-permute-start | bytes 30728 | tf_op jit(solution)/shard_map/ppermute | solution.py:26
  10.9 14.5 %collective-permute-start = (f32[5,1,512]{2,1,0:T(1,128)S(1)}, f32[5,1,512]{2,1,0:T(1,128)}, u32[]{:S(2)}, u32[]{:S(2)}) collective-permute-start(f32[5,1,512]{2,1,0:T(1,128)S(1)} %get-tuple-element.96), channel_id=1, source_target_pairs={{4,0},{8,4},{12,8},{16,12},{20,16},{24,20},{28,24},{5,1},{9,5},{13... | collective-permute-start | bytes 30728 | tf_op jit(solution)/shard_map/ppermute | solution.py:29
  15.8 15.8 %all-to-all-start = ((f32[6,32,16]{2,0,1:T(8,128)}), f32[6,32,16]{2,0,1:T(8,128)S(1)}, u32[]{:S(2)}, u32[]{:S(2)}) async-start(f32[6,32,16]{2,0,1:T(8,128)} %copy.42), calls=%async_computation | async-start | bytes 262144 | tf_op jit(solution)/shard_map/all_to_all | solution.py:144
  32.4 12.2 %all-to-all-start.1 = ((f32[5,32,16]{2,0,1:T(8,128)}), f32[5,32,16]{2,0,1:T(8,128)S(1)}, u32[]{:S(2)}, u32[]{:S(2)}) async-start(f32[5,32,16]{2,0,1:T(8,128)} %copy.44), calls=%async_computation.1 | async-start | bytes 262144 | tf_op jit(solution)/shard_map/all_to_all | solution.py:146
  50.2 12.0 %collective-permute-start.7 = (f32[5,64,1]{2,1,0:T(8,128)}, f32[5,64,1]{2,1,0:T(8,128)S(1)}, u32[]{:S(2)}, u32[]{:S(2)}) collective-permute-start(f32[5,64,1]{2,1,0:T(8,128)} %get-tuple-element.93), channel_id=1, source_target_pairs={{0,1},{1,2},{2,3},{3,0},{4,5},{5,6},{6,7},{7,4},{8,9},{9,10},{10,1... | collective-permute-start | bytes 3848 | tf_op jit(solution)/shard_map/ppermute | solution.py:26
  50.5 11.7 %collective-permute-start.6 = (f32[5,64,1]{2,1,0:T(8,128)}, f32[5,64,1]{2,1,0:T(8,128)S(1)}, u32[]{:S(2)}, u32[]{:S(2)}) collective-permute-start(f32[5,64,1]{2,1,0:T(8,128)} %get-tuple-element.92), channel_id=1, source_target_pairs={{1,0},{2,1},{3,2},{0,3},{5,4},{6,5},{7,6},{4,7},{9,8},{10,9},{11,1... | collective-permute-start | bytes 3848 | tf_op jit(solution)/shard_map/ppermute | solution.py:29
  52.0 10.2 %collective-permute-start.5 = (f32[5,1,512]{2,1,0:T(1,128)S(1)}, f32[5,1,512]{2,1,0:T(1,128)S(1)}, u32[]{:S(2)}, u32[]{:S(2)}) collective-permute-start(f32[5,1,512]{2,1,0:T(1,128)S(1)} %get-tuple-element.95), channel_id=1, source_target_pairs={{0,4},{4,8},{8,12},{12,16},{16,20},{20,24},{24,28},{1,5},{5,9},{9,... | collective-permute-start | bytes 30728 | tf_op jit(solution)/shard_map/ppermute | solution.py:26
  54.6 7.6 %collective-permute-start.4 = (f32[5,1,512]{2,1,0:T(1,128)S(1)}, f32[5,1,512]{2,1,0:T(1,128)S(1)}, u32[]{:S(2)}, u32[]{:S(2)}) collective-permute-start(f32[5,1,512]{2,1,0:T(1,128)S(1)} %get-tuple-element.94), channel_id=1, source_target_pairs={{4,0},{8,4},{12,8},{16,12},{20,16},{24,20},{28,24},{5,1},{9,5},{13... | collective-permute-start | bytes 30728 | tf_op jit(solution)/shard_map/ppermute | solution.py:29
  57.5 22.2 %all-to-all-start.2 = ((f32[6,32,16]{2,0,1:T(8,128)}), f32[6,32,16]{2,0,1:T(8,128)}, u32[]{:S(2)}, u32[]{:S(2)}) async-start(f32[6,32,16]{2,0,1:T(8,128)} %copy.47), calls=%async_computation.2 | async-start | bytes 262144 | tf_op jit(solution)/shard_map/all_to_all | solution.py:144
  65.7 6.7 %collective-permute-start.11 = (f32[5,64,1]{2,1,0:T(8,128)S(1)}, f32[5,64,1]{2,1,0:T(8,128)S(1)}, u32[]{:S(2)}, u32[]{:S(2)}) collective-permute-start(f32[5,64,1]{2,1,0:T(8,128)S(1)} %get-tuple-element.87), channel_id=1, source_target_pairs={{0,1},{1,2},{2,3},{3,0},{4,5},{5,6},{6,7},{7,4},{8,9},{9,10},{10,1... | collective-permute-start | bytes 3848 | tf_op jit(solution)/shard_map/ppermute | solution.py:26
  66.0 6.5 %collective-permute-start.10 = (f32[5,64,1]{2,1,0:T(8,128)S(1)}, f32[5,64,1]{2,1,0:T(8,128)S(1)}, u32[]{:S(2)}, u32[]{:S(2)}) collective-permute-start(f32[5,64,1]{2,1,0:T(8,128)S(1)} %get-tuple-element.86), channel_id=1, source_target_pairs={{1,0},{2,1},{3,2},{0,3},{5,4},{6,5},{7,6},{4,7},{9,8},{10,9},{11,1... | collective-permute-start | bytes 3848 | tf_op jit(solution)/shard_map/ppermute | solution.py:29
  82.3 13.8 %all-to-all-start.3 = ((f32[5,32,16]{2,0,1:T(8,128)}), f32[5,32,16]{2,0,1:T(8,128)}, u32[]{:S(2)}, u32[]{:S(2)}) async-start(f32[5,32,16]{2,0,1:T(8,128)} %copy.49), calls=%async_computation.3 | async-start | bytes 262144 | tf_op jit(solution)/shard_map/all_to_all | solution.py:146
  103.3 11.9 %collective-permute-start.15 = (f32[5,64,1]{2,1,0:T(8,128)}, f32[5,64,1]{2,1,0:T(8,128)S(1)}, u32[]{:S(2)}, u32[]{:S(2)}) collective-permute-start(f32[5,64,1]{2,1,0:T(8,128)} %get-tuple-element.81), channel_id=1, source_target_pairs={{0,1},{1,2},{2,3},{3,0},{4,5},{5,6},{6,7},{7,4},{8,9},{9,10},{10,1... | collective-permute-start | bytes 3848 | tf_op jit(solution)/shard_map/ppermute | solution.py:26
  103.5 11.7 %collective-permute-start.14 = (f32[5,64,1]{2,1,0:T(8,128)}, f32[5,64,1]{2,1,0:T(8,128)}, u32[]{:S(2)}, u32[]{:S(2)}) collective-permute-start(f32[5,64,1]{2,1,0:T(8,128)} %get-tuple-element.80), channel_id=1, source_target_pairs={{1,0},{2,1},{3,2},{0,3},{5,4},{6,5},{7,6},{4,7},{9,8},{10,9},{11,1... | collective-permute-start | bytes 3848 | tf_op jit(solution)/shard_map/ppermute | solution.py:29
  105.1 10.2 %collective-permute-start.13 = (f32[5,1,512]{2,1,0:T(1,128)}, f32[5,1,512]{2,1,0:T(1,128)S(1)}, u32[]{:S(2)}, u32[]{:S(2)}) collective-permute-start(f32[5,1,512]{2,1,0:T(1,128)} %get-tuple-element.83), channel_id=1, source_target_pairs={{0,4},{4,8},{8,12},{12,16},{16,20},{20,24},{24,28},{1,5},{5,9},{9,... | collective-permute-start | bytes 30728 | tf_op jit(solution)/shard_map/ppermute | solution.py:26
  107.6 7.6 %collective-permute-start.12 = (f32[5,1,512]{2,1,0:T(1,128)}, f32[5,1,512]{2,1,0:T(1,128)}, u32[]{:S(2)}, u32[]{:S(2)}) collective-permute-start(f32[5,1,512]{2,1,0:T(1,128)} %get-tuple-element.82), channel_id=1, source_target_pairs={{4,0},{8,4},{12,8},{16,12},{20,16},{24,20},{28,24},{5,1},{9,5},{13... | collective-permute-start | bytes 30728 | tf_op jit(solution)/shard_map/ppermute | solution.py:29
  110.5 24.3 %all-to-all-start.4 = ((f32[6,32,16]{2,0,1:T(8,128)}), f32[6,32,16]{2,0,1:T(8,128)}, u32[]{:S(2)}, u32[]{:S(2)}) async-start(f32[6,32,16]{2,0,1:T(8,128)} %copy.52), calls=%async_computation.4 | async-start | bytes 262144 | tf_op jit(solution)/shard_map/all_to_all | solution.py:144
  120.9 6.7 %collective-permute-start.19 = (f32[5,64,1]{2,1,0:T(8,128)S(1)}, f32[5,64,1]{2,1,0:T(8,128)S(1)}, u32[]{:S(2)}, u32[]{:S(2)}) collective-permute-start(f32[5,64,1]{2,1,0:T(8,128)S(1)} %get-tuple-element.75), channel_id=1, source_target_pairs={{0,1},{1,2},{2,3},{3,0},{4,5},{5,6},{6,7},{7,4},{8,9},{9,10},{10,1... | collective-permute-start | bytes 3848 | tf_op jit(solution)/shard_map/ppermute | solution.py:26
  121.1 6.5 %collective-permute-start.18 = (f32[5,64,1]{2,1,0:T(8,128)S(1)}, f32[5,64,1]{2,1,0:T(8,128)S(1)}, u32[]{:S(2)}, u32[]{:S(2)}) collective-permute-start(f32[5,64,1]{2,1,0:T(8,128)S(1)} %get-tuple-element.74), channel_id=1, source_target_pairs={{1,0},{2,1},{3,2},{0,3},{5,4},{6,5},{7,6},{4,7},{9,8},{10,9},{11,1... | collective-permute-start | bytes 3848 | tf_op jit(solution)/shard_map/ppermute | solution.py:29
  138.1 13.8 %all-to-all-start.5 = ((f32[5,32,16]{2,0,1:T(8,128)}), f32[5,32,16]{2,0,1:T(8,128)}, u32[]{:S(2)}, u32[]{:S(2)}) async-start(f32[5,32,16]{2,0,1:T(8,128)} %copy.54), calls=%async_computation.5 | async-start | bytes 262144 | tf_op jit(solution)/shard_map/all_to_all | solution.py:146
  157.4 9.4 %collective-permute-start.21 = (f32[5,1,512]{2,1,0:T(1,128)S(1)}, f32[5,1,512]{2,1,0:T(1,128)S(1)}, u32[]{:S(2)}, u32[]{:S(2)}) collective-permute-start(f32[5,1,512]{2,1,0:T(1,128)S(1)} %get-tuple-element.69), channel_id=1, source_target_pairs={{0,4},{4,8},{8,12},{12,16},{16,20},{20,24},{24,28},{1,5},{5,9},{9,... | collective-permute-start | bytes 30728 | tf_op jit(solution)/shard_map/ppermute | solution.py:26
  159.9 6.8 %collective-permute-start.20 = (f32[5,1,512]{2,1,0:T(1,128)S(1)}, f32[5,1,512]{2,1,0:T(1,128)S(1)}, u32[]{:S(2)}, u32[]{:S(2)}) collective-permute-start(f32[5,1,512]{2,1,0:T(1,128)S(1)} %get-tuple-element.68), channel_id=1, source_target_pairs={{4,0},{8,4},{12,8},{16,12},{20,16},{24,20},{28,24},{5,1},{9,5},{13... | collective-permute-start | bytes 30728 | tf_op jit(solution)/shard_map/ppermute | solution.py:29
  (73 other events, 532.1 us)
where the time goes:
time: 181 us; the launch traced here: 180 us
  starting transfers between devices  70.6 us (39%)
  other arithmetic  33.8 us (19%)
  waiting for transfers between devices  31.5 us (17%)
  local copies, waits for them, and re-layouts  22 us (12%)
  matrix products  12.6 us (7%)
  blocking collectives  6.92 us (4%)
  between operations  2.45 us (1%)
    ppermute x12, starting transfers between devices, extended(): lax.ppermute(lax.slice_in_dim(block, block.shape[dim] - width, None, axis...  20.6 us
    all_to_all x3, waiting for transfers between devices, weld_force(): lax.all_to_all(on_far, ('sec', 'girth'), split_axis=1, concat_axis=1, til...  18.4 us
    ppermute x12, starting transfers between devices, extended(): lax.ppermute(lax.slice_in_dim(block, 0, width, axis=dim), axis, backward)  17.6 us
    all_to_all x3, starting transfers between devices, weld_force(): lax.all_to_all(outgoing, ('sec', 'girth'), split_axis=1, concat_axis=1, t...  17 us
    all_to_all x3, starting transfers between devices, weld_force(): lax.all_to_all(on_far, ('sec', 'girth'), split_axis=1, concat_axis=1, til...  15.4 us
    unnamed x17, other arithmetic  8.35 us
    dot_general x3, matrix products, weld_force(): jnp.dot(spread, column_select, precision=lax.Precision.HIGHEST, preferred...  8.08 us
    ppermute x12, waiting for transfers between devices, extended(): lax.ppermute(lax.slice_in_dim(block, 0, width, axis=dim), axis, backward)  7.57 us
  transfers between devices with their start and end apart: 30, of which 7 were waited for; matrix products, arithmetic and copies ran while one was open for 17% of the time, Pallas kernels for 0%

commit v1 on v0

v1 whole, which is shorter than its diff:
```python
import functools

import jax
import jax.numpy as jnp
from jax import lax
from jax.experimental import pallas as pl
from jax.experimental.pallas import tpu as pltpu
from jax.sharding import PartitionSpec as P

STEPS = 3
FIELDS = 5
RESULTS = 8
PAD_ROWS = 8
LANES = 128
VMEM_BYTES = 40 * 1024 * 1024

young_modulus = 4.0
poisson_ratio = 0.3
plate_modulus = young_modulus / (1.0 - poisson_ratio * poisson_ratio)
shear_modulus = young_modulus / (2.0 * (1.0 + poisson_ratio))
shear_factor = 5.0 / 6.0
time_step = 0.2
spacing_mm = 50.0
rotary_share = 1.0 / 12.0

F32 = jnp.float32
BF16 = jnp.bfloat16


def split(values):
    high = values.astype(BF16)
    low = (values - high.astype(F32)).astype(BF16)
    return high, low


def dot(a, b, contract):
    return lax.dot_general(a, b, (contract, ((), ())), preferred_element_type=F32)


def slot_marks(devices, slots):
    total = devices * slots
    lane = lax.broadcasted_iota(jnp.int32, (devices, total), 1)
    device = lax.broadcasted_iota(jnp.int32, (devices, total), 0)
    by_device = (lane // slots == device).astype(F32).astype(BF16)
    lane = lax.broadcasted_iota(jnp.int32, (slots, total), 1)
    place = lax.broadcasted_iota(jnp.int32, (slots, total), 0)
    by_place = (lane % slots == place).astype(F32)
    return by_device, by_place


def expand(blocks, by_device, by_place):
    slots, total = by_place.shape
    wide = dot(blocks, by_device, ((0,), (0,)))
    wide = wide.reshape(wide.shape[0] // slots, slots, total) * by_place[None]
    return jnp.sum(wide, axis=1)


def collapse(rows, by_device, by_place):
    slots, _ = by_place.shape
    marks = by_place.astype(BF16)
    pieces = []
    for part in (0, 1):
        blocks = [split(row)[part] * marks for row in rows]
        blocks += [jnp.zeros_like(marks)] * (LANES // slots - len(rows))
        pieces.append(jnp.concatenate(blocks, axis=0))
    return dot(by_device, pieces[0], ((1,), (1,))) + dot(by_device, pieces[1], ((1,), (1,)))


def pick(fields, column_marks, row_marks):
    rows = fields[0].shape[0]
    parts = [split(field) for field in fields]
    high = jnp.concatenate([part[0] for part in parts], axis=0)
    low = jnp.concatenate([part[1] for part in parts], axis=0)
    by_column = dot(high, column_marks, ((1,), (0,))) + dot(low, column_marks, ((1,), (0,)))
    marks = row_marks.astype(F32)
    return [
        jnp.sum(by_column[rows * f : rows * (f + 1)] * marks, axis=0, keepdims=True)
        for f in range(len(fields))
    ]


def spread(pulls, column_marks, row_marks):
    high, low = split(pulls)
    total = None
    for part in (high, low):
        marked = jnp.concatenate(
            [part[f : f + 1] * row_marks for f in range(FIELDS)], axis=0
        )
        summed = dot(marked, column_marks, ((1,), (1,)))
        total = summed if total is None else total + summed
    return total


def place():
    sec, girth = lax.axis_index("sec"), lax.axis_index("girth")
    return sec, girth, lax.axis_size("sec"), lax.axis_size("girth")


def tile_of(ref, device):
    return ref[pl.ds(pl.multiple_of(device * 8, 8), 8), :]


def set_tile(ref, device, value):
    ref[pl.ds(pl.multiple_of(device * 8, 8), 8), :] = value


def girth_neighbours():
    sec, girth, _, girths = place()
    left = sec * girths + lax.rem(girth + girths - 1, girths)
    right = sec * girths + lax.rem(girth + 1, girths)
    return left, right


def corner_neighbours():
    sec, girth, secs, girths = place()
    me = sec * girths + girth
    out = []
    for step in (-1, 1):
        row = sec + step
        inside = jnp.logical_and(row >= 0, row < secs)
        for turn in (girths - 1, 1):
            device = row * girths + lax.rem(girth + turn, girths)
            out.append((jnp.where(inside, device, me), inside))
    return out


def edge_rows(columns):
    rows = columns[0][0].shape[0]
    lane = lax.broadcasted_iota(jnp.int32, (rows, LANES), 1)
    halves = [jnp.zeros((rows, LANES), F32), jnp.zeros((rows, LANES), F32)]
    for value, source, half, row in columns:
        moved = pltpu.roll(value, (row - source) % LANES, 1)
        halves[half] = jnp.where(lane == row, moved, halves[half])
    return jnp.concatenate(halves, axis=0).T


def edge_columns(left_tile, right_tile):
    stacked = jnp.concatenate(
        [left_tile, right_tile, jnp.zeros((LANES - 16, LANES), F32)], axis=0
    )
    turned = stacked.T
    return turned[: LANES // 2], turned[LANES // 2 :]


def edge_block(pieces):
    rows = pieces[0][0].shape[0]
    lane = lax.broadcasted_iota(jnp.int32, (rows, LANES), 1)
    block = jnp.zeros((rows, LANES), F32)
    for value, source, target in pieces:
        block = jnp.where(lane == target, pltpu.roll(value, (target - source) % LANES, 1), block)
    return block


def row_chunk(ref, f, start):
    count = ref.shape[1]
    if start < 0:
        return jnp.concatenate([ref[f, count + start : count, :], ref[f, 0 : 8 + start, :]], axis=0)
    if start + 8 > count:
        return jnp.concatenate([ref[f, start:count, :], ref[f, 0 : start + 8 - count, :]], axis=0)
    return ref[f, start : start + 8, :]


def difference_x(ref, f, start):
    return row_chunk(ref, f, start + 1) - row_chunk(ref, f, start - 1)


def difference_y(value):
    lanes = value.shape[1]
    return pltpu.roll(value, lanes - 1, 1) - pltpu.roll(value, 1, 1)


def radial_return(xx, yy, xy):
    offset = xx - 0.5 * yy
    square = offset * offset + 0.75 * yy * yy + 3.0 * xy * xy
    scale = lax.rsqrt(jnp.maximum(square, 1.0))
    return xx * scale, yy * scale, xy * scale


def stress_chunk(vel_ref, stress, plate, start):
    current = [vel_ref[f, start : start + 8, :] for f in range(FIELDS)]
    along_x = [difference_x(vel_ref, f, start) for f in range(FIELDS)]
    along_y = [difference_y(value) for value in current]
    normal = 0.5 * time_step * plate_modulus
    skew = 0.5 * time_step * shear_modulus
    arm = 0.5 * plate
    membrane = radial_return(
        stress[0] + normal * (along_x[0] + poisson_ratio * along_y[1]),
        stress[1] + normal * (along_y[1] + poisson_ratio * along_x[0]),
        stress[2] + skew * (along_y[0] + along_x[1]),
    )
    bending = radial_return(
        stress[3] + (normal * arm) * (along_x[3] + poisson_ratio * along_y[4]),
        stress[4] + (normal * arm) * (along_y[4] + poisson_ratio * along_x[3]),
        stress[5] + (skew * arm) * (along_y[3] + along_x[4]),
    )
    shear = (
        stress[6] + skew * (along_x[2] + 2.0 * current[3]),
        stress[7] + skew * (along_y[2] + 2.0 * current[4]),
    )
    return membrane + bending + shear


def resultants(stress, plate):
    arm = plate * plate * (1.0 / 6.0)
    shear = shear_factor * plate
    return (
        [plate * value for value in stress[0:3]]
        + [arm * value for value in stress[3:6]]
        + [shear * value for value in stress[6:8]]
    )


def force_chunk(res_ref, start, cols):
    def both(x, y):
        along_x = difference_x(res_ref, x, start)[:, :cols]
        along_y = difference_y(res_ref[y, start : start + 8, :])[:, :cols]
        return 0.5 * (along_x + along_y)

    return [
        both(0, 2),
        both(2, 1),
        both(6, 7),
        both(3, 5) - res_ref[6, start : start + 8, :cols],
        both(5, 4) - res_ref[7, start : start + 8, :cols],
    ]


def send_edges(payload, near, far, halo_rows, corners):
    devices = payload.shape[0] // 8
    payload[...] = jnp.zeros(payload.shape, F32)
    payload[pl.ds(0, devices, stride=8), :] = near
    payload[pl.ds(1, devices, stride=8), :] = far
    row = lax.broadcasted_iota(jnp.int32, (8, LANES), 0)
    for device, tile in zip(girth_neighbours(), (halo_rows[0:8], halo_rows[8:16])):
        set_tile(payload, device, jnp.where(row < 2, tile_of(payload, device), tile))
    for (device, _), corner in zip(corner_neighbours(), corners):
        set_tile(payload, device, jnp.where(row == 7, corner, tile_of(payload, device)))


def start_kernel(
    disp, stress, thickness, weld_from, weld_to, weld_stiff,
    payload, to_next, to_last, column_marks, row_marks, picked, spring,
):
    rows, cols = thickness.shape
    _, devices, slots = weld_from.shape
    shift = cols.bit_length() - 1
    by_device, by_place = slot_marks(devices, slots)
    near, far = weld_from[0], weld_to[0]
    stiff = jnp.where(near >= 0, weld_stiff[0], 0.0)
    index_parts = []
    for index in (near, far):
        index = jnp.maximum(index, 0)
        column = index & (cols - 1)
        index_parts += [index >> shift, column >> 1, column & 1]
    index_parts = [part.astype(F32).astype(BF16) for part in index_parts]
    index_parts += list(split(stiff))
    wide = [expand(part, by_device, by_place) for part in index_parts]
    row_index = jnp.concatenate([wide[0], wide[3]], axis=1)
    column_index = jnp.concatenate([2.0 * wide[1] + wide[2], 2.0 * wide[4] + wide[5]], axis=1)
    stiff_row = wide[6] + wide[7]
    total = row_index.shape[1]
    spring[...] = jnp.broadcast_to(stiff_row, spring.shape)
    row_iota = lax.broadcasted_iota(jnp.int32, (rows, total), 0).astype(F32)
    row_hits = (row_iota == row_index).astype(F32).astype(BF16)
    row_marks[...] = row_hits
    for start in range(0, cols, 64):
        iota = (lax.broadcasted_iota(jnp.int32, (64, total), 0) + start).astype(F32)
        column_marks[start : start + 64, :] = (iota == column_index).astype(F32).astype(BF16)
    values = pick([disp[f] for f in range(FIELDS)], column_marks[...], row_hits)
    picked[...] = jnp.concatenate(values + [values[0]] * 3, axis=0)
    half = total // 2
    near_out = collapse([value[:, :half] for value in values] + [stiff_row], by_device, by_place)
    far_out = collapse([value[:, half:] for value in values], by_device, by_place)

    plate = thickness[...].astype(F32) * (1.0 / spacing_mm)
    columns = []
    for f in range(RESULTS + 1):
        left = stress[f, :, 0:LANES] if f < RESULTS else plate[:, 0:LANES]
        right = stress[f, :, cols - LANES :] if f < RESULTS else plate[:, cols - LANES :]
        columns.append((left, 0, f // 5, 2 + f % 5))
        columns.append((right, LANES - 1, f // 5, 10 + f % 5))
    halo_rows = edge_rows(columns)
    send_edges(payload, near_out, far_out, halo_rows, [])
    for ref, row in ((to_next, rows - 1), (to_last, 0)):
        ref[...] = jnp.zeros(ref.shape, F32)
        for f in range(RESULTS):
            ref[f : f + 1, :] = stress[f, row : row + 1, :]
        ref[RESULTS : RESULTS + 1, :] = plate[row : row + 1, :]


def fill_halo(ref, f, above, below, sides, corner):
    rows, cols = ref.shape[1] - PAD_ROWS, ref.shape[2] - LANES
    depth = above.shape[0]
    ref[f, rows:, :cols] = jnp.concatenate(
        [below, jnp.zeros((PAD_ROWS - 2 * depth, cols), F32), above], axis=0
    )
    ref[f, :rows, cols:] = sides
    ref[f, rows:, cols:] = corner


def load_velocity(vel_ext, velocity, incoming, above, below):
    rows = velocity.shape[1]
    cols = velocity.shape[2]
    left, right = girth_neighbours()
    first, second = edge_columns(tile_of(incoming, left), tile_of(incoming, right))
    row = lax.broadcasted_iota(jnp.int32, (8, LANES), 0)
    corner_tiles = [
        jnp.broadcast_to(jnp.where(inside, tile_of(incoming, device)[7:8], 0.0), (8, LANES))
        for device, inside in corner_neighbours()
    ]
    for f in range(FIELDS):
        vel_ext[f, :rows, :cols] = velocity[f]
        sides = edge_block(
            [
                (first, 2 + f, LANES - 2),
                (second, 2 + f, LANES - 1),
                (first, 10 + f, 0),
                (second, 10 + f, 1),
            ]
        )
        upper = edge_block([(corner_tiles[0], f, LANES - 1), (corner_tiles[1], f, 0)])
        lower = edge_block([(corner_tiles[2], f, LANES - 1), (corner_tiles[3], f, 0)])
        corner = jnp.where(row == 0, lower, jnp.where(row == 7, upper, 0.0))
        fill_halo(
            vel_ext, f, above[2 * f : 2 * f + 2, :], below[2 * f : 2 * f + 2, :], sides, corner
        )


def load_stress(stress_ext, plate_ext, stress, thickness, incoming, above, below):
    rows, cols = thickness.shape
    left, right = girth_neighbours()
    halves = edge_columns(tile_of(incoming, left), tile_of(incoming, right))
    plate_ext[0, :rows, :cols] = thickness[...].astype(F32) * (1.0 / spacing_mm)
    empty = jnp.zeros((PAD_ROWS, LANES), F32)
    for f in range(RESULTS + 1):
        lane = 2 + f % 5
        half = halves[f // 5]
        sides = edge_block([(half, lane, LANES - 1), (half, 8 + lane, 0)])
        ref, k = (stress_ext, f) if f < RESULTS else (plate_ext, 0)
        if f < RESULTS:
            ref[k, :rows, :cols] = stress[f]
        fill_halo(ref, k, above[f : f + 1, :], below[f : f + 1, :], sides, empty)


def step_kernel(first, last, *refs):
    if first:
        (incoming, above, below, stress, thickness, velocity, disp, pressure,
         column_marks, row_marks, picked, spring) = refs[:12]
        out = refs[12:]
        plate_ext, spring_out = out[:2]
        out = out[2:]
    else:
        (incoming, above, below, stress, plate_ext, velocity, disp, pressure,
         column_marks, row_marks, picked, spring) = refs[:12]
        out = refs[12:]
    stress_ext, velocity_out, disp_out = out[:3]
    out = out[3:]
    if last:
        to_left, to_right, to_next, to_last, res_ext, vel_ext, weld = out
    else:
        picked_out, payload, to_next, to_last, res_ext, vel_ext, weld = out

    _, rows, cols = velocity.shape
    devices = incoming.shape[0] // 8
    total = picked.shape[1]
    half = total // 2
    by_device, by_place = slot_marks(devices, half // devices)

    other = []
    for row in (1, 0):
        high, low = split(incoming[pl.ds(row, devices, stride=8), :])
        other.append(expand(high, by_device, by_place) + expand(low, by_device, by_place))
    if first:
        stiffness = jnp.concatenate([spring[0:1, :], other[1][5:6]], axis=1)
        spring_out[...] = jnp.broadcast_to(stiffness, spring_out.shape)
    else:
        stiffness = spring[0:1, :]
    field = lax.broadcasted_iota(jnp.int32, (8, total), 0)
    scale = jnp.where(field < 3, 1.0, rotary_share) * stiffness
    pulls = scale * (jnp.concatenate(other, axis=1) - picked[...])
    weld[...] = spread(pulls, column_marks[...], row_marks[...])

    if first:
        load_stress(stress_ext, plate_ext, stress, thickness, incoming, above, below)
        for start in range(0, rows + PAD_ROWS, 8):
            chunk = [stress_ext[k, start : start + 8, :] for k in range(RESULTS)]
            for k, value in enumerate(resultants(chunk, plate_ext[0, start : start + 8, :])):
                res_ext[k, start : start + 8, :] = value
    else:
        load_velocity(vel_ext, velocity, incoming, above, below)
        for start in range(0, rows + PAD_ROWS, 8):
            plate = plate_ext[0, start : start + 8, :]
            chunk = [stress[k, start : start + 8, :] for k in range(RESULTS)]
            chunk = stress_chunk(vel_ext, chunk, plate, start)
            for k, value in enumerate(chunk):
                stress_ext[k, start : start + 8, :] = value
            for k, value in enumerate(resultants(chunk, plate)):
                res_ext[k, start : start + 8, :] = value

    for start in range(0, rows, 8):
        part = slice(start, start + 8)
        plate = plate_ext[0, part, :cols]
        linear = time_step / plate
        angular = (12.0 * linear) / (1.0 + plate * plate)
        force = force_chunk(res_ext, start, cols)
        force[2] = force[2] + pressure[part, :]
        for f in range(FIELDS):
            joined = force[f] + weld[f * rows + start : f * rows + start + 8, :]
            speed = velocity[f, part, :] + (linear if f < 3 else angular) * joined
            velocity_out[f, part, :] = speed
            disp_out[f, part, :] = disp[f, part, :] + time_step * speed

    ends = (cols - LANES, cols)
    if last:
        columns = []
        for f in range(FIELDS):
            columns.append((velocity_out[f, :, 0:LANES], 0, 0, f))
            columns.append((velocity_out[f, :, ends[0] : ends[1]], LANES - 1, 0, 8 + f))
        halo_rows = edge_rows(columns)
        to_left[...] = halo_rows[0:8]
        to_right[...] = halo_rows[8:16]
        for ref, row in ((to_next, rows - 1), (to_last, 0)):
            ref[...] = jnp.zeros(ref.shape, F32)
            for f in range(FIELDS):
                ref[f : f + 1, :] = velocity_out[f, row : row + 1, :]
        return
    values = pick([disp_out[f] for f in range(FIELDS)], column_marks[...], row_marks[...])
    picked_out[...] = jnp.concatenate(values + [values[0]] * 3, axis=0)
    near_out = collapse([value[:, :half] for value in values], by_device, by_place)
    far_out = collapse([value[:, half:] for value in values], by_device, by_place)
    columns = []
    for f in range(FIELDS):
        left_lanes = velocity_out[f, :, 0:LANES]
        right_lanes = velocity_out[f, :, ends[0] : ends[1]]
        for depth in (0, 1):
            columns.append((left_lanes, depth, depth, 2 + f))
            columns.append((right_lanes, LANES - 2 + depth, depth, 10 + f))
    corners = []
    lane = lax.broadcasted_iota(jnp.int32, (8, LANES), 1)
    for row in (0, rows - 1):
        tile = slice(row // 8 * 8, row // 8 * 8 + 8)
        for side in (0, 1):
            value = jnp.zeros((8, LANES), F32)
            for f in range(FIELDS):
                part = velocity_out[f, tile, ends[0] : ends[1]] if side else velocity_out[f, tile, 0:LANES]
                source = LANES - 1 if side else 0
                value = jnp.where(lane == f, pltpu.roll(part, (f - source) % LANES, 1), value)
            corners.append(jnp.broadcast_to(value[row % 8 : row % 8 + 1], (8, LANES)))
    send_edges(payload, near_out, far_out, edge_rows(columns), corners)
    for ref, start in ((to_next, rows - 2), (to_last, 0)):
        ref[...] = jnp.zeros(ref.shape, F32)
        for f in range(FIELDS):
            ref[2 * f : 2 * f + 2, :] = velocity_out[f, start : start + 2, :]


def final_kernel(
    from_left, from_right, above, below, stress, plate_ext, velocity, height,
    stress_out, moment, vel_ext,
):
    _, rows, cols = velocity.shape
    first, _ = edge_columns(from_left[...], from_right[...])
    empty = jnp.zeros((PAD_ROWS, LANES), F32)
    for f in range(FIELDS):
        vel_ext[f, :rows, :cols] = velocity[f]
        sides = edge_block([(first, f, LANES - 1), (first, 8 + f, 0)])
        fill_halo(vel_ext, f, above[f : f + 1, :], below[f : f + 1, :], sides, empty)
    weight = height[0:1, :]
    parts = []
    for start in range(0, rows, 8):
        part = slice(start, start + 8)
        chunk = [stress[k, part, :] for k in range(RESULTS)]
        plate = plate_ext[0, part, :]
        chunk = stress_chunk(vel_ext, chunk, plate, start)
        for k, value in enumerate(chunk):
            stress_out[k, part, :] = value[:, :cols]
        weighted = plate[:, :cols] * chunk[0][:, :cols] * weight
        parts.append(jnp.sum(weighted, axis=1, keepdims=True))
    column = jnp.broadcast_to(jnp.concatenate(parts, axis=0), (rows, LANES))
    if rows < LANES:
        column = jnp.concatenate([column, jnp.zeros((LANES - rows, LANES), F32)], axis=0)
    moment[...] = column.T[0:8, :rows]


def call(kernel, outs, scratch, *operands):
    whole = pl.BlockSpec(memory_space=pltpu.VMEM)
    return pl.pallas_call(
        kernel,
        out_shape=[jax.ShapeDtypeStruct(shape, dtype) for shape, dtype in outs],
        in_specs=[whole] * len(operands),
        out_specs=[whole] * len(outs),
        scratch_shapes=[pltpu.VMEM(shape, dtype) for shape, dtype in scratch],
        compiler_params=pltpu.CompilerParams(vmem_limit_bytes=VMEM_BYTES),
    )(*operands)


def to_next_section(values):
    count = lax.axis_size("sec")
    return lax.ppermute(values, "sec", [(i, i + 1) for i in range(count - 1)])


def to_last_section(values):
    count = lax.axis_size("sec")
    return lax.ppermute(values, "sec", [(i + 1, i) for i in range(count - 1)])


def turn(values, step):
    count = lax.axis_size("girth")
    return lax.ppermute(values, "girth", [(i, (i + step) % count) for i in range(count)])


def local(displacement, velocity, stress, thickness, pressure, weld_from, weld_to, weld_stiff):
    rows, cols = thickness.shape
    _, devices, slots = weld_from.shape
    total = 2 * devices * slots
    girth_total = cols * lax.axis_size("girth")
    column = (lax.axis_index("girth") * cols + lax.iota(jnp.int32, cols)).astype(F32)
    height = jnp.sin(2.0 * jnp.pi / girth_total * (column + 0.5)) / girth_total
    height = jnp.broadcast_to(height[None, :], (8, cols))

    message = (devices * 8, LANES)
    strip = (16, cols)
    block = (FIELDS, rows, cols)
    stress_shape = (RESULTS, rows + PAD_ROWS, cols + LANES)
    plate_shape = (1, rows + PAD_ROWS, cols + LANES)
    slot_rows = (8, total)
    scratch = [
        (stress_shape, F32),
        ((FIELDS, rows + PAD_ROWS, cols + LANES), F32),
        ((FIELDS * rows, cols), F32),
    ]

    payload, to_next, to_last, column_marks, row_marks, picked, spring = call(
        start_kernel,
        [
            (message, F32), (strip, F32), (strip, F32), ((cols, total), BF16),
            ((rows, total), BF16), (slot_rows, F32), ((8, total // 2), F32),
        ],
        [],
        displacement, stress, thickness, weld_from, weld_to, weld_stiff,
    )
    plate = None
    for step in range(STEPS):
        first, last = step == 0, step == STEPS - 1
        incoming = lax.all_to_all(payload, ("sec", "girth"), 0, 0, tiled=True)
        above, below = to_next_section(to_next), to_last_section(to_last)
        outs = [(stress_shape, F32), (block, F32), (block, F32)]
        if first:
            outs = [(plate_shape, F32), (slot_rows, F32)] + outs
        if last:
            edge = (8, LANES)
            outs += [(edge, F32), (edge, F32), ((8, cols), F32), ((8, cols), F32)]
        else:
            outs += [(slot_rows, F32), (message, F32), (strip, F32), (strip, F32)]
        results = call(
            functools.partial(step_kernel, first, last),
            outs,
            scratch,
            incoming, above, below, stress, thickness if first else plate, velocity,
            displacement, pressure, column_marks, row_marks, picked, spring,
        )
        if first:
            plate, spring = results[:2]
            results = results[2:]
        stress, velocity, displacement = results[:3]
        if last:
            to_left, to_right, to_next, to_last = results[3:]
        else:
            picked, payload, to_next, to_last = results[3:]

    from_left, from_right = turn(to_right, 1), turn(to_left, -1)
    above, below = to_next_section(to_next), to_last_section(to_last)
    stress, partial_moment = call(
        final_kernel,
        [((RESULTS, rows, cols), F32), ((8, rows), F32)],
        [((FIELDS, rows + PAD_ROWS, cols + LANES), F32)],
        from_left, from_right, above, below, stress, plate, velocity, height,
    )
    moment = lax.psum(partial_moment[0], "girth")
    return (displacement, velocity, stress, moment)


def solution(mesh):
    in_specs = (
        P(None, "sec", "girth"),
        P(None, "sec", "girth"),
        P(None, "sec", "girth"),
        P("sec", "girth"),
        P("sec", "girth"),
        P(("sec", "girth"), None, None),
        P(("sec", "girth"), None, None),
        P(("sec", "girth"), None, None),
    )
    out_specs = (
        P(None, "sec", "girth"),
        P(None, "sec", "girth"),
        P(None, "sec", "girth"),
        P("sec"),
    )
    return jax.shard_map(local, mesh=mesh, in_specs=in_specs, out_specs=out_specs, check_vma=False)
```

time: 181 us -> 104 us (0.57)
  other arithmetic: 33.8 us -> 0.05 us
  starting transfers between devices: 70.6 us -> 40.6 us
  waiting for transfers between devices: 31.5 us -> 15.8 us
  Pallas kernels: 0 us -> 14 us
  matrix products: 12.6 us -> 0 us
  local copies, waits for them, and re-layouts: 22 us -> 24.5 us
    all_to_all x6 -> x3, waiting for transfers between devices: 20.2 us -> 0.01 us  [local(): incoming = lax.all_to_all(payload, ('sec', 'girth'), 0, 0, tiled=True)]
    unnamed x153 -> x61, local copies, waits for them, and re-layouts: 6.64 us -> 24.5 us
    ppermute x24 -> x10, starting transfers between devices: 38.2 us -> 22.2 us  [the longest x4 15.3 us: to_next_section(): return lax.ppermute(values, 'sec', [(i, i + 1) for i in range(count - 1)])]
    all_to_all x6 -> x3, starting transfers between devices: 32.4 us -> 18.3 us  [local(): incoming = lax.all_to_all(payload, ('sec', 'girth'), 0, 0, tiled=True)]
    mul x23 -> x0, other arithmetic: 14 us -> none  [the longest x5 4.68 us: along_girth(): return 0.5 * (padded[:, :, 2:] - padded[:, :, :-2])]
    pallas_call x0 -> x5, Pallas kernels: none -> 14 us  [call(): pl.pallas_call(kernel, out_shape=[jax.ShapeDtypeStruct(shape, dtype) for...]
    dot_general x6 -> x0, matrix products: 12.6 us -> none  [the longest x3 8.08 us: weld_force(): jnp.dot(spread, column_select, precision=lax.Precision.HIGHEST, preferred...]
    unnamed x17 -> x0, other arithmetic: 8.35 us -> none
  transfers between devices with their start and end apart: 30 -> 13, of which waited for: 7 -> 8; matrix products, arithmetic and copies ran while one was open for 17% -> 0% of each run, Pallas kernels for 0% -> 0%
where the time goes in v1:
time: 104 us; the launch traced here: 102 us
  starting transfers between devices  40.6 us (39%)
  local copies, waits for them, and re-layouts  24.5 us (24%)
  waiting for transfers between devices  15.8 us (15%)
  Pallas kernels  14 us (13%)
  blocking collectives  6.63 us (6%)
    unnamed x61, local copies, waits for them, and re-layouts  24.5 us
    all_to_all x3, starting transfers between devices, local(): incoming = lax.all_to_all(payload, ('sec', 'girth'), 0, 0, tiled=True)  18.3 us
    ppermute x4, starting transfers between devices, to_next_section(): return lax.ppermute(values, 'sec', [(i, i + 1) for i in range(count - 1)])  15.3 us
    pallas_call x5, Pallas kernels, call(): pl.pallas_call(kernel, out_shape=[jax.ShapeDtypeStruct(shape, dtype) for...  14 us
    ppermute x4, waiting for transfers between devices, to_last_section(): return lax.ppermute(values, 'sec', [(i + 1, i) for i in range(count - 1)])  13.4 us
    psum x1, blocking collectives, local(): moment = lax.psum(partial_moment[0], 'girth')  6.63 us
    ppermute x4, starting transfers between devices, to_last_section(): return lax.ppermute(values, 'sec', [(i + 1, i) for i in range(count - 1)])  5.17 us
  transfers between devices with their start and end apart: 13, of which 8 were waited for; matrix products, arithmetic and copies ran while one was open for 0% of the time, Pallas kernels for 0%

profile of v1, /device:TPU:0, one launch (start us, length us, event | category | flops | bytes accessed | tf_op | source)
XLA Modules:
  0.0 102.4 jit_solution(1758062827874550260)
XLA Ops:
  2.9 1.2 %copy-done = f32[8,64,512]{2,1,0:T(8,128)S(1)} copy-done((f32[8,64,512]{2,1,0:T(8,128)S(1)}, f32[8,64,512]{2,1,0:T(8,128)}, u32[]{:S(2)}) %copy-start) | copy-done | bytes 1048600
  6.2 2.0 %shard_map.111 = (f32[256,128]{1,0:T(8,128)}, f32[16,512]{1,0:T(8,128)S(1)}, f32[16,512]{1,0:T(8,128)S(1)}, bf16[512,1024]{1,0:T(8,128)(2,1)S(1)}, bf16[64,1024]...) custom-call(f32[5,64,512]{2,1,0:T(8,128)S(1)} %copy-done.2, f32[8,64,512]{2,1,0:T(8,128)S(1)} %copy-done, ...), custom_call_target="tpu_custom_call" | custom-call | tf_op jit(solution)/shard_map/pallas_call | solution.py:486
  8.8 7.3 %all-to-all-start = ((f32[32,8,128]{2,1,0:T(8,128)}), f32[32,8,128]{2,1,0:T(8,128)S(1)}, u32[]{:S(2)}, u32[]{:S(2)}) async-start(f32[32,8,128]{2,1,0:T(8,128)} %bitcast), calls=%async_computation | async-start | bytes 262144 | tf_op jit(solution)/shard_map/all_to_all | solution.py:544
  16.1 3.7 %collective-permute-start = (f32[16,512]{1,0:T(8,128)S(1)}, f32[16,512]{1,0:T(8,128)S(1)}, u32[]{:S(2)}, u32[]{:S(2)}) collective-permute-start(f32[16,512]{1,0:T(8,128)S(1)} %get-tuple-element.37), channel_id=1, source_target_pairs={{0,4},{4,8},{8,12},{12,16},{16,20},{20,24},{24,28},{1,5},{5,9},{9,... | collective-permute-start | bytes 98312 | tf_op jit(solution)/shard_map/ppermute | solution.py:498
  19.8 1.3 %collective-permute-start.1 = (f32[16,512]{1,0:T(8,128)}, f32[16,512]{1,0:T(8,128)S(1)}, u32[]{:S(2)}, u32[]{:S(2)}) collective-permute-start(f32[16,512]{1,0:T(8,128)} %copy-done.28), channel_id=1, source_target_pairs={{4,0},{8,4},{12,8},{16,12},{20,16},{24,20},{28,24},{5,1},{9,5},{13... | collective-permute-start | bytes 98312 | tf_op jit(solution)/shard_map/ppermute | solution.py:503
  22.0 3.8 %collective-permute-done.1.refs_2_ = f32[16,512]{1,0:T(8,128)S(1)} collective-permute-done((f32[16,512]{1,0:T(8,128)}, f32[16,512]{1,0:T(8,128)S(1)}, u32[]{:S(2)}, u32[]{:S(2)}) %collective-permute-start.1) | collective-permute-done | bytes 32800 | tf_op jit(solution)/shard_map/ppermute | solution.py:503
  29.1 2.7 %shard_map.112 = (f32[1,72,640]{2,1,0:T(8,128)S(1)}, f32[8,1024]{1,0:T(8,128)S(1)}, f32[8,72,640]{2,1,0:T(8,128)S(1)}, f32[5,64,512]{2,1,0:T(8,128)S(1)}, f32[5,...) custom-call(f32[256,128]{1,0:T(8,128)S(1)} %bitcast.8, ...), custom_call_target="tpu_custom_call" | custom-call | tf_op jit(solution)/shard_map/pallas_call | solution.py:486
  37.0 5.5 %all-to-all-start.1 = ((f32[32,8,128]{2,1,0:T(8,128)}), f32[32,8,128]{2,1,0:T(8,128)S(1)}, u32[]{:S(2)}, u32[]{:S(2)}) async-start(f32[32,8,128]{2,1,0:T(8,128)} %bitcast.11), calls=%async_computation.1 | async-start | bytes 262144 | tf_op jit(solution)/shard_map/all_to_all | solution.py:544
  42.6 3.7 %collective-permute-start.2 = (f32[16,512]{1,0:T(8,128)}, f32[16,512]{1,0:T(8,128)S(1)}, u32[]{:S(2)}, u32[]{:S(2)}) collective-permute-start(f32[16,512]{1,0:T(8,128)} %copy-done.27), channel_id=1, source_target_pairs={{0,4},{4,8},{8,12},{12,16},{16,20},{20,24},{24,28},{1,5},{5,9},{9,... | collective-permute-start | bytes 98312 | tf_op jit(solution)/shard_map/ppermute | solution.py:498
  46.2 1.3 %collective-permute-start.3 = (f32[16,512]{1,0:T(8,128)}, f32[16,512]{1,0:T(8,128)S(1)}, u32[]{:S(2)}, u32[]{:S(2)}) collective-permute-start(f32[16,512]{1,0:T(8,128)} %copy-done.26), channel_id=1, source_target_pairs={{4,0},{8,4},{12,8},{16,12},{20,16},{24,20},{28,24},{5,1},{9,5},{13... | collective-permute-start | bytes 98312 | tf_op jit(solution)/shard_map/ppermute | solution.py:503
  48.1 4.1 %collective-permute-done.3.refs_2_ = f32[16,512]{1,0:T(8,128)S(1)} collective-permute-done((f32[16,512]{1,0:T(8,128)}, f32[16,512]{1,0:T(8,128)S(1)}, u32[]{:S(2)}, u32[]{:S(2)}) %collective-permute-start.3) | collective-permute-done | bytes 32800 | tf_op jit(solution)/shard_map/ppermute | solution.py:503
  52.3 1.4 %copy-done.5 = f32[8,72,640]{2,1,0:T(8,128)S(1)} copy-done((f32[8,72,640]{2,1,0:T(8,128)S(1)}, f32[8,72,640]{2,1,0:T(8,128)}, u32[]{:S(2)}) %copy-start.5) | copy-done | bytes 1474584
  56.6 3.9 %shard_map.113 = (f32[8,72,640]{2,1,0:T(8,128)S(1)}, f32[5,64,512]{2,1,0:T(8,128)S(1)}, f32[5,64,512]{2,1,0:T(8,128)S(1)}, f32[8,1024]{1,0:T(8,128)S(1)}, f32[25...) custom-call(f32[256,128]{1,0:T(8,128)S(1)} %bitcast.10, f32[16,512]{1,0:T(8,128)S(1)} %collective-permute-done.2.refs_1_, ...), custom_call_target="tpu_custom_call" | custom-call | tf_op jit(solution)/shard_map/pallas_call | solution.py:486
  62.1 5.5 %all-to-all-start.2 = ((f32[32,8,128]{2,1,0:T(8,128)}), f32[32,8,128]{2,1,0:T(8,128)S(1)}, u32[]{:S(2)}, u32[]{:S(2)}) async-start(f32[32,8,128]{2,1,0:T(8,128)} %bitcast.4), calls=%async_computation.2 | async-start | bytes 262144 | tf_op jit(solution)/shard_map/all_to_all | solution.py:544
  67.6 3.7 %collective-permute-start.4 = (f32[16,512]{1,0:T(8,128)S(1)}, f32[16,512]{1,0:T(8,128)S(1)}, u32[]{:S(2)}, u32[]{:S(2)}) collective-permute-start(f32[16,512]{1,0:T(8,128)S(1)} %get-tuple-element.53), channel_id=1, source_target_pairs={{0,4},{4,8},{8,12},{12,16},{16,20},{20,24},{24,28},{1,5},{5,9},{9,... | collective-permute-start | bytes 98312 | tf_op jit(solution)/shard_map/ppermute | solution.py:498
  71.3 1.3 %collective-permute-start.5 = (f32[16,512]{1,0:T(8,128)S(1)}, f32[16,512]{1,0:T(8,128)S(1)}, u32[]{:S(2)}, u32[]{:S(2)}) collective-permute-start(f32[16,512]{1,0:T(8,128)S(1)} %get-tuple-element.54), channel_id=1, source_target_pairs={{4,0},{8,4},{12,8},{16,12},{20,16},{24,20},{28,24},{5,1},{9,5},{13... | collective-permute-start | bytes 98312 | tf_op jit(solution)/shard_map/ppermute | solution.py:503
  72.9 4.2 %collective-permute-done.5.refs_2_ = f32[16,512]{1,0:T(8,128)S(1)} collective-permute-done((f32[16,512]{1,0:T(8,128)S(1)}, f32[16,512]{1,0:T(8,128)S(1)}, u32[]{:S(2)}, u32[]{:S(2)}) %collective-permute-start.5) | collective-permute-done | bytes 32800 | tf_op jit(solution)/shard_map/ppermute | solution.py:503
  79.3 3.4 %shard_map.114 = (f32[8,72,640]{2,1,0:T(8,128)S(1)}, f32[5,64,512]{2,1,0:T(8,128)}, f32[5,64,512]{2,1,0:T(8,128)}, f32[8,128]{1,0:T(8,128)S(1)}, f32[8,128]{1,0:...) custom-call(f32[256,128]{1,0:T(8,128)S(1)} %bitcast.9, f32[16,512]{1,0:T(8,128)S(1)} %collective-permute-done.4.refs_1_, ...), custom_call_target="tpu_custom_call" | custom-call | tf_op jit(solution)/shard_map/pallas_call | solution.py:486
  82.7 4.3 %collective-permute-start.8 = (f32[8,512]{1,0:T(8,128)S(1)}, f32[8,512]{1,0:T(8,128)S(1)}, u32[]{:S(2)}, u32[]{:S(2)}) collective-permute-start(f32[8,512]{1,0:T(8,128)S(1)} %get-tuple-element.63), channel_id=1, source_target_pairs={{0,4},{4,8},{8,12},{12,16},{16,20},{20,24},{24,28},{1,5},{5,9},{9,... | collective-permute-start | bytes 49160 | tf_op jit(solution)/shard_map/ppermute | solution.py:498
  87.0 1.3 %collective-permute-start.9 = (f32[8,512]{1,0:T(8,128)S(1)}, f32[8,512]{1,0:T(8,128)S(1)}, u32[]{:S(2)}, u32[]{:S(2)}) collective-permute-start(f32[8,512]{1,0:T(8,128)S(1)} %get-tuple-element.64), channel_id=1, source_target_pairs={{4,0},{8,4},{12,8},{16,12},{20,16},{24,20},{28,24},{5,1},{9,5},{13... | collective-permute-start | bytes 49160 | tf_op jit(solution)/shard_map/ppermute | solution.py:503
  88.3 1.7 %collective-permute-start.7 = (f32[8,128]{1,0:T(8,128)S(1)}, f32[8,128]{1,0:T(8,128)S(1)}, u32[]{:S(2)}, u32[]{:S(2)}) collective-permute-start(f32[8,128]{1,0:T(8,128)S(1)} %get-tuple-element.62), channel_id=1, source_target_pairs={{0,3},{1,0},{2,1},{3,2},{4,7},{5,4},{6,5},{7,6},{8,11},{9,8},{10,9... | collective-permute-start | bytes 12296 | tf_op jit(solution)/shard_map/ppermute | solution.py:508
  90.1 1.2 %collective-permute-done.6.from_left = f32[8,128]{1,0:T(8,128)S(1)} collective-permute-done((f32[8,128]{1,0:T(8,128)S(1)}, f32[8,128]{1,0:T(8,128)S(1)}, u32[]{:S(2)}, u32[]{:S(2)}) %collective-permute-start.6) | collective-permute-done | bytes 4128 | tf_op jit(solution)/shard_map/ppermute | solution.py:508
  93.7 2.1 %shard_map.115 = (f32[8,64,512]{2,1,0:T(8,128)}, f32[8,64]{1,0:T(8,128)S(1)}) custom-call(f32[8,128]{1,0:T(8,128)S(1)} %collective-permute-done.6.from_left, f32[8,128]{1,0:T(8,128)S(1)} %collective-permute-done.7.from_right, f32[8,512]{1,0:T(8,128)S(1)} %collective-permute-done.8.above, f32[8,512]{1,0:T(8,128)S(1)} %collective-permute-done.9.below, ...), custom_call_target="tpu_custom_call" | custom-call | tf_op jit(solution)/shard_map/pallas_call | solution.py:486
  95.8 6.6 %psum.7 = f32[64]{0:T(128)} all-reduce(f32[64]{0:T(128)S(1)} %slice_bitcast_fusion), channel_id=1, replica_groups=mesh['sec'=8,'girth'=4] {'girth'}, use_global_device_ids=true, to_apply=%region_0.0 | all-reduce | flops 64 | bytes 512 | tf_op jit(solution)/shard_map/psum | solution.py:578
  (72 shorter events, 24.4 us)
Async XLA Ops:
  2.9 1.2 %copy-start = (f32[8,64,512]{2,1,0:T(8,128)S(1)}, f32[8,64,512]{2,1,0:T(8,128)}, u32[]{:S(2)}) copy-start(f32[8,64,512]{2,1,0:T(8,128)} %refs_3_.1) | copy-start | bytes 3145732
  6.2 20.3 %copy-start.1 = (f32[8,64,512]{2,1,0:T(8,128)S(1)}, f32[8,64,512]{2,1,0:T(8,128)}, u32[]{:S(2)}) copy-start(f32[8,64,512]{2,1,0:T(8,128)} %refs_3_.1) | copy-start | bytes 3145732
  6.2 20.3 %copy-start.3 = (f32[5,64,512]{2,1,0:T(8,128)S(1)}, f32[5,64,512]{2,1,0:T(8,128)}, u32[]{:S(2)}) copy-start(f32[5,64,512]{2,1,0:T(8,128)} %refs_6_.1) | copy-start | bytes 1966084
  6.2 20.3 %copy-start.6 = (f32[64,512]{1,0:T(8,128)S(1)}, f32[64,512]{1,0:T(8,128)}, u32[]{:S(2)}) copy-start(f32[64,512]{1,0:T(8,128)} %refs_7_.5) | copy-start | bytes 393220
  6.2 20.3 %copy-start.18 = (s32[64,512]{1,0:T(8,128)S(1)}, s32[64,512]{1,0:T(8,128)}, u32[]{:S(2)}) copy-start(s32[64,512]{1,0:T(8,128)} %refs_4_.1) | copy-start | bytes 393220
  8.8 17.6 %all-to-all-start = ((f32[32,8,128]{2,1,0:T(8,128)}), f32[32,8,128]{2,1,0:T(8,128)S(1)}, u32[]{:S(2)}, u32[]{:S(2)}) async-start(f32[32,8,128]{2,1,0:T(8,128)} %bitcast), calls=%async_computation | async-start | bytes 262144 | tf_op jit(solution)/shard_map/all_to_all | solution.py:544
  16.1 5.3 %collective-permute-start = (f32[16,512]{1,0:T(8,128)S(1)}, f32[16,512]{1,0:T(8,128)S(1)}, u32[]{:S(2)}, u32[]{:S(2)}) collective-permute-start(f32[16,512]{1,0:T(8,128)S(1)} %get-tuple-element.37), channel_id=1, source_target_pairs={{0,4},{4,8},{8,12},{12,16},{16,20},{20,24},{24,28},{1,5},{5,9},{9,... | collective-permute-start | bytes 98312 | tf_op jit(solution)/shard_map/ppermute | solution.py:498
  19.8 6.0 %collective-permute-start.1 = (f32[16,512]{1,0:T(8,128)}, f32[16,512]{1,0:T(8,128)S(1)}, u32[]{:S(2)}, u32[]{:S(2)}) collective-permute-start(f32[16,512]{1,0:T(8,128)} %copy-done.28), channel_id=1, source_target_pairs={{4,0},{8,4},{12,8},{16,12},{20,16},{24,20},{28,24},{5,1},{9,5},{13... | collective-permute-start | bytes 98312 | tf_op jit(solution)/shard_map/ppermute | solution.py:503
  26.5 1.1 %copy-start.8 = (f32[5,64,512]{2,1,0:T(8,128)S(1)}, f32[5,64,512]{2,1,0:T(8,128)}, u32[]{:S(2)}) copy-start(f32[5,64,512]{2,1,0:T(8,128)} %refs_5_.1) | copy-start | bytes 1966084
  31.7 1.2 %copy-start.4 = (f32[8,72,640]{2,1,0:T(8,128)}, f32[8,72,640]{2,1,0:T(8,128)S(1)}, u32[]{:S(2)}) copy-start(f32[8,72,640]{2,1,0:T(8,128)S(1)} %get-tuple-element.46.refs_3_) | copy-start | bytes 4423684
  37.0 15.2 %all-to-all-start.1 = ((f32[32,8,128]{2,1,0:T(8,128)}), f32[32,8,128]{2,1,0:T(8,128)S(1)}, u32[]{:S(2)}, u32[]{:S(2)}) async-start(f32[32,8,128]{2,1,0:T(8,128)} %bitcast.11), calls=%async_computation.1 | async-start | bytes 262144 | tf_op jit(solution)/shard_map/all_to_all | solution.py:544
  42.6 5.6 %collective-permute-start.2 = (f32[16,512]{1,0:T(8,128)}, f32[16,512]{1,0:T(8,128)S(1)}, u32[]{:S(2)}, u32[]{:S(2)}) collective-permute-start(f32[16,512]{1,0:T(8,128)} %copy-done.27), channel_id=1, source_target_pairs={{0,4},{4,8},{8,12},{12,16},{16,20},{20,24},{24,28},{1,5},{5,9},{9,... | collective-permute-start | bytes 98312 | tf_op jit(solution)/shard_map/ppermute | solution.py:498
  46.2 6.0 %collective-permute-start.3 = (f32[16,512]{1,0:T(8,128)}, f32[16,512]{1,0:T(8,128)S(1)}, u32[]{:S(2)}, u32[]{:S(2)}) collective-permute-start(f32[16,512]{1,0:T(8,128)} %copy-done.26), channel_id=1, source_target_pairs={{4,0},{8,4},{12,8},{16,12},{20,16},{24,20},{28,24},{5,1},{9,5},{13... | collective-permute-start | bytes 98312 | tf_op jit(solution)/shard_map/ppermute | solution.py:503
  52.3 1.4 %copy-start.5 = (f32[8,72,640]{2,1,0:T(8,128)S(1)}, f32[8,72,640]{2,1,0:T(8,128)}, u32[]{:S(2)}) copy-start(f32[8,72,640]{2,1,0:T(8,128)} %copy-done.4) | copy-start | bytes 4423684
  53.6 1.1 %copy-start.14 = (f32[5,64,512]{2,1,0:T(8,128)S(1)}, f32[5,64,512]{2,1,0:T(8,128)}, u32[]{:S(2)}) copy-start(f32[5,64,512]{2,1,0:T(8,128)} %copy-done.13) | copy-start | bytes 1966084
  62.1 15.0 %all-to-all-start.2 = ((f32[32,8,128]{2,1,0:T(8,128)}), f32[32,8,128]{2,1,0:T(8,128)S(1)}, u32[]{:S(2)}, u32[]{:S(2)}) async-start(f32[32,8,128]{2,1,0:T(8,128)} %bitcast.4), calls=%async_computation.2 | async-start | bytes 262144 | tf_op jit(solution)/shard_map/all_to_all | solution.py:544
  67.6 5.3 %collective-permute-start.4 = (f32[16,512]{1,0:T(8,128)S(1)}, f32[16,512]{1,0:T(8,128)S(1)}, u32[]{:S(2)}, u32[]{:S(2)}) collective-permute-start(f32[16,512]{1,0:T(8,128)S(1)} %get-tuple-element.53), channel_id=1, source_target_pairs={{0,4},{4,8},{8,12},{12,16},{16,20},{20,24},{24,28},{1,5},{5,9},{9,... | collective-permute-start | bytes 98312 | tf_op jit(solution)/shard_map/ppermute | solution.py:498
  71.3 5.8 %collective-permute-start.5 = (f32[16,512]{1,0:T(8,128)S(1)}, f32[16,512]{1,0:T(8,128)S(1)}, u32[]{:S(2)}, u32[]{:S(2)}) collective-permute-start(f32[16,512]{1,0:T(8,128)S(1)} %get-tuple-element.54), channel_id=1, source_target_pairs={{4,0},{8,4},{12,8},{16,12},{20,16},{24,20},{28,24},{5,1},{9,5},{13... | collective-permute-start | bytes 98312 | tf_op jit(solution)/shard_map/ppermute | solution.py:503
  77.1 1.1 %copy-start.10 = (f32[5,64,512]{2,1,0:T(8,128)S(1)}, f32[5,64,512]{2,1,0:T(8,128)}, u32[]{:S(2)}) copy-start(f32[5,64,512]{2,1,0:T(8,128)} %copy-done.9) | copy-start | bytes 1966084
  82.7 8.7 %collective-permute-start.8 = (f32[8,512]{1,0:T(8,128)S(1)}, f32[8,512]{1,0:T(8,128)S(1)}, u32[]{:S(2)}, u32[]{:S(2)}) collective-permute-start(f32[8,512]{1,0:T(8,128)S(1)} %get-tuple-element.63), channel_id=1, source_target_pairs={{0,4},{4,8},{8,12},{12,16},{16,20},{20,24},{24,28},{1,5},{5,9},{9,... | collective-permute-start | bytes 49160 | tf_op jit(solution)/shard_map/ppermute | solution.py:498
  87.0 5.6 %collective-permute-start.9 = (f32[8,512]{1,0:T(8,128)S(1)}, f32[8,512]{1,0:T(8,128)S(1)}, u32[]{:S(2)}, u32[]{:S(2)}) collective-permute-start(f32[8,512]{1,0:T(8,128)S(1)} %get-tuple-element.64), channel_id=1, source_target_pairs={{4,0},{8,4},{12,8},{16,12},{20,16},{24,20},{28,24},{5,1},{9,5},{13... | collective-permute-start | bytes 49160 | tf_op jit(solution)/shard_map/ppermute | solution.py:503
  88.3 3.1 %collective-permute-start.6 = (f32[8,128]{1,0:T(8,128)S(1)}, f32[8,128]{1,0:T(8,128)S(1)}, u32[]{:S(2)}, u32[]{:S(2)}) collective-permute-start(f32[8,128]{1,0:T(8,128)S(1)} %get-tuple-element.61), channel_id=1, source_target_pairs={{0,1},{1,2},{2,3},{3,0},{4,5},{5,6},{6,7},{7,4},{8,9},{9,10},{10,1... | collective-permute-start | bytes 12296 | tf_op jit(solution)/shard_map/ppermute | solution.py:508
  88.3 3.1 %collective-permute-start.7 = (f32[8,128]{1,0:T(8,128)S(1)}, f32[8,128]{1,0:T(8,128)S(1)}, u32[]{:S(2)}, u32[]{:S(2)}) collective-permute-start(f32[8,128]{1,0:T(8,128)S(1)} %get-tuple-element.62), channel_id=1, source_target_pairs={{0,3},{1,0},{2,1},{3,2},{4,7},{5,4},{6,5},{7,6},{8,11},{9,8},{10,9... | collective-permute-start | bytes 12296 | tf_op jit(solution)/shard_map/ppermute | solution.py:508
  92.6 1.1 %copy-start.7 = (f32[5,64,512]{2,1,0:T(8,128)S(1)}, f32[5,64,512]{2,1,0:T(8,128)}, u32[]{:S(2)}) copy-start(f32[5,64,512]{2,1,0:T(8,128)} %get-tuple-element.33.velocity) | copy-start | bytes 1966084
  (18 other events, 14.1 us)

commit v2 on v1

--- a/solution.py
+++ b/solution.py
@@ -12,7 +12,7 @@
 RESULTS = 8
 PAD_ROWS = 8
 LANES = 128
-VMEM_BYTES = 40 * 1024 * 1024
+VMEM_PER_SLOT = 5 * 1024
 
 young_modulus = 4.0
 poisson_ratio = 0.3
@@ -48,9 +48,9 @@
     return by_device, by_place
 
 
-def expand(blocks, by_device, by_place):
+def expand(blocks, by_device, by_place, turned=False):
     slots, total = by_place.shape
-    wide = dot(blocks, by_device, ((0,), (0,)))
+    wide = dot(blocks, by_device, ((1 if turned else 0,), (0,)))
     wide = wide.reshape(wide.shape[0] // slots, slots, total) * by_place[None]
     return jnp.sum(wide, axis=1)
 
@@ -237,14 +237,42 @@
         set_tile(payload, device, jnp.where(row == 7, corner, tile_of(payload, device)))
 
 
+def fetch(done, pairs):
+    copies = [
+        pltpu.make_async_copy(source, target, done.at[k])
+        for k, (source, target) in enumerate(pairs)
+    ]
+    for copy in copies:
+        copy.start()
+    return copies
+
+
 def start_kernel(
-    disp, stress, thickness, weld_from, weld_to, weld_stiff,
+    disp_in, stress_in, thickness_in, from_in, to_in, stiff_in,
     payload, to_next, to_last, column_marks, row_marks, picked, spring,
+    disp, stress_left, stress_right, stress_top, stress_bottom, thickness,
+    weld_from, weld_to, weld_stiff, done,
 ):
     rows, cols = thickness.shape
-    _, devices, slots = weld_from.shape
+    _, slots, devices = weld_from.shape
+    copies = fetch(
+        done,
+        [
+            (from_in, weld_from),
+            (to_in, weld_to),
+            (stiff_in, weld_stiff),
+            (disp_in, disp),
+            (thickness_in, thickness),
+            (stress_in.at[:, :, 0:LANES], stress_left),
+            (stress_in.at[:, :, cols - LANES : cols], stress_right),
+            (stress_in.at[:, 0:8, :], stress_top),
+            (stress_in.at[:, rows - 8 : rows, :], stress_bottom),
+        ],
+    )
     shift = cols.bit_length() - 1
     by_device, by_place = slot_marks(devices, slots)
+    for copy in copies[:3]:
+        copy.wait()
     near, far = weld_from[0], weld_to[0]
     stiff = jnp.where(near >= 0, weld_stiff[0], 0.0)
     index_parts = []
@@ -254,7 +282,7 @@
         index_parts += [index >> shift, column >> 1, column & 1]
     index_parts = [part.astype(F32).astype(BF16) for part in index_parts]
     index_parts += list(split(stiff))
-    wide = [expand(part, by_device, by_place) for part in index_parts]
+    wide = [expand(part, by_device, by_place, turned=True) for part in index_parts]
     row_index = jnp.concatenate([wide[0], wide[3]], axis=1)
     column_index = jnp.concatenate([2.0 * wide[1] + wide[2], 2.0 * wide[4] + wide[5]], axis=1)
     stiff_row = wide[6] + wide[7]
@@ -266,25 +294,28 @@
     for start in range(0, cols, 64):
         iota = (lax.broadcasted_iota(jnp.int32, (64, total), 0) + start).astype(F32)
         column_marks[start : start + 64, :] = (iota == column_index).astype(F32).astype(BF16)
+    copies[3].wait()
     values = pick([disp[f] for f in range(FIELDS)], column_marks[...], row_hits)
     picked[...] = jnp.concatenate(values + [values[0]] * 3, axis=0)
     half = total // 2
     near_out = collapse([value[:, :half] for value in values] + [stiff_row], by_device, by_place)
     far_out = collapse([value[:, half:] for value in values], by_device, by_place)
 
+    for copy in copies[4:]:
+        copy.wait()
     plate = thickness[...].astype(F32) * (1.0 / spacing_mm)
     columns = []
     for f in range(RESULTS + 1):
-        left = stress[f, :, 0:LANES] if f < RESULTS else plate[:, 0:LANES]
-        right = stress[f, :, cols - LANES :] if f < RESULTS else plate[:, cols - LANES :]
+        left = stress_left[f] if f < RESULTS else plate[:, 0:LANES]
+        right = stress_right[f] if f < RESULTS else plate[:, cols - LANES :]
         columns.append((left, 0, f // 5, 2 + f % 5))
         columns.append((right, LANES - 1, f // 5, 10 + f % 5))
     halo_rows = edge_rows(columns)
     send_edges(payload, near_out, far_out, halo_rows, [])
-    for ref, row in ((to_next, rows - 1), (to_last, 0)):
+    for ref, stress, row in ((to_next, stress_bottom, rows - 1), (to_last, stress_top, 0)):
         ref[...] = jnp.zeros(ref.shape, F32)
         for f in range(RESULTS):
-            ref[f : f + 1, :] = stress[f, row : row + 1, :]
+            ref[f : f + 1, :] = stress[f, row % 8 : row % 8 + 1, :]
         ref[RESULTS : RESULTS + 1, :] = plate[row : row + 1, :]
 
 
@@ -326,7 +357,7 @@
         )
 
 
-def load_stress(stress_ext, plate_ext, stress, thickness, incoming, above, below):
+def load_stress(stress_ext, plate_ext, thickness, incoming, above, below):
     rows, cols = thickness.shape
     left, right = girth_neighbours()
     halves = edge_columns(tile_of(incoming, left), tile_of(incoming, right))
@@ -337,28 +368,35 @@
         half = halves[f // 5]
         sides = edge_block([(half, lane, LANES - 1), (half, 8 + lane, 0)])
         ref, k = (stress_ext, f) if f < RESULTS else (plate_ext, 0)
-        if f < RESULTS:
-            ref[k, :rows, :cols] = stress[f]
         fill_halo(ref, k, above[f : f + 1, :], below[f : f + 1, :], sides, empty)
 
 
 def step_kernel(first, last, *refs):
+    (stress, plate_ext, velocity, disp, pressure,
+     incoming, above, below, column_marks, row_marks, picked, spring) = refs[:12]
+    out = refs[12:]
     if first:
-        (incoming, above, below, stress, thickness, velocity, disp, pressure,
-         column_marks, row_marks, picked, spring) = refs[:12]
-        out = refs[12:]
         plate_ext, spring_out = out[:2]
         out = out[2:]
-    else:
-        (incoming, above, below, stress, plate_ext, velocity, disp, pressure,
-         column_marks, row_marks, picked, spring) = refs[:12]
-        out = refs[12:]
     stress_ext, velocity_out, disp_out = out[:3]
     out = out[3:]
     if last:
         to_left, to_right, to_next, to_last, res_ext, vel_ext, weld = out
     else:
-        picked_out, payload, to_next, to_last, res_ext, vel_ext, weld = out
+        picked_out, payload, to_next, to_last, res_ext, vel_ext, weld = out[:7]
+    if first:
+        velocity_in, disp_in, pressure_in, thickness_in = velocity, disp, pressure, refs[1]
+        velocity, disp, pressure, thickness, done = out[7:]
+        copies = fetch(
+            done,
+            [
+                (stress, stress_ext.at[:, : velocity.shape[1], : velocity.shape[2]]),
+                (thickness_in, thickness),
+                (velocity_in, velocity),
+                (disp_in, disp),
+                (pressure_in, pressure),
+            ],
+        )
 
     _, rows, cols = velocity.shape
     devices = incoming.shape[0] // 8
@@ -381,7 +419,9 @@
     weld[...] = spread(pulls, column_marks[...], row_marks[...])
 
     if first:
-        load_stress(stress_ext, plate_ext, stress, thickness, incoming, above, below)
+        for copy in copies:
+            copy.wait()
+        load_stress(stress_ext, plate_ext, thickness, incoming, above, below)
         for start in range(0, rows + PAD_ROWS, 8):
             chunk = [stress_ext[k, start : start + 8, :] for k in range(RESULTS)]
             for k, value in enumerate(resultants(chunk, plate_ext[0, start : start + 8, :])):
@@ -481,15 +521,22 @@
     moment[...] = column.T[0:8, :rows]
 
 
-def call(kernel, outs, scratch, *operands):
+def call(kernel, vmem_bytes, outs, scratch, *operands, far=0):
+    operands = [
+        pltpu.with_memory_space_constraint(value, pltpu.HBM) if k < far else value
+        for k, value in enumerate(operands)
+    ]
     whole = pl.BlockSpec(memory_space=pltpu.VMEM)
+    scratch = [pltpu.VMEM(shape, dtype) for shape, dtype in scratch]
+    if far:
+        scratch.append(pltpu.SemaphoreType.DMA((9,)))
     return pl.pallas_call(
         kernel,
         out_shape=[jax.ShapeDtypeStruct(shape, dtype) for shape, dtype in outs],
-        in_specs=[whole] * len(operands),
+        in_specs=[pl.BlockSpec(memory_space=pltpu.HBM)] * far + [whole] * (len(operands) - far),
         out_specs=[whole] * len(outs),
-        scratch_shapes=[pltpu.VMEM(shape, dtype) for shape, dtype in scratch],
-        compiler_params=pltpu.CompilerParams(vmem_limit_bytes=VMEM_BYTES),
+        scratch_shapes=scratch,
+        compiler_params=pltpu.CompilerParams(vmem_limit_bytes=vmem_bytes),
     )(*operands)
 
 
@@ -517,6 +564,7 @@
     height = jnp.sin(2.0 * jnp.pi / girth_total * (column + 0.5)) / girth_total
     height = jnp.broadcast_to(height[None, :], (8, cols))
 
+    vmem_bytes = 8 * 1024 * 1024 + total * VMEM_PER_SLOT
     message = (devices * 8, LANES)
     strip = (16, cols)
     block = (FIELDS, rows, cols)
@@ -529,14 +577,26 @@
         ((FIELDS * rows, cols), F32),
     ]
 
+    first_scratch = [
+        (block, F32), (block, F32), ((rows, cols), F32), ((rows, cols), jnp.int32),
+    ]
+
     payload, to_next, to_last, column_marks, row_marks, picked, spring = call(
         start_kernel,
+        vmem_bytes,
         [
             (message, F32), (strip, F32), (strip, F32), ((cols, total), BF16),
             ((rows, total), BF16), (slot_rows, F32), ((8, total // 2), F32),
         ],
-        [],
-        displacement, stress, thickness, weld_from, weld_to, weld_stiff,
+        [
+            (block, F32), ((RESULTS, rows, LANES), F32), ((RESULTS, rows, LANES), F32),
+            ((RESULTS, 8, cols), F32), ((RESULTS, 8, cols), F32), ((rows, cols), jnp.int32),
+            ((1, slots, devices), jnp.int32), ((1, slots, devices), jnp.int32),
+            ((1, slots, devices), F32),
+        ],
+        displacement, stress, thickness,
+        *[jnp.swapaxes(array, 1, 2) for array in (weld_from, weld_to, weld_stiff)],
+        far=6,
     )
     plate = None
     for step in range(STEPS):
@@ -553,10 +613,12 @@
             outs += [(slot_rows, F32), (message, F32), (strip, F32), (strip, F32)]
         results = call(
             functools.partial(step_kernel, first, last),
+            vmem_bytes,
             outs,
-            scratch,
-            incoming, above, below, stress, thickness if first else plate, velocity,
-            displacement, pressure, column_marks, row_marks, picked, spring,
+            scratch + (first_scratch if first else []),
+            stress, thickness if first else plate, velocity, displacement, pressure,
+            incoming, above, below, column_marks, row_marks, picked, spring,
+            far=5 if first else 0,
         )
         if first:
             plate, spring = results[:2]
@@ -571,6 +633,7 @@
     above, below = to_next_section(to_next), to_last_section(to_last)
     stress, partial_moment = call(
         final_kernel,
+        vmem_bytes,
         [((RESULTS, rows, cols), F32), ((8, rows), F32)],
         [((FIELDS, rows + PAD_ROWS, cols + LANES), F32)],
         from_left, from_right, above, below, stress, plate, velocity, height,

time: 104 us -> 93.4 us (0.90)
  local copies, waits for them, and re-layouts: 24.5 us -> 11.3 us
  Pallas kernels: 14 us -> 17.4 us
    unnamed x61 -> x24, local copies, waits for them, and re-layouts: 24.5 us -> 11.3 us
    pallas_call x5, Pallas kernels: 14 us -> 17.4 us  [call(): pl.pallas_call(kernel, out_shape=[jax.ShapeDtypeStruct(shape, dtype) for...]
where the time goes in v2:
time: 93.4 us; the launch traced here: 92.6 us
  starting transfers between devices  40.5 us (43%)
  Pallas kernels  17.4 us (19%)
  waiting for transfers between devices  16 us (17%)
  local copies, waits for them, and re-layouts  11.3 us (12%)
  blocking collectives  6.63 us (7%)
    all_to_all x3, starting transfers between devices, local(): incoming = lax.all_to_all(payload, ('sec', 'girth'), 0, 0, tiled=True)  18.3 us
    pallas_call x5, Pallas kernels, call(): pl.pallas_call(kernel, out_shape=[jax.ShapeDtypeStruct(shape, dtype) for...  17.4 us
    ppermute x4, starting transfers between devices, to_next_section(): return lax.ppermute(values, 'sec', [(i, i + 1) for i in range(count - 1)])  15.3 us
    ppermute x4, waiting for transfers between devices, to_last_section(): return lax.ppermute(values, 'sec', [(i + 1, i) for i in range(count - 1)])  13.9 us
    unnamed x24, local copies, waits for them, and re-layouts  11.3 us
    psum x1, blocking collectives, local(): moment = lax.psum(partial_moment[0], 'girth')  6.63 us
    ppermute x4, starting transfers between devices, to_last_section(): return lax.ppermute(values, 'sec', [(i + 1, i) for i in range(count - 1)])  5.17 us
  transfers between devices with their start and end apart: 13, of which 8 were waited for; matrix products, arithmetic and copies ran while one was open for 0% of the time, Pallas kernels for 0%

profile of v2, /device:TPU:0, one launch (start us, length us, event | category | flops | bytes accessed | tf_op | source)
XLA Modules:
  0.0 92.6 jit_solution(14145533953710188978)
XLA Ops:
  0.6 3.2 %shard_map.111 = (f32[256,128]{1,0:T(8,128)}, f32[16,512]{1,0:T(8,128)S(1)}, f32[16,512]{1,0:T(8,128)S(1)}, bf16[512,1024]{1,0:T(8,128)(2,1)S(1)}, bf16[64,1024]...) custom-call(f32[5,64,512]{2,1,0:T(8,128)} %refs_3_.1, f32[8,64,512]{2,1,0:T(8,128)} %refs_0_.1, ...), custom_call_target="tpu_custom_call" | custom-call | tf_op jit(solution)/shard_map/pallas_call | solution.py:533
  3.9 7.3 %all-to-all-start = ((f32[32,8,128]{2,1,0:T(8,128)}), f32[32,8,128]{2,1,0:T(8,128)S(1)}, u32[]{:S(2)}, u32[]{:S(2)}) async-start(f32[32,8,128]{2,1,0:T(8,128)} %bitcast.3), calls=%async_computation | async-start | bytes 262144 | tf_op jit(solution)/shard_map/all_to_all | solution.py:604
  11.2 3.7 %collective-permute-start = (f32[16,512]{1,0:T(8,128)S(1)}, f32[16,512]{1,0:T(8,128)S(1)}, u32[]{:S(2)}, u32[]{:S(2)}) collective-permute-start(f32[16,512]{1,0:T(8,128)S(1)} %get-tuple-element.37), channel_id=1, source_target_pairs={{0,4},{4,8},{8,12},{12,16},{16,20},{20,24},{24,28},{1,5},{5,9},{9,... | collective-permute-start | bytes 98312 | tf_op jit(solution)/shard_map/ppermute | solution.py:545
  14.9 1.3 %collective-permute-start.1 = (f32[16,512]{1,0:T(8,128)S(1)}, f32[16,512]{1,0:T(8,128)S(1)}, u32[]{:S(2)}, u32[]{:S(2)}) collective-permute-start(f32[16,512]{1,0:T(8,128)S(1)} %get-tuple-element.38), channel_id=1, source_target_pairs={{4,0},{8,4},{12,8},{16,12},{20,16},{24,20},{28,24},{5,1},{9,5},{13... | collective-permute-start | bytes 98312 | tf_op jit(solution)/shard_map/ppermute | solution.py:550
  16.4 4.2 %collective-permute-done.1.refs_7_ = f32[16,512]{1,0:T(8,128)S(1)} collective-permute-done((f32[16,512]{1,0:T(8,128)S(1)}, f32[16,512]{1,0:T(8,128)S(1)}, u32[]{:S(2)}, u32[]{:S(2)}) %collective-permute-start.1) | collective-permute-done | bytes 32800 | tf_op jit(solution)/shard_map/ppermute | solution.py:550
  20.7 4.6 %shard_map.112 = (f32[1,72,640]{2,1,0:T(8,128)S(1)}, f32[8,1024]{1,0:T(8,128)S(1)}, f32[8,72,640]{2,1,0:T(8,128)S(1)}, f32[5,64,512]{2,1,0:T(8,128)S(1)}, f32[5,...) custom-call(f32[8,64,512]{2,1,0:T(8,128)} %refs_0_.1, ...), custom_call_target="tpu_custom_call" | custom-call | tf_op jit(solution)/shard_map/pallas_call | solution.py:533
  28.1 5.5 %all-to-all-start.1 = ((f32[32,8,128]{2,1,0:T(8,128)}), f32[32,8,128]{2,1,0:T(8,128)S(1)}, u32[]{:S(2)}, u32[]{:S(2)}) async-start(f32[32,8,128]{2,1,0:T(8,128)} %bitcast.5), calls=%async_computation.1 | async-start | bytes 262144 | tf_op jit(solution)/shard_map/all_to_all | solution.py:604
  33.6 3.7 %collective-permute-start.2 = (f32[16,512]{1,0:T(8,128)S(1)}, f32[16,512]{1,0:T(8,128)S(1)}, u32[]{:S(2)}, u32[]{:S(2)}) collective-permute-start(f32[16,512]{1,0:T(8,128)S(1)} %get-tuple-element.48), channel_id=1, source_target_pairs={{0,4},{4,8},{8,12},{12,16},{16,20},{20,24},{24,28},{1,5},{5,9},{9,... | collective-permute-start | bytes 98312 | tf_op jit(solution)/shard_map/ppermute | solution.py:545
  37.3 1.3 %collective-permute-start.3 = (f32[16,512]{1,0:T(8,128)S(1)}, f32[16,512]{1,0:T(8,128)S(1)}, u32[]{:S(2)}, u32[]{:S(2)}) collective-permute-start(f32[16,512]{1,0:T(8,128)S(1)} %get-tuple-element.49), channel_id=1, source_target_pairs={{4,0},{8,4},{12,8},{16,12},{20,16},{24,20},{28,24},{5,1},{9,5},{13... | collective-permute-start | bytes 98312 | tf_op jit(solution)/shard_map/ppermute | solution.py:550
  38.9 4.2 %collective-permute-done.3.refs_7_ = f32[16,512]{1,0:T(8,128)S(1)} collective-permute-done((f32[16,512]{1,0:T(8,128)S(1)}, f32[16,512]{1,0:T(8,128)S(1)}, u32[]{:S(2)}, u32[]{:S(2)}) %collective-permute-start.3) | collective-permute-done | bytes 32800 | tf_op jit(solution)/shard_map/ppermute | solution.py:550
  43.1 1.4 %copy-done.1 = f32[8,72,640]{2,1,0:T(8,128)S(1)} copy-done((f32[8,72,640]{2,1,0:T(8,128)S(1)}, f32[8,72,640]{2,1,0:T(8,128)}, u32[]{:S(2)}) %copy-start.1) | copy-done | bytes 1474584
  46.7 4.0 %shard_map.113 = (f32[8,72,640]{2,1,0:T(8,128)S(1)}, f32[5,64,512]{2,1,0:T(8,128)S(1)}, f32[5,64,512]{2,1,0:T(8,128)S(1)}, f32[8,1024]{1,0:T(8,128)S(1)}, f32[25...) custom-call(f32[8,72,640]{2,1,0:T(8,128)S(1)} %copy-done.1, ...), custom_call_target="tpu_custom_call" | custom-call | tf_op jit(solution)/shard_map/pallas_call | solution.py:533
  52.3 5.5 %all-to-all-start.2 = ((f32[32,8,128]{2,1,0:T(8,128)}), f32[32,8,128]{2,1,0:T(8,128)S(1)}, u32[]{:S(2)}, u32[]{:S(2)}) async-start(f32[32,8,128]{2,1,0:T(8,128)} %bitcast.7), calls=%async_computation.2 | async-start | bytes 262144 | tf_op jit(solution)/shard_map/all_to_all | solution.py:604
  57.9 3.7 %collective-permute-start.4 = (f32[16,512]{1,0:T(8,128)S(1)}, f32[16,512]{1,0:T(8,128)S(1)}, u32[]{:S(2)}, u32[]{:S(2)}) collective-permute-start(f32[16,512]{1,0:T(8,128)S(1)} %get-tuple-element.56), channel_id=1, source_target_pairs={{0,4},{4,8},{8,12},{12,16},{16,20},{20,24},{24,28},{1,5},{5,9},{9,... | collective-permute-start | bytes 98312 | tf_op jit(solution)/shard_map/ppermute | solution.py:545
  61.5 1.3 %collective-permute-start.5 = (f32[16,512]{1,0:T(8,128)S(1)}, f32[16,512]{1,0:T(8,128)S(1)}, u32[]{:S(2)}, u32[]{:S(2)}) collective-permute-start(f32[16,512]{1,0:T(8,128)S(1)} %get-tuple-element.57), channel_id=1, source_target_pairs={{4,0},{8,4},{12,8},{16,12},{20,16},{24,20},{28,24},{5,1},{9,5},{13... | collective-permute-start | bytes 98312 | tf_op jit(solution)/shard_map/ppermute | solution.py:550
  63.1 4.2 %collective-permute-done.5.refs_7_ = f32[16,512]{1,0:T(8,128)S(1)} collective-permute-done((f32[16,512]{1,0:T(8,128)S(1)}, f32[16,512]{1,0:T(8,128)S(1)}, u32[]{:S(2)}, u32[]{:S(2)}) %collective-permute-start.5) | collective-permute-done | bytes 32800 | tf_op jit(solution)/shard_map/ppermute | solution.py:550
  69.5 3.4 %shard_map.114 = (f32[8,72,640]{2,1,0:T(8,128)S(1)}, f32[5,64,512]{2,1,0:T(8,128)}, f32[5,64,512]{2,1,0:T(8,128)}, f32[8,128]{1,0:T(8,128)S(1)}, f32[8,128]{1,0:...) custom-call(f32[8,72,640]{2,1,0:T(8,128)S(1)} %get-tuple-element.52.refs_0_, ...), custom_call_target="tpu_custom_call" | custom-call | tf_op jit(solution)/shard_map/pallas_call | solution.py:533
  72.9 4.3 %collective-permute-start.8 = (f32[8,512]{1,0:T(8,128)S(1)}, f32[8,512]{1,0:T(8,128)S(1)}, u32[]{:S(2)}, u32[]{:S(2)}) collective-permute-start(f32[8,512]{1,0:T(8,128)S(1)} %get-tuple-element.63), channel_id=1, source_target_pairs={{0,4},{4,8},{8,12},{12,16},{16,20},{20,24},{24,28},{1,5},{5,9},{9,... | collective-permute-start | bytes 49160 | tf_op jit(solution)/shard_map/ppermute | solution.py:545
  77.2 1.3 %collective-permute-start.9 = (f32[8,512]{1,0:T(8,128)S(1)}, f32[8,512]{1,0:T(8,128)S(1)}, u32[]{:S(2)}, u32[]{:S(2)}) collective-permute-start(f32[8,512]{1,0:T(8,128)S(1)} %get-tuple-element.64), channel_id=1, source_target_pairs={{4,0},{8,4},{12,8},{16,12},{20,16},{24,20},{28,24},{5,1},{9,5},{13... | collective-permute-start | bytes 49160 | tf_op jit(solution)/shard_map/ppermute | solution.py:550
  78.6 1.7 %collective-permute-start.7 = (f32[8,128]{1,0:T(8,128)S(1)}, f32[8,128]{1,0:T(8,128)S(1)}, u32[]{:S(2)}, u32[]{:S(2)}) collective-permute-start(f32[8,128]{1,0:T(8,128)S(1)} %get-tuple-element.62), channel_id=1, source_target_pairs={{0,3},{1,0},{2,1},{3,2},{4,7},{5,4},{6,5},{7,6},{8,11},{9,8},{10,9... | collective-permute-start | bytes 12296 | tf_op jit(solution)/shard_map/ppermute | solution.py:555
  80.4 1.2 %collective-permute-done.6.from_left = f32[8,128]{1,0:T(8,128)S(1)} collective-permute-done((f32[8,128]{1,0:T(8,128)S(1)}, f32[8,128]{1,0:T(8,128)S(1)}, u32[]{:S(2)}, u32[]{:S(2)}) %collective-permute-start.6) | collective-permute-done | bytes 4128 | tf_op jit(solution)/shard_map/ppermute | solution.py:555
  81.6 1.2 %collective-permute-done.9.below = f32[8,512]{1,0:T(8,128)S(1)} collective-permute-done((f32[8,512]{1,0:T(8,128)S(1)}, f32[8,512]{1,0:T(8,128)S(1)}, u32[]{:S(2)}, u32[]{:S(2)}) %collective-permute-start.9) | collective-permute-done | bytes 16416 | tf_op jit(solution)/shard_map/ppermute | solution.py:550
  83.9 2.1 %shard_map.115 = (f32[8,64,512]{2,1,0:T(8,128)}, f32[8,64]{1,0:T(8,128)S(1)}) custom-call(f32[8,128]{1,0:T(8,128)S(1)} %collective-permute-done.6.from_left, f32[8,128]{1,0:T(8,128)S(1)} %collective-permute-done.7.from_right, f32[8,512]{1,0:T(8,128)S(1)} %collective-permute-done.8.above, f32[8,512]{1,0:T(8,128)S(1)} %collective-permute-done.9.below, ...), custom_call_target="tpu_custom_call" | custom-call | tf_op jit(solution)/shard_map/pallas_call | solution.py:533
  86.0 6.6 %psum.7 = f32[64]{0:T(128)} all-reduce(f32[64]{0:T(128)S(1)} %slice_bitcast_fusion), channel_id=1, replica_groups=mesh['sec'=8,'girth'=4] {'girth'}, use_global_device_ids=true, to_apply=%region_0.0 | all-reduce | flops 64 | bytes 512 | tf_op jit(solution)/shard_map/psum | solution.py:641
  (35 shorter events, 10.9 us)
Async XLA Ops:
  3.9 16.8 %all-to-all-start = ((f32[32,8,128]{2,1,0:T(8,128)}), f32[32,8,128]{2,1,0:T(8,128)S(1)}, u32[]{:S(2)}, u32[]{:S(2)}) async-start(f32[32,8,128]{2,1,0:T(8,128)} %bitcast.3), calls=%async_computation | async-start | bytes 262144 | tf_op jit(solution)/shard_map/all_to_all | solution.py:604
  11.2 5.3 %collective-permute-start = (f32[16,512]{1,0:T(8,128)S(1)}, f32[16,512]{1,0:T(8,128)S(1)}, u32[]{:S(2)}, u32[]{:S(2)}) collective-permute-start(f32[16,512]{1,0:T(8,128)S(1)} %get-tuple-element.37), channel_id=1, source_target_pairs={{0,4},{4,8},{8,12},{12,16},{16,20},{20,24},{24,28},{1,5},{5,9},{9,... | collective-permute-start | bytes 98312 | tf_op jit(solution)/shard_map/ppermute | solution.py:545
  14.9 5.8 %collective-permute-start.1 = (f32[16,512]{1,0:T(8,128)S(1)}, f32[16,512]{1,0:T(8,128)S(1)}, u32[]{:S(2)}, u32[]{:S(2)}) collective-permute-start(f32[16,512]{1,0:T(8,128)S(1)} %get-tuple-element.38), channel_id=1, source_target_pairs={{4,0},{8,4},{12,8},{16,12},{20,16},{24,20},{28,24},{5,1},{9,5},{13... | collective-permute-start | bytes 98312 | tf_op jit(solution)/shard_map/ppermute | solution.py:550
  20.7 22.4 %copy-start.2 = (f32[64,512]{1,0:T(8,128)S(1)}, f32[64,512]{1,0:T(8,128)}, u32[]{:S(2)}) copy-start(f32[64,512]{1,0:T(8,128)} %refs_4_.5) | copy-start | bytes 393220
  25.3 1.1 %copy-start = (f32[8,72,640]{2,1,0:T(8,128)}, f32[8,72,640]{2,1,0:T(8,128)S(1)}, u32[]{:S(2)}) copy-start(f32[8,72,640]{2,1,0:T(8,128)S(1)} %get-tuple-element.43.refs_0_) | copy-start | bytes 4423684
  26.4 0.8 copy-start.8
  27.3 0.8 copy-start.10
  28.1 15.0 %all-to-all-start.1 = ((f32[32,8,128]{2,1,0:T(8,128)}), f32[32,8,128]{2,1,0:T(8,128)S(1)}, u32[]{:S(2)}, u32[]{:S(2)}) async-start(f32[32,8,128]{2,1,0:T(8,128)} %bitcast.5), calls=%async_computation.1 | async-start | bytes 262144 | tf_op jit(solution)/shard_map/all_to_all | solution.py:604
  33.6 5.3 %collective-permute-start.2 = (f32[16,512]{1,0:T(8,128)S(1)}, f32[16,512]{1,0:T(8,128)S(1)}, u32[]{:S(2)}, u32[]{:S(2)}) collective-permute-start(f32[16,512]{1,0:T(8,128)S(1)} %get-tuple-element.48), channel_id=1, source_target_pairs={{0,4},{4,8},{8,12},{12,16},{16,20},{20,24},{24,28},{1,5},{5,9},{9,... | collective-permute-start | bytes 98312 | tf_op jit(solution)/shard_map/ppermute | solution.py:545
  37.3 5.8 %collective-permute-start.3 = (f32[16,512]{1,0:T(8,128)S(1)}, f32[16,512]{1,0:T(8,128)S(1)}, u32[]{:S(2)}, u32[]{:S(2)}) collective-permute-start(f32[16,512]{1,0:T(8,128)S(1)} %get-tuple-element.49), channel_id=1, source_target_pairs={{4,0},{8,4},{12,8},{16,12},{20,16},{24,20},{28,24},{5,1},{9,5},{13... | collective-permute-start | bytes 98312 | tf_op jit(solution)/shard_map/ppermute | solution.py:550
  43.1 1.4 %copy-start.1 = (f32[8,72,640]{2,1,0:T(8,128)S(1)}, f32[8,72,640]{2,1,0:T(8,128)}, u32[]{:S(2)}) copy-start(f32[8,72,640]{2,1,0:T(8,128)} %copy-done) | copy-start | bytes 4423684
  44.5 1.1 %copy-start.9 = (f32[5,64,512]{2,1,0:T(8,128)S(1)}, f32[5,64,512]{2,1,0:T(8,128)}, u32[]{:S(2)}) copy-start(f32[5,64,512]{2,1,0:T(8,128)} %copy-done.8) | copy-start | bytes 1966084
  45.6 1.1 %copy-start.11 = (f32[5,64,512]{2,1,0:T(8,128)S(1)}, f32[5,64,512]{2,1,0:T(8,128)}, u32[]{:S(2)}) copy-start(f32[5,64,512]{2,1,0:T(8,128)} %copy-done.10) | copy-start | bytes 1966084
  50.7 0.8 copy-start.4
  52.3 15.0 %all-to-all-start.2 = ((f32[32,8,128]{2,1,0:T(8,128)}), f32[32,8,128]{2,1,0:T(8,128)S(1)}, u32[]{:S(2)}, u32[]{:S(2)}) async-start(f32[32,8,128]{2,1,0:T(8,128)} %bitcast.7), calls=%async_computation.2 | async-start | bytes 262144 | tf_op jit(solution)/shard_map/all_to_all | solution.py:604
  57.9 5.3 %collective-permute-start.4 = (f32[16,512]{1,0:T(8,128)S(1)}, f32[16,512]{1,0:T(8,128)S(1)}, u32[]{:S(2)}, u32[]{:S(2)}) collective-permute-start(f32[16,512]{1,0:T(8,128)S(1)} %get-tuple-element.56), channel_id=1, source_target_pairs={{0,4},{4,8},{8,12},{12,16},{16,20},{20,24},{24,28},{1,5},{5,9},{9,... | collective-permute-start | bytes 98312 | tf_op jit(solution)/shard_map/ppermute | solution.py:545
  61.5 5.8 %collective-permute-start.5 = (f32[16,512]{1,0:T(8,128)S(1)}, f32[16,512]{1,0:T(8,128)S(1)}, u32[]{:S(2)}, u32[]{:S(2)}) collective-permute-start(f32[16,512]{1,0:T(8,128)S(1)} %get-tuple-element.57), channel_id=1, source_target_pairs={{4,0},{8,4},{12,8},{16,12},{20,16},{24,20},{28,24},{5,1},{9,5},{13... | collective-permute-start | bytes 98312 | tf_op jit(solution)/shard_map/ppermute | solution.py:550
  67.4 1.1 %copy-start.5 = (f32[5,64,512]{2,1,0:T(8,128)S(1)}, f32[5,64,512]{2,1,0:T(8,128)}, u32[]{:S(2)}) copy-start(f32[5,64,512]{2,1,0:T(8,128)} %copy-done.4) | copy-start | bytes 1966084
  68.4 1.1 %copy-start.7 = (f32[5,64,512]{2,1,0:T(8,128)S(1)}, f32[5,64,512]{2,1,0:T(8,128)}, u32[]{:S(2)}) copy-start(f32[5,64,512]{2,1,0:T(8,128)} %copy-done.6) | copy-start | bytes 1966084
  72.9 8.7 %collective-permute-start.8 = (f32[8,512]{1,0:T(8,128)S(1)}, f32[8,512]{1,0:T(8,128)S(1)}, u32[]{:S(2)}, u32[]{:S(2)}) collective-permute-start(f32[8,512]{1,0:T(8,128)S(1)} %get-tuple-element.63), channel_id=1, source_target_pairs={{0,4},{4,8},{8,12},{12,16},{16,20},{20,24},{24,28},{1,5},{5,9},{9,... | collective-permute-start | bytes 49160 | tf_op jit(solution)/shard_map/ppermute | solution.py:545
  77.2 5.6 %collective-permute-start.9 = (f32[8,512]{1,0:T(8,128)S(1)}, f32[8,512]{1,0:T(8,128)S(1)}, u32[]{:S(2)}, u32[]{:S(2)}) collective-permute-start(f32[8,512]{1,0:T(8,128)S(1)} %get-tuple-element.64), channel_id=1, source_target_pairs={{4,0},{8,4},{12,8},{16,12},{20,16},{24,20},{28,24},{5,1},{9,5},{13... | collective-permute-start | bytes 49160 | tf_op jit(solution)/shard_map/ppermute | solution.py:550
  78.5 3.1 %collective-permute-start.6 = (f32[8,128]{1,0:T(8,128)S(1)}, f32[8,128]{1,0:T(8,128)S(1)}, u32[]{:S(2)}, u32[]{:S(2)}) collective-permute-start(f32[8,128]{1,0:T(8,128)S(1)} %get-tuple-element.61), channel_id=1, source_target_pairs={{0,1},{1,2},{2,3},{3,0},{4,5},{5,6},{6,7},{7,4},{8,9},{9,10},{10,1... | collective-permute-start | bytes 12296 | tf_op jit(solution)/shard_map/ppermute | solution.py:555
  78.6 3.1 %collective-permute-start.7 = (f32[8,128]{1,0:T(8,128)S(1)}, f32[8,128]{1,0:T(8,128)S(1)}, u32[]{:S(2)}, u32[]{:S(2)}) collective-permute-start(f32[8,128]{1,0:T(8,128)S(1)} %get-tuple-element.62), channel_id=1, source_target_pairs={{0,3},{1,0},{2,1},{3,2},{4,7},{5,4},{6,5},{7,6},{8,11},{9,8},{10,9... | collective-permute-start | bytes 12296 | tf_op jit(solution)/shard_map/ppermute | solution.py:555
  82.8 1.1 %copy-start.3 = (f32[5,64,512]{2,1,0:T(8,128)S(1)}, f32[5,64,512]{2,1,0:T(8,128)}, u32[]{:S(2)}) copy-start(f32[5,64,512]{2,1,0:T(8,128)} %get-tuple-element.33.velocity) | copy-start | bytes 1966084
  (1 other events, 0.8 us)

commit v3 on v2

--- a/solution.py
+++ b/solution.py
@@ -329,9 +329,7 @@
     ref[f, rows:, cols:] = corner
 
 
-def load_velocity(vel_ext, velocity, incoming, above, below):
-    rows = velocity.shape[1]
-    cols = velocity.shape[2]
+def load_velocity(vel_ext, incoming, above, below):
     left, right = girth_neighbours()
     first, second = edge_columns(tile_of(incoming, left), tile_of(incoming, right))
     row = lax.broadcasted_iota(jnp.int32, (8, LANES), 0)
@@ -340,7 +338,6 @@
         for device, inside in corner_neighbours()
     ]
     for f in range(FIELDS):
-        vel_ext[f, :rows, :cols] = velocity[f]
         sides = edge_block(
             [
                 (first, 2 + f, LANES - 2),
@@ -372,37 +369,47 @@
 
 
 def step_kernel(first, last, *refs):
-    (stress, plate_ext, velocity, disp, pressure,
-     incoming, above, below, column_marks, row_marks, picked, spring) = refs[:12]
-    out = refs[12:]
+    (stress_in, velocity_in, disp_in, thickness_in, pressure_in) = refs[:5]
+    if first:
+        incoming, above, below, column_marks, row_marks, picked, spring = refs[5:12]
+        out = refs[12:]
+    else:
+        incoming, above, below, column_marks, row_marks, picked, spring, plate_ext = refs[5:13]
+        out = refs[13:]
+    stress_out, velocity_out, disp_out = out[:3]
+    out = out[3:]
     if first:
         plate_ext, spring_out = out[:2]
         out = out[2:]
-    stress_ext, velocity_out, disp_out = out[:3]
-    out = out[3:]
     if last:
-        to_left, to_right, to_next, to_last, res_ext, vel_ext, weld = out
+        to_left, to_right, to_next, to_last = out[:4]
     else:
-        picked_out, payload, to_next, to_last, res_ext, vel_ext, weld = out[:7]
-    if first:
-        velocity_in, disp_in, pressure_in, thickness_in = velocity, disp, pressure, refs[1]
-        velocity, disp, pressure, thickness, done = out[7:]
-        copies = fetch(
-            done,
-            [
-                (stress, stress_ext.at[:, : velocity.shape[1], : velocity.shape[2]]),
-                (thickness_in, thickness),
-                (velocity_in, velocity),
-                (disp_in, disp),
-                (pressure_in, pressure),
-            ],
-        )
+        picked_out, payload, to_next, to_last = out[:4]
+    (stress_ext, res_ext, vel_ext, weld, velocity, disp, thickness, pressure,
+     got, sent) = out[4:]
 
     _, rows, cols = velocity.shape
     devices = incoming.shape[0] // 8
     total = picked.shape[1]
     half = total // 2
     by_device, by_place = slot_marks(devices, half // devices)
+    inner = (slice(None), slice(0, rows), slice(0, cols))
+    copies = fetch(
+        got,
+        [
+            (velocity_in, vel_ext.at[inner] if not first else velocity),
+            (stress_in, stress_ext.at[inner] if first else stress_ext),
+            (disp_in, disp),
+            (pressure_in, pressure),
+        ]
+        + ([(thickness_in, thickness)] if first else []),
+    )
+    sends = []
+
+    def send(source, target):
+        copy = pltpu.make_async_copy(source, target, sent.at[len(sends)])
+        copy.start()
+        sends.append(copy)
 
     other = []
     for row in (1, 0):
@@ -418,24 +425,22 @@
     pulls = scale * (jnp.concatenate(other, axis=1) - picked[...])
     weld[...] = spread(pulls, column_marks[...], row_marks[...])
 
+    for copy in copies:
+        copy.wait()
     if first:
-        for copy in copies:
-            copy.wait()
         load_stress(stress_ext, plate_ext, thickness, incoming, above, below)
-        for start in range(0, rows + PAD_ROWS, 8):
-            chunk = [stress_ext[k, start : start + 8, :] for k in range(RESULTS)]
-            for k, value in enumerate(resultants(chunk, plate_ext[0, start : start + 8, :])):
-                res_ext[k, start : start + 8, :] = value
     else:
-        load_velocity(vel_ext, velocity, incoming, above, below)
-        for start in range(0, rows + PAD_ROWS, 8):
-            plate = plate_ext[0, start : start + 8, :]
-            chunk = [stress[k, start : start + 8, :] for k in range(RESULTS)]
+        load_velocity(vel_ext, incoming, above, below)
+    for start in range(0, rows + PAD_ROWS, 8):
+        plate = plate_ext[0, start : start + 8, :]
+        chunk = [stress_ext[k, start : start + 8, :] for k in range(RESULTS)]
+        if not first:
             chunk = stress_chunk(vel_ext, chunk, plate, start)
             for k, value in enumerate(chunk):
                 stress_ext[k, start : start + 8, :] = value
-            for k, value in enumerate(resultants(chunk, plate)):
-                res_ext[k, start : start + 8, :] = value
+        for k, value in enumerate(resultants(chunk, plate)):
+            res_ext[k, start : start + 8, :] = value
+    send(stress_ext, stress_out)
 
     for start in range(0, rows, 8):
         part = slice(start, start + 8)
@@ -446,32 +451,39 @@
         force[2] = force[2] + pressure[part, :]
         for f in range(FIELDS):
             joined = force[f] + weld[f * rows + start : f * rows + start + 8, :]
-            speed = velocity[f, part, :] + (linear if f < 3 else angular) * joined
-            velocity_out[f, part, :] = speed
-            disp_out[f, part, :] = disp[f, part, :] + time_step * speed
+            before = velocity[f, part, :] if first else vel_ext[f, part, :cols]
+            speed = before + (linear if f < 3 else angular) * joined
+            velocity[f, part, :] = speed
+            disp[f, part, :] = disp[f, part, :] + time_step * speed
+        if start % 32 == 24:
+            done = slice(start - 24, start + 8)
+            for source, target in ((velocity, velocity_out), (disp, disp_out)):
+                send(source.at[:, done, :], target.at[:, done, :])
 
     ends = (cols - LANES, cols)
     if last:
         columns = []
         for f in range(FIELDS):
-            columns.append((velocity_out[f, :, 0:LANES], 0, 0, f))
-            columns.append((velocity_out[f, :, ends[0] : ends[1]], LANES - 1, 0, 8 + f))
+            columns.append((velocity[f, :, 0:LANES], 0, 0, f))
+            columns.append((velocity[f, :, ends[0] : ends[1]], LANES - 1, 0, 8 + f))
         halo_rows = edge_rows(columns)
         to_left[...] = halo_rows[0:8]
         to_right[...] = halo_rows[8:16]
         for ref, row in ((to_next, rows - 1), (to_last, 0)):
             ref[...] = jnp.zeros(ref.shape, F32)
             for f in range(FIELDS):
-                ref[f : f + 1, :] = velocity_out[f, row : row + 1, :]
+                ref[f : f + 1, :] = velocity[f, row : row + 1, :]
+        for copy in sends:
+            copy.wait()
         return
-    values = pick([disp_out[f] for f in range(FIELDS)], column_marks[...], row_marks[...])
+    values = pick([disp[f] for f in range(FIELDS)], column_marks[...], row_marks[...])
     picked_out[...] = jnp.concatenate(values + [values[0]] * 3, axis=0)
     near_out = collapse([value[:, :half] for value in values], by_device, by_place)
     far_out = collapse([value[:, half:] for value in values], by_device, by_place)
     columns = []
     for f in range(FIELDS):
-        left_lanes = velocity_out[f, :, 0:LANES]
-        right_lanes = velocity_out[f, :, ends[0] : ends[1]]
+        left_lanes = velocity[f, :, 0:LANES]
+        right_lanes = velocity[f, :, ends[0] : ends[1]]
         for depth in (0, 1):
             columns.append((left_lanes, depth, depth, 2 + f))
             columns.append((right_lanes, LANES - 2 + depth, depth, 10 + f))
@@ -482,7 +494,7 @@
         for side in (0, 1):
             value = jnp.zeros((8, LANES), F32)
             for f in range(FIELDS):
-                part = velocity_out[f, tile, ends[0] : ends[1]] if side else velocity_out[f, tile, 0:LANES]
+                part = velocity[f, tile, ends[0] : ends[1]] if side else velocity[f, tile, 0:LANES]
                 source = LANES - 1 if side else 0
                 value = jnp.where(lane == f, pltpu.roll(part, (f - source) % LANES, 1), value)
             corners.append(jnp.broadcast_to(value[row % 8 : row % 8 + 1], (8, LANES)))
@@ -490,51 +502,69 @@
     for ref, start in ((to_next, rows - 2), (to_last, 0)):
         ref[...] = jnp.zeros(ref.shape, F32)
         for f in range(FIELDS):
-            ref[2 * f : 2 * f + 2, :] = velocity_out[f, start : start + 2, :]
+            ref[2 * f : 2 * f + 2, :] = velocity[f, start : start + 2, :]
+    for copy in sends:
+        copy.wait()
 
 
 def final_kernel(
-    from_left, from_right, above, below, stress, plate_ext, velocity, height,
-    stress_out, moment, vel_ext,
+    stress_in, velocity_in, from_left, from_right, above, below, plate_ext, height,
+    stress_out, moment, stress, vel_ext, got, sent,
 ):
-    _, rows, cols = velocity.shape
+    rows, cols = vel_ext.shape[1] - PAD_ROWS, vel_ext.shape[2] - LANES
+    inner = (slice(None), slice(0, rows), slice(0, cols))
+    copies = fetch(got, [(velocity_in, vel_ext.at[inner]), (stress_in, stress)])
     first, _ = edge_columns(from_left[...], from_right[...])
     empty = jnp.zeros((PAD_ROWS, LANES), F32)
     for f in range(FIELDS):
-        vel_ext[f, :rows, :cols] = velocity[f]
         sides = edge_block([(first, f, LANES - 1), (first, 8 + f, 0)])
         fill_halo(vel_ext, f, above[f : f + 1, :], below[f : f + 1, :], sides, empty)
+    for copy in copies:
+        copy.wait()
     weight = height[0:1, :]
     parts = []
+    sends = []
     for start in range(0, rows, 8):
         part = slice(start, start + 8)
         chunk = [stress[k, part, :] for k in range(RESULTS)]
         plate = plate_ext[0, part, :]
         chunk = stress_chunk(vel_ext, chunk, plate, start)
         for k, value in enumerate(chunk):
-            stress_out[k, part, :] = value[:, :cols]
+            stress[k, part, :] = value
+        if start % 16 == 8:
+            done = slice(start - 8, start + 8)
+            copy = pltpu.make_async_copy(
+                stress.at[:, done, :cols], stress_out.at[:, done, :], sent.at[len(sends)]
+            )
+            copy.start()
+            sends.append(copy)
         weighted = plate[:, :cols] * chunk[0][:, :cols] * weight
         parts.append(jnp.sum(weighted, axis=1, keepdims=True))
     column = jnp.broadcast_to(jnp.concatenate(parts, axis=0), (rows, LANES))
     if rows < LANES:
         column = jnp.concatenate([column, jnp.zeros((LANES - rows, LANES), F32)], axis=0)
     moment[...] = column.T[0:8, :rows]
-
-
-def call(kernel, vmem_bytes, outs, scratch, *operands, far=0):
+    for copy in sends:
+        copy.wait()
+
+
+def call(kernel, vmem_bytes, outs, scratch, *operands, far=0, far_out=0, copies=(1,)):
     operands = [
         pltpu.with_memory_space_constraint(value, pltpu.HBM) if k < far else value
         for k, value in enumerate(operands)
     ]
     whole = pl.BlockSpec(memory_space=pltpu.VMEM)
+    away = pl.BlockSpec(memory_space=pltpu.HBM)
     scratch = [pltpu.VMEM(shape, dtype) for shape, dtype in scratch]
-    if far:
-        scratch.append(pltpu.SemaphoreType.DMA((9,)))
+    scratch += [pltpu.SemaphoreType.DMA((count,)) for count in copies]
     return pl.pallas_call(
         kernel,
-        out_shape=[jax.ShapeDtypeStruct(shape, dtype) for shape, dtype in outs],
-        in_specs=[pl.BlockSpec(memory_space=pltpu.HBM)] * far + [whole] * (len(operands) - far),
-        out_specs=[whole] * len(outs),
+        out_shape=[
+            pltpu.HBM(shape, dtype) if k < far_out else jax.ShapeDtypeStruct(shape, dtype)
+            for k, (shape, dtype) in enumerate(outs)
+        ],
+        in_specs=[away] * far + [whole] * (len(operands) - far),
+        out_specs=[away] * far_out + [whole] * (len(outs) - far_out),
         scratch_shapes=scratch,
         compiler_params=pltpu.CompilerParams(vmem_limit_bytes=vmem_bytes),
     )(*operands)
@@ -573,12 +603,13 @@
     slot_rows = (8, total)
     scratch = [
         (stress_shape, F32),
+        (stress_shape, F32),
         ((FIELDS, rows + PAD_ROWS, cols + LANES), F32),
         ((FIELDS * rows, cols), F32),
-    ]
-
-    first_scratch = [
-        (block, F32), (block, F32), ((rows, cols), F32), ((rows, cols), jnp.int32),
+        (block, F32),
+        (block, F32),
+        ((rows, cols), jnp.int32),
+        ((rows, cols), F32),
     ]
 
     payload, to_next, to_last, column_marks, row_marks, picked, spring = call(
@@ -597,6 +628,7 @@
         displacement, stress, thickness,
         *[jnp.swapaxes(array, 1, 2) for array in (weld_from, weld_to, weld_stiff)],
         far=6,
+        copies=(9,),
     )
     plate = None
     for step in range(STEPS):
@@ -605,7 +637,7 @@
         above, below = to_next_section(to_next), to_last_section(to_last)
         outs = [(stress_shape, F32), (block, F32), (block, F32)]
         if first:
-            outs = [(plate_shape, F32), (slot_rows, F32)] + outs
+            outs += [(plate_shape, F32), (slot_rows, F32)]
         if last:
             edge = (8, LANES)
             outs += [(edge, F32), (edge, F32), ((8, cols), F32), ((8, cols), F32)]
@@ -615,19 +647,23 @@
             functools.partial(step_kernel, first, last),
             vmem_bytes,
             outs,
-            scratch + (first_scratch if first else []),
-            stress, thickness if first else plate, velocity, displacement, pressure,
+            scratch,
+            stress, velocity, displacement, thickness, pressure,
             incoming, above, below, column_marks, row_marks, picked, spring,
-            far=5 if first else 0,
+            *([] if first else [plate]),
+            far=5,
+            far_out=3,
+            copies=(5, 1 + 2 * (rows // 32)),
         )
+        stress, velocity, displacement = results[:3]
+        results = results[3:]
         if first:
             plate, spring = results[:2]
             results = results[2:]
-        stress, velocity, displacement = results[:3]
         if last:
-            to_left, to_right, to_next, to_last = results[3:]
+            to_left, to_right, to_next, to_last = results
         else:
-            picked, payload, to_next, to_last = results[3:]
+            picked, payload, to_next, to_last = results
 
     from_left, from_right = turn(to_right, 1), turn(to_left, -1)
     above, below = to_next_section(to_next), to_last_section(to_last)
@@ -635,8 +671,11 @@
         final_kernel,
         vmem_bytes,
         [((RESULTS, rows, cols), F32), ((8, rows), F32)],
-        [((FIELDS, rows + PAD_ROWS, cols + LANES), F32)],
-        from_left, from_right, above, below, stress, plate, velocity, height,
+        [(stress_shape, F32), ((FIELDS, rows + PAD_ROWS, cols + LANES), F32)],
+        stress, velocity, from_left, from_right, above, below, plate, height,
+        far=2,
+        far_out=1,
+        copies=(2, rows // 16),
     )
     moment = lax.psum(partial_moment[0], "girth")
     return (displacement, velocity, stress, moment)

time: 93.4 us -> 86.8 us (0.929)
  local copies, waits for them, and re-layouts: 11.3 us -> 0.01 us
  Pallas kernels: 17.4 us -> 22.1 us
    unnamed x24 -> x0, local copies, waits for them, and re-layouts: 11.3 us -> none
    pallas_call x5, Pallas kernels: 17.4 us -> 22.1 us  [call(): pl.pallas_call(kernel, out_shape=[pltpu.HBM(shape, dtype) if k < far_out...]
where the time goes in v3:
time: 86.8 us; the launch traced here: 86.2 us
  starting transfers between devices  40.6 us (47%)
  Pallas kernels  22.1 us (25%)
  waiting for transfers between devices  16 us (18%)
  blocking collectives  6.67 us (8%)
    pallas_call x5, Pallas kernels, call(): pl.pallas_call(kernel, out_shape=[pltpu.HBM(shape, dtype) if k < far_out...  22.1 us
    all_to_all x3, starting transfers between devices, local(): incoming = lax.all_to_all(payload, ('sec', 'girth'), 0, 0, tiled=True)  18.3 us
    ppermute x4, starting transfers between devices, to_next_section(): return lax.ppermute(values, 'sec', [(i, i + 1) for i in range(count - 1)])  15.3 us
    ppermute x4, waiting for transfers between devices, to_last_section(): return lax.ppermute(values, 'sec', [(i + 1, i) for i in range(count - 1)])  13.9 us
    psum x1, blocking collectives, local(): moment = lax.psum(partial_moment[0], 'girth')  6.67 us
    ppermute x4, starting transfers between devices, to_last_section(): return lax.ppermute(values, 'sec', [(i + 1, i) for i in range(count - 1)])  5.17 us
    ppermute x2, starting transfers between devices, turn(): lax.ppermute(values, 'girth', [(i, (i + step) % count) for i in range(cou...  1.79 us
  transfers between devices with their start and end apart: 13, of which 8 were waited for; matrix products, arithmetic and copies ran while one was open for 0% of the time, Pallas kernels for 0%

profile of v3, /device:TPU:0, one launch (start us, length us, event | category | flops | bytes accessed | tf_op | source)
XLA Modules:
  0.0 86.2 jit_solution(12103200373055680257)
XLA Ops:
  0.6 3.2 %shard_map.111 = (f32[256,128]{1,0:T(8,128)}, f32[16,512]{1,0:T(8,128)S(1)}, f32[16,512]{1,0:T(8,128)S(1)}, bf16[512,1024]{1,0:T(8,128)(2,1)S(1)}, bf16[64,1024]...) custom-call(f32[5,64,512]{2,1,0:T(8,128)} %refs_2_.1, f32[8,64,512]{2,1,0:T(8,128)} %refs_0_.1, ...), custom_call_target="tpu_custom_call" | custom-call | tf_op jit(solution)/shard_map/pallas_call | solution.py:560
  3.9 7.3 %all-to-all-start = ((f32[32,8,128]{2,1,0:T(8,128)}), f32[32,8,128]{2,1,0:T(8,128)S(1)}, u32[]{:S(2)}, u32[]{:S(2)}) async-start(f32[32,8,128]{2,1,0:T(8,128)} %bitcast.3), calls=%async_computation | async-start | bytes 262144 | tf_op jit(solution)/shard_map/all_to_all | solution.py:636
  11.2 3.7 %collective-permute-start = (f32[16,512]{1,0:T(8,128)S(1)}, f32[16,512]{1,0:T(8,128)S(1)}, u32[]{:S(2)}, u32[]{:S(2)}) collective-permute-start(f32[16,512]{1,0:T(8,128)S(1)} %get-tuple-element.37), channel_id=1, source_target_pairs={{0,4},{4,8},{8,12},{12,16},{16,20},{20,24},{24,28},{1,5},{5,9},{9,... | collective-permute-start | bytes 98312 | tf_op jit(solution)/shard_map/ppermute | solution.py:575
  14.9 1.3 %collective-permute-start.1 = (f32[16,512]{1,0:T(8,128)S(1)}, f32[16,512]{1,0:T(8,128)S(1)}, u32[]{:S(2)}, u32[]{:S(2)}) collective-permute-start(f32[16,512]{1,0:T(8,128)S(1)} %get-tuple-element.38), channel_id=1, source_target_pairs={{4,0},{8,4},{12,8},{16,12},{20,16},{24,20},{28,24},{5,1},{9,5},{13... | collective-permute-start | bytes 98312 | tf_op jit(solution)/shard_map/ppermute | solution.py:580
  16.2 0.3 collective-permute-done.refs_6_
  16.4 4.2 %collective-permute-done.1.refs_7_ = f32[16,512]{1,0:T(8,128)S(1)} collective-permute-done((f32[16,512]{1,0:T(8,128)S(1)}, f32[16,512]{1,0:T(8,128)S(1)}, u32[]{:S(2)}, u32[]{:S(2)}) %collective-permute-start.1) | collective-permute-done | bytes 32800 | tf_op jit(solution)/shard_map/ppermute | solution.py:580
  20.7 4.8 %shard_map.112 = (f32[8,72,640]{2,1,0:T(8,128)}, f32[5,64,512]{2,1,0:T(8,128)}, f32[5,64,512]{2,1,0:T(8,128)}, f32[1,72,640]{2,1,0:T(8,128)S(1)}, f32[8,1024]{1,...) custom-call(f32[8,64,512]{2,1,0:T(8,128)} %refs_0_.1, ...), custom_call_target="tpu_custom_call" | custom-call | tf_op jit(solution)/shard_map/pallas_call | solution.py:560
  25.5 5.5 %all-to-all-start.1 = ((f32[32,8,128]{2,1,0:T(8,128)}), f32[32,8,128]{2,1,0:T(8,128)S(1)}, u32[]{:S(2)}, u32[]{:S(2)}) async-start(f32[32,8,128]{2,1,0:T(8,128)} %bitcast.5), calls=%async_computation.1 | async-start | bytes 262144 | tf_op jit(solution)/shard_map/all_to_all | solution.py:636
  31.0 3.7 %collective-permute-start.2 = (f32[16,512]{1,0:T(8,128)S(1)}, f32[16,512]{1,0:T(8,128)S(1)}, u32[]{:S(2)}, u32[]{:S(2)}) collective-permute-start(f32[16,512]{1,0:T(8,128)S(1)} %get-tuple-element.47), channel_id=1, source_target_pairs={{0,4},{4,8},{8,12},{12,16},{16,20},{20,24},{24,28},{1,5},{5,9},{9,... | collective-permute-start | bytes 98312 | tf_op jit(solution)/shard_map/ppermute | solution.py:575
  34.7 1.3 %collective-permute-start.3 = (f32[16,512]{1,0:T(8,128)S(1)}, f32[16,512]{1,0:T(8,128)S(1)}, u32[]{:S(2)}, u32[]{:S(2)}) collective-permute-start(f32[16,512]{1,0:T(8,128)S(1)} %get-tuple-element.48), channel_id=1, source_target_pairs={{4,0},{8,4},{12,8},{16,12},{20,16},{24,20},{28,24},{5,1},{9,5},{13... | collective-permute-start | bytes 98312 | tf_op jit(solution)/shard_map/ppermute | solution.py:580
  36.2 4.2 %collective-permute-done.3.refs_7_ = f32[16,512]{1,0:T(8,128)S(1)} collective-permute-done((f32[16,512]{1,0:T(8,128)S(1)}, f32[16,512]{1,0:T(8,128)S(1)}, u32[]{:S(2)}, u32[]{:S(2)}) %collective-permute-start.3) | collective-permute-done | bytes 32800 | tf_op jit(solution)/shard_map/ppermute | solution.py:580
  40.5 5.6 %shard_map.113 = (f32[8,72,640]{2,1,0:T(8,128)}, f32[5,64,512]{2,1,0:T(8,128)}, f32[5,64,512]{2,1,0:T(8,128)}, f32[8,1024]{1,0:T(8,128)S(1)}, f32[256,128]{1,0:T...) custom-call(f32[8,72,640]{2,1,0:T(8,128)} %get-tuple-element.43.refs_0_, f32[5,64,512]{2,1,0:T(8,128)} %get-tuple-element.44.refs_1_, ...), custom_call_target="tpu_custom_call" | custom-call | tf_op jit(solution)/shard_map/pallas_call | solution.py:560
  46.1 5.5 %all-to-all-start.2 = ((f32[32,8,128]{2,1,0:T(8,128)}), f32[32,8,128]{2,1,0:T(8,128)S(1)}, u32[]{:S(2)}, u32[]{:S(2)}) async-start(f32[32,8,128]{2,1,0:T(8,128)} %bitcast.7), calls=%async_computation.2 | async-start | bytes 262144 | tf_op jit(solution)/shard_map/all_to_all | solution.py:636
  51.6 3.7 %collective-permute-start.4 = (f32[16,512]{1,0:T(8,128)S(1)}, f32[16,512]{1,0:T(8,128)S(1)}, u32[]{:S(2)}, u32[]{:S(2)}) collective-permute-start(f32[16,512]{1,0:T(8,128)S(1)} %get-tuple-element.56), channel_id=1, source_target_pairs={{0,4},{4,8},{8,12},{12,16},{16,20},{20,24},{24,28},{1,5},{5,9},{9,... | collective-permute-start | bytes 98312 | tf_op jit(solution)/shard_map/ppermute | solution.py:575
  55.3 1.3 %collective-permute-start.5 = (f32[16,512]{1,0:T(8,128)S(1)}, f32[16,512]{1,0:T(8,128)S(1)}, u32[]{:S(2)}, u32[]{:S(2)}) collective-permute-start(f32[16,512]{1,0:T(8,128)S(1)} %get-tuple-element.57), channel_id=1, source_target_pairs={{4,0},{8,4},{12,8},{16,12},{20,16},{24,20},{28,24},{5,1},{9,5},{13... | collective-permute-start | bytes 98312 | tf_op jit(solution)/shard_map/ppermute | solution.py:580
  56.9 4.2 %collective-permute-done.5.refs_7_ = f32[16,512]{1,0:T(8,128)S(1)} collective-permute-done((f32[16,512]{1,0:T(8,128)S(1)}, f32[16,512]{1,0:T(8,128)S(1)}, u32[]{:S(2)}, u32[]{:S(2)}) %collective-permute-start.5) | collective-permute-done | bytes 32800 | tf_op jit(solution)/shard_map/ppermute | solution.py:580
  61.1 5.0 %shard_map.114 = (f32[8,72,640]{2,1,0:T(8,128)}, f32[5,64,512]{2,1,0:T(8,128)}, f32[5,64,512]{2,1,0:T(8,128)}, f32[8,128]{1,0:T(8,128)S(1)}, f32[8,128]{1,0:T(8,...) custom-call(f32[8,72,640]{2,1,0:T(8,128)} %get-tuple-element.52.refs_0_, f32[5,64,512]{2,1,0:T(8,128)} %get-tuple-element.53.refs_1_, ...), custom_call_target="tpu_custom_call" | custom-call | tf_op jit(solution)/shard_map/pallas_call | solution.py:560
  66.1 4.3 %collective-permute-start.8 = (f32[8,512]{1,0:T(8,128)S(1)}, f32[8,512]{1,0:T(8,128)S(1)}, u32[]{:S(2)}, u32[]{:S(2)}) collective-permute-start(f32[8,512]{1,0:T(8,128)S(1)} %get-tuple-element.64), channel_id=1, source_target_pairs={{0,4},{4,8},{8,12},{12,16},{16,20},{20,24},{24,28},{1,5},{5,9},{9,... | collective-permute-start | bytes 49160 | tf_op jit(solution)/shard_map/ppermute | solution.py:575
  70.4 1.3 %collective-permute-start.9 = (f32[8,512]{1,0:T(8,128)S(1)}, f32[8,512]{1,0:T(8,128)S(1)}, u32[]{:S(2)}, u32[]{:S(2)}) collective-permute-start(f32[8,512]{1,0:T(8,128)S(1)} %get-tuple-element.65), channel_id=1, source_target_pairs={{4,0},{8,4},{12,8},{16,12},{20,16},{24,20},{28,24},{5,1},{9,5},{13... | collective-permute-start | bytes 49160 | tf_op jit(solution)/shard_map/ppermute | solution.py:580
  71.8 1.7 %collective-permute-start.7 = (f32[8,128]{1,0:T(8,128)S(1)}, f32[8,128]{1,0:T(8,128)S(1)}, u32[]{:S(2)}, u32[]{:S(2)}) collective-permute-start(f32[8,128]{1,0:T(8,128)S(1)} %get-tuple-element.63), channel_id=1, source_target_pairs={{0,3},{1,0},{2,1},{3,2},{4,7},{5,4},{6,5},{7,6},{8,11},{9,8},{10,9... | collective-permute-start | bytes 12296 | tf_op jit(solution)/shard_map/ppermute | solution.py:585
  73.6 1.2 %collective-permute-done.6.from_left = f32[8,128]{1,0:T(8,128)S(1)} collective-permute-done((f32[8,128]{1,0:T(8,128)S(1)}, f32[8,128]{1,0:T(8,128)S(1)}, u32[]{:S(2)}, u32[]{:S(2)}) %collective-permute-start.6) | collective-permute-done | bytes 4128 | tf_op jit(solution)/shard_map/ppermute | solution.py:585
  74.8 1.2 %collective-permute-done.9.below = f32[8,512]{1,0:T(8,128)S(1)} collective-permute-done((f32[8,512]{1,0:T(8,128)S(1)}, f32[8,512]{1,0:T(8,128)S(1)}, u32[]{:S(2)}, u32[]{:S(2)}) %collective-permute-start.9) | collective-permute-done | bytes 16416 | tf_op jit(solution)/shard_map/ppermute | solution.py:580
  76.1 3.4 %shard_map.115 = (f32[8,64,512]{2,1,0:T(8,128)}, f32[8,64]{1,0:T(8,128)S(1)}) custom-call(f32[8,72,640]{2,1,0:T(8,128)} %get-tuple-element.61.stress_in, f32[5,64,512]{2,1,0:T(8,128)} %get-tuple-element.33.velocity_in, f32[8,128]{1,0:T(8,128)S(1)} %collective-permute-done.6.from_left, f32[8,128]{1,0:T(8,128)S(1)} %collective-permute-done.7.from_right, ...), custom_call_target="tpu_custom_call" | custom-call | tf_op jit(solution)/shard_map/pallas_call | solution.py:560
  79.5 6.7 %psum.7 = f32[64]{0:T(128)} all-reduce(f32[64]{0:T(128)S(1)} %slice_bitcast_fusion), channel_id=1, replica_groups=mesh['sec'=8,'girth'=4] {'girth'}, use_global_device_ids=true, to_apply=%region_0.0 | all-reduce | flops 64 | bytes 512 | tf_op jit(solution)/shard_map/psum | solution.py:680
  (11 shorter events, 0.7 us)
Async XLA Ops:
  3.9 16.8 %all-to-all-start = ((f32[32,8,128]{2,1,0:T(8,128)}), f32[32,8,128]{2,1,0:T(8,128)S(1)}, u32[]{:S(2)}, u32[]{:S(2)}) async-start(f32[32,8,128]{2,1,0:T(8,128)} %bitcast.3), calls=%async_computation | async-start | bytes 262144 | tf_op jit(solution)/shard_map/all_to_all | solution.py:636
  11.2 5.3 %collective-permute-start = (f32[16,512]{1,0:T(8,128)S(1)}, f32[16,512]{1,0:T(8,128)S(1)}, u32[]{:S(2)}, u32[]{:S(2)}) collective-permute-start(f32[16,512]{1,0:T(8,128)S(1)} %get-tuple-element.37), channel_id=1, source_target_pairs={{0,4},{4,8},{8,12},{12,16},{16,20},{20,24},{24,28},{1,5},{5,9},{9,... | collective-permute-start | bytes 98312 | tf_op jit(solution)/shard_map/ppermute | solution.py:575
  14.9 5.8 %collective-permute-start.1 = (f32[16,512]{1,0:T(8,128)S(1)}, f32[16,512]{1,0:T(8,128)S(1)}, u32[]{:S(2)}, u32[]{:S(2)}) collective-permute-start(f32[16,512]{1,0:T(8,128)S(1)} %get-tuple-element.38), channel_id=1, source_target_pairs={{4,0},{8,4},{12,8},{16,12},{20,16},{24,20},{28,24},{5,1},{9,5},{13... | collective-permute-start | bytes 98312 | tf_op jit(solution)/shard_map/ppermute | solution.py:580
  25.5 15.0 %all-to-all-start.1 = ((f32[32,8,128]{2,1,0:T(8,128)}), f32[32,8,128]{2,1,0:T(8,128)S(1)}, u32[]{:S(2)}, u32[]{:S(2)}) async-start(f32[32,8,128]{2,1,0:T(8,128)} %bitcast.5), calls=%async_computation.1 | async-start | bytes 262144 | tf_op jit(solution)/shard_map/all_to_all | solution.py:636
  31.0 5.3 %collective-permute-start.2 = (f32[16,512]{1,0:T(8,128)S(1)}, f32[16,512]{1,0:T(8,128)S(1)}, u32[]{:S(2)}, u32[]{:S(2)}) collective-permute-start(f32[16,512]{1,0:T(8,128)S(1)} %get-tuple-element.47), channel_id=1, source_target_pairs={{0,4},{4,8},{8,12},{12,16},{16,20},{20,24},{24,28},{1,5},{5,9},{9,... | collective-permute-start | bytes 98312 | tf_op jit(solution)/shard_map/ppermute | solution.py:575
  34.7 5.8 %collective-permute-start.3 = (f32[16,512]{1,0:T(8,128)S(1)}, f32[16,512]{1,0:T(8,128)S(1)}, u32[]{:S(2)}, u32[]{:S(2)}) collective-permute-start(f32[16,512]{1,0:T(8,128)S(1)} %get-tuple-element.48), channel_id=1, source_target_pairs={{4,0},{8,4},{12,8},{16,12},{20,16},{24,20},{28,24},{5,1},{9,5},{13... | collective-permute-start | bytes 98312 | tf_op jit(solution)/shard_map/ppermute | solution.py:580
  46.1 15.0 %all-to-all-start.2 = ((f32[32,8,128]{2,1,0:T(8,128)}), f32[32,8,128]{2,1,0:T(8,128)S(1)}, u32[]{:S(2)}, u32[]{:S(2)}) async-start(f32[32,8,128]{2,1,0:T(8,128)} %bitcast.7), calls=%async_computation.2 | async-start | bytes 262144 | tf_op jit(solution)/shard_map/all_to_all | solution.py:636
  51.6 5.3 %collective-permute-start.4 = (f32[16,512]{1,0:T(8,128)S(1)}, f32[16,512]{1,0:T(8,128)S(1)}, u32[]{:S(2)}, u32[]{:S(2)}) collective-permute-start(f32[16,512]{1,0:T(8,128)S(1)} %get-tuple-element.56), channel_id=1, source_target_pairs={{0,4},{4,8},{8,12},{12,16},{16,20},{20,24},{24,28},{1,5},{5,9},{9,... | collective-permute-start | bytes 98312 | tf_op jit(solution)/shard_map/ppermute | solution.py:575
  55.3 5.8 %collective-permute-start.5 = (f32[16,512]{1,0:T(8,128)S(1)}, f32[16,512]{1,0:T(8,128)S(1)}, u32[]{:S(2)}, u32[]{:S(2)}) collective-permute-start(f32[16,512]{1,0:T(8,128)S(1)} %get-tuple-element.57), channel_id=1, source_target_pairs={{4,0},{8,4},{12,8},{16,12},{20,16},{24,20},{28,24},{5,1},{9,5},{13... | collective-permute-start | bytes 98312 | tf_op jit(solution)/shard_map/ppermute | solution.py:580
  66.1 8.7 %collective-permute-start.8 = (f32[8,512]{1,0:T(8,128)S(1)}, f32[8,512]{1,0:T(8,128)S(1)}, u32[]{:S(2)}, u32[]{:S(2)}) collective-permute-start(f32[8,512]{1,0:T(8,128)S(1)} %get-tuple-element.64), channel_id=1, source_target_pairs={{0,4},{4,8},{8,12},{12,16},{16,20},{20,24},{24,28},{1,5},{5,9},{9,... | collective-permute-start | bytes 49160 | tf_op jit(solution)/shard_map/ppermute | solution.py:575
  70.4 5.6 %collective-permute-start.9 = (f32[8,512]{1,0:T(8,128)S(1)}, f32[8,512]{1,0:T(8,128)S(1)}, u32[]{:S(2)}, u32[]{:S(2)}) collective-permute-start(f32[8,512]{1,0:T(8,128)S(1)} %get-tuple-element.65), channel_id=1, source_target_pairs={{4,0},{8,4},{12,8},{16,12},{20,16},{24,20},{28,24},{5,1},{9,5},{13... | collective-permute-start | bytes 49160 | tf_op jit(solution)/shard_map/ppermute | solution.py:580
  71.7 3.1 %collective-permute-start.6 = (f32[8,128]{1,0:T(8,128)S(1)}, f32[8,128]{1,0:T(8,128)S(1)}, u32[]{:S(2)}, u32[]{:S(2)}) collective-permute-start(f32[8,128]{1,0:T(8,128)S(1)} %get-tuple-element.62), channel_id=1, source_target_pairs={{0,1},{1,2},{2,3},{3,0},{4,5},{5,6},{6,7},{7,4},{8,9},{9,10},{10,1... | collective-permute-start | bytes 12296 | tf_op jit(solution)/shard_map/ppermute | solution.py:585
  71.8 3.1 %collective-permute-start.7 = (f32[8,128]{1,0:T(8,128)S(1)}, f32[8,128]{1,0:T(8,128)S(1)}, u32[]{:S(2)}, u32[]{:S(2)}) collective-permute-start(f32[8,128]{1,0:T(8,128)S(1)} %get-tuple-element.63), channel_id=1, source_target_pairs={{0,3},{1,0},{2,1},{3,2},{4,7},{5,4},{6,5},{7,6},{8,11},{9,8},{10,9... | collective-permute-start | bytes 12296 | tf_op jit(solution)/shard_map/ppermute | solution.py:585

commit v4 on v3

--- a/solution.py
+++ b/solution.py
@@ -37,11 +37,20 @@
     return lax.dot_general(a, b, (contract, ((), ())), preferred_element_type=F32)
 
 
-def slot_marks(devices, slots):
+def device_marks(devices, slots, outgoing=False):
     total = devices * slots
     lane = lax.broadcasted_iota(jnp.int32, (devices, total), 1)
     device = lax.broadcasted_iota(jnp.int32, (devices, total), 0)
-    by_device = (lane // slots == device).astype(F32).astype(BF16)
+    if outgoing:
+        girths = lax.axis_size("girth")
+        secs = devices // girths
+        device = device % secs * girths + device // secs
+    return (lane // slots == device).astype(F32).astype(BF16)
+
+
+def slot_marks(devices, slots):
+    total = devices * slots
+    by_device = device_marks(devices, slots)
     lane = lax.broadcasted_iota(jnp.int32, (slots, total), 1)
     place = lax.broadcasted_iota(jnp.int32, (slots, total), 0)
     by_place = (lane % slots == place).astype(F32)
@@ -230,11 +239,18 @@
     payload[...] = jnp.zeros(payload.shape, F32)
     payload[pl.ds(0, devices, stride=8), :] = near
     payload[pl.ds(1, devices, stride=8), :] = far
+    _, _, secs, girths = place()
     row = lax.broadcasted_iota(jnp.int32, (8, LANES), 0)
+
+    def slot_of(device):
+        return lax.rem(device, girths) * secs + lax.div(device, girths)
+
     for device, tile in zip(girth_neighbours(), (halo_rows[0:8], halo_rows[8:16])):
-        set_tile(payload, device, jnp.where(row < 2, tile_of(payload, device), tile))
+        slot = slot_of(device)
+        set_tile(payload, slot, jnp.where(row < 2, tile_of(payload, slot), tile))
     for (device, _), corner in zip(corner_neighbours(), corners):
-        set_tile(payload, device, jnp.where(row == 7, corner, tile_of(payload, device)))
+        slot = slot_of(device)
+        set_tile(payload, slot, jnp.where(row == 7, corner, tile_of(payload, slot)))
 
 
 def fetch(done, pairs):
@@ -298,8 +314,9 @@
     values = pick([disp[f] for f in range(FIELDS)], column_marks[...], row_hits)
     picked[...] = jnp.concatenate(values + [values[0]] * 3, axis=0)
     half = total // 2
-    near_out = collapse([value[:, :half] for value in values] + [stiff_row], by_device, by_place)
-    far_out = collapse([value[:, half:] for value in values], by_device, by_place)
+    outgoing = device_marks(devices, slots, outgoing=True)
+    near_out = collapse([value[:, :half] for value in values] + [stiff_row], outgoing, by_place)
+    far_out = collapse([value[:, half:] for value in values], outgoing, by_place)
 
     for copy in copies[4:]:
         copy.wait()
@@ -478,8 +495,9 @@
         return
     values = pick([disp[f] for f in range(FIELDS)], column_marks[...], row_marks[...])
     picked_out[...] = jnp.concatenate(values + [values[0]] * 3, axis=0)
-    near_out = collapse([value[:, :half] for value in values], by_device, by_place)
-    far_out = collapse([value[:, half:] for value in values], by_device, by_place)
+    outgoing = device_marks(devices, half // devices, outgoing=True)
+    near_out = collapse([value[:, :half] for value in values], outgoing, by_place)
+    far_out = collapse([value[:, half:] for value in values], outgoing, by_place)
     columns = []
     for f in range(FIELDS):
         left_lanes = velocity[f, :, 0:LANES]
@@ -580,6 +598,15 @@
     return lax.ppermute(values, "sec", [(i + 1, i) for i in range(count - 1)])
 
 
+def exchange(tiles):
+    secs, girths = lax.axis_size("sec"), lax.axis_size("girth")
+    shape = (8, LANES)
+    near = lax.all_to_all(tiles.reshape((girths, secs) + shape), "girth", 0, 0, tiled=True)
+    near = jnp.swapaxes(near, 0, 1)
+    far = lax.all_to_all(near, "sec", 0, 0, tiled=True)
+    return far.reshape(tiles.shape)
+
+
 def turn(values, step):
     count = lax.axis_size("girth")
     return lax.ppermute(values, "girth", [(i, (i + step) % count) for i in range(count)])
@@ -633,7 +660,7 @@
     plate = None
     for step in range(STEPS):
         first, last = step == 0, step == STEPS - 1
-        incoming = lax.all_to_all(payload, ("sec", "girth"), 0, 0, tiled=True)
+        incoming = exchange(payload)
         above, below = to_next_section(to_next), to_last_section(to_last)
         outs = [(stress_shape, F32), (block, F32), (block, F32)]
         if first:

time: 86.8 us -> 110 us (1.27)
  blocking collectives: 6.67 us -> 29.4 us
  local copies, waits for them, and re-layouts: 0.01 us -> 2 us
  Pallas kernels: 22.1 us -> 20.8 us
    all_to_all x0 -> x3, blocking collectives: none -> 22.7 us  [exchange(): lax.all_to_all(tiles.reshape((girths, secs) + shape), 'girth', 0, 0, tile...]
    transpose x0 -> x3, local copies, waits for them, and re-layouts: none -> 1.99 us  [exchange(): near = jnp.swapaxes(near, 0, 1)]
    all_to_all x3, starting transfers between devices: 18.3 us -> 16.7 us  [exchange(): far = lax.all_to_all(near, 'sec', 0, 0, tiled=True)]
    pallas_call x5, Pallas kernels: 22.1 us -> 20.8 us  [call(): pl.pallas_call(kernel, out_shape=[pltpu.HBM(shape, dtype) if k < far_out...]
where the time goes in v4:
time: 110 us; the launch traced here: 109 us
  starting transfers between devices  39.7 us (36%)
  blocking collectives  29.4 us (27%)
  Pallas kernels  20.8 us (19%)
  waiting for transfers between devices  16 us (15%)
  local copies, waits for them, and re-layouts  2 us (2%)
    all_to_all x3, blocking collectives, exchange(): lax.all_to_all(tiles.reshape((girths, secs) + shape), 'girth', 0, 0, tile...  22.7 us
    pallas_call x5, Pallas kernels, call(): pl.pallas_call(kernel, out_shape=[pltpu.HBM(shape, dtype) if k < far_out...  20.8 us
    all_to_all x3, starting transfers between devices, exchange(): far = lax.all_to_all(near, 'sec', 0, 0, tiled=True)  16.7 us
    ppermute x4, starting transfers between devices, to_next_section(): return lax.ppermute(values, 'sec', [(i, i + 1) for i in range(count - 1)])  16 us
    ppermute x4, waiting for transfers between devices, to_last_section(): return lax.ppermute(values, 'sec', [(i + 1, i) for i in range(count - 1)])  13.9 us
    psum x1, blocking collectives, local(): moment = lax.psum(partial_moment[0], 'girth')  6.67 us
    ppermute x4, starting transfers between devices, to_last_section(): return lax.ppermute(values, 'sec', [(i + 1, i) for i in range(count - 1)])  5.17 us
  transfers between devices with their start and end apart: 13, of which 8 were waited for; matrix products, arithmetic and copies ran while one was open for 0% of the time, Pallas kernels for 0%

profile of v4, /device:TPU:0, one launch (start us, length us, event | category | flops | bytes accessed | tf_op | source)
XLA Modules:
  0.0 108.6 jit_solution(17102987114200681991)
XLA Ops:
  0.6 2.6 %shard_map.111 = (f32[256,128]{1,0:T(8,128)S(1)}, f32[16,512]{1,0:T(8,128)S(1)}, f32[16,512]{1,0:T(8,128)S(1)}, bf16[512,1024]{1,0:T(8,128)(2,1)S(1)}, bf16[64,1...) custom-call(f32[5,64,512]{2,1,0:T(8,128)} %refs_2_.1, f32[8,64,512]{2,1,0:T(8,128)} %refs_0_.1, ...), custom_call_target="tpu_custom_call" | custom-call | tf_op jit(solution)/shard_map/pallas_call | solution.py:578
  3.2 8.6 %all_to_all.30 = f32[4,8,8,128]{3,2,1,0:T(8,128)S(1)} all-to-all(f32[4,8,8,128]{3,2,1,0:T(8,128)S(1)} %bitcast.19), channel_id=1, replica_groups=mesh['sec'=8,'girth'=4] {'girth'}, dimensions={0} | all-to-all | bytes 262144 | tf_op jit(solution)/shard_map/all_to_all | solution.py:604
  12.5 5.8 %all-to-all-start.1 = ((f32[8,4,8,128]{3,2,1,0:T(8,128)}), f32[8,4,8,128]{3,2,1,0:T(8,128)S(1)}, u32[]{:S(2)}, u32[]{:S(2)}) async-start(f32[8,4,8,128]{3,2,1,0:T(8,128)} %copy.18), calls=%async_computation.1 | async-start | bytes 262144 | tf_op jit(solution)/shard_map/all_to_all | solution.py:606
  18.4 3.9 %collective-permute-start = (f32[16,512]{1,0:T(8,128)S(1)}, f32[16,512]{1,0:T(8,128)S(1)}, u32[]{:S(2)}, u32[]{:S(2)}) collective-permute-start(f32[16,512]{1,0:T(8,128)S(1)} %get-tuple-element.37), channel_id=1, source_target_pairs={{0,4},{4,8},{8,12},{12,16},{16,20},{20,24},{24,28},{1,5},{5,9},{9,... | collective-permute-start | bytes 98312 | tf_op jit(solution)/shard_map/ppermute | solution.py:593
  22.3 1.3 %collective-permute-start.1 = (f32[16,512]{1,0:T(8,128)S(1)}, f32[16,512]{1,0:T(8,128)S(1)}, u32[]{:S(2)}, u32[]{:S(2)}) collective-permute-start(f32[16,512]{1,0:T(8,128)S(1)} %get-tuple-element.38), channel_id=1, source_target_pairs={{4,0},{8,4},{12,8},{16,12},{20,16},{24,20},{28,24},{5,1},{9,5},{13... | collective-permute-start | bytes 98312 | tf_op jit(solution)/shard_map/ppermute | solution.py:598
  23.9 4.2 %collective-permute-done.1.refs_7_ = f32[16,512]{1,0:T(8,128)S(1)} collective-permute-done((f32[16,512]{1,0:T(8,128)S(1)}, f32[16,512]{1,0:T(8,128)S(1)}, u32[]{:S(2)}, u32[]{:S(2)}) %collective-permute-start.1) | collective-permute-done | bytes 32800 | tf_op jit(solution)/shard_map/ppermute | solution.py:598
  28.1 4.1 %shard_map.112 = (f32[8,72,640]{2,1,0:T(8,128)}, f32[5,64,512]{2,1,0:T(8,128)}, f32[5,64,512]{2,1,0:T(8,128)}, f32[1,72,640]{2,1,0:T(8,128)S(1)}, f32[8,1024]{1,...) custom-call(f32[8,64,512]{2,1,0:T(8,128)} %refs_0_.1, ...), custom_call_target="tpu_custom_call" | custom-call | tf_op jit(solution)/shard_map/pallas_call | solution.py:578
  32.2 7.0 %all_to_all.31 = f32[4,8,8,128]{3,2,1,0:T(8,128)S(1)} all-to-all(f32[4,8,8,128]{3,2,1,0:T(8,128)S(1)} %bitcast.17), channel_id=1, replica_groups=mesh['sec'=8,'girth'=4] {'girth'}, dimensions={0} | all-to-all | bytes 262144 | tf_op jit(solution)/shard_map/all_to_all | solution.py:604
  39.9 5.4 %all-to-all-start.3 = ((f32[8,4,8,128]{3,2,1,0:T(8,128)}), f32[8,4,8,128]{3,2,1,0:T(8,128)S(1)}, u32[]{:S(2)}, u32[]{:S(2)}) async-start(f32[8,4,8,128]{3,2,1,0:T(8,128)} %copy.19), calls=%async_computation.3 | async-start | bytes 262144 | tf_op jit(solution)/shard_map/all_to_all | solution.py:606
  45.4 3.9 %collective-permute-start.2 = (f32[16,512]{1,0:T(8,128)S(1)}, f32[16,512]{1,0:T(8,128)S(1)}, u32[]{:S(2)}, u32[]{:S(2)}) collective-permute-start(f32[16,512]{1,0:T(8,128)S(1)} %get-tuple-element.47), channel_id=1, source_target_pairs={{0,4},{4,8},{8,12},{12,16},{16,20},{20,24},{24,28},{1,5},{5,9},{9,... | collective-permute-start | bytes 98312 | tf_op jit(solution)/shard_map/ppermute | solution.py:593
  49.3 1.3 %collective-permute-start.3 = (f32[16,512]{1,0:T(8,128)S(1)}, f32[16,512]{1,0:T(8,128)S(1)}, u32[]{:S(2)}, u32[]{:S(2)}) collective-permute-start(f32[16,512]{1,0:T(8,128)S(1)} %get-tuple-element.48), channel_id=1, source_target_pairs={{4,0},{8,4},{12,8},{16,12},{20,16},{24,20},{28,24},{5,1},{9,5},{13... | collective-permute-start | bytes 98312 | tf_op jit(solution)/shard_map/ppermute | solution.py:598
  50.9 4.2 %collective-permute-done.3.refs_7_ = f32[16,512]{1,0:T(8,128)S(1)} collective-permute-done((f32[16,512]{1,0:T(8,128)S(1)}, f32[16,512]{1,0:T(8,128)S(1)}, u32[]{:S(2)}, u32[]{:S(2)}) %collective-permute-start.3) | collective-permute-done | bytes 32800 | tf_op jit(solution)/shard_map/ppermute | solution.py:598
  55.1 5.6 %shard_map.113 = (f32[8,72,640]{2,1,0:T(8,128)}, f32[5,64,512]{2,1,0:T(8,128)}, f32[5,64,512]{2,1,0:T(8,128)}, f32[8,1024]{1,0:T(8,128)S(1)}, f32[256,128]{1,0:T...) custom-call(f32[8,72,640]{2,1,0:T(8,128)} %get-tuple-element.43.refs_0_, ...), custom_call_target="tpu_custom_call" | custom-call | tf_op jit(solution)/shard_map/pallas_call | solution.py:578
  60.7 7.0 %all_to_all.32 = f32[4,8,8,128]{3,2,1,0:T(8,128)S(1)} all-to-all(f32[4,8,8,128]{3,2,1,0:T(8,128)S(1)} %bitcast.18), channel_id=1, replica_groups=mesh['sec'=8,'girth'=4] {'girth'}, dimensions={0} | all-to-all | bytes 262144 | tf_op jit(solution)/shard_map/all_to_all | solution.py:604
  68.4 5.4 %all-to-all-start.5 = ((f32[8,4,8,128]{3,2,1,0:T(8,128)}), f32[8,4,8,128]{3,2,1,0:T(8,128)S(1)}, u32[]{:S(2)}, u32[]{:S(2)}) async-start(f32[8,4,8,128]{3,2,1,0:T(8,128)} %copy.20), calls=%async_computation.5 | async-start | bytes 262144 | tf_op jit(solution)/shard_map/all_to_all | solution.py:606
  73.9 3.9 %collective-permute-start.4 = (f32[16,512]{1,0:T(8,128)S(1)}, f32[16,512]{1,0:T(8,128)S(1)}, u32[]{:S(2)}, u32[]{:S(2)}) collective-permute-start(f32[16,512]{1,0:T(8,128)S(1)} %get-tuple-element.56), channel_id=1, source_target_pairs={{0,4},{4,8},{8,12},{12,16},{16,20},{20,24},{24,28},{1,5},{5,9},{9,... | collective-permute-start | bytes 98312 | tf_op jit(solution)/shard_map/ppermute | solution.py:593
  77.8 1.3 %collective-permute-start.5 = (f32[16,512]{1,0:T(8,128)S(1)}, f32[16,512]{1,0:T(8,128)S(1)}, u32[]{:S(2)}, u32[]{:S(2)}) collective-permute-start(f32[16,512]{1,0:T(8,128)S(1)} %get-tuple-element.57), channel_id=1, source_target_pairs={{4,0},{8,4},{12,8},{16,12},{20,16},{24,20},{28,24},{5,1},{9,5},{13... | collective-permute-start | bytes 98312 | tf_op jit(solution)/shard_map/ppermute | solution.py:598
  79.4 4.2 %collective-permute-done.5.refs_7_ = f32[16,512]{1,0:T(8,128)S(1)} collective-permute-done((f32[16,512]{1,0:T(8,128)S(1)}, f32[16,512]{1,0:T(8,128)S(1)}, u32[]{:S(2)}, u32[]{:S(2)}) %collective-permute-start.5) | collective-permute-done | bytes 32800 | tf_op jit(solution)/shard_map/ppermute | solution.py:598
  83.6 5.0 %shard_map.114 = (f32[8,72,640]{2,1,0:T(8,128)}, f32[5,64,512]{2,1,0:T(8,128)}, f32[5,64,512]{2,1,0:T(8,128)}, f32[8,128]{1,0:T(8,128)S(1)}, f32[8,128]{1,0:T(8,...) custom-call(f32[8,72,640]{2,1,0:T(8,128)} %get-tuple-element.52.refs_0_, f32[5,64,512]{2,1,0:T(8,128)} %get-tuple-element.53.refs_1_, ...), custom_call_target="tpu_custom_call" | custom-call | tf_op jit(solution)/shard_map/pallas_call | solution.py:578
  88.6 4.3 %collective-permute-start.8 = (f32[8,512]{1,0:T(8,128)S(1)}, f32[8,512]{1,0:T(8,128)S(1)}, u32[]{:S(2)}, u32[]{:S(2)}) collective-permute-start(f32[8,512]{1,0:T(8,128)S(1)} %get-tuple-element.64), channel_id=1, source_target_pairs={{0,4},{4,8},{8,12},{12,16},{16,20},{20,24},{24,28},{1,5},{5,9},{9,... | collective-permute-start | bytes 49160 | tf_op jit(solution)/shard_map/ppermute | solution.py:593
  92.9 1.3 %collective-permute-start.9 = (f32[8,512]{1,0:T(8,128)S(1)}, f32[8,512]{1,0:T(8,128)S(1)}, u32[]{:S(2)}, u32[]{:S(2)}) collective-permute-start(f32[8,512]{1,0:T(8,128)S(1)} %get-tuple-element.65), channel_id=1, source_target_pairs={{4,0},{8,4},{12,8},{16,12},{20,16},{24,20},{28,24},{5,1},{9,5},{13... | collective-permute-start | bytes 49160 | tf_op jit(solution)/shard_map/ppermute | solution.py:598
  94.3 1.7 %collective-permute-start.7 = (f32[8,128]{1,0:T(8,128)S(1)}, f32[8,128]{1,0:T(8,128)S(1)}, u32[]{:S(2)}, u32[]{:S(2)}) collective-permute-start(f32[8,128]{1,0:T(8,128)S(1)} %get-tuple-element.63), channel_id=1, source_target_pairs={{0,3},{1,0},{2,1},{3,2},{4,7},{5,4},{6,5},{7,6},{8,11},{9,8},{10,9... | collective-permute-start | bytes 12296 | tf_op jit(solution)/shard_map/ppermute | solution.py:612
  98.5 3.4 %shard_map.115 = (f32[8,64,512]{2,1,0:T(8,128)}, f32[8,64]{1,0:T(8,128)S(1)}) custom-call(f32[8,72,640]{2,1,0:T(8,128)} %get-tuple-element.61.stress_in, f32[5,64,512]{2,1,0:T(8,128)} %get-tuple-element.33.velocity_in, f32[8,128]{1,0:T(8,128)S(1)} %collective-permute-done.6.from_left, f32[8,128]{1,0:T(8,128)S(1)} %collective-permute-done.7.from_right, ...), custom_call_target="tpu_custom_call" | custom-call | tf_op jit(solution)/shard_map/pallas_call | solution.py:578
  102.0 6.7 %psum.7 = f32[64]{0:T(128)} all-reduce(f32[64]{0:T(128)S(1)} %slice_bitcast_fusion), channel_id=1, replica_groups=mesh['sec'=8,'girth'=4] {'girth'}, use_global_device_ids=true, to_apply=%region_0.0 | all-reduce | flops 64 | bytes 512 | tf_op jit(solution)/shard_map/psum | solution.py:707
  (17 shorter events, 5.4 us)
Async XLA Ops:
  12.5 15.6 %all-to-all-start.1 = ((f32[8,4,8,128]{3,2,1,0:T(8,128)}), f32[8,4,8,128]{3,2,1,0:T(8,128)S(1)}, u32[]{:S(2)}, u32[]{:S(2)}) async-start(f32[8,4,8,128]{3,2,1,0:T(8,128)} %copy.18), calls=%async_computation.1 | async-start | bytes 262144 | tf_op jit(solution)/shard_map/all_to_all | solution.py:606
  18.4 5.5 %collective-permute-start = (f32[16,512]{1,0:T(8,128)S(1)}, f32[16,512]{1,0:T(8,128)S(1)}, u32[]{:S(2)}, u32[]{:S(2)}) collective-permute-start(f32[16,512]{1,0:T(8,128)S(1)} %get-tuple-element.37), channel_id=1, source_target_pairs={{0,4},{4,8},{8,12},{12,16},{16,20},{20,24},{24,28},{1,5},{5,9},{9,... | collective-permute-start | bytes 98312 | tf_op jit(solution)/shard_map/ppermute | solution.py:593
  22.3 5.8 %collective-permute-start.1 = (f32[16,512]{1,0:T(8,128)S(1)}, f32[16,512]{1,0:T(8,128)S(1)}, u32[]{:S(2)}, u32[]{:S(2)}) collective-permute-start(f32[16,512]{1,0:T(8,128)S(1)} %get-tuple-element.38), channel_id=1, source_target_pairs={{4,0},{8,4},{12,8},{16,12},{20,16},{24,20},{28,24},{5,1},{9,5},{13... | collective-permute-start | bytes 98312 | tf_op jit(solution)/shard_map/ppermute | solution.py:598
  39.9 15.2 %all-to-all-start.3 = ((f32[8,4,8,128]{3,2,1,0:T(8,128)}), f32[8,4,8,128]{3,2,1,0:T(8,128)S(1)}, u32[]{:S(2)}, u32[]{:S(2)}) async-start(f32[8,4,8,128]{3,2,1,0:T(8,128)} %copy.19), calls=%async_computation.3 | async-start | bytes 262144 | tf_op jit(solution)/shard_map/all_to_all | solution.py:606
  45.4 5.5 %collective-permute-start.2 = (f32[16,512]{1,0:T(8,128)S(1)}, f32[16,512]{1,0:T(8,128)S(1)}, u32[]{:S(2)}, u32[]{:S(2)}) collective-permute-start(f32[16,512]{1,0:T(8,128)S(1)} %get-tuple-element.47), channel_id=1, source_target_pairs={{0,4},{4,8},{8,12},{12,16},{16,20},{20,24},{24,28},{1,5},{5,9},{9,... | collective-permute-start | bytes 98312 | tf_op jit(solution)/shard_map/ppermute | solution.py:593
  49.3 5.8 %collective-permute-start.3 = (f32[16,512]{1,0:T(8,128)S(1)}, f32[16,512]{1,0:T(8,128)S(1)}, u32[]{:S(2)}, u32[]{:S(2)}) collective-permute-start(f32[16,512]{1,0:T(8,128)S(1)} %get-tuple-element.48), channel_id=1, source_target_pairs={{4,0},{8,4},{12,8},{16,12},{20,16},{24,20},{28,24},{5,1},{9,5},{13... | collective-permute-start | bytes 98312 | tf_op jit(solution)/shard_map/ppermute | solution.py:598
  68.4 15.2 %all-to-all-start.5 = ((f32[8,4,8,128]{3,2,1,0:T(8,128)}), f32[8,4,8,128]{3,2,1,0:T(8,128)S(1)}, u32[]{:S(2)}, u32[]{:S(2)}) async-start(f32[8,4,8,128]{3,2,1,0:T(8,128)} %copy.20), calls=%async_computation.5 | async-start | bytes 262144 | tf_op jit(solution)/shard_map/all_to_all | solution.py:606
  73.9 5.5 %collective-permute-start.4 = (f32[16,512]{1,0:T(8,128)S(1)}, f32[16,512]{1,0:T(8,128)S(1)}, u32[]{:S(2)}, u32[]{:S(2)}) collective-permute-start(f32[16,512]{1,0:T(8,128)S(1)} %get-tuple-element.56), channel_id=1, source_target_pairs={{0,4},{4,8},{8,12},{12,16},{16,20},{20,24},{24,28},{1,5},{5,9},{9,... | collective-permute-start | bytes 98312 | tf_op jit(solution)/shard_map/ppermute | solution.py:593
  77.8 5.8 %collective-permute-start.5 = (f32[16,512]{1,0:T(8,128)S(1)}, f32[16,512]{1,0:T(8,128)S(1)}, u32[]{:S(2)}, u32[]{:S(2)}) collective-permute-start(f32[16,512]{1,0:T(8,128)S(1)} %get-tuple-element.57), channel_id=1, source_target_pairs={{4,0},{8,4},{12,8},{16,12},{20,16},{24,20},{28,24},{5,1},{9,5},{13... | collective-permute-start | bytes 98312 | tf_op jit(solution)/shard_map/ppermute | solution.py:598
  88.6 8.7 %collective-permute-start.8 = (f32[8,512]{1,0:T(8,128)S(1)}, f32[8,512]{1,0:T(8,128)S(1)}, u32[]{:S(2)}, u32[]{:S(2)}) collective-permute-start(f32[8,512]{1,0:T(8,128)S(1)} %get-tuple-element.64), channel_id=1, source_target_pairs={{0,4},{4,8},{8,12},{12,16},{16,20},{20,24},{24,28},{1,5},{5,9},{9,... | collective-permute-start | bytes 49160 | tf_op jit(solution)/shard_map/ppermute | solution.py:593
  92.9 5.6 %collective-permute-start.9 = (f32[8,512]{1,0:T(8,128)S(1)}, f32[8,512]{1,0:T(8,128)S(1)}, u32[]{:S(2)}, u32[]{:S(2)}) collective-permute-start(f32[8,512]{1,0:T(8,128)S(1)} %get-tuple-element.65), channel_id=1, source_target_pairs={{4,0},{8,4},{12,8},{16,12},{20,16},{24,20},{28,24},{5,1},{9,5},{13... | collective-permute-start | bytes 49160 | tf_op jit(solution)/shard_map/ppermute | solution.py:598
  94.2 3.1 %collective-permute-start.6 = (f32[8,128]{1,0:T(8,128)S(1)}, f32[8,128]{1,0:T(8,128)S(1)}, u32[]{:S(2)}, u32[]{:S(2)}) collective-permute-start(f32[8,128]{1,0:T(8,128)S(1)} %get-tuple-element.62), channel_id=1, source_target_pairs={{0,1},{1,2},{2,3},{3,0},{4,5},{5,6},{6,7},{7,4},{8,9},{9,10},{10,1... | collective-permute-start | bytes 12296 | tf_op jit(solution)/shard_map/ppermute | solution.py:612
  94.3 3.1 %collective-permute-start.7 = (f32[8,128]{1,0:T(8,128)S(1)}, f32[8,128]{1,0:T(8,128)S(1)}, u32[]{:S(2)}, u32[]{:S(2)}) collective-permute-start(f32[8,128]{1,0:T(8,128)S(1)} %get-tuple-element.63), channel_id=1, source_target_pairs={{0,3},{1,0},{2,1},{3,2},{4,7},{5,4},{6,5},{7,6},{8,11},{9,8},{10,9... | collective-permute-start | bytes 12296 | tf_op jit(solution)/shard_map/ppermute | solution.py:612

commit v5 on v3

--- a/solution.py
+++ b/solution.py
@@ -8,6 +8,7 @@
 from jax.sharding import PartitionSpec as P
 
 STEPS = 3
+CORNER_LANE = 112
 FIELDS = 5
 RESULTS = 8
 PAD_ROWS = 8
@@ -104,13 +105,6 @@
     ref[pl.ds(pl.multiple_of(device * 8, 8), 8), :] = value
 
 
-def girth_neighbours():
-    sec, girth, _, girths = place()
-    left = sec * girths + lax.rem(girth + girths - 1, girths)
-    right = sec * girths + lax.rem(girth + 1, girths)
-    return left, right
-
-
 def corner_neighbours():
     sec, girth, secs, girths = place()
     me = sec * girths + girth
@@ -225,16 +219,23 @@
     ]
 
 
-def send_edges(payload, near, far, halo_rows, corners):
-    devices = payload.shape[0] // 8
-    payload[...] = jnp.zeros(payload.shape, F32)
-    payload[pl.ds(0, devices, stride=8), :] = near
-    payload[pl.ds(1, devices, stride=8), :] = far
+def send_joints(payload, near, far, corners):
+    devices = payload.shape[0] // 2
+    payload[pl.ds(0, devices, stride=2), :] = near
+    payload[pl.ds(1, devices, stride=2), :] = far
     row = lax.broadcasted_iota(jnp.int32, (8, LANES), 0)
-    for device, tile in zip(girth_neighbours(), (halo_rows[0:8], halo_rows[8:16])):
-        set_tile(payload, device, jnp.where(row < 2, tile_of(payload, device), tile))
+    lane = lax.broadcasted_iota(jnp.int32, (8, LANES), 1)
+    free = jnp.logical_and(lane >= CORNER_LANE, lane < CORNER_LANE + FIELDS)
     for (device, _), corner in zip(corner_neighbours(), corners):
-        set_tile(payload, device, jnp.where(row == 7, corner, tile_of(payload, device)))
+        tile = lax.div(device, 4)
+        here = jnp.logical_and(free, row == 2 * lax.rem(device, 4))
+        set_tile(payload, tile, jnp.where(here, corner, tile_of(payload, tile)))
+
+
+def corner_of(incoming, device):
+    row = lax.broadcasted_iota(jnp.int32, (8, LANES), 0)
+    tile = tile_of(incoming, lax.div(device, 4))
+    return jnp.sum(jnp.where(row == 2 * lax.rem(device, 4), tile, 0.0), axis=0, keepdims=True)
 
 
 def fetch(done, pairs):
@@ -249,7 +250,8 @@
 
 def start_kernel(
     disp_in, stress_in, thickness_in, from_in, to_in, stiff_in,
-    payload, to_next, to_last, column_marks, row_marks, picked, spring,
+    payload, to_next, to_last, to_left, to_right,
+    column_marks, row_marks, picked, spring,
     disp, stress_left, stress_right, stress_top, stress_bottom, thickness,
     weld_from, weld_to, weld_stiff, done,
 ):
@@ -311,7 +313,9 @@
         columns.append((left, 0, f // 5, 2 + f % 5))
         columns.append((right, LANES - 1, f // 5, 10 + f % 5))
     halo_rows = edge_rows(columns)
-    send_edges(payload, near_out, far_out, halo_rows, [])
+    to_left[...] = halo_rows[0:8]
+    to_right[...] = halo_rows[8:16]
+    send_joints(payload, near_out, far_out, [])
     for ref, stress, row in ((to_next, stress_bottom, rows - 1), (to_last, stress_top, 0)):
         ref[...] = jnp.zeros(ref.shape, F32)
         for f in range(RESULTS):
@@ -329,12 +333,11 @@
     ref[f, rows:, cols:] = corner
 
 
-def load_velocity(vel_ext, incoming, above, below):
-    left, right = girth_neighbours()
-    first, second = edge_columns(tile_of(incoming, left), tile_of(incoming, right))
+def load_velocity(vel_ext, incoming, above, below, from_left, from_right):
+    first, second = edge_columns(from_left[...], from_right[...])
     row = lax.broadcasted_iota(jnp.int32, (8, LANES), 0)
     corner_tiles = [
-        jnp.broadcast_to(jnp.where(inside, tile_of(incoming, device)[7:8], 0.0), (8, LANES))
+        jnp.broadcast_to(jnp.where(inside, corner_of(incoming, device), 0.0), (8, LANES))
         for device, inside in corner_neighbours()
     ]
     for f in range(FIELDS):
@@ -346,18 +349,17 @@
                 (second, 10 + f, 1),
             ]
         )
-        upper = edge_block([(corner_tiles[0], f, LANES - 1), (corner_tiles[1], f, 0)])
-        lower = edge_block([(corner_tiles[2], f, LANES - 1), (corner_tiles[3], f, 0)])
+        upper = edge_block([(corner_tiles[0], CORNER_LANE + f, LANES - 1), (corner_tiles[1], CORNER_LANE + f, 0)])
+        lower = edge_block([(corner_tiles[2], CORNER_LANE + f, LANES - 1), (corner_tiles[3], CORNER_LANE + f, 0)])
         corner = jnp.where(row == 0, lower, jnp.where(row == 7, upper, 0.0))
         fill_halo(
             vel_ext, f, above[2 * f : 2 * f + 2, :], below[2 * f : 2 * f + 2, :], sides, corner
         )
 
 
-def load_stress(stress_ext, plate_ext, thickness, incoming, above, below):
+def load_stress(stress_ext, plate_ext, thickness, above, below, from_left, from_right):
     rows, cols = thickness.shape
-    left, right = girth_neighbours()
-    halves = edge_columns(tile_of(incoming, left), tile_of(incoming, right))
+    halves = edge_columns(from_left[...], from_right[...])
     plate_ext[0, :rows, :cols] = thickness[...].astype(F32) * (1.0 / spacing_mm)
     empty = jnp.zeros((PAD_ROWS, LANES), F32)
     for f in range(RESULTS + 1):
@@ -371,25 +373,27 @@
 def step_kernel(first, last, *refs):
     (stress_in, velocity_in, disp_in, thickness_in, pressure_in) = refs[:5]
     if first:
-        incoming, above, below, column_marks, row_marks, picked, spring = refs[5:12]
-        out = refs[12:]
+        out = refs[14:]
     else:
-        incoming, above, below, column_marks, row_marks, picked, spring, plate_ext = refs[5:13]
-        out = refs[13:]
+        plate_ext = refs[14]
+        out = refs[15:]
+    (incoming, above, below, from_left, from_right,
+     column_marks, row_marks, picked, spring) = refs[5:14]
     stress_out, velocity_out, disp_out = out[:3]
     out = out[3:]
     if first:
         plate_ext, spring_out = out[:2]
         out = out[2:]
-    if last:
-        to_left, to_right, to_next, to_last = out[:4]
-    else:
-        picked_out, payload, to_next, to_last = out[:4]
+    to_left, to_right, to_next, to_last = out[:4]
+    out = out[4:]
+    if not last:
+        picked_out, payload = out[:2]
+        out = out[2:]
     (stress_ext, res_ext, vel_ext, weld, velocity, disp, thickness, pressure,
-     got, sent) = out[4:]
+     got, sent) = out
 
     _, rows, cols = velocity.shape
-    devices = incoming.shape[0] // 8
+    devices = incoming.shape[0] // 2
     total = picked.shape[1]
     half = total // 2
     by_device, by_place = slot_marks(devices, half // devices)
@@ -413,7 +417,7 @@
 
     other = []
     for row in (1, 0):
-        high, low = split(incoming[pl.ds(row, devices, stride=8), :])
+        high, low = split(incoming[pl.ds(row, devices, stride=2), :])
         other.append(expand(high, by_device, by_place) + expand(low, by_device, by_place))
     if first:
         stiffness = jnp.concatenate([spring[0:1, :], other[1][5:6]], axis=1)
@@ -428,9 +432,9 @@
     for copy in copies:
         copy.wait()
     if first:
-        load_stress(stress_ext, plate_ext, thickness, incoming, above, below)
+        load_stress(stress_ext, plate_ext, thickness, above, below, from_left, from_right)
     else:
-        load_velocity(vel_ext, incoming, above, below)
+        load_velocity(vel_ext, incoming, above, below, from_left, from_right)
     for start in range(0, rows + PAD_ROWS, 8):
         plate = plate_ext[0, start : start + 8, :]
         chunk = [stress_ext[k, start : start + 8, :] for k in range(RESULTS)]
@@ -496,9 +500,13 @@
             for f in range(FIELDS):
                 part = velocity[f, tile, ends[0] : ends[1]] if side else velocity[f, tile, 0:LANES]
                 source = LANES - 1 if side else 0
-                value = jnp.where(lane == f, pltpu.roll(part, (f - source) % LANES, 1), value)
+                target = CORNER_LANE + f
+                value = jnp.where(lane == target, pltpu.roll(part, (target - source) % LANES, 1), value)
             corners.append(jnp.broadcast_to(value[row % 8 : row % 8 + 1], (8, LANES)))
-    send_edges(payload, near_out, far_out, edge_rows(columns), corners)
+    halo_rows = edge_rows(columns)
+    to_left[...] = halo_rows[0:8]
+    to_right[...] = halo_rows[8:16]
+    send_joints(payload, near_out, far_out, corners)
     for ref, start in ((to_next, rows - 2), (to_last, 0)):
         ref[...] = jnp.zeros(ref.shape, F32)
         for f in range(FIELDS):
@@ -580,6 +588,12 @@
     return lax.ppermute(values, "sec", [(i + 1, i) for i in range(count - 1)])
 
 
+def exchange(joints):
+    blocks = joints.reshape(joints.shape[0] // 2, 2, LANES)
+    blocks = lax.all_to_all(blocks, ("sec", "girth"), 0, 0, tiled=True)
+    return blocks.reshape(joints.shape)
+
+
 def turn(values, step):
     count = lax.axis_size("girth")
     return lax.ppermute(values, "girth", [(i, (i + step) % count) for i in range(count)])
@@ -595,7 +609,8 @@
     height = jnp.broadcast_to(height[None, :], (8, cols))
 
     vmem_bytes = 8 * 1024 * 1024 + total * VMEM_PER_SLOT
-    message = (devices * 8, LANES)
+    message = (devices * 2, LANES)
+    edge = (8, LANES)
     strip = (16, cols)
     block = (FIELDS, rows, cols)
     stress_shape = (RESULTS, rows + PAD_ROWS, cols + LANES)
@@ -612,12 +627,12 @@
         ((rows, cols), F32),
     ]
 
-    payload, to_next, to_last, column_marks, row_marks, picked, spring = call(
+    payload, to_next, to_last, to_left, to_right, column_marks, row_marks, picked, spring = call(
         start_kernel,
         vmem_bytes,
         [
-            (message, F32), (strip, F32), (strip, F32), ((cols, total), BF16),
-            ((rows, total), BF16), (slot_rows, F32), ((8, total // 2), F32),
+            (message, F32), (strip, F32), (strip, F32), (edge, F32), (edge, F32),
+            ((cols, total), BF16), ((rows, total), BF16), (slot_rows, F32), ((8, total // 2), F32),
         ],
         [
             (block, F32), ((RESULTS, rows, LANES), F32), ((RESULTS, rows, LANES), F32),
@@ -633,23 +648,24 @@
     plate = None
     for step in range(STEPS):
         first, last = step == 0, step == STEPS - 1
-        incoming = lax.all_to_all(payload, ("sec", "girth"), 0, 0, tiled=True)
+        incoming = exchange(payload)
+        from_left, from_right = turn(to_right, 1), turn(to_left, -1)
         above, below = to_next_section(to_next), to_last_section(to_last)
         outs = [(stress_shape, F32), (block, F32), (block, F32)]
         if first:
             outs += [(plate_shape, F32), (slot_rows, F32)]
-        if last:
-            edge = (8, LANES)
-            outs += [(edge, F32), (edge, F32), ((8, cols), F32), ((8, cols), F32)]
-        else:
-            outs += [(slot_rows, F32), (message, F32), (strip, F32), (strip, F32)]
+        halo = (8, cols) if last else strip
+        outs += [(edge, F32), (edge, F32), (halo, F32), (halo, F32)]
+        if not last:
+            outs += [(slot_rows, F32), (message, F32)]
         results = call(
             functools.partial(step_kernel, first, last),
             vmem_bytes,
             outs,
             scratch,
             stress, velocity, displacement, thickness, pressure,
-            incoming, above, below, column_marks, row_marks, picked, spring,
+            incoming, above, below, from_left, from_right,
+            column_marks, row_marks, picked, spring,
             *([] if first else [plate]),
             far=5,
             far_out=3,
@@ -660,10 +676,9 @@
         if first:
             plate, spring = results[:2]
             results = results[2:]
-        if last:
-            to_left, to_right, to_next, to_last = results
-        else:
-            picked, payload, to_next, to_last = results
+        to_left, to_right, to_next, to_last = results[:4]
+        if not last:
+            picked, payload = results[4:]
 
     from_left, from_right = turn(to_right, 1), turn(to_left, -1)
     above, below = to_next_section(to_next), to_last_section(to_last)

time: 86.8 us -> 87.4 us (level)
  starting transfers between devices: 40.6 us -> 46.1 us
  waiting for transfers between devices: 16 us -> 10.6 us
    ppermute x4, waiting for transfers between devices: 13.9 us -> 5.36 us  [to_last_section(): return lax.ppermute(values, 'sec', [(i + 1, i) for i in range(count - 1)])]
    ppermute x2 -> x8, starting transfers between devices: 1.79 us -> 7.17 us  [turn(): lax.ppermute(values, 'girth', [(i, (i + step) % count) for i in range(cou...]
    ppermute x2 -> x8, waiting for transfers between devices: 1.28 us -> 5.27 us  [turn(): lax.ppermute(values, 'girth', [(i, (i + step) % count) for i in range(cou...]
  transfers between devices with their start and end apart: 13 -> 19, of which waited for: 8 -> 8; matrix products, arithmetic and copies ran while one was open for 0% -> 0% of each run, Pallas kernels for 0% -> 0%
where the time goes in v5:
time: 87.4 us; the launch traced here: 86.4 us
  starting transfers between devices  46.1 us (53%)
  Pallas kernels  22.2 us (25%)
  waiting for transfers between devices  10.6 us (12%)
  blocking collectives  6.65 us (8%)
    pallas_call x5, Pallas kernels, call(): pl.pallas_call(kernel, out_shape=[pltpu.HBM(shape, dtype) if k < far_out...  22.2 us
    all_to_all x3, starting transfers between devices, exchange(): blocks = lax.all_to_all(blocks, ('sec', 'girth'), 0, 0, tiled=True)  18.5 us
    ppermute x4, starting transfers between devices, to_next_section(): return lax.ppermute(values, 'sec', [(i, i + 1) for i in range(count - 1)])  15.3 us
    ppermute x8, starting transfers between devices, turn(): lax.ppermute(values, 'girth', [(i, (i + step) % count) for i in range(cou...  7.17 us
    psum x1, blocking collectives, local(): moment = lax.psum(partial_moment[0], 'girth')  6.65 us
    ppermute x4, waiting for transfers between devices, to_last_section(): return lax.ppermute(values, 'sec', [(i + 1, i) for i in range(count - 1)])  5.36 us
    ppermute x8, waiting for transfers between devices, turn(): lax.ppermute(values, 'girth', [(i, (i + step) % count) for i in range(cou...  5.27 us
    ppermute x4, starting transfers between devices, to_last_section(): return lax.ppermute(values, 'sec', [(i + 1, i) for i in range(count - 1)])  5.17 us
  transfers between devices with their start and end apart: 19, of which 8 were waited for; matrix products, arithmetic and copies ran while one was open for 0% of the time, Pallas kernels for 0%

profile of v5, /device:TPU:0, one launch (start us, length us, event | category | flops | bytes accessed | tf_op | source)
XLA Modules:
  0.0 86.4 jit_solution(12293178083318137009)
XLA Ops:
  0.6 3.0 %shard_map.111 = (f32[64,128]{1,0:T(8,128)}, f32[16,512]{1,0:T(8,128)S(1)}, f32[16,512]{1,0:T(8,128)S(1)}, f32[8,128]{1,0:T(8,128)S(1)}, f32[8,128]{1,0:T(8,128)...) custom-call(f32[5,64,512]{2,1,0:T(8,128)} %refs_2_.1, ...), custom_call_target="tpu_custom_call" | custom-call | tf_op jit(solution)/shard_map/pallas_call | solution.py:568
  3.7 7.3 %all-to-all-start = ((f32[32,2,128]{2,1,0:T(2,128)}), f32[32,2,128]{2,1,0:T(2,128)S(1)}, u32[]{:S(2)}, u32[]{:S(2)}) async-start(f32[32,2,128]{2,1,0:T(2,128)} %bitcast.3), calls=%async_computation | async-start | bytes 65536 | tf_op jit(solution)/shard_map/all_to_all | solution.py:593
  11.0 3.7 %collective-permute-start = (f32[16,512]{1,0:T(8,128)S(1)}, f32[16,512]{1,0:T(8,128)S(1)}, u32[]{:S(2)}, u32[]{:S(2)}) collective-permute-start(f32[16,512]{1,0:T(8,128)S(1)} %get-tuple-element.43), channel_id=1, source_target_pairs={{0,4},{4,8},{8,12},{12,16},{16,20},{20,24},{24,28},{1,5},{5,9},{9,... | collective-permute-start | bytes 98312 | tf_op jit(solution)/shard_map/ppermute | solution.py:583
  14.7 1.3 %collective-permute-start.1 = (f32[16,512]{1,0:T(8,128)S(1)}, f32[16,512]{1,0:T(8,128)S(1)}, u32[]{:S(2)}, u32[]{:S(2)}) collective-permute-start(f32[16,512]{1,0:T(8,128)S(1)} %get-tuple-element.44), channel_id=1, source_target_pairs={{4,0},{8,4},{12,8},{16,12},{20,16},{24,20},{28,24},{5,1},{9,5},{13... | collective-permute-start | bytes 98312 | tf_op jit(solution)/shard_map/ppermute | solution.py:588
  16.0 1.7 %collective-permute-start.3 = (f32[8,128]{1,0:T(8,128)S(1)}, f32[8,128]{1,0:T(8,128)S(1)}, u32[]{:S(2)}, u32[]{:S(2)}) collective-permute-start(f32[8,128]{1,0:T(8,128)S(1)} %get-tuple-element.46), channel_id=1, source_target_pairs={{0,3},{1,0},{2,1},{3,2},{4,7},{5,4},{6,5},{7,6},{8,11},{9,8},{10,9... | collective-permute-start | bytes 12296 | tf_op jit(solution)/shard_map/ppermute | solution.py:599
  19.1 1.4 %collective-permute-done.1.refs_7_ = f32[16,512]{1,0:T(8,128)S(1)} collective-permute-done((f32[16,512]{1,0:T(8,128)S(1)}, f32[16,512]{1,0:T(8,128)S(1)}, u32[]{:S(2)}, u32[]{:S(2)}) %collective-permute-start.1) | collective-permute-done | bytes 32800 | tf_op jit(solution)/shard_map/ppermute | solution.py:588
  20.5 5.0 %shard_map.112 = (f32[8,72,640]{2,1,0:T(8,128)}, f32[5,64,512]{2,1,0:T(8,128)}, f32[5,64,512]{2,1,0:T(8,128)}, f32[1,72,640]{2,1,0:T(8,128)S(1)}, f32[8,1024]{1,...) custom-call(f32[8,64,512]{2,1,0:T(8,128)} %refs_0_.1, ...), custom_call_target="tpu_custom_call" | custom-call | tf_op jit(solution)/shard_map/pallas_call | solution.py:568
  25.5 5.6 %all-to-all-start.1 = ((f32[32,2,128]{2,1,0:T(2,128)}), f32[32,2,128]{2,1,0:T(2,128)S(1)}, u32[]{:S(2)}, u32[]{:S(2)}) async-start(f32[32,2,128]{2,1,0:T(2,128)} %bitcast.5), calls=%async_computation.1 | async-start | bytes 65536 | tf_op jit(solution)/shard_map/all_to_all | solution.py:593
  31.1 3.7 %collective-permute-start.4 = (f32[16,512]{1,0:T(8,128)S(1)}, f32[16,512]{1,0:T(8,128)S(1)}, u32[]{:S(2)}, u32[]{:S(2)}) collective-permute-start(f32[16,512]{1,0:T(8,128)S(1)} %get-tuple-element.55), channel_id=1, source_target_pairs={{0,4},{4,8},{8,12},{12,16},{16,20},{20,24},{24,28},{1,5},{5,9},{9,... | collective-permute-start | bytes 98312 | tf_op jit(solution)/shard_map/ppermute | solution.py:583
  34.8 1.3 %collective-permute-start.5 = (f32[16,512]{1,0:T(8,128)S(1)}, f32[16,512]{1,0:T(8,128)S(1)}, u32[]{:S(2)}, u32[]{:S(2)}) collective-permute-start(f32[16,512]{1,0:T(8,128)S(1)} %get-tuple-element.56), channel_id=1, source_target_pairs={{4,0},{8,4},{12,8},{16,12},{20,16},{24,20},{28,24},{5,1},{9,5},{13... | collective-permute-start | bytes 98312 | tf_op jit(solution)/shard_map/ppermute | solution.py:588
  36.2 1.7 %collective-permute-start.7 = (f32[8,128]{1,0:T(8,128)S(1)}, f32[8,128]{1,0:T(8,128)S(1)}, u32[]{:S(2)}, u32[]{:S(2)}) collective-permute-start(f32[8,128]{1,0:T(8,128)S(1)} %get-tuple-element.58), channel_id=1, source_target_pairs={{0,3},{1,0},{2,1},{3,2},{4,7},{5,4},{6,5},{7,6},{8,11},{9,8},{10,9... | collective-permute-start | bytes 12296 | tf_op jit(solution)/shard_map/ppermute | solution.py:599
  39.2 1.4 %collective-permute-done.5.refs_7_ = f32[16,512]{1,0:T(8,128)S(1)} collective-permute-done((f32[16,512]{1,0:T(8,128)S(1)}, f32[16,512]{1,0:T(8,128)S(1)}, u32[]{:S(2)}, u32[]{:S(2)}) %collective-permute-start.5) | collective-permute-done | bytes 32800 | tf_op jit(solution)/shard_map/ppermute | solution.py:588
  40.6 5.7 %shard_map.113 = (f32[8,72,640]{2,1,0:T(8,128)}, f32[5,64,512]{2,1,0:T(8,128)}, f32[5,64,512]{2,1,0:T(8,128)}, f32[8,128]{1,0:T(8,128)S(1)}, f32[8,128]{1,0:T(8,...) custom-call(f32[8,72,640]{2,1,0:T(8,128)} %get-tuple-element.51.refs_0_, ...), custom_call_target="tpu_custom_call" | custom-call | tf_op jit(solution)/shard_map/pallas_call | solution.py:568
  46.3 5.6 %all-to-all-start.2 = ((f32[32,2,128]{2,1,0:T(2,128)}), f32[32,2,128]{2,1,0:T(2,128)S(1)}, u32[]{:S(2)}, u32[]{:S(2)}) async-start(f32[32,2,128]{2,1,0:T(2,128)} %bitcast.7), calls=%async_computation.2 | async-start | bytes 65536 | tf_op jit(solution)/shard_map/all_to_all | solution.py:593
  51.9 3.7 %collective-permute-start.8 = (f32[16,512]{1,0:T(8,128)S(1)}, f32[16,512]{1,0:T(8,128)S(1)}, u32[]{:S(2)}, u32[]{:S(2)}) collective-permute-start(f32[16,512]{1,0:T(8,128)S(1)} %get-tuple-element.66), channel_id=1, source_target_pairs={{0,4},{4,8},{8,12},{12,16},{16,20},{20,24},{24,28},{1,5},{5,9},{9,... | collective-permute-start | bytes 98312 | tf_op jit(solution)/shard_map/ppermute | solution.py:583
  55.6 1.3 %collective-permute-start.9 = (f32[16,512]{1,0:T(8,128)S(1)}, f32[16,512]{1,0:T(8,128)S(1)}, u32[]{:S(2)}, u32[]{:S(2)}) collective-permute-start(f32[16,512]{1,0:T(8,128)S(1)} %get-tuple-element.67), channel_id=1, source_target_pairs={{4,0},{8,4},{12,8},{16,12},{20,16},{24,20},{28,24},{5,1},{9,5},{13... | collective-permute-start | bytes 98312 | tf_op jit(solution)/shard_map/ppermute | solution.py:588
  57.0 1.7 %collective-permute-start.11 = (f32[8,128]{1,0:T(8,128)S(1)}, f32[8,128]{1,0:T(8,128)S(1)}, u32[]{:S(2)}, u32[]{:S(2)}) collective-permute-start(f32[8,128]{1,0:T(8,128)S(1)} %get-tuple-element.69), channel_id=1, source_target_pairs={{0,3},{1,0},{2,1},{3,2},{4,7},{5,4},{6,5},{7,6},{8,11},{9,8},{10,9... | collective-permute-start | bytes 12296 | tf_op jit(solution)/shard_map/ppermute | solution.py:599
  60.0 1.4 %collective-permute-done.9.refs_7_ = f32[16,512]{1,0:T(8,128)S(1)} collective-permute-done((f32[16,512]{1,0:T(8,128)S(1)}, f32[16,512]{1,0:T(8,128)S(1)}, u32[]{:S(2)}, u32[]{:S(2)}) %collective-permute-start.9) | collective-permute-done | bytes 32800 | tf_op jit(solution)/shard_map/ppermute | solution.py:588
  61.4 5.0 %shard_map.114 = (f32[8,72,640]{2,1,0:T(8,128)}, f32[5,64,512]{2,1,0:T(8,128)}, f32[5,64,512]{2,1,0:T(8,128)}, f32[8,128]{1,0:T(8,128)S(1)}, f32[8,128]{1,0:T(8,...) custom-call(f32[8,72,640]{2,1,0:T(8,128)} %get-tuple-element.62.refs_0_, f32[5,64,512]{2,1,0:T(8,128)} %get-tuple-element.63.refs_1_, ...), custom_call_target="tpu_custom_call" | custom-call | tf_op jit(solution)/shard_map/pallas_call | solution.py:568
  66.4 4.3 %collective-permute-start.14 = (f32[8,512]{1,0:T(8,128)S(1)}, f32[8,512]{1,0:T(8,128)S(1)}, u32[]{:S(2)}, u32[]{:S(2)}) collective-permute-start(f32[8,512]{1,0:T(8,128)S(1)} %get-tuple-element.76), channel_id=1, source_target_pairs={{0,4},{4,8},{8,12},{12,16},{16,20},{20,24},{24,28},{1,5},{5,9},{9,... | collective-permute-start | bytes 49160 | tf_op jit(solution)/shard_map/ppermute | solution.py:583
  70.7 1.3 %collective-permute-start.15 = (f32[8,512]{1,0:T(8,128)S(1)}, f32[8,512]{1,0:T(8,128)S(1)}, u32[]{:S(2)}, u32[]{:S(2)}) collective-permute-start(f32[8,512]{1,0:T(8,128)S(1)} %get-tuple-element.77), channel_id=1, source_target_pairs={{4,0},{8,4},{12,8},{16,12},{20,16},{24,20},{28,24},{5,1},{9,5},{13... | collective-permute-start | bytes 49160 | tf_op jit(solution)/shard_map/ppermute | solution.py:588
  72.2 1.6 %collective-permute-start.13 = (f32[8,128]{1,0:T(8,128)S(1)}, f32[8,128]{1,0:T(8,128)S(1)}, u32[]{:S(2)}, u32[]{:S(2)}) collective-permute-start(f32[8,128]{1,0:T(8,128)S(1)} %get-tuple-element.75), channel_id=1, source_target_pairs={{0,3},{1,0},{2,1},{3,2},{4,7},{5,4},{6,5},{7,6},{8,11},{9,8},{10,9... | collective-permute-start | bytes 12296 | tf_op jit(solution)/shard_map/ppermute | solution.py:599
  76.4 3.4 %shard_map.115 = (f32[8,64,512]{2,1,0:T(8,128)}, f32[8,64]{1,0:T(8,128)S(1)}) custom-call(f32[8,72,640]{2,1,0:T(8,128)} %get-tuple-element.73.stress_in, f32[5,64,512]{2,1,0:T(8,128)} %get-tuple-element.39.velocity_in, f32[8,128]{1,0:T(8,128)S(1)} %collective-permute-done.12.from_left, f32[8,128]{1,0:T(8,128)S(1)} %collective-permute-done.13.from_right, ...), custom_call_target="tpu_custom_call" | custom-call | tf_op jit(solution)/shard_map/pallas_call | solution.py:568
  79.8 6.7 %psum.7 = f32[64]{0:T(128)} all-reduce(f32[64]{0:T(128)S(1)} %slice_bitcast_fusion), channel_id=1, replica_groups=mesh['sec'=8,'girth'=4] {'girth'}, use_global_device_ids=true, to_apply=%region_0.0 | all-reduce | flops 64 | bytes 512 | tf_op jit(solution)/shard_map/psum | solution.py:695
  (23 shorter events, 7.0 us)
Async XLA Ops:
  3.7 16.8 %all-to-all-start = ((f32[32,2,128]{2,1,0:T(2,128)}), f32[32,2,128]{2,1,0:T(2,128)S(1)}, u32[]{:S(2)}, u32[]{:S(2)}) async-start(f32[32,2,128]{2,1,0:T(2,128)} %bitcast.3), calls=%async_computation | async-start | bytes 65536 | tf_op jit(solution)/shard_map/all_to_all | solution.py:593
  11.0 8.1 %collective-permute-start = (f32[16,512]{1,0:T(8,128)S(1)}, f32[16,512]{1,0:T(8,128)S(1)}, u32[]{:S(2)}, u32[]{:S(2)}) collective-permute-start(f32[16,512]{1,0:T(8,128)S(1)} %get-tuple-element.43), channel_id=1, source_target_pairs={{0,4},{4,8},{8,12},{12,16},{16,20},{20,24},{24,28},{1,5},{5,9},{9,... | collective-permute-start | bytes 98312 | tf_op jit(solution)/shard_map/ppermute | solution.py:583
  14.7 5.8 %collective-permute-start.1 = (f32[16,512]{1,0:T(8,128)S(1)}, f32[16,512]{1,0:T(8,128)S(1)}, u32[]{:S(2)}, u32[]{:S(2)}) collective-permute-start(f32[16,512]{1,0:T(8,128)S(1)} %get-tuple-element.44), channel_id=1, source_target_pairs={{4,0},{8,4},{12,8},{16,12},{20,16},{24,20},{28,24},{5,1},{9,5},{13... | collective-permute-start | bytes 98312 | tf_op jit(solution)/shard_map/ppermute | solution.py:588
  16.0 3.1 %collective-permute-start.2 = (f32[8,128]{1,0:T(8,128)S(1)}, f32[8,128]{1,0:T(8,128)S(1)}, u32[]{:S(2)}, u32[]{:S(2)}) collective-permute-start(f32[8,128]{1,0:T(8,128)S(1)} %get-tuple-element.45), channel_id=1, source_target_pairs={{0,1},{1,2},{2,3},{3,0},{4,5},{5,6},{6,7},{7,4},{8,9},{9,10},{10,1... | collective-permute-start | bytes 12296 | tf_op jit(solution)/shard_map/ppermute | solution.py:599
  16.0 3.1 %collective-permute-start.3 = (f32[8,128]{1,0:T(8,128)S(1)}, f32[8,128]{1,0:T(8,128)S(1)}, u32[]{:S(2)}, u32[]{:S(2)}) collective-permute-start(f32[8,128]{1,0:T(8,128)S(1)} %get-tuple-element.46), channel_id=1, source_target_pairs={{0,3},{1,0},{2,1},{3,2},{4,7},{5,4},{6,5},{7,6},{8,11},{9,8},{10,9... | collective-permute-start | bytes 12296 | tf_op jit(solution)/shard_map/ppermute | solution.py:599
  25.5 15.1 %all-to-all-start.1 = ((f32[32,2,128]{2,1,0:T(2,128)}), f32[32,2,128]{2,1,0:T(2,128)S(1)}, u32[]{:S(2)}, u32[]{:S(2)}) async-start(f32[32,2,128]{2,1,0:T(2,128)} %bitcast.5), calls=%async_computation.1 | async-start | bytes 65536 | tf_op jit(solution)/shard_map/all_to_all | solution.py:593
  31.1 8.1 %collective-permute-start.4 = (f32[16,512]{1,0:T(8,128)S(1)}, f32[16,512]{1,0:T(8,128)S(1)}, u32[]{:S(2)}, u32[]{:S(2)}) collective-permute-start(f32[16,512]{1,0:T(8,128)S(1)} %get-tuple-element.55), channel_id=1, source_target_pairs={{0,4},{4,8},{8,12},{12,16},{16,20},{20,24},{24,28},{1,5},{5,9},{9,... | collective-permute-start | bytes 98312 | tf_op jit(solution)/shard_map/ppermute | solution.py:583
  34.8 5.8 %collective-permute-start.5 = (f32[16,512]{1,0:T(8,128)S(1)}, f32[16,512]{1,0:T(8,128)S(1)}, u32[]{:S(2)}, u32[]{:S(2)}) collective-permute-start(f32[16,512]{1,0:T(8,128)S(1)} %get-tuple-element.56), channel_id=1, source_target_pairs={{4,0},{8,4},{12,8},{16,12},{20,16},{24,20},{28,24},{5,1},{9,5},{13... | collective-permute-start | bytes 98312 | tf_op jit(solution)/shard_map/ppermute | solution.py:588
  36.1 3.1 %collective-permute-start.6 = (f32[8,128]{1,0:T(8,128)S(1)}, f32[8,128]{1,0:T(8,128)S(1)}, u32[]{:S(2)}, u32[]{:S(2)}) collective-permute-start(f32[8,128]{1,0:T(8,128)S(1)} %get-tuple-element.57), channel_id=1, source_target_pairs={{0,1},{1,2},{2,3},{3,0},{4,5},{5,6},{6,7},{7,4},{8,9},{9,10},{10,1... | collective-permute-start | bytes 12296 | tf_op jit(solution)/shard_map/ppermute | solution.py:599
  36.2 3.1 %collective-permute-start.7 = (f32[8,128]{1,0:T(8,128)S(1)}, f32[8,128]{1,0:T(8,128)S(1)}, u32[]{:S(2)}, u32[]{:S(2)}) collective-permute-start(f32[8,128]{1,0:T(8,128)S(1)} %get-tuple-element.58), channel_id=1, source_target_pairs={{0,3},{1,0},{2,1},{3,2},{4,7},{5,4},{6,5},{7,6},{8,11},{9,8},{10,9... | collective-permute-start | bytes 12296 | tf_op jit(solution)/shard_map/ppermute | solution.py:599
  46.3 15.1 %all-to-all-start.2 = ((f32[32,2,128]{2,1,0:T(2,128)}), f32[32,2,128]{2,1,0:T(2,128)S(1)}, u32[]{:S(2)}, u32[]{:S(2)}) async-start(f32[32,2,128]{2,1,0:T(2,128)} %bitcast.7), calls=%async_computation.2 | async-start | bytes 65536 | tf_op jit(solution)/shard_map/all_to_all | solution.py:593
  51.9 8.1 %collective-permute-start.8 = (f32[16,512]{1,0:T(8,128)S(1)}, f32[16,512]{1,0:T(8,128)S(1)}, u32[]{:S(2)}, u32[]{:S(2)}) collective-permute-start(f32[16,512]{1,0:T(8,128)S(1)} %get-tuple-element.66), channel_id=1, source_target_pairs={{0,4},{4,8},{8,12},{12,16},{16,20},{20,24},{24,28},{1,5},{5,9},{9,... | collective-permute-start | bytes 98312 | tf_op jit(solution)/shard_map/ppermute | solution.py:583
  55.6 5.8 %collective-permute-start.9 = (f32[16,512]{1,0:T(8,128)S(1)}, f32[16,512]{1,0:T(8,128)S(1)}, u32[]{:S(2)}, u32[]{:S(2)}) collective-permute-start(f32[16,512]{1,0:T(8,128)S(1)} %get-tuple-element.67), channel_id=1, source_target_pairs={{4,0},{8,4},{12,8},{16,12},{20,16},{24,20},{28,24},{5,1},{9,5},{13... | collective-permute-start | bytes 98312 | tf_op jit(solution)/shard_map/ppermute | solution.py:588
  56.9 3.1 %collective-permute-start.10 = (f32[8,128]{1,0:T(8,128)S(1)}, f32[8,128]{1,0:T(8,128)S(1)}, u32[]{:S(2)}, u32[]{:S(2)}) collective-permute-start(f32[8,128]{1,0:T(8,128)S(1)} %get-tuple-element.68), channel_id=1, source_target_pairs={{0,1},{1,2},{2,3},{3,0},{4,5},{5,6},{6,7},{7,4},{8,9},{9,10},{10,1... | collective-permute-start | bytes 12296 | tf_op jit(solution)/shard_map/ppermute | solution.py:599
  57.0 3.1 %collective-permute-start.11 = (f32[8,128]{1,0:T(8,128)S(1)}, f32[8,128]{1,0:T(8,128)S(1)}, u32[]{:S(2)}, u32[]{:S(2)}) collective-permute-start(f32[8,128]{1,0:T(8,128)S(1)} %get-tuple-element.69), channel_id=1, source_target_pairs={{0,3},{1,0},{2,1},{3,2},{4,7},{5,4},{6,5},{7,6},{8,11},{9,8},{10,9... | collective-permute-start | bytes 12296 | tf_op jit(solution)/shard_map/ppermute | solution.py:599
  66.4 8.7 %collective-permute-start.14 = (f32[8,512]{1,0:T(8,128)S(1)}, f32[8,512]{1,0:T(8,128)S(1)}, u32[]{:S(2)}, u32[]{:S(2)}) collective-permute-start(f32[8,512]{1,0:T(8,128)S(1)} %get-tuple-element.76), channel_id=1, source_target_pairs={{0,4},{4,8},{8,12},{12,16},{16,20},{20,24},{24,28},{1,5},{5,9},{9,... | collective-permute-start | bytes 49160 | tf_op jit(solution)/shard_map/ppermute | solution.py:583
  70.7 5.7 %collective-permute-start.15 = (f32[8,512]{1,0:T(8,128)S(1)}, f32[8,512]{1,0:T(8,128)S(1)}, u32[]{:S(2)}, u32[]{:S(2)}) collective-permute-start(f32[8,512]{1,0:T(8,128)S(1)} %get-tuple-element.77), channel_id=1, source_target_pairs={{4,0},{8,4},{12,8},{16,12},{20,16},{24,20},{28,24},{5,1},{9,5},{13... | collective-permute-start | bytes 49160 | tf_op jit(solution)/shard_map/ppermute | solution.py:588
  72.0 3.1 %collective-permute-start.12 = (f32[8,128]{1,0:T(8,128)S(1)}, f32[8,128]{1,0:T(8,128)S(1)}, u32[]{:S(2)}, u32[]{:S(2)}) collective-permute-start(f32[8,128]{1,0:T(8,128)S(1)} %get-tuple-element.74), channel_id=1, source_target_pairs={{0,1},{1,2},{2,3},{3,0},{4,5},{5,6},{6,7},{7,4},{8,9},{9,10},{10,1... | collective-permute-start | bytes 12296 | tf_op jit(solution)/shard_map/ppermute | solution.py:599
  72.2 2.9 %collective-permute-start.13 = (f32[8,128]{1,0:T(8,128)S(1)}, f32[8,128]{1,0:T(8,128)S(1)}, u32[]{:S(2)}, u32[]{:S(2)}) collective-permute-start(f32[8,128]{1,0:T(8,128)S(1)} %get-tuple-element.75), channel_id=1, source_target_pairs={{0,3},{1,0},{2,1},{3,2},{4,7},{5,4},{6,5},{7,6},{8,11},{9,8},{10,9... | collective-permute-start | bytes 12296 | tf_op jit(solution)/shard_map/ppermute | solution.py:599

commit v6 on v5

--- a/solution.py
+++ b/solution.py
@@ -232,6 +232,27 @@
         set_tile(payload, tile, jnp.where(here, corner, tile_of(payload, tile)))
 
 
+def in_order(axis, low, high):
+    even = lax.rem(lax.axis_index(axis), 2) == 0
+    return jnp.where(even, high, low), jnp.where(even, low, high)
+
+
+def send_sides(pair, halo_rows):
+    for ref, value in zip(pair, in_order("girth", halo_rows[0:8], halo_rows[8:16])):
+        ref[...] = value
+
+
+def send_ends(pair, low, high):
+    for ref in pair:
+        ref[...] = jnp.zeros(ref.shape, F32)
+    start = 0
+    for top, bottom in zip(low, high):
+        count = top.shape[0]
+        for ref, value in zip(pair, in_order("sec", top, bottom)):
+            ref[start : start + count, :] = value
+        start += count
+
+
 def corner_of(incoming, device):
     row = lax.broadcasted_iota(jnp.int32, (8, LANES), 0)
     tile = tile_of(incoming, lax.div(device, 4))
@@ -250,13 +271,14 @@
 
 def start_kernel(
     disp_in, stress_in, thickness_in, from_in, to_in, stiff_in,
-    payload, to_next, to_last, to_left, to_right,
+    payload, sec_first, sec_second, girth_first, girth_second,
     column_marks, row_marks, picked, spring,
     disp, stress_left, stress_right, stress_top, stress_bottom, thickness,
     weld_from, weld_to, weld_stiff, done,
 ):
     rows, cols = thickness.shape
     _, slots, devices = weld_from.shape
+    sec_pair, girth_pair = (sec_first, sec_second), (girth_first, girth_second)
     copies = fetch(
         done,
         [
@@ -312,15 +334,13 @@
         right = stress_right[f] if f < RESULTS else plate[:, cols - LANES :]
         columns.append((left, 0, f // 5, 2 + f % 5))
         columns.append((right, LANES - 1, f // 5, 10 + f % 5))
-    halo_rows = edge_rows(columns)
-    to_left[...] = halo_rows[0:8]
-    to_right[...] = halo_rows[8:16]
+    send_sides(girth_pair, edge_rows(columns))
     send_joints(payload, near_out, far_out, [])
-    for ref, stress, row in ((to_next, stress_bottom, rows - 1), (to_last, stress_top, 0)):
-        ref[...] = jnp.zeros(ref.shape, F32)
-        for f in range(RESULTS):
-            ref[f : f + 1, :] = stress[f, row % 8 : row % 8 + 1, :]
-        ref[RESULTS : RESULTS + 1, :] = plate[row : row + 1, :]
+    send_ends(
+        sec_pair,
+        [stress_top[f, 0:1, :] for f in range(RESULTS)] + [plate[0:1, :]],
+        [stress_bottom[f, 7:8, :] for f in range(RESULTS)] + [plate[rows - 1 : rows, :]],
+    )
 
 
 def fill_halo(ref, f, above, below, sides, corner):
@@ -333,8 +353,8 @@
     ref[f, rows:, cols:] = corner
 
 
-def load_velocity(vel_ext, incoming, above, below, from_left, from_right):
-    first, second = edge_columns(from_left[...], from_right[...])
+def load_velocity(vel_ext, incoming, above, below, left, right):
+    first, second = edge_columns(left, right)
     row = lax.broadcasted_iota(jnp.int32, (8, LANES), 0)
     corner_tiles = [
         jnp.broadcast_to(jnp.where(inside, corner_of(incoming, device), 0.0), (8, LANES))
@@ -357,9 +377,9 @@
         )
 
 
-def load_stress(stress_ext, plate_ext, thickness, above, below, from_left, from_right):
+def load_stress(stress_ext, plate_ext, thickness, above, below, left, right):
     rows, cols = thickness.shape
-    halves = edge_columns(from_left[...], from_right[...])
+    halves = edge_columns(left, right)
     plate_ext[0, :rows, :cols] = thickness[...].astype(F32) * (1.0 / spacing_mm)
     empty = jnp.zeros((PAD_ROWS, LANES), F32)
     for f in range(RESULTS + 1):
@@ -377,14 +397,14 @@
     else:
         plate_ext = refs[14]
         out = refs[15:]
-    (incoming, above, below, from_left, from_right,
+    (incoming, sec_first, sec_second, girth_first, girth_second,
      column_marks, row_marks, picked, spring) = refs[5:14]
     stress_out, velocity_out, disp_out = out[:3]
     out = out[3:]
     if first:
         plate_ext, spring_out = out[:2]
         out = out[2:]
-    to_left, to_right, to_next, to_last = out[:4]
+    girth_pair, sec_pair = out[0:2], out[2:4]
     out = out[4:]
     if not last:
         picked_out, payload = out[:2]
@@ -429,12 +449,14 @@
     pulls = scale * (jnp.concatenate(other, axis=1) - picked[...])
     weld[...] = spread(pulls, column_marks[...], row_marks[...])
 
+    above, below = in_order("sec", sec_first[...], sec_second[...])
+    left, right = in_order("girth", girth_first[...], girth_second[...])
     for copy in copies:
         copy.wait()
     if first:
-        load_stress(stress_ext, plate_ext, thickness, above, below, from_left, from_right)
+        load_stress(stress_ext, plate_ext, thickness, above, below, left, right)
     else:
-        load_velocity(vel_ext, incoming, above, below, from_left, from_right)
+        load_velocity(vel_ext, incoming, above, below, left, right)
     for start in range(0, rows + PAD_ROWS, 8):
         plate = plate_ext[0, start : start + 8, :]
         chunk = [stress_ext[k, start : start + 8, :] for k in range(RESULTS)]
@@ -470,13 +492,12 @@
         for f in range(FIELDS):
             columns.append((velocity[f, :, 0:LANES], 0, 0, f))
             columns.append((velocity[f, :, ends[0] : ends[1]], LANES - 1, 0, 8 + f))
-        halo_rows = edge_rows(columns)
-        to_left[...] = halo_rows[0:8]
-        to_right[...] = halo_rows[8:16]
-        for ref, row in ((to_next, rows - 1), (to_last, 0)):
-            ref[...] = jnp.zeros(ref.shape, F32)
-            for f in range(FIELDS):
-                ref[f : f + 1, :] = velocity[f, row : row + 1, :]
+        send_sides(girth_pair, edge_rows(columns))
+        send_ends(
+            sec_pair,
+            [velocity[f, 0:1, :] for f in range(FIELDS)],
+            [velocity[f, rows - 1 : rows, :] for f in range(FIELDS)],
+        )
         for copy in sends:
             copy.wait()
         return
@@ -503,26 +524,27 @@
                 target = CORNER_LANE + f
                 value = jnp.where(lane == target, pltpu.roll(part, (target - source) % LANES, 1), value)
             corners.append(jnp.broadcast_to(value[row % 8 : row % 8 + 1], (8, LANES)))
-    halo_rows = edge_rows(columns)
-    to_left[...] = halo_rows[0:8]
-    to_right[...] = halo_rows[8:16]
+    send_sides(girth_pair, edge_rows(columns))
     send_joints(payload, near_out, far_out, corners)
-    for ref, start in ((to_next, rows - 2), (to_last, 0)):
-        ref[...] = jnp.zeros(ref.shape, F32)
-        for f in range(FIELDS):
-            ref[2 * f : 2 * f + 2, :] = velocity[f, start : start + 2, :]
+    send_ends(
+        sec_pair,
+        [velocity[f, 0:2, :] for f in range(FIELDS)],
+        [velocity[f, rows - 2 : rows, :] for f in range(FIELDS)],
+    )
     for copy in sends:
         copy.wait()
 
 
 def final_kernel(
-    stress_in, velocity_in, from_left, from_right, above, below, plate_ext, height,
+    stress_in, velocity_in, sec_first, sec_second, girth_first, girth_second, plate_ext, height,
     stress_out, moment, stress, vel_ext, got, sent,
 ):
     rows, cols = vel_ext.shape[1] - PAD_ROWS, vel_ext.shape[2] - LANES
     inner = (slice(None), slice(0, rows), slice(0, cols))
     copies = fetch(got, [(velocity_in, vel_ext.at[inner]), (stress_in, stress)])
-    first, _ = edge_columns(from_left[...], from_right[...])
+    above, below = in_order("sec", sec_first[...], sec_second[...])
+    left, right = in_order("girth", girth_first[...], girth_second[...])
+    first, _ = edge_columns(left, right)
     empty = jnp.zeros((PAD_ROWS, LANES), F32)
     for f in range(FIELDS):
         sides = edge_block([(first, f, LANES - 1), (first, 8 + f, 0)])
@@ -578,25 +600,20 @@
     )(*operands)
 
 
-def to_next_section(values):
-    count = lax.axis_size("sec")
-    return lax.ppermute(values, "sec", [(i, i + 1) for i in range(count - 1)])
-
-
-def to_last_section(values):
-    count = lax.axis_size("sec")
-    return lax.ppermute(values, "sec", [(i + 1, i) for i in range(count - 1)])
+def swap(pair, axis, around):
+    count = lax.axis_size(axis)
+    out = []
+    for start, value in enumerate(pair):
+        couples = [(i, (i + 1) % count) for i in range(start, count, 2)]
+        couples = [(i, j) for i, j in couples if j > i or around]
+        out.append(lax.ppermute(value, axis, couples + [(j, i) for i, j in couples]))
+    return out
 
 
 def exchange(joints):
     blocks = joints.reshape(joints.shape[0] // 2, 2, LANES)
     blocks = lax.all_to_all(blocks, ("sec", "girth"), 0, 0, tiled=True)
     return blocks.reshape(joints.shape)
-
-
-def turn(values, step):
-    count = lax.axis_size("girth")
-    return lax.ppermute(values, "girth", [(i, (i + step) % count) for i in range(count)])
 
 
 def local(displacement, velocity, stress, thickness, pressure, weld_from, weld_to, weld_stiff):
@@ -627,7 +644,8 @@
         ((rows, cols), F32),
     ]
 
-    payload, to_next, to_last, to_left, to_right, column_marks, row_marks, picked, spring = call(
+    (payload, sec_first, sec_second, girth_first, girth_second,
+     column_marks, row_marks, picked, spring) = call(
         start_kernel,
         vmem_bytes,
         [
@@ -649,8 +667,8 @@
     for step in range(STEPS):
         first, last = step == 0, step == STEPS - 1
         incoming = exchange(payload)
-        from_left, from_right = turn(to_right, 1), turn(to_left, -1)
-        above, below = to_next_section(to_next), to_last_section(to_last)
+        ends = swap((sec_first, sec_second), "sec", False)
+        sides = swap((girth_first, girth_second), "girth", True)
         outs = [(stress_shape, F32), (block, F32), (block, F32)]
         if first:
             outs += [(plate_shape, F32), (slot_rows, F32)]
@@ -664,7 +682,7 @@
             outs,
             scratch,
             stress, velocity, displacement, thickness, pressure,
-            incoming, above, below, from_left, from_right,
+            incoming, *ends, *sides,
             column_marks, row_marks, picked, spring,
             *([] if first else [plate]),
             far=5,
@@ -676,18 +694,18 @@
         if first:
             plate, spring = results[:2]
             results = results[2:]
-        to_left, to_right, to_next, to_last = results[:4]
+        girth_first, girth_second, sec_first, sec_second = results[:4]
         if not last:
             picked, payload = results[4:]
 
-    from_left, from_right = turn(to_right, 1), turn(to_left, -1)
-    above, below = to_next_section(to_next), to_last_section(to_last)
+    ends = swap((sec_first, sec_second), "sec", False)
+    sides = swap((girth_first, girth_second), "girth", True)
     stress, partial_moment = call(
         final_kernel,
         vmem_bytes,
         [((RESULTS, rows, cols), F32), ((8, rows), F32)],
         [(stress_shape, F32), ((FIELDS, rows + PAD_ROWS, cols + LANES), F32)],
-        stress, velocity, from_left, from_right, above, below, plate, height,
+        stress, velocity, *ends, *sides, plate, height,
         far=2,
         far_out=1,
         copies=(2, rows // 16),

time: 87.4 us -> 80 us (0.915)
  the two profiles are of different devices: /device:TPU:0 before, /device:TPU:4 now
where the time goes in v6:
time: 80 us; the launch traced here: 79.5 us
  starting transfers between devices  42.4 us (53%)
  Pallas kernels  22.5 us (28%)
  blocking collectives  7.69 us (10%)
  waiting for transfers between devices  6.03 us (8%)
  between operations  0.81 us (1%)
    ppermute x16, starting transfers between devices, swap(): lax.ppermute(value, axis, couples + [(j, i) for i, j in couples])  26.2 us
    pallas_call x5, Pallas kernels, call(): pl.pallas_call(kernel, out_shape=[pltpu.HBM(shape, dtype) if k < far_out...  22.5 us
    all_to_all x3, starting transfers between devices, exchange(): blocks = lax.all_to_all(blocks, ('sec', 'girth'), 0, 0, tiled=True)  16.2 us
    psum x1, blocking collectives, local(): moment = lax.psum(partial_moment[0], 'girth')  7.69 us
    ppermute x16, waiting for transfers between devices, swap(): lax.ppermute(value, axis, couples + [(j, i) for i, j in couples])  6.02 us
  transfers between devices with their start and end apart: 19, of which 4 were waited for; matrix products, arithmetic and copies ran while one was open for 0% of the time, Pallas kernels for 0%

profile of v6, /device:TPU:4, one launch (start us, length us, event | category | flops | bytes accessed | tf_op | source)
XLA Modules:
  0.0 79.5 jit_solution(17615315040205023859)
XLA Ops:
  0.6 3.0 %shard_map.111 = (f32[64,128]{1,0:T(8,128)}, f32[16,512]{1,0:T(8,128)S(1)}, f32[16,512]{1,0:T(8,128)S(1)}, f32[8,128]{1,0:T(8,128)S(1)}, f32[8,128]{1,0:T(8,128)...) custom-call(f32[5,64,512]{2,1,0:T(8,128)} %refs_2_.1, ...), custom_call_target="tpu_custom_call" | custom-call | tf_op jit(solution)/shard_map/pallas_call | solution.py:590
  3.7 6.1 %all-to-all-start = ((f32[32,2,128]{2,1,0:T(2,128)}), f32[32,2,128]{2,1,0:T(2,128)S(1)}, u32[]{:S(2)}, u32[]{:S(2)}) async-start(f32[32,2,128]{2,1,0:T(2,128)} %bitcast.3), calls=%async_computation | async-start | bytes 65536 | tf_op jit(solution)/shard_map/all_to_all | solution.py:615
  9.8 0.3 collective-permute-start
  10.1 4.6 %collective-permute-start.1 = (f32[16,512]{1,0:T(8,128)S(1)}, f32[16,512]{1,0:T(8,128)S(1)}, u32[]{:S(2)}, u32[]{:S(2)}) collective-permute-start(f32[16,512]{1,0:T(8,128)S(1)} %get-tuple-element.44), channel_id=1, source_target_pairs={{4,8},{12,16},{20,24},{8,4},{16,12},{24,20},{5,9},{13,17},{21,25},... | collective-permute-start | bytes 98312 | tf_op jit(solution)/shard_map/ppermute | solution.py:609
  14.8 1.6 %collective-permute-start.3 = (f32[8,128]{1,0:T(8,128)S(1)}, f32[8,128]{1,0:T(8,128)S(1)}, u32[]{:S(2)}, u32[]{:S(2)}) collective-permute-start(f32[8,128]{1,0:T(8,128)S(1)} %get-tuple-element.46), channel_id=1, source_target_pairs={{1,2},{3,0},{2,1},{0,3},{5,6},{7,4},{6,5},{4,7},{9,10},{11,8},{10,... | collective-permute-start | bytes 12296 | tf_op jit(solution)/shard_map/ppermute | solution.py:609
  16.4 1.5 %collective-permute-done.3.refs_9_ = f32[8,128]{1,0:T(8,128)S(1)} collective-permute-done((f32[8,128]{1,0:T(8,128)S(1)}, f32[8,128]{1,0:T(8,128)S(1)}, u32[]{:S(2)}, u32[]{:S(2)}) %collective-permute-start.3) | collective-permute-done | bytes 4128 | tf_op jit(solution)/shard_map/ppermute | solution.py:609
  17.9 5.0 %shard_map.112 = (f32[8,72,640]{2,1,0:T(8,128)}, f32[5,64,512]{2,1,0:T(8,128)}, f32[5,64,512]{2,1,0:T(8,128)}, f32[1,72,640]{2,1,0:T(8,128)S(1)}, f32[8,1024]{1,...) custom-call(f32[8,64,512]{2,1,0:T(8,128)} %refs_0_.1, ...), custom_call_target="tpu_custom_call" | custom-call | tf_op jit(solution)/shard_map/pallas_call | solution.py:590
  22.9 5.1 %all-to-all-start.1 = ((f32[32,2,128]{2,1,0:T(2,128)}), f32[32,2,128]{2,1,0:T(2,128)S(1)}, u32[]{:S(2)}, u32[]{:S(2)}) async-start(f32[32,2,128]{2,1,0:T(2,128)} %bitcast.5), calls=%async_computation.1 | async-start | bytes 65536 | tf_op jit(solution)/shard_map/all_to_all | solution.py:615
  28.0 0.3 collective-permute-start.4
  28.3 4.6 %collective-permute-start.5 = (f32[16,512]{1,0:T(8,128)S(1)}, f32[16,512]{1,0:T(8,128)S(1)}, u32[]{:S(2)}, u32[]{:S(2)}) collective-permute-start(f32[16,512]{1,0:T(8,128)S(1)} %get-tuple-element.56), channel_id=1, source_target_pairs={{4,8},{12,16},{20,24},{8,4},{16,12},{24,20},{5,9},{13,17},{21,25},... | collective-permute-start | bytes 98312 | tf_op jit(solution)/shard_map/ppermute | solution.py:609
  33.0 1.6 %collective-permute-start.7 = (f32[8,128]{1,0:T(8,128)S(1)}, f32[8,128]{1,0:T(8,128)S(1)}, u32[]{:S(2)}, u32[]{:S(2)}) collective-permute-start(f32[8,128]{1,0:T(8,128)S(1)} %get-tuple-element.58), channel_id=1, source_target_pairs={{1,2},{3,0},{2,1},{0,3},{5,6},{7,4},{6,5},{4,7},{9,10},{11,8},{10,... | collective-permute-start | bytes 12296 | tf_op jit(solution)/shard_map/ppermute | solution.py:609
  34.5 1.5 %collective-permute-done.7.refs_9_ = f32[8,128]{1,0:T(8,128)S(1)} collective-permute-done((f32[8,128]{1,0:T(8,128)S(1)}, f32[8,128]{1,0:T(8,128)S(1)}, u32[]{:S(2)}, u32[]{:S(2)}) %collective-permute-start.7) | collective-permute-done | bytes 4128 | tf_op jit(solution)/shard_map/ppermute | solution.py:609
  36.1 6.0 %shard_map.113 = (f32[8,72,640]{2,1,0:T(8,128)}, f32[5,64,512]{2,1,0:T(8,128)}, f32[5,64,512]{2,1,0:T(8,128)}, f32[8,128]{1,0:T(8,128)S(1)}, f32[8,128]{1,0:T(8,...) custom-call(f32[8,72,640]{2,1,0:T(8,128)} %get-tuple-element.51.refs_0_, ...), custom_call_target="tpu_custom_call" | custom-call | tf_op jit(solution)/shard_map/pallas_call | solution.py:590
  42.1 5.0 %all-to-all-start.2 = ((f32[32,2,128]{2,1,0:T(2,128)}), f32[32,2,128]{2,1,0:T(2,128)S(1)}, u32[]{:S(2)}, u32[]{:S(2)}) async-start(f32[32,2,128]{2,1,0:T(2,128)} %bitcast.7), calls=%async_computation.2 | async-start | bytes 65536 | tf_op jit(solution)/shard_map/all_to_all | solution.py:615
  47.1 0.3 collective-permute-start.8
  47.5 4.6 %collective-permute-start.9 = (f32[16,512]{1,0:T(8,128)S(1)}, f32[16,512]{1,0:T(8,128)S(1)}, u32[]{:S(2)}, u32[]{:S(2)}) collective-permute-start(f32[16,512]{1,0:T(8,128)S(1)} %get-tuple-element.67), channel_id=1, source_target_pairs={{4,8},{12,16},{20,24},{8,4},{16,12},{24,20},{5,9},{13,17},{21,25},... | collective-permute-start | bytes 98312 | tf_op jit(solution)/shard_map/ppermute | solution.py:609
  52.1 1.6 %collective-permute-start.11 = (f32[8,128]{1,0:T(8,128)S(1)}, f32[8,128]{1,0:T(8,128)S(1)}, u32[]{:S(2)}, u32[]{:S(2)}) collective-permute-start(f32[8,128]{1,0:T(8,128)S(1)} %get-tuple-element.69), channel_id=1, source_target_pairs={{1,2},{3,0},{2,1},{0,3},{5,6},{7,4},{6,5},{4,7},{9,10},{11,8},{10,... | collective-permute-start | bytes 12296 | tf_op jit(solution)/shard_map/ppermute | solution.py:609
  53.7 1.5 %collective-permute-done.11.refs_9_ = f32[8,128]{1,0:T(8,128)S(1)} collective-permute-done((f32[8,128]{1,0:T(8,128)S(1)}, f32[8,128]{1,0:T(8,128)S(1)}, u32[]{:S(2)}, u32[]{:S(2)}) %collective-permute-start.11) | collective-permute-done | bytes 4128 | tf_op jit(solution)/shard_map/ppermute | solution.py:609
  55.2 5.0 %shard_map.114 = (f32[8,72,640]{2,1,0:T(8,128)}, f32[5,64,512]{2,1,0:T(8,128)}, f32[5,64,512]{2,1,0:T(8,128)}, f32[8,128]{1,0:T(8,128)S(1)}, f32[8,128]{1,0:T(8,...) custom-call(f32[8,72,640]{2,1,0:T(8,128)} %get-tuple-element.62.refs_0_, f32[5,64,512]{2,1,0:T(8,128)} %get-tuple-element.63.refs_1_, ...), custom_call_target="tpu_custom_call" | custom-call | tf_op jit(solution)/shard_map/pallas_call | solution.py:590
  60.3 4.8 %collective-permute-start.13 = (f32[8,512]{1,0:T(8,128)S(1)}, f32[8,512]{1,0:T(8,128)S(1)}, u32[]{:S(2)}, u32[]{:S(2)}) collective-permute-start(f32[8,512]{1,0:T(8,128)S(1)} %get-tuple-element.75), channel_id=1, source_target_pairs={{4,8},{12,16},{20,24},{8,4},{16,12},{24,20},{5,9},{13,17},{21,25},... | collective-permute-start | bytes 49160 | tf_op jit(solution)/shard_map/ppermute | solution.py:609
  65.2 1.6 %collective-permute-start.15 = (f32[8,128]{1,0:T(8,128)S(1)}, f32[8,128]{1,0:T(8,128)S(1)}, u32[]{:S(2)}, u32[]{:S(2)}) collective-permute-start(f32[8,128]{1,0:T(8,128)S(1)} %get-tuple-element.77), channel_id=1, source_target_pairs={{1,2},{3,0},{2,1},{0,3},{5,6},{7,4},{6,5},{4,7},{9,10},{11,8},{10,... | collective-permute-start | bytes 12296 | tf_op jit(solution)/shard_map/ppermute | solution.py:609
  66.9 1.4 %collective-permute-done.15.girth_second = f32[8,128]{1,0:T(8,128)S(1)} collective-permute-done((f32[8,128]{1,0:T(8,128)S(1)}, f32[8,128]{1,0:T(8,128)S(1)}, u32[]{:S(2)}, u32[]{:S(2)}) %collective-permute-start.15) | collective-permute-done | bytes 4128 | tf_op jit(solution)/shard_map/ppermute | solution.py:609
  68.4 3.4 %shard_map.115 = (f32[8,64,512]{2,1,0:T(8,128)}, f32[8,64]{1,0:T(8,128)S(1)}) custom-call(f32[8,72,640]{2,1,0:T(8,128)} %get-tuple-element.73.stress_in, f32[5,64,512]{2,1,0:T(8,128)} %get-tuple-element.39.velocity_in, f32[8,512]{1,0:T(8,128)S(1)} %collective-permute-done.12.sec_first, f32[8,512]{1,0:T(8,128)S(1)} %collective-permute-done.13.sec_second, ...), custom_call_target="tpu_custom_call" | custom-call | tf_op jit(solution)/shard_map/pallas_call | solution.py:590
  71.8 7.7 %psum.7 = f32[64]{0:T(128)} all-reduce(f32[64]{0:T(128)S(1)} %slice_bitcast_fusion), channel_id=1, replica_groups=mesh['sec'=8,'girth'=4] {'girth'}, use_global_device_ids=true, to_apply=%region_0.0 | all-reduce | flops 64 | bytes 512 | tf_op jit(solution)/shard_map/psum | solution.py:713
  (23 shorter events, 0.4 us)
Async XLA Ops:
  3.7 14.2 %all-to-all-start = ((f32[32,2,128]{2,1,0:T(2,128)}), f32[32,2,128]{2,1,0:T(2,128)S(1)}, u32[]{:S(2)}, u32[]{:S(2)}) async-start(f32[32,2,128]{2,1,0:T(2,128)} %bitcast.3), calls=%async_computation | async-start | bytes 65536 | tf_op jit(solution)/shard_map/all_to_all | solution.py:615
  9.8 8.1 %collective-permute-start = (f32[16,512]{1,0:T(8,128)S(1)}, f32[16,512]{1,0:T(8,128)S(1)}, u32[]{:S(2)}, u32[]{:S(2)}) collective-permute-start(f32[16,512]{1,0:T(8,128)S(1)} %get-tuple-element.43), channel_id=1, source_target_pairs={{0,4},{8,12},{16,20},{24,28},{4,0},{12,8},{20,16},{28,24},{1,5},{9... | collective-permute-start | bytes 98312 | tf_op jit(solution)/shard_map/ppermute | solution.py:609
  10.1 7.8 %collective-permute-start.1 = (f32[16,512]{1,0:T(8,128)S(1)}, f32[16,512]{1,0:T(8,128)S(1)}, u32[]{:S(2)}, u32[]{:S(2)}) collective-permute-start(f32[16,512]{1,0:T(8,128)S(1)} %get-tuple-element.44), channel_id=1, source_target_pairs={{4,8},{12,16},{20,24},{8,4},{16,12},{24,20},{5,9},{13,17},{21,25},... | collective-permute-start | bytes 98312 | tf_op jit(solution)/shard_map/ppermute | solution.py:609
  14.7 1.7 %collective-permute-start.2 = (f32[8,128]{1,0:T(8,128)S(1)}, f32[8,128]{1,0:T(8,128)S(1)}, u32[]{:S(2)}, u32[]{:S(2)}) collective-permute-start(f32[8,128]{1,0:T(8,128)S(1)} %get-tuple-element.45), channel_id=1, source_target_pairs={{0,1},{2,3},{1,0},{3,2},{4,5},{6,7},{5,4},{7,6},{8,9},{10,11},{9,8... | collective-permute-start | bytes 12296 | tf_op jit(solution)/shard_map/ppermute | solution.py:609
  14.8 3.1 %collective-permute-start.3 = (f32[8,128]{1,0:T(8,128)S(1)}, f32[8,128]{1,0:T(8,128)S(1)}, u32[]{:S(2)}, u32[]{:S(2)}) collective-permute-start(f32[8,128]{1,0:T(8,128)S(1)} %get-tuple-element.46), channel_id=1, source_target_pairs={{1,2},{3,0},{2,1},{0,3},{5,6},{7,4},{6,5},{4,7},{9,10},{11,8},{10,... | collective-permute-start | bytes 12296 | tf_op jit(solution)/shard_map/ppermute | solution.py:609
  22.9 13.2 %all-to-all-start.1 = ((f32[32,2,128]{2,1,0:T(2,128)}), f32[32,2,128]{2,1,0:T(2,128)S(1)}, u32[]{:S(2)}, u32[]{:S(2)}) async-start(f32[32,2,128]{2,1,0:T(2,128)} %bitcast.5), calls=%async_computation.1 | async-start | bytes 65536 | tf_op jit(solution)/shard_map/all_to_all | solution.py:615
  28.0 8.1 %collective-permute-start.4 = (f32[16,512]{1,0:T(8,128)S(1)}, f32[16,512]{1,0:T(8,128)S(1)}, u32[]{:S(2)}, u32[]{:S(2)}) collective-permute-start(f32[16,512]{1,0:T(8,128)S(1)} %get-tuple-element.55), channel_id=1, source_target_pairs={{0,4},{8,12},{16,20},{24,28},{4,0},{12,8},{20,16},{28,24},{1,5},{9... | collective-permute-start | bytes 98312 | tf_op jit(solution)/shard_map/ppermute | solution.py:609
  28.3 7.8 %collective-permute-start.5 = (f32[16,512]{1,0:T(8,128)S(1)}, f32[16,512]{1,0:T(8,128)S(1)}, u32[]{:S(2)}, u32[]{:S(2)}) collective-permute-start(f32[16,512]{1,0:T(8,128)S(1)} %get-tuple-element.56), channel_id=1, source_target_pairs={{4,8},{12,16},{20,24},{8,4},{16,12},{24,20},{5,9},{13,17},{21,25},... | collective-permute-start | bytes 98312 | tf_op jit(solution)/shard_map/ppermute | solution.py:609
  32.9 1.7 %collective-permute-start.6 = (f32[8,128]{1,0:T(8,128)S(1)}, f32[8,128]{1,0:T(8,128)S(1)}, u32[]{:S(2)}, u32[]{:S(2)}) collective-permute-start(f32[8,128]{1,0:T(8,128)S(1)} %get-tuple-element.57), channel_id=1, source_target_pairs={{0,1},{2,3},{1,0},{3,2},{4,5},{6,7},{5,4},{7,6},{8,9},{10,11},{9,8... | collective-permute-start | bytes 12296 | tf_op jit(solution)/shard_map/ppermute | solution.py:609
  33.0 3.1 %collective-permute-start.7 = (f32[8,128]{1,0:T(8,128)S(1)}, f32[8,128]{1,0:T(8,128)S(1)}, u32[]{:S(2)}, u32[]{:S(2)}) collective-permute-start(f32[8,128]{1,0:T(8,128)S(1)} %get-tuple-element.58), channel_id=1, source_target_pairs={{1,2},{3,0},{2,1},{0,3},{5,6},{7,4},{6,5},{4,7},{9,10},{11,8},{10,... | collective-permute-start | bytes 12296 | tf_op jit(solution)/shard_map/ppermute | solution.py:609
  42.1 13.1 %all-to-all-start.2 = ((f32[32,2,128]{2,1,0:T(2,128)}), f32[32,2,128]{2,1,0:T(2,128)S(1)}, u32[]{:S(2)}, u32[]{:S(2)}) async-start(f32[32,2,128]{2,1,0:T(2,128)} %bitcast.7), calls=%async_computation.2 | async-start | bytes 65536 | tf_op jit(solution)/shard_map/all_to_all | solution.py:615
  47.1 8.1 %collective-permute-start.8 = (f32[16,512]{1,0:T(8,128)S(1)}, f32[16,512]{1,0:T(8,128)S(1)}, u32[]{:S(2)}, u32[]{:S(2)}) collective-permute-start(f32[16,512]{1,0:T(8,128)S(1)} %get-tuple-element.66), channel_id=1, source_target_pairs={{0,4},{8,12},{16,20},{24,28},{4,0},{12,8},{20,16},{28,24},{1,5},{9... | collective-permute-start | bytes 98312 | tf_op jit(solution)/shard_map/ppermute | solution.py:609
  47.5 7.8 %collective-permute-start.9 = (f32[16,512]{1,0:T(8,128)S(1)}, f32[16,512]{1,0:T(8,128)S(1)}, u32[]{:S(2)}, u32[]{:S(2)}) collective-permute-start(f32[16,512]{1,0:T(8,128)S(1)} %get-tuple-element.67), channel_id=1, source_target_pairs={{4,8},{12,16},{20,24},{8,4},{16,12},{24,20},{5,9},{13,17},{21,25},... | collective-permute-start | bytes 98312 | tf_op jit(solution)/shard_map/ppermute | solution.py:609
  52.0 1.7 %collective-permute-start.10 = (f32[8,128]{1,0:T(8,128)S(1)}, f32[8,128]{1,0:T(8,128)S(1)}, u32[]{:S(2)}, u32[]{:S(2)}) collective-permute-start(f32[8,128]{1,0:T(8,128)S(1)} %get-tuple-element.68), channel_id=1, source_target_pairs={{0,1},{2,3},{1,0},{3,2},{4,5},{6,7},{5,4},{7,6},{8,9},{10,11},{9,8... | collective-permute-start | bytes 12296 | tf_op jit(solution)/shard_map/ppermute | solution.py:609
  52.1 3.1 %collective-permute-start.11 = (f32[8,128]{1,0:T(8,128)S(1)}, f32[8,128]{1,0:T(8,128)S(1)}, u32[]{:S(2)}, u32[]{:S(2)}) collective-permute-start(f32[8,128]{1,0:T(8,128)S(1)} %get-tuple-element.69), channel_id=1, source_target_pairs={{1,2},{3,0},{2,1},{0,3},{5,6},{7,4},{6,5},{4,7},{9,10},{11,8},{10,... | collective-permute-start | bytes 12296 | tf_op jit(solution)/shard_map/ppermute | solution.py:609
  60.3 8.1 %collective-permute-start.12 = (f32[8,512]{1,0:T(8,128)S(1)}, f32[8,512]{1,0:T(8,128)S(1)}, u32[]{:S(2)}, u32[]{:S(2)}) collective-permute-start(f32[8,512]{1,0:T(8,128)S(1)} %get-tuple-element.74), channel_id=1, source_target_pairs={{0,4},{8,12},{16,20},{24,28},{4,0},{12,8},{20,16},{28,24},{1,5},{9... | collective-permute-start | bytes 49160 | tf_op jit(solution)/shard_map/ppermute | solution.py:609
  60.3 8.0 %collective-permute-start.13 = (f32[8,512]{1,0:T(8,128)S(1)}, f32[8,512]{1,0:T(8,128)S(1)}, u32[]{:S(2)}, u32[]{:S(2)}) collective-permute-start(f32[8,512]{1,0:T(8,128)S(1)} %get-tuple-element.75), channel_id=1, source_target_pairs={{4,8},{12,16},{20,24},{8,4},{16,12},{24,20},{5,9},{13,17},{21,25},... | collective-permute-start | bytes 49160 | tf_op jit(solution)/shard_map/ppermute | solution.py:609
  65.2 1.7 %collective-permute-start.14 = (f32[8,128]{1,0:T(8,128)S(1)}, f32[8,128]{1,0:T(8,128)S(1)}, u32[]{:S(2)}, u32[]{:S(2)}) collective-permute-start(f32[8,128]{1,0:T(8,128)S(1)} %get-tuple-element.76), channel_id=1, source_target_pairs={{0,1},{2,3},{1,0},{3,2},{4,5},{6,7},{5,4},{7,6},{8,9},{10,11},{9,8... | collective-permute-start | bytes 12296 | tf_op jit(solution)/shard_map/ppermute | solution.py:609
  65.2 3.1 %collective-permute-start.15 = (f32[8,128]{1,0:T(8,128)S(1)}, f32[8,128]{1,0:T(8,128)S(1)}, u32[]{:S(2)}, u32[]{:S(2)}) collective-permute-start(f32[8,128]{1,0:T(8,128)S(1)} %get-tuple-element.77), channel_id=1, source_target_pairs={{1,2},{3,0},{2,1},{0,3},{5,6},{7,4},{6,5},{4,7},{9,10},{11,8},{10,... | collective-permute-start | bytes 12296 | tf_op jit(solution)/shard_map/ppermute | solution.py:609

commit v7 on v6

--- a/solution.py
+++ b/solution.py
@@ -353,7 +353,7 @@
     ref[f, rows:, cols:] = corner
 
 
-def load_velocity(vel_ext, incoming, above, below, left, right):
+def load_velocity(vel_ext, velocity, incoming, above, below, left, right):
     first, second = edge_columns(left, right)
     row = lax.broadcasted_iota(jnp.int32, (8, LANES), 0)
     corner_tiles = [
@@ -361,6 +361,7 @@
         for device, inside in corner_neighbours()
     ]
     for f in range(FIELDS):
+        vel_ext[f, : velocity.shape[1], : velocity.shape[2]] = velocity[f]
         sides = edge_block(
             [
                 (first, 2 + f, LANES - 2),
@@ -391,26 +392,39 @@
 
 
 def step_kernel(first, last, *refs):
-    (stress_in, velocity_in, disp_in, thickness_in, pressure_in) = refs[:5]
     if first:
-        out = refs[14:]
+        stress_in, velocity_in, disp_in, thickness_in, pressure_in = refs[:5]
+        refs = refs[5:]
     else:
-        plate_ext = refs[14]
-        out = refs[15:]
+        pressure_in, stress_in, velocity_in, disp_in = refs[:4]
+        refs = refs[4:]
     (incoming, sec_first, sec_second, girth_first, girth_second,
-     column_marks, row_marks, picked, spring) = refs[5:14]
-    stress_out, velocity_out, disp_out = out[:3]
-    out = out[3:]
+     column_marks, row_marks, picked, spring) = refs[:9]
+    refs = refs[9:]
+    if not first:
+        plate_ext, refs = refs[0], refs[1:]
+    if last:
+        velocity_out, disp_out, stress_ext, velocity = refs[:4]
+        refs = refs[4:]
+    else:
+        stress_ext, velocity, disp = refs[:3]
+        refs = refs[3:]
     if first:
-        plate_ext, spring_out = out[:2]
-        out = out[2:]
-    girth_pair, sec_pair = out[0:2], out[2:4]
-    out = out[4:]
+        plate_ext, spring_out = refs[:2]
+        refs = refs[2:]
+    girth_pair, sec_pair = refs[0:2], refs[2:4]
+    refs = refs[4:]
     if not last:
-        picked_out, payload = out[:2]
-        out = out[2:]
-    (stress_ext, res_ext, vel_ext, weld, velocity, disp, thickness, pressure,
-     got, sent) = out
+        picked_out, payload = refs[:2]
+        refs = refs[2:]
+    res_ext, vel_ext, weld, pressure = refs[:4]
+    refs = refs[4:]
+    if first:
+        thickness, got = refs
+    elif last:
+        disp, got, sent = refs
+    else:
+        (got,) = refs
 
     _, rows, cols = velocity.shape
     devices = incoming.shape[0] // 2
@@ -418,22 +432,16 @@
     half = total // 2
     by_device, by_place = slot_marks(devices, half // devices)
     inner = (slice(None), slice(0, rows), slice(0, cols))
-    copies = fetch(
-        got,
-        [
-            (velocity_in, vel_ext.at[inner] if not first else velocity),
-            (stress_in, stress_ext.at[inner] if first else stress_ext),
+    pairs = [(pressure_in, pressure)]
+    if first:
+        pairs += [
+            (stress_in, stress_ext.at[inner]),
+            (velocity_in, velocity),
             (disp_in, disp),
-            (pressure_in, pressure),
+            (thickness_in, thickness),
         ]
-        + ([(thickness_in, thickness)] if first else []),
-    )
+    copies = fetch(got, pairs)
     sends = []
-
-    def send(source, target):
-        copy = pltpu.make_async_copy(source, target, sent.at[len(sends)])
-        copy.start()
-        sends.append(copy)
 
     other = []
     for row in (1, 0):
@@ -456,17 +464,17 @@
     if first:
         load_stress(stress_ext, plate_ext, thickness, above, below, left, right)
     else:
-        load_velocity(vel_ext, incoming, above, below, left, right)
+        load_velocity(vel_ext, velocity_in, incoming, above, below, left, right)
     for start in range(0, rows + PAD_ROWS, 8):
         plate = plate_ext[0, start : start + 8, :]
-        chunk = [stress_ext[k, start : start + 8, :] for k in range(RESULTS)]
+        source = stress_ext if first else stress_in
+        chunk = [source[k, start : start + 8, :] for k in range(RESULTS)]
         if not first:
             chunk = stress_chunk(vel_ext, chunk, plate, start)
             for k, value in enumerate(chunk):
                 stress_ext[k, start : start + 8, :] = value
         for k, value in enumerate(resultants(chunk, plate)):
             res_ext[k, start : start + 8, :] = value
-    send(stress_ext, stress_out)
 
     for start in range(0, rows, 8):
         part = slice(start, start + 8)
@@ -477,14 +485,19 @@
         force[2] = force[2] + pressure[part, :]
         for f in range(FIELDS):
             joined = force[f] + weld[f * rows + start : f * rows + start + 8, :]
-            before = velocity[f, part, :] if first else vel_ext[f, part, :cols]
-            speed = before + (linear if f < 3 else angular) * joined
+            speed = (velocity if first else velocity_in)[f, part, :]
+            speed = speed + (linear if f < 3 else angular) * joined
             velocity[f, part, :] = speed
-            disp[f, part, :] = disp[f, part, :] + time_step * speed
-        if start % 32 == 24:
+            moved = (disp if first else disp_in)[f, part, :]
+            disp[f, part, :] = moved + time_step * speed
+        if last and start % 32 == 24:
             done = slice(start - 24, start + 8)
             for source, target in ((velocity, velocity_out), (disp, disp_out)):
-                send(source.at[:, done, :], target.at[:, done, :])
+                copy = pltpu.make_async_copy(
+                    source.at[:, done, :], target.at[:, done, :], sent.at[len(sends)]
+                )
+                copy.start()
+                sends.append(copy)
 
     ends = (cols - LANES, cols)
     if last:
@@ -531,26 +544,21 @@
         [velocity[f, 0:2, :] for f in range(FIELDS)],
         [velocity[f, rows - 2 : rows, :] for f in range(FIELDS)],
     )
-    for copy in sends:
-        copy.wait()
 
 
 def final_kernel(
-    stress_in, velocity_in, sec_first, sec_second, girth_first, girth_second, plate_ext, height,
-    stress_out, moment, stress, vel_ext, got, sent,
+    stress, velocity, sec_first, sec_second, girth_first, girth_second, plate_ext, height,
+    stress_out, moment, made, vel_ext, sent,
 ):
     rows, cols = vel_ext.shape[1] - PAD_ROWS, vel_ext.shape[2] - LANES
-    inner = (slice(None), slice(0, rows), slice(0, cols))
-    copies = fetch(got, [(velocity_in, vel_ext.at[inner]), (stress_in, stress)])
     above, below = in_order("sec", sec_first[...], sec_second[...])
     left, right = in_order("girth", girth_first[...], girth_second[...])
     first, _ = edge_columns(left, right)
     empty = jnp.zeros((PAD_ROWS, LANES), F32)
     for f in range(FIELDS):
+        vel_ext[f, :rows, :cols] = velocity[f]
         sides = edge_block([(first, f, LANES - 1), (first, 8 + f, 0)])
         fill_halo(vel_ext, f, above[f : f + 1, :], below[f : f + 1, :], sides, empty)
-    for copy in copies:
-        copy.wait()
     weight = height[0:1, :]
     parts = []
     sends = []
@@ -560,11 +568,11 @@
         plate = plate_ext[0, part, :]
         chunk = stress_chunk(vel_ext, chunk, plate, start)
         for k, value in enumerate(chunk):
-            stress[k, part, :] = value
+            made[k, part, :] = value[:, :cols]
         if start % 16 == 8:
             done = slice(start - 8, start + 8)
             copy = pltpu.make_async_copy(
-                stress.at[:, done, :cols], stress_out.at[:, done, :], sent.at[len(sends)]
+                made.at[:, done, :], stress_out.at[:, done, :], sent.at[len(sends)]
             )
             copy.start()
             sends.append(copy)
@@ -578,10 +586,19 @@
         copy.wait()
 
 
-def call(kernel, vmem_bytes, outs, scratch, *operands, far=0, far_out=0, copies=(1,)):
+def call(kernel, vmem_bytes, outs, scratch, *operands, far=0, kept=0, far_out=0, kept_out=0, copies):
+    def placed(k, away, here):
+        return pltpu.HBM if k < away else pltpu.VMEM if k < away + here else None
+
     operands = [
-        pltpu.with_memory_space_constraint(value, pltpu.HBM) if k < far else value
+        pltpu.with_memory_space_constraint(value, placed(k, far, kept))
+        if placed(k, far, kept) is not None
+        else value
         for k, value in enumerate(operands)
+    ]
+    results = [
+        (placed(k, far_out, kept_out) or jax.ShapeDtypeStruct)(shape, dtype)
+        for k, (shape, dtype) in enumerate(outs)
     ]
     whole = pl.BlockSpec(memory_space=pltpu.VMEM)
     away = pl.BlockSpec(memory_space=pltpu.HBM)
@@ -589,10 +606,7 @@
     scratch += [pltpu.SemaphoreType.DMA((count,)) for count in copies]
     return pl.pallas_call(
         kernel,
-        out_shape=[
-            pltpu.HBM(shape, dtype) if k < far_out else jax.ShapeDtypeStruct(shape, dtype)
-            for k, (shape, dtype) in enumerate(outs)
-        ],
+        out_shape=results,
         in_specs=[away] * far + [whole] * (len(operands) - far),
         out_specs=[away] * far_out + [whole] * (len(outs) - far_out),
         scratch_shapes=scratch,
@@ -608,6 +622,18 @@
         couples = [(i, j) for i, j in couples if j > i or around]
         out.append(lax.ppermute(value, axis, couples + [(j, i) for i, j in couples]))
     return out
+
+
+def sum_over(value, axis):
+    count = lax.axis_size(axis)
+    if count & (count - 1):
+        return lax.psum(value, axis)
+    parts = [value] + [
+        lax.ppermute(value, axis, [(i, i ^ step) for i in range(count)]) for step in range(1, count)
+    ]
+    while len(parts) > 1:
+        parts = [a + b for a, b in zip(parts[0::2], parts[1::2])]
+    return parts[0]
 
 
 def exchange(joints):
@@ -635,12 +661,8 @@
     slot_rows = (8, total)
     scratch = [
         (stress_shape, F32),
-        (stress_shape, F32),
         ((FIELDS, rows + PAD_ROWS, cols + LANES), F32),
         ((FIELDS * rows, cols), F32),
-        (block, F32),
-        (block, F32),
-        ((rows, cols), jnp.int32),
         ((rows, cols), F32),
     ]
 
@@ -669,28 +691,38 @@
         incoming = exchange(payload)
         ends = swap((sec_first, sec_second), "sec", False)
         sides = swap((girth_first, girth_second), "girth", True)
-        outs = [(stress_shape, F32), (block, F32), (block, F32)]
+        outs = [(stress_shape, F32), (block, F32)] + [(block, F32)] * (not last)
         if first:
             outs += [(plate_shape, F32), (slot_rows, F32)]
+        if last:
+            outs = [(block, F32), (block, F32)] + outs
         halo = (8, cols) if last else strip
         outs += [(edge, F32), (edge, F32), (halo, F32), (halo, F32)]
         if not last:
             outs += [(slot_rows, F32), (message, F32)]
+        state = [stress, velocity, displacement]
+        own = [((rows, cols), jnp.int32)] if first else [(block, F32)] if last else []
         results = call(
             functools.partial(step_kernel, first, last),
             vmem_bytes,
             outs,
-            scratch,
-            stress, velocity, displacement, thickness, pressure,
+            scratch + own,
+            *(state + [thickness, pressure] if first else [pressure] + state),
             incoming, *ends, *sides,
             column_marks, row_marks, picked, spring,
             *([] if first else [plate]),
-            far=5,
-            far_out=3,
-            copies=(5, 1 + 2 * (rows // 32)),
+            far=5 if first else 1,
+            kept=0 if first else 3,
+            far_out=2 if last else 0,
+            kept_out=2 if last else 3,
+            copies=(5, 2 * (rows // 32)) if last else (5,),
         )
-        stress, velocity, displacement = results[:3]
-        results = results[3:]
+        if last:
+            velocity_out, displacement, stress, velocity = results[:4]
+            results = results[4:]
+        else:
+            stress, velocity, displacement = results[:3]
+            results = results[3:]
         if first:
             plate, spring = results[:2]
             results = results[2:]
@@ -704,14 +736,14 @@
         final_kernel,
         vmem_bytes,
         [((RESULTS, rows, cols), F32), ((8, rows), F32)],
-        [(stress_shape, F32), ((FIELDS, rows + PAD_ROWS, cols + LANES), F32)],
+        [((RESULTS, rows, cols), F32), ((FIELDS, rows + PAD_ROWS, cols + LANES), F32)],
         stress, velocity, *ends, *sides, plate, height,
-        far=2,
+        kept=2,
         far_out=1,
-        copies=(2, rows // 16),
-    )
-    moment = lax.psum(partial_moment[0], "girth")
-    return (displacement, velocity, stress, moment)
+        copies=(rows // 16,),
+    )
+    moment = sum_over(partial_moment, "girth")[0]
+    return (displacement, velocity_out, stress, moment)
 
 
 def solution(mesh):

time: 80 us -> 91.4 us (1.14)
  the two profiles are of different devices: /device:TPU:4 before, /device:TPU:5 now
where the time goes in v7:
time: 91.4 us; the launch traced here: 90.5 us
  starting transfers between devices  43.7 us (48%)
  Pallas kernels  18.4 us (20%)
  local copies, waits for them, and re-layouts  17.5 us (19%)
  waiting for transfers between devices  10 us (11%)
    ppermute x16, starting transfers between devices, swap(): lax.ppermute(value, axis, couples + [(j, i) for i, j in couples])  25.6 us
    pallas_call x5, Pallas kernels, call(): pl.pallas_call(kernel, out_shape=results, in_specs=[away] * far + [whole]...  18.4 us
    unnamed x42, local copies, waits for them, and re-layouts  16.9 us
    all_to_all x3, starting transfers between devices, exchange(): blocks = lax.all_to_all(blocks, ('sec', 'girth'), 0, 0, tiled=True)  15.9 us
    ppermute x16, waiting for transfers between devices, swap(): lax.ppermute(value, axis, couples + [(j, i) for i, j in couples])  7.54 us
    ppermute x3, waiting for transfers between devices, sum_over(): lax.ppermute(value, axis, [(i, i ^ step) for i in range(count)])  2.48 us
    ppermute x3, starting transfers between devices, sum_over(): lax.ppermute(value, axis, [(i, i ^ step) for i in range(count)])  2.21 us
  transfers between devices with their start and end apart: 22, of which 6 were waited for; matrix products, arithmetic and copies ran while one was open for 0% of the time, Pallas kernels for 0%

profile of v7, /device:TPU:5, one launch (start us, length us, event | category | flops | bytes accessed | tf_op | source)
XLA Modules:
  0.0 90.5 jit_solution(9320435995439409725)
XLA Ops:
  0.6 3.0 %shard_map.111 = (f32[64,128]{1,0:T(8,128)}, f32[16,512]{1,0:T(8,128)S(1)}, f32[16,512]{1,0:T(8,128)S(1)}, f32[8,128]{1,0:T(8,128)S(1)}, f32[8,128]{1,0:T(8,128)...) custom-call(f32[5,64,512]{2,1,0:T(8,128)} %refs_2_.1, ...), custom_call_target="tpu_custom_call" | custom-call | tf_op jit(solution)/shard_map/pallas_call | solution.py:607
  3.7 6.4 %all-to-all-start = ((f32[32,2,128]{2,1,0:T(2,128)}), f32[32,2,128]{2,1,0:T(2,128)S(1)}, u32[]{:S(2)}, u32[]{:S(2)}) async-start(f32[32,2,128]{2,1,0:T(2,128)} %bitcast.3), calls=%async_computation | async-start | bytes 65536 | tf_op jit(solution)/shard_map/all_to_all | solution.py:641
  10.3 4.2 %collective-permute-start.1 = (f32[16,512]{1,0:T(8,128)S(1)}, f32[16,512]{1,0:T(8,128)S(1)}, u32[]{:S(2)}, u32[]{:S(2)}) collective-permute-start(f32[16,512]{1,0:T(8,128)S(1)} %get-tuple-element.45), channel_id=1, source_target_pairs={{4,8},{12,16},{20,24},{8,4},{16,12},{24,20},{5,9},{13,17},{21,25},... | collective-permute-start | bytes 98312 | tf_op jit(solution)/shard_map/ppermute | solution.py:623
  15.4 1.1 %collective-permute-start.3 = (f32[8,128]{1,0:T(8,128)S(1)}, f32[8,128]{1,0:T(8,128)S(1)}, u32[]{:S(2)}, u32[]{:S(2)}) collective-permute-start(f32[8,128]{1,0:T(8,128)S(1)} %get-tuple-element.47), channel_id=1, source_target_pairs={{1,2},{3,0},{2,1},{0,3},{5,6},{7,4},{6,5},{4,7},{9,10},{11,8},{10,... | collective-permute-start | bytes 12296 | tf_op jit(solution)/shard_map/ppermute | solution.py:623
  16.6 1.9 %collective-permute-done.3.refs_9_ = f32[8,128]{1,0:T(8,128)S(1)} collective-permute-done((f32[8,128]{1,0:T(8,128)S(1)}, f32[8,128]{1,0:T(8,128)S(1)}, u32[]{:S(2)}, u32[]{:S(2)}) %collective-permute-start.3) | collective-permute-done | bytes 4128 | tf_op jit(solution)/shard_map/ppermute | solution.py:623
  18.5 4.5 %shard_map.112 = (f32[8,72,640]{2,1,0:T(8,128)S(1)}, f32[5,64,512]{2,1,0:T(8,128)S(1)}, f32[5,64,512]{2,1,0:T(8,128)S(1)}, f32[1,72,640]{2,1,0:T(8,128)S(1)}, f3...) custom-call(f32[8,64,512]{2,1,0:T(8,128)} %refs_0_.3, ...), custom_call_target="tpu_custom_call" | custom-call | tf_op jit(solution)/shard_map/pallas_call | solution.py:607
  23.0 1.1 %copy-done = f32[8,72,640]{2,1,0:T(8,128)} copy-done((f32[8,72,640]{2,1,0:T(8,128)}, f32[8,72,640]{2,1,0:T(8,128)S(1)}, u32[]{:S(2)}) %copy-start) | copy-done | bytes 1474584
  26.4 4.8 %all-to-all-start.1 = ((f32[32,2,128]{2,1,0:T(2,128)}), f32[32,2,128]{2,1,0:T(2,128)S(1)}, u32[]{:S(2)}, u32[]{:S(2)}) async-start(f32[32,2,128]{2,1,0:T(2,128)} %bitcast.5), calls=%async_computation.1 | async-start | bytes 65536 | tf_op jit(solution)/shard_map/all_to_all | solution.py:641
  31.3 4.2 %collective-permute-start.5 = (f32[16,512]{1,0:T(8,128)S(1)}, f32[16,512]{1,0:T(8,128)S(1)}, u32[]{:S(2)}, u32[]{:S(2)}) collective-permute-start(f32[16,512]{1,0:T(8,128)S(1)} %get-tuple-element.57), channel_id=1, source_target_pairs={{4,8},{12,16},{20,24},{8,4},{16,12},{24,20},{5,9},{13,17},{21,25},... | collective-permute-start | bytes 98312 | tf_op jit(solution)/shard_map/ppermute | solution.py:623
  36.5 1.1 %collective-permute-start.7 = (f32[8,128]{1,0:T(8,128)S(1)}, f32[8,128]{1,0:T(8,128)S(1)}, u32[]{:S(2)}, u32[]{:S(2)}) collective-permute-start(f32[8,128]{1,0:T(8,128)S(1)} %get-tuple-element.59), channel_id=1, source_target_pairs={{1,2},{3,0},{2,1},{0,3},{5,6},{7,4},{6,5},{4,7},{9,10},{11,8},{10,... | collective-permute-start | bytes 12296 | tf_op jit(solution)/shard_map/ppermute | solution.py:623
  37.6 1.9 %collective-permute-done.7.refs_8_ = f32[8,128]{1,0:T(8,128)S(1)} collective-permute-done((f32[8,128]{1,0:T(8,128)S(1)}, f32[8,128]{1,0:T(8,128)S(1)}, u32[]{:S(2)}, u32[]{:S(2)}) %collective-permute-start.7) | collective-permute-done | bytes 4128 | tf_op jit(solution)/shard_map/ppermute | solution.py:623
  41.4 1.4 %copy-done.1 = f32[8,72,640]{2,1,0:T(8,128)S(1)} copy-done((f32[8,72,640]{2,1,0:T(8,128)S(1)}, f32[8,72,640]{2,1,0:T(8,128)}, u32[]{:S(2)}) %copy-start.1) | copy-done | bytes 1474584
  48.0 4.0 %shard_map.113 = (f32[8,72,640]{2,1,0:T(8,128)S(1)}, f32[5,64,512]{2,1,0:T(8,128)S(1)}, f32[5,64,512]{2,1,0:T(8,128)S(1)}, f32[8,128]{1,0:T(8,128)S(1)}, f32[8,1...) custom-call(f32[64,512]{1,0:T(8,128)} %refs_0_.5, ...), custom_call_target="tpu_custom_call" | custom-call | tf_op jit(solution)/shard_map/pallas_call | solution.py:607
  55.3 4.7 %all-to-all-start.2 = ((f32[32,2,128]{2,1,0:T(2,128)}), f32[32,2,128]{2,1,0:T(2,128)}, u32[]{:S(2)}, u32[]{:S(2)}) async-start(f32[32,2,128]{2,1,0:T(2,128)} %bitcast.13), calls=%async_computation.2 | async-start | bytes 65536 | tf_op jit(solution)/shard_map/all_to_all | solution.py:641
  60.2 4.2 %collective-permute-start.9 = (f32[16,512]{1,0:T(8,128)}, f32[16,512]{1,0:T(8,128)}, u32[]{:S(2)}, u32[]{:S(2)}) collective-permute-start(f32[16,512]{1,0:T(8,128)} %copy-done.19), channel_id=1, source_target_pairs={{4,8},{12,16},{20,24},{8,4},{16,12},{24,20},{5,9},{13,17},{21,25},... | collective-permute-start | bytes 98312 | tf_op jit(solution)/shard_map/ppermute | solution.py:623
  65.4 1.1 %collective-permute-start.11 = (f32[8,128]{1,0:T(8,128)S(1)}, f32[8,128]{1,0:T(8,128)S(1)}, u32[]{:S(2)}, u32[]{:S(2)}) collective-permute-start(f32[8,128]{1,0:T(8,128)S(1)} %get-tuple-element.70), channel_id=1, source_target_pairs={{1,2},{3,0},{2,1},{0,3},{5,6},{7,4},{6,5},{4,7},{9,10},{11,8},{10,... | collective-permute-start | bytes 12296 | tf_op jit(solution)/shard_map/ppermute | solution.py:623
  66.5 1.9 %collective-permute-done.11.refs_8_ = f32[8,128]{1,0:T(8,128)S(1)} collective-permute-done((f32[8,128]{1,0:T(8,128)S(1)}, f32[8,128]{1,0:T(8,128)S(1)}, u32[]{:S(2)}, u32[]{:S(2)}) %collective-permute-start.11) | collective-permute-done | bytes 4128 | tf_op jit(solution)/shard_map/ppermute | solution.py:623
  70.3 5.1 %shard_map.114 = (f32[5,64,512]{2,1,0:T(8,128)}, f32[5,64,512]{2,1,0:T(8,128)}, f32[8,72,640]{2,1,0:T(8,128)S(1)}, f32[5,64,512]{2,1,0:T(8,128)S(1)}, f32[8,128]...) custom-call(f32[64,512]{1,0:T(8,128)} %refs_0_.5, ...), custom_call_target="tpu_custom_call" | custom-call | tf_op jit(solution)/shard_map/pallas_call | solution.py:607
  75.4 4.3 %collective-permute-start.13 = (f32[8,512]{1,0:T(8,128)S(1)}, f32[8,512]{1,0:T(8,128)S(1)}, u32[]{:S(2)}, u32[]{:S(2)}) collective-permute-start(f32[8,512]{1,0:T(8,128)S(1)} %get-tuple-element.77), channel_id=1, source_target_pairs={{4,8},{12,16},{20,24},{8,4},{16,12},{24,20},{5,9},{13,17},{21,25},... | collective-permute-start | bytes 49160 | tf_op jit(solution)/shard_map/ppermute | solution.py:623
  80.4 1.2 %collective-permute-start.15 = (f32[8,128]{1,0:T(8,128)S(1)}, f32[8,128]{1,0:T(8,128)S(1)}, u32[]{:S(2)}, u32[]{:S(2)}) collective-permute-start(f32[8,128]{1,0:T(8,128)S(1)} %get-tuple-element.79), channel_id=1, source_target_pairs={{1,2},{3,0},{2,1},{0,3},{5,6},{7,4},{6,5},{4,7},{9,10},{11,8},{10,... | collective-permute-start | bytes 12296 | tf_op jit(solution)/shard_map/ppermute | solution.py:623
  81.6 1.8 %collective-permute-done.15.girth_second = f32[8,128]{1,0:T(8,128)S(1)} collective-permute-done((f32[8,128]{1,0:T(8,128)S(1)}, f32[8,128]{1,0:T(8,128)S(1)}, u32[]{:S(2)}, u32[]{:S(2)}) %collective-permute-start.15) | collective-permute-done | bytes 4128 | tf_op jit(solution)/shard_map/ppermute | solution.py:623
  83.4 1.8 %shard_map.115 = (f32[8,64,512]{2,1,0:T(8,128)}, f32[8,64]{1,0:T(8,128)S(1)}) custom-call(f32[8,72,640]{2,1,0:T(8,128)S(1)} %get-tuple-element.74.stress, f32[5,64,512]{2,1,0:T(8,128)S(1)} %get-tuple-element.75.velocity, f32[8,512]{1,0:T(8,128)S(1)} %collective-permute-done.12.sec_first, f32[8,512]{1,0:T(8,128)S(1)} %collective-permute-done.13.sec_second, ...), custom_call_target="tpu_custom_call" | custom-call | tf_op jit(solution)/shard_map/pallas_call | solution.py:607
  85.4 1.2 %collective-permute-start.17 = (f32[8,64]{1,0:T(8,128)S(1)}, f32[8,64]{1,0:T(8,128)S(1)}, u32[]{:S(2)}, u32[]{:S(2)}) collective-permute-start(f32[8,64]{1,0:T(8,128)S(1)} %get-tuple-element.81), channel_id=1, source_target_pairs={{0,2},{1,3},{2,0},{3,1},{4,6},{5,7},{6,4},{7,5},{8,10},{9,11},{10,... | collective-permute-start | bytes 6152 | tf_op jit(solution)/shard_map/ppermute | solution.py:632
  87.9 2.1 %collective-permute-done.18 = f32[8,64]{1,0:T(8,128)S(1)} collective-permute-done((f32[8,64]{1,0:T(8,128)S(1)}, f32[8,64]{1,0:T(8,128)S(1)}, u32[]{:S(2)}, u32[]{:S(2)}) %collective-permute-start.18) | collective-permute-done | bytes 2080 | tf_op jit(solution)/shard_map/ppermute | solution.py:632
  (71 shorter events, 20.6 us)
Async XLA Ops:
  3.7 14.8 %all-to-all-start = ((f32[32,2,128]{2,1,0:T(2,128)}), f32[32,2,128]{2,1,0:T(2,128)S(1)}, u32[]{:S(2)}, u32[]{:S(2)}) async-start(f32[32,2,128]{2,1,0:T(2,128)} %bitcast.3), calls=%async_computation | async-start | bytes 65536 | tf_op jit(solution)/shard_map/all_to_all | solution.py:641
  10.1 8.4 %collective-permute-start = (f32[16,512]{1,0:T(8,128)S(1)}, f32[16,512]{1,0:T(8,128)S(1)}, u32[]{:S(2)}, u32[]{:S(2)}) collective-permute-start(f32[16,512]{1,0:T(8,128)S(1)} %get-tuple-element.44), channel_id=1, source_target_pairs={{0,4},{8,12},{16,20},{24,28},{4,0},{12,8},{20,16},{28,24},{1,5},{9... | collective-permute-start | bytes 98312 | tf_op jit(solution)/shard_map/ppermute | solution.py:623
  10.3 8.2 %collective-permute-start.1 = (f32[16,512]{1,0:T(8,128)S(1)}, f32[16,512]{1,0:T(8,128)S(1)}, u32[]{:S(2)}, u32[]{:S(2)}) collective-permute-start(f32[16,512]{1,0:T(8,128)S(1)} %get-tuple-element.45), channel_id=1, source_target_pairs={{4,8},{12,16},{20,24},{8,4},{16,12},{24,20},{5,9},{13,17},{21,25},... | collective-permute-start | bytes 98312 | tf_op jit(solution)/shard_map/ppermute | solution.py:623
  14.4 2.1 %collective-permute-start.2 = (f32[8,128]{1,0:T(8,128)S(1)}, f32[8,128]{1,0:T(8,128)S(1)}, u32[]{:S(2)}, u32[]{:S(2)}) collective-permute-start(f32[8,128]{1,0:T(8,128)S(1)} %get-tuple-element.46), channel_id=1, source_target_pairs={{0,1},{2,3},{1,0},{3,2},{4,5},{6,7},{5,4},{7,6},{8,9},{10,11},{9,8... | collective-permute-start | bytes 12296 | tf_op jit(solution)/shard_map/ppermute | solution.py:623
  15.4 3.0 %collective-permute-start.3 = (f32[8,128]{1,0:T(8,128)S(1)}, f32[8,128]{1,0:T(8,128)S(1)}, u32[]{:S(2)}, u32[]{:S(2)}) collective-permute-start(f32[8,128]{1,0:T(8,128)S(1)} %get-tuple-element.47), channel_id=1, source_target_pairs={{1,2},{3,0},{2,1},{0,3},{5,6},{7,4},{6,5},{4,7},{9,10},{11,8},{10,... | collective-permute-start | bytes 12296 | tf_op jit(solution)/shard_map/ppermute | solution.py:623
  23.0 1.1 %copy-start = (f32[8,72,640]{2,1,0:T(8,128)}, f32[8,72,640]{2,1,0:T(8,128)S(1)}, u32[]{:S(2)}) copy-start(f32[8,72,640]{2,1,0:T(8,128)S(1)} %get-tuple-element.52.refs_1_) | copy-start | bytes 4423684
  26.4 14.4 %all-to-all-start.1 = ((f32[32,2,128]{2,1,0:T(2,128)}), f32[32,2,128]{2,1,0:T(2,128)S(1)}, u32[]{:S(2)}, u32[]{:S(2)}) async-start(f32[32,2,128]{2,1,0:T(2,128)} %bitcast.5), calls=%async_computation.1 | async-start | bytes 65536 | tf_op jit(solution)/shard_map/all_to_all | solution.py:641
  31.2 8.4 %collective-permute-start.4 = (f32[16,512]{1,0:T(8,128)S(1)}, f32[16,512]{1,0:T(8,128)S(1)}, u32[]{:S(2)}, u32[]{:S(2)}) collective-permute-start(f32[16,512]{1,0:T(8,128)S(1)} %get-tuple-element.56), channel_id=1, source_target_pairs={{0,4},{8,12},{16,20},{24,28},{4,0},{12,8},{20,16},{28,24},{1,5},{9... | collective-permute-start | bytes 98312 | tf_op jit(solution)/shard_map/ppermute | solution.py:623
  31.3 8.8 %collective-permute-start.5 = (f32[16,512]{1,0:T(8,128)S(1)}, f32[16,512]{1,0:T(8,128)S(1)}, u32[]{:S(2)}, u32[]{:S(2)}) collective-permute-start(f32[16,512]{1,0:T(8,128)S(1)} %get-tuple-element.57), channel_id=1, source_target_pairs={{4,8},{12,16},{20,24},{8,4},{16,12},{24,20},{5,9},{13,17},{21,25},... | collective-permute-start | bytes 98312 | tf_op jit(solution)/shard_map/ppermute | solution.py:623
  35.5 2.1 %collective-permute-start.6 = (f32[8,128]{1,0:T(8,128)S(1)}, f32[8,128]{1,0:T(8,128)S(1)}, u32[]{:S(2)}, u32[]{:S(2)}) collective-permute-start(f32[8,128]{1,0:T(8,128)S(1)} %get-tuple-element.58), channel_id=1, source_target_pairs={{0,1},{2,3},{1,0},{3,2},{4,5},{6,7},{5,4},{7,6},{8,9},{10,11},{9,8... | collective-permute-start | bytes 12296 | tf_op jit(solution)/shard_map/ppermute | solution.py:623
  36.5 3.0 %collective-permute-start.7 = (f32[8,128]{1,0:T(8,128)S(1)}, f32[8,128]{1,0:T(8,128)S(1)}, u32[]{:S(2)}, u32[]{:S(2)}) collective-permute-start(f32[8,128]{1,0:T(8,128)S(1)} %get-tuple-element.59), channel_id=1, source_target_pairs={{1,2},{3,0},{2,1},{0,3},{5,6},{7,4},{6,5},{4,7},{9,10},{11,8},{10,... | collective-permute-start | bytes 12296 | tf_op jit(solution)/shard_map/ppermute | solution.py:623
  41.4 1.4 %copy-start.1 = (f32[8,72,640]{2,1,0:T(8,128)S(1)}, f32[8,72,640]{2,1,0:T(8,128)}, u32[]{:S(2)}) copy-start(f32[8,72,640]{2,1,0:T(8,128)} %copy-done) | copy-start | bytes 4423684
  55.3 13.1 %all-to-all-start.2 = ((f32[32,2,128]{2,1,0:T(2,128)}), f32[32,2,128]{2,1,0:T(2,128)}, u32[]{:S(2)}, u32[]{:S(2)}) async-start(f32[32,2,128]{2,1,0:T(2,128)} %bitcast.13), calls=%async_computation.2 | async-start | bytes 65536 | tf_op jit(solution)/shard_map/all_to_all | solution.py:641
  60.0 8.4 %collective-permute-start.8 = (f32[16,512]{1,0:T(8,128)}, f32[16,512]{1,0:T(8,128)}, u32[]{:S(2)}, u32[]{:S(2)}) collective-permute-start(f32[16,512]{1,0:T(8,128)} %copy-done.20), channel_id=1, source_target_pairs={{0,4},{8,12},{16,20},{24,28},{4,0},{12,8},{20,16},{28,24},{1,5},{9... | collective-permute-start | bytes 98312 | tf_op jit(solution)/shard_map/ppermute | solution.py:623
  60.2 8.2 %collective-permute-start.9 = (f32[16,512]{1,0:T(8,128)}, f32[16,512]{1,0:T(8,128)}, u32[]{:S(2)}, u32[]{:S(2)}) collective-permute-start(f32[16,512]{1,0:T(8,128)} %copy-done.19), channel_id=1, source_target_pairs={{4,8},{12,16},{20,24},{8,4},{16,12},{24,20},{5,9},{13,17},{21,25},... | collective-permute-start | bytes 98312 | tf_op jit(solution)/shard_map/ppermute | solution.py:623
  64.4 2.1 %collective-permute-start.10 = (f32[8,128]{1,0:T(8,128)S(1)}, f32[8,128]{1,0:T(8,128)S(1)}, u32[]{:S(2)}, u32[]{:S(2)}) collective-permute-start(f32[8,128]{1,0:T(8,128)S(1)} %get-tuple-element.69), channel_id=1, source_target_pairs={{0,1},{2,3},{1,0},{3,2},{4,5},{6,7},{5,4},{7,6},{8,9},{10,11},{9,8... | collective-permute-start | bytes 12296 | tf_op jit(solution)/shard_map/ppermute | solution.py:623
  65.4 3.0 %collective-permute-start.11 = (f32[8,128]{1,0:T(8,128)S(1)}, f32[8,128]{1,0:T(8,128)S(1)}, u32[]{:S(2)}, u32[]{:S(2)}) collective-permute-start(f32[8,128]{1,0:T(8,128)S(1)} %get-tuple-element.70), channel_id=1, source_target_pairs={{1,2},{3,0},{2,1},{0,3},{5,6},{7,4},{6,5},{4,7},{9,10},{11,8},{10,... | collective-permute-start | bytes 12296 | tf_op jit(solution)/shard_map/ppermute | solution.py:623
  75.3 8.1 %collective-permute-start.12 = (f32[8,512]{1,0:T(8,128)S(1)}, f32[8,512]{1,0:T(8,128)S(1)}, u32[]{:S(2)}, u32[]{:S(2)}) collective-permute-start(f32[8,512]{1,0:T(8,128)S(1)} %get-tuple-element.76), channel_id=1, source_target_pairs={{0,4},{8,12},{16,20},{24,28},{4,0},{12,8},{20,16},{28,24},{1,5},{9... | collective-permute-start | bytes 49160 | tf_op jit(solution)/shard_map/ppermute | solution.py:623
  75.4 8.0 %collective-permute-start.13 = (f32[8,512]{1,0:T(8,128)S(1)}, f32[8,512]{1,0:T(8,128)S(1)}, u32[]{:S(2)}, u32[]{:S(2)}) collective-permute-start(f32[8,512]{1,0:T(8,128)S(1)} %get-tuple-element.77), channel_id=1, source_target_pairs={{4,8},{12,16},{20,24},{8,4},{16,12},{24,20},{5,9},{13,17},{21,25},... | collective-permute-start | bytes 49160 | tf_op jit(solution)/shard_map/ppermute | solution.py:623
  79.7 1.9 %collective-permute-start.14 = (f32[8,128]{1,0:T(8,128)S(1)}, f32[8,128]{1,0:T(8,128)S(1)}, u32[]{:S(2)}, u32[]{:S(2)}) collective-permute-start(f32[8,128]{1,0:T(8,128)S(1)} %get-tuple-element.78), channel_id=1, source_target_pairs={{0,1},{2,3},{1,0},{3,2},{4,5},{6,7},{5,4},{7,6},{8,9},{10,11},{9,8... | collective-permute-start | bytes 12296 | tf_op jit(solution)/shard_map/ppermute | solution.py:623
  80.4 3.0 %collective-permute-start.15 = (f32[8,128]{1,0:T(8,128)S(1)}, f32[8,128]{1,0:T(8,128)S(1)}, u32[]{:S(2)}, u32[]{:S(2)}) collective-permute-start(f32[8,128]{1,0:T(8,128)S(1)} %get-tuple-element.79), channel_id=1, source_target_pairs={{1,2},{3,0},{2,1},{0,3},{5,6},{7,4},{6,5},{4,7},{9,10},{11,8},{10,... | collective-permute-start | bytes 12296 | tf_op jit(solution)/shard_map/ppermute | solution.py:623
  85.3 2.2 %collective-permute-start.16 = (f32[8,64]{1,0:T(8,128)S(1)}, f32[8,64]{1,0:T(8,128)S(1)}, u32[]{:S(2)}, u32[]{:S(2)}) collective-permute-start(f32[8,64]{1,0:T(8,128)S(1)} %get-tuple-element.81), channel_id=1, source_target_pairs={{0,1},{1,0},{2,3},{3,2},{4,5},{5,4},{6,7},{7,6},{8,9},{9,8},{10,11... | collective-permute-start | bytes 6152 | tf_op jit(solution)/shard_map/ppermute | solution.py:632
  85.4 2.5 %collective-permute-start.17 = (f32[8,64]{1,0:T(8,128)S(1)}, f32[8,64]{1,0:T(8,128)S(1)}, u32[]{:S(2)}, u32[]{:S(2)}) collective-permute-start(f32[8,64]{1,0:T(8,128)S(1)} %get-tuple-element.81), channel_id=1, source_target_pairs={{0,2},{1,3},{2,0},{3,1},{4,6},{5,7},{6,4},{7,5},{8,10},{9,11},{10,... | collective-permute-start | bytes 6152 | tf_op jit(solution)/shard_map/ppermute | solution.py:632
  86.6 3.3 %collective-permute-start.18 = (f32[8,64]{1,0:T(8,128)S(1)}, f32[8,64]{1,0:T(8,128)S(1)}, u32[]{:S(2)}, u32[]{:S(2)}) collective-permute-start(f32[8,64]{1,0:T(8,128)S(1)} %get-tuple-element.81), channel_id=1, source_target_pairs={{0,3},{1,2},{2,1},{3,0},{4,7},{5,6},{6,5},{7,4},{8,11},{9,10},{10,... | collective-permute-start | bytes 6152 | tf_op jit(solution)/shard_map/ppermute | solution.py:632
  (19 other events, 14.5 us)

commit v8 on v6

--- a/solution.py
+++ b/solution.py
@@ -9,6 +9,7 @@
 
 STEPS = 3
 CORNER_LANE = 112
+PIECE = 24
 FIELDS = 5
 RESULTS = 8
 PAD_ROWS = 8
@@ -267,6 +268,10 @@
     for copy in copies:
         copy.start()
     return copies
+
+
+def pieces(rows):
+    return [slice(0, PIECE), slice(PIECE, 2 * PIECE), slice(2 * PIECE, rows)]
 
 
 def start_kernel(
@@ -417,17 +422,20 @@
     total = picked.shape[1]
     half = total // 2
     by_device, by_place = slot_marks(devices, half // devices)
-    inner = (slice(None), slice(0, rows), slice(0, cols))
-    copies = fetch(
-        got,
-        [
-            (velocity_in, vel_ext.at[inner] if not first else velocity),
-            (stress_in, stress_ext.at[inner] if first else stress_ext),
-            (disp_in, disp),
-            (pressure_in, pressure),
+    if first:
+        pairs = [(thickness_in, thickness)]
+        pairs += [
+            (stress_in.at[:, part, :], stress_ext.at[:, part, 0:cols]) for part in pieces(rows)
         ]
-        + ([(thickness_in, thickness)] if first else []),
-    )
+        pairs += [(velocity_in, velocity)]
+    else:
+        pairs = [(velocity_in, vel_ext.at[:, 0:rows, 0:cols])]
+        pairs += [
+            (stress_in.at[:, part, :], stress_ext.at[:, part, :])
+            for part in pieces(rows + PAD_ROWS)
+        ]
+    pairs += [(disp_in, disp), (pressure_in, pressure)]
+    copies = fetch(got, pairs)
     sends = []
 
     def send(source, target):
@@ -451,13 +459,14 @@
 
     above, below = in_order("sec", sec_first[...], sec_second[...])
     left, right = in_order("girth", girth_first[...], girth_second[...])
-    for copy in copies:
-        copy.wait()
+    copies[0].wait()
     if first:
         load_stress(stress_ext, plate_ext, thickness, above, below, left, right)
     else:
         load_velocity(vel_ext, incoming, above, below, left, right)
     for start in range(0, rows + PAD_ROWS, 8):
+        if start in (0, PIECE, 2 * PIECE):
+            copies[1 + start // PIECE].wait()
         plate = plate_ext[0, start : start + 8, :]
         chunk = [stress_ext[k, start : start + 8, :] for k in range(RESULTS)]
         if not first:
@@ -466,7 +475,11 @@
                 stress_ext[k, start : start + 8, :] = value
         for k, value in enumerate(resultants(chunk, plate)):
             res_ext[k, start : start + 8, :] = value
-    send(stress_ext, stress_out)
+        for part in pieces(rows + PAD_ROWS):
+            if part.stop == start + 8:
+                send(stress_ext.at[:, part, :], stress_out.at[:, part, :])
+    for copy in copies[4:]:
+        copy.wait()
 
     for start in range(0, rows, 8):
         part = slice(start, start + 8)
@@ -540,8 +553,9 @@
     stress_out, moment, stress, vel_ext, got, sent,
 ):
     rows, cols = vel_ext.shape[1] - PAD_ROWS, vel_ext.shape[2] - LANES
-    inner = (slice(None), slice(0, rows), slice(0, cols))
-    copies = fetch(got, [(velocity_in, vel_ext.at[inner]), (stress_in, stress)])
+    pairs = [(velocity_in, vel_ext.at[:, 0:rows, 0:cols])]
+    pairs += [(stress_in.at[:, part, :], stress.at[:, part, :]) for part in pieces(rows)]
+    copies = fetch(got, pairs)
     above, below = in_order("sec", sec_first[...], sec_second[...])
     left, right = in_order("girth", girth_first[...], girth_second[...])
     first, _ = edge_columns(left, right)
@@ -549,12 +563,13 @@
     for f in range(FIELDS):
         sides = edge_block([(first, f, LANES - 1), (first, 8 + f, 0)])
         fill_halo(vel_ext, f, above[f : f + 1, :], below[f : f + 1, :], sides, empty)
-    for copy in copies:
-        copy.wait()
+    copies[0].wait()
     weight = height[0:1, :]
     parts = []
     sends = []
     for start in range(0, rows, 8):
+        if start in (0, PIECE, 2 * PIECE):
+            copies[1 + start // PIECE].wait()
         part = slice(start, start + 8)
         chunk = [stress[k, part, :] for k in range(RESULTS)]
         plate = plate_ext[0, part, :]
@@ -608,6 +623,18 @@
         couples = [(i, j) for i, j in couples if j > i or around]
         out.append(lax.ppermute(value, axis, couples + [(j, i) for i, j in couples]))
     return out
+
+
+def sum_over(value, axis):
+    count = lax.axis_size(axis)
+    if count & (count - 1):
+        return lax.psum(value, axis)
+    parts = [value] + [
+        lax.ppermute(value, axis, [(i, i ^ step) for i in range(count)]) for step in range(1, count)
+    ]
+    while len(parts) > 1:
+        parts = [a + b for a, b in zip(parts[0::2], parts[1::2])]
+    return parts[0]
 
 
 def exchange(joints):
@@ -687,7 +714,7 @@
             *([] if first else [plate]),
             far=5,
             far_out=3,
-            copies=(5, 1 + 2 * (rows // 32)),
+            copies=(7, 3 + 2 * (rows // 32)),
         )
         stress, velocity, displacement = results[:3]
         results = results[3:]
@@ -708,9 +735,9 @@
         stress, velocity, *ends, *sides, plate, height,
         far=2,
         far_out=1,
-        copies=(2, rows // 16),
-    )
-    moment = lax.psum(partial_moment[0], "girth")
+        copies=(4, rows // 16),
+    )
+    moment = sum_over(partial_moment, "girth")[0]
     return (displacement, velocity, stress, moment)
 
 

time: 80 us -> 75.2 us (0.940)
  the two profiles are of different devices: /device:TPU:4 before, /device:TPU:5 now
where the time goes in v8:
time: 75.2 us; the launch traced here: 74.8 us
  starting transfers between devices  43.7 us (58%)
  Pallas kernels  19.7 us (26%)
  waiting for transfers between devices  10 us (13%)
  between operations  0.77 us (1%)
    ppermute x16, starting transfers between devices, swap(): lax.ppermute(value, axis, couples + [(j, i) for i, j in couples])  25.6 us
    pallas_call x5, Pallas kernels, call(): pl.pallas_call(kernel, out_shape=[pltpu.HBM(shape, dtype) if k < far_out...  19.7 us
    all_to_all x3, starting transfers between devices, exchange(): blocks = lax.all_to_all(blocks, ('sec', 'girth'), 0, 0, tiled=True)  15.9 us
    ppermute x16, waiting for transfers between devices, swap(): lax.ppermute(value, axis, couples + [(j, i) for i, j in couples])  7.55 us
    ppermute x3, waiting for transfers between devices, sum_over(): lax.ppermute(value, axis, [(i, i ^ step) for i in range(count)])  2.48 us
    ppermute x3, starting transfers between devices, sum_over(): lax.ppermute(value, axis, [(i, i ^ step) for i in range(count)])  2.21 us
  transfers between devices with their start and end apart: 22, of which 6 were waited for; matrix products, arithmetic and copies ran while one was open for 0% of the time, Pallas kernels for 0%

profile of v8, /device:TPU:5, one launch (start us, length us, event | category | flops | bytes accessed | tf_op | source)
XLA Modules:
  0.0 74.8 jit_solution(18136882307409388115)
XLA Ops:
  0.6 3.0 %shard_map.111 = (f32[64,128]{1,0:T(8,128)}, f32[16,512]{1,0:T(8,128)S(1)}, f32[16,512]{1,0:T(8,128)S(1)}, f32[8,128]{1,0:T(8,128)S(1)}, f32[8,128]{1,0:T(8,128)...) custom-call(f32[5,64,512]{2,1,0:T(8,128)} %refs_2_.1, ...), custom_call_target="tpu_custom_call" | custom-call | tf_op jit(solution)/shard_map/pallas_call | solution.py:605
  3.7 6.4 %all-to-all-start = ((f32[32,2,128]{2,1,0:T(2,128)}), f32[32,2,128]{2,1,0:T(2,128)S(1)}, u32[]{:S(2)}, u32[]{:S(2)}) async-start(f32[32,2,128]{2,1,0:T(2,128)} %bitcast.3), calls=%async_computation | async-start | bytes 65536 | tf_op jit(solution)/shard_map/all_to_all | solution.py:642
  10.3 4.2 %collective-permute-start.1 = (f32[16,512]{1,0:T(8,128)S(1)}, f32[16,512]{1,0:T(8,128)S(1)}, u32[]{:S(2)}, u32[]{:S(2)}) collective-permute-start(f32[16,512]{1,0:T(8,128)S(1)} %get-tuple-element.44), channel_id=1, source_target_pairs={{4,8},{12,16},{20,24},{8,4},{16,12},{24,20},{5,9},{13,17},{21,25},... | collective-permute-start | bytes 98312 | tf_op jit(solution)/shard_map/ppermute | solution.py:624
  15.4 1.1 %collective-permute-start.3 = (f32[8,128]{1,0:T(8,128)S(1)}, f32[8,128]{1,0:T(8,128)S(1)}, u32[]{:S(2)}, u32[]{:S(2)}) collective-permute-start(f32[8,128]{1,0:T(8,128)S(1)} %get-tuple-element.46), channel_id=1, source_target_pairs={{1,2},{3,0},{2,1},{0,3},{5,6},{7,4},{6,5},{4,7},{9,10},{11,8},{10,... | collective-permute-start | bytes 12296 | tf_op jit(solution)/shard_map/ppermute | solution.py:624
  16.6 1.9 %collective-permute-done.3.refs_9_ = f32[8,128]{1,0:T(8,128)S(1)} collective-permute-done((f32[8,128]{1,0:T(8,128)S(1)}, f32[8,128]{1,0:T(8,128)S(1)}, u32[]{:S(2)}, u32[]{:S(2)}) %collective-permute-start.3) | collective-permute-done | bytes 4128 | tf_op jit(solution)/shard_map/ppermute | solution.py:624
  18.5 4.2 %shard_map.112 = (f32[8,72,640]{2,1,0:T(8,128)}, f32[5,64,512]{2,1,0:T(8,128)}, f32[5,64,512]{2,1,0:T(8,128)}, f32[1,72,640]{2,1,0:T(8,128)S(1)}, f32[8,1024]{1,...) custom-call(f32[8,64,512]{2,1,0:T(8,128)} %refs_0_.1, ...), custom_call_target="tpu_custom_call" | custom-call | tf_op jit(solution)/shard_map/pallas_call | solution.py:605
  22.7 4.8 %all-to-all-start.1 = ((f32[32,2,128]{2,1,0:T(2,128)}), f32[32,2,128]{2,1,0:T(2,128)S(1)}, u32[]{:S(2)}, u32[]{:S(2)}) async-start(f32[32,2,128]{2,1,0:T(2,128)} %bitcast.5), calls=%async_computation.1 | async-start | bytes 65536 | tf_op jit(solution)/shard_map/all_to_all | solution.py:642
  27.6 4.2 %collective-permute-start.5 = (f32[16,512]{1,0:T(8,128)S(1)}, f32[16,512]{1,0:T(8,128)S(1)}, u32[]{:S(2)}, u32[]{:S(2)}) collective-permute-start(f32[16,512]{1,0:T(8,128)S(1)} %get-tuple-element.56), channel_id=1, source_target_pairs={{4,8},{12,16},{20,24},{8,4},{16,12},{24,20},{5,9},{13,17},{21,25},... | collective-permute-start | bytes 98312 | tf_op jit(solution)/shard_map/ppermute | solution.py:624
  31.8 1.0 %collective-permute-start.6 = (f32[8,128]{1,0:T(8,128)S(1)}, f32[8,128]{1,0:T(8,128)S(1)}, u32[]{:S(2)}, u32[]{:S(2)}) collective-permute-start(f32[8,128]{1,0:T(8,128)S(1)} %get-tuple-element.57), channel_id=1, source_target_pairs={{0,1},{2,3},{1,0},{3,2},{4,5},{6,7},{5,4},{7,6},{8,9},{10,11},{9,8... | collective-permute-start | bytes 12296 | tf_op jit(solution)/shard_map/ppermute | solution.py:624
  32.8 1.1 %collective-permute-start.7 = (f32[8,128]{1,0:T(8,128)S(1)}, f32[8,128]{1,0:T(8,128)S(1)}, u32[]{:S(2)}, u32[]{:S(2)}) collective-permute-start(f32[8,128]{1,0:T(8,128)S(1)} %get-tuple-element.58), channel_id=1, source_target_pairs={{1,2},{3,0},{2,1},{0,3},{5,6},{7,4},{6,5},{4,7},{9,10},{11,8},{10,... | collective-permute-start | bytes 12296 | tf_op jit(solution)/shard_map/ppermute | solution.py:624
  34.0 1.9 %collective-permute-done.7.refs_9_ = f32[8,128]{1,0:T(8,128)S(1)} collective-permute-done((f32[8,128]{1,0:T(8,128)S(1)}, f32[8,128]{1,0:T(8,128)S(1)}, u32[]{:S(2)}, u32[]{:S(2)}) %collective-permute-start.7) | collective-permute-done | bytes 4128 | tf_op jit(solution)/shard_map/ppermute | solution.py:624
  35.9 5.1 %shard_map.113 = (f32[8,72,640]{2,1,0:T(8,128)}, f32[5,64,512]{2,1,0:T(8,128)}, f32[5,64,512]{2,1,0:T(8,128)}, f32[8,128]{1,0:T(8,128)S(1)}, f32[8,128]{1,0:T(8,...) custom-call(f32[8,72,640]{2,1,0:T(8,128)} %get-tuple-element.51.refs_0_, ...), custom_call_target="tpu_custom_call" | custom-call | tf_op jit(solution)/shard_map/pallas_call | solution.py:605
  41.0 4.8 %all-to-all-start.2 = ((f32[32,2,128]{2,1,0:T(2,128)}), f32[32,2,128]{2,1,0:T(2,128)S(1)}, u32[]{:S(2)}, u32[]{:S(2)}) async-start(f32[32,2,128]{2,1,0:T(2,128)} %bitcast.7), calls=%async_computation.2 | async-start | bytes 65536 | tf_op jit(solution)/shard_map/all_to_all | solution.py:642
  45.9 4.2 %collective-permute-start.9 = (f32[16,512]{1,0:T(8,128)S(1)}, f32[16,512]{1,0:T(8,128)S(1)}, u32[]{:S(2)}, u32[]{:S(2)}) collective-permute-start(f32[16,512]{1,0:T(8,128)S(1)} %get-tuple-element.67), channel_id=1, source_target_pairs={{4,8},{12,16},{20,24},{8,4},{16,12},{24,20},{5,9},{13,17},{21,25},... | collective-permute-start | bytes 98312 | tf_op jit(solution)/shard_map/ppermute | solution.py:624
  50.1 1.0 %collective-permute-start.10 = (f32[8,128]{1,0:T(8,128)S(1)}, f32[8,128]{1,0:T(8,128)S(1)}, u32[]{:S(2)}, u32[]{:S(2)}) collective-permute-start(f32[8,128]{1,0:T(8,128)S(1)} %get-tuple-element.68), channel_id=1, source_target_pairs={{0,1},{2,3},{1,0},{3,2},{4,5},{6,7},{5,4},{7,6},{8,9},{10,11},{9,8... | collective-permute-start | bytes 12296 | tf_op jit(solution)/shard_map/ppermute | solution.py:624
  51.1 1.1 %collective-permute-start.11 = (f32[8,128]{1,0:T(8,128)S(1)}, f32[8,128]{1,0:T(8,128)S(1)}, u32[]{:S(2)}, u32[]{:S(2)}) collective-permute-start(f32[8,128]{1,0:T(8,128)S(1)} %get-tuple-element.69), channel_id=1, source_target_pairs={{1,2},{3,0},{2,1},{0,3},{5,6},{7,4},{6,5},{4,7},{9,10},{11,8},{10,... | collective-permute-start | bytes 12296 | tf_op jit(solution)/shard_map/ppermute | solution.py:624
  52.2 1.9 %collective-permute-done.11.refs_9_ = f32[8,128]{1,0:T(8,128)S(1)} collective-permute-done((f32[8,128]{1,0:T(8,128)S(1)}, f32[8,128]{1,0:T(8,128)S(1)}, u32[]{:S(2)}, u32[]{:S(2)}) %collective-permute-start.11) | collective-permute-done | bytes 4128 | tf_op jit(solution)/shard_map/ppermute | solution.py:624
  54.1 4.3 %shard_map.114 = (f32[8,72,640]{2,1,0:T(8,128)}, f32[5,64,512]{2,1,0:T(8,128)}, f32[5,64,512]{2,1,0:T(8,128)}, f32[8,128]{1,0:T(8,128)S(1)}, f32[8,128]{1,0:T(8,...) custom-call(f32[8,72,640]{2,1,0:T(8,128)} %get-tuple-element.62.refs_0_, f32[5,64,512]{2,1,0:T(8,128)} %get-tuple-element.63.refs_1_, ...), custom_call_target="tpu_custom_call" | custom-call | tf_op jit(solution)/shard_map/pallas_call | solution.py:605
  58.5 4.3 %collective-permute-start.13 = (f32[8,512]{1,0:T(8,128)S(1)}, f32[8,512]{1,0:T(8,128)S(1)}, u32[]{:S(2)}, u32[]{:S(2)}) collective-permute-start(f32[8,512]{1,0:T(8,128)S(1)} %get-tuple-element.75), channel_id=1, source_target_pairs={{4,8},{12,16},{20,24},{8,4},{16,12},{24,20},{5,9},{13,17},{21,25},... | collective-permute-start | bytes 49160 | tf_op jit(solution)/shard_map/ppermute | solution.py:624
  63.4 1.2 %collective-permute-start.15 = (f32[8,128]{1,0:T(8,128)S(1)}, f32[8,128]{1,0:T(8,128)S(1)}, u32[]{:S(2)}, u32[]{:S(2)}) collective-permute-start(f32[8,128]{1,0:T(8,128)S(1)} %get-tuple-element.77), channel_id=1, source_target_pairs={{1,2},{3,0},{2,1},{0,3},{5,6},{7,4},{6,5},{4,7},{9,10},{11,8},{10,... | collective-permute-start | bytes 12296 | tf_op jit(solution)/shard_map/ppermute | solution.py:624
  64.7 1.8 %collective-permute-done.15.girth_second = f32[8,128]{1,0:T(8,128)S(1)} collective-permute-done((f32[8,128]{1,0:T(8,128)S(1)}, f32[8,128]{1,0:T(8,128)S(1)}, u32[]{:S(2)}, u32[]{:S(2)}) %collective-permute-start.15) | collective-permute-done | bytes 4128 | tf_op jit(solution)/shard_map/ppermute | solution.py:624
  66.5 3.1 %shard_map.115 = (f32[8,64,512]{2,1,0:T(8,128)}, f32[8,64]{1,0:T(8,128)S(1)}) custom-call(f32[8,72,640]{2,1,0:T(8,128)} %get-tuple-element.73.stress_in, f32[5,64,512]{2,1,0:T(8,128)} %get-tuple-element.39.velocity_in, f32[8,512]{1,0:T(8,128)S(1)} %collective-permute-done.12.sec_first, f32[8,512]{1,0:T(8,128)S(1)} %collective-permute-done.13.sec_second, ...), custom_call_target="tpu_custom_call" | custom-call | tf_op jit(solution)/shard_map/pallas_call | solution.py:605
  69.7 1.2 %collective-permute-start.17 = (f32[8,64]{1,0:T(8,128)S(1)}, f32[8,64]{1,0:T(8,128)S(1)}, u32[]{:S(2)}, u32[]{:S(2)}) collective-permute-start(f32[8,64]{1,0:T(8,128)S(1)} %get-tuple-element.79), channel_id=1, source_target_pairs={{0,2},{1,3},{2,0},{3,1},{4,6},{5,7},{6,4},{7,5},{8,10},{9,11},{10,... | collective-permute-start | bytes 6152 | tf_op jit(solution)/shard_map/ppermute | solution.py:633
  72.2 2.1 %collective-permute-done.18 = f32[8,64]{1,0:T(8,128)S(1)} collective-permute-done((f32[8,64]{1,0:T(8,128)S(1)}, f32[8,64]{1,0:T(8,128)S(1)}, u32[]{:S(2)}, u32[]{:S(2)}) %collective-permute-start.18) | collective-permute-done | bytes 2080 | tf_op jit(solution)/shard_map/ppermute | solution.py:633
  (29 shorter events, 4.2 us)
Async XLA Ops:
  3.7 14.8 %all-to-all-start = ((f32[32,2,128]{2,1,0:T(2,128)}), f32[32,2,128]{2,1,0:T(2,128)S(1)}, u32[]{:S(2)}, u32[]{:S(2)}) async-start(f32[32,2,128]{2,1,0:T(2,128)} %bitcast.3), calls=%async_computation | async-start | bytes 65536 | tf_op jit(solution)/shard_map/all_to_all | solution.py:642
  10.1 8.4 %collective-permute-start = (f32[16,512]{1,0:T(8,128)S(1)}, f32[16,512]{1,0:T(8,128)S(1)}, u32[]{:S(2)}, u32[]{:S(2)}) collective-permute-start(f32[16,512]{1,0:T(8,128)S(1)} %get-tuple-element.43), channel_id=1, source_target_pairs={{0,4},{8,12},{16,20},{24,28},{4,0},{12,8},{20,16},{28,24},{1,5},{9... | collective-permute-start | bytes 98312 | tf_op jit(solution)/shard_map/ppermute | solution.py:624
  10.3 8.2 %collective-permute-start.1 = (f32[16,512]{1,0:T(8,128)S(1)}, f32[16,512]{1,0:T(8,128)S(1)}, u32[]{:S(2)}, u32[]{:S(2)}) collective-permute-start(f32[16,512]{1,0:T(8,128)S(1)} %get-tuple-element.44), channel_id=1, source_target_pairs={{4,8},{12,16},{20,24},{8,4},{16,12},{24,20},{5,9},{13,17},{21,25},... | collective-permute-start | bytes 98312 | tf_op jit(solution)/shard_map/ppermute | solution.py:624
  14.4 2.1 %collective-permute-start.2 = (f32[8,128]{1,0:T(8,128)S(1)}, f32[8,128]{1,0:T(8,128)S(1)}, u32[]{:S(2)}, u32[]{:S(2)}) collective-permute-start(f32[8,128]{1,0:T(8,128)S(1)} %get-tuple-element.45), channel_id=1, source_target_pairs={{0,1},{2,3},{1,0},{3,2},{4,5},{6,7},{5,4},{7,6},{8,9},{10,11},{9,8... | collective-permute-start | bytes 12296 | tf_op jit(solution)/shard_map/ppermute | solution.py:624
  15.4 3.0 %collective-permute-start.3 = (f32[8,128]{1,0:T(8,128)S(1)}, f32[8,128]{1,0:T(8,128)S(1)}, u32[]{:S(2)}, u32[]{:S(2)}) collective-permute-start(f32[8,128]{1,0:T(8,128)S(1)} %get-tuple-element.46), channel_id=1, source_target_pairs={{1,2},{3,0},{2,1},{0,3},{5,6},{7,4},{6,5},{4,7},{9,10},{11,8},{10,... | collective-permute-start | bytes 12296 | tf_op jit(solution)/shard_map/ppermute | solution.py:624
  22.7 13.2 %all-to-all-start.1 = ((f32[32,2,128]{2,1,0:T(2,128)}), f32[32,2,128]{2,1,0:T(2,128)S(1)}, u32[]{:S(2)}, u32[]{:S(2)}) async-start(f32[32,2,128]{2,1,0:T(2,128)} %bitcast.5), calls=%async_computation.1 | async-start | bytes 65536 | tf_op jit(solution)/shard_map/all_to_all | solution.py:642
  27.5 8.4 %collective-permute-start.4 = (f32[16,512]{1,0:T(8,128)S(1)}, f32[16,512]{1,0:T(8,128)S(1)}, u32[]{:S(2)}, u32[]{:S(2)}) collective-permute-start(f32[16,512]{1,0:T(8,128)S(1)} %get-tuple-element.55), channel_id=1, source_target_pairs={{0,4},{8,12},{16,20},{24,28},{4,0},{12,8},{20,16},{28,24},{1,5},{9... | collective-permute-start | bytes 98312 | tf_op jit(solution)/shard_map/ppermute | solution.py:624
  27.6 8.2 %collective-permute-start.5 = (f32[16,512]{1,0:T(8,128)S(1)}, f32[16,512]{1,0:T(8,128)S(1)}, u32[]{:S(2)}, u32[]{:S(2)}) collective-permute-start(f32[16,512]{1,0:T(8,128)S(1)} %get-tuple-element.56), channel_id=1, source_target_pairs={{4,8},{12,16},{20,24},{8,4},{16,12},{24,20},{5,9},{13,17},{21,25},... | collective-permute-start | bytes 98312 | tf_op jit(solution)/shard_map/ppermute | solution.py:624
  31.8 2.1 %collective-permute-start.6 = (f32[8,128]{1,0:T(8,128)S(1)}, f32[8,128]{1,0:T(8,128)S(1)}, u32[]{:S(2)}, u32[]{:S(2)}) collective-permute-start(f32[8,128]{1,0:T(8,128)S(1)} %get-tuple-element.57), channel_id=1, source_target_pairs={{0,1},{2,3},{1,0},{3,2},{4,5},{6,7},{5,4},{7,6},{8,9},{10,11},{9,8... | collective-permute-start | bytes 12296 | tf_op jit(solution)/shard_map/ppermute | solution.py:624
  32.8 3.0 %collective-permute-start.7 = (f32[8,128]{1,0:T(8,128)S(1)}, f32[8,128]{1,0:T(8,128)S(1)}, u32[]{:S(2)}, u32[]{:S(2)}) collective-permute-start(f32[8,128]{1,0:T(8,128)S(1)} %get-tuple-element.58), channel_id=1, source_target_pairs={{1,2},{3,0},{2,1},{0,3},{5,6},{7,4},{6,5},{4,7},{9,10},{11,8},{10,... | collective-permute-start | bytes 12296 | tf_op jit(solution)/shard_map/ppermute | solution.py:624
  41.0 13.1 %all-to-all-start.2 = ((f32[32,2,128]{2,1,0:T(2,128)}), f32[32,2,128]{2,1,0:T(2,128)S(1)}, u32[]{:S(2)}, u32[]{:S(2)}) async-start(f32[32,2,128]{2,1,0:T(2,128)} %bitcast.7), calls=%async_computation.2 | async-start | bytes 65536 | tf_op jit(solution)/shard_map/all_to_all | solution.py:642
  45.7 8.4 %collective-permute-start.8 = (f32[16,512]{1,0:T(8,128)S(1)}, f32[16,512]{1,0:T(8,128)S(1)}, u32[]{:S(2)}, u32[]{:S(2)}) collective-permute-start(f32[16,512]{1,0:T(8,128)S(1)} %get-tuple-element.66), channel_id=1, source_target_pairs={{0,4},{8,12},{16,20},{24,28},{4,0},{12,8},{20,16},{28,24},{1,5},{9... | collective-permute-start | bytes 98312 | tf_op jit(solution)/shard_map/ppermute | solution.py:624
  45.9 8.2 %collective-permute-start.9 = (f32[16,512]{1,0:T(8,128)S(1)}, f32[16,512]{1,0:T(8,128)S(1)}, u32[]{:S(2)}, u32[]{:S(2)}) collective-permute-start(f32[16,512]{1,0:T(8,128)S(1)} %get-tuple-element.67), channel_id=1, source_target_pairs={{4,8},{12,16},{20,24},{8,4},{16,12},{24,20},{5,9},{13,17},{21,25},... | collective-permute-start | bytes 98312 | tf_op jit(solution)/shard_map/ppermute | solution.py:624
  50.1 2.1 %collective-permute-start.10 = (f32[8,128]{1,0:T(8,128)S(1)}, f32[8,128]{1,0:T(8,128)S(1)}, u32[]{:S(2)}, u32[]{:S(2)}) collective-permute-start(f32[8,128]{1,0:T(8,128)S(1)} %get-tuple-element.68), channel_id=1, source_target_pairs={{0,1},{2,3},{1,0},{3,2},{4,5},{6,7},{5,4},{7,6},{8,9},{10,11},{9,8... | collective-permute-start | bytes 12296 | tf_op jit(solution)/shard_map/ppermute | solution.py:624
  51.1 3.0 %collective-permute-start.11 = (f32[8,128]{1,0:T(8,128)S(1)}, f32[8,128]{1,0:T(8,128)S(1)}, u32[]{:S(2)}, u32[]{:S(2)}) collective-permute-start(f32[8,128]{1,0:T(8,128)S(1)} %get-tuple-element.69), channel_id=1, source_target_pairs={{1,2},{3,0},{2,1},{0,3},{5,6},{7,4},{6,5},{4,7},{9,10},{11,8},{10,... | collective-permute-start | bytes 12296 | tf_op jit(solution)/shard_map/ppermute | solution.py:624
  58.4 8.1 %collective-permute-start.12 = (f32[8,512]{1,0:T(8,128)S(1)}, f32[8,512]{1,0:T(8,128)S(1)}, u32[]{:S(2)}, u32[]{:S(2)}) collective-permute-start(f32[8,512]{1,0:T(8,128)S(1)} %get-tuple-element.74), channel_id=1, source_target_pairs={{0,4},{8,12},{16,20},{24,28},{4,0},{12,8},{20,16},{28,24},{1,5},{9... | collective-permute-start | bytes 49160 | tf_op jit(solution)/shard_map/ppermute | solution.py:624
  58.5 8.0 %collective-permute-start.13 = (f32[8,512]{1,0:T(8,128)S(1)}, f32[8,512]{1,0:T(8,128)S(1)}, u32[]{:S(2)}, u32[]{:S(2)}) collective-permute-start(f32[8,512]{1,0:T(8,128)S(1)} %get-tuple-element.75), channel_id=1, source_target_pairs={{4,8},{12,16},{20,24},{8,4},{16,12},{24,20},{5,9},{13,17},{21,25},... | collective-permute-start | bytes 49160 | tf_op jit(solution)/shard_map/ppermute | solution.py:624
  62.8 1.9 %collective-permute-start.14 = (f32[8,128]{1,0:T(8,128)S(1)}, f32[8,128]{1,0:T(8,128)S(1)}, u32[]{:S(2)}, u32[]{:S(2)}) collective-permute-start(f32[8,128]{1,0:T(8,128)S(1)} %get-tuple-element.76), channel_id=1, source_target_pairs={{0,1},{2,3},{1,0},{3,2},{4,5},{6,7},{5,4},{7,6},{8,9},{10,11},{9,8... | collective-permute-start | bytes 12296 | tf_op jit(solution)/shard_map/ppermute | solution.py:624
  63.4 3.0 %collective-permute-start.15 = (f32[8,128]{1,0:T(8,128)S(1)}, f32[8,128]{1,0:T(8,128)S(1)}, u32[]{:S(2)}, u32[]{:S(2)}) collective-permute-start(f32[8,128]{1,0:T(8,128)S(1)} %get-tuple-element.77), channel_id=1, source_target_pairs={{1,2},{3,0},{2,1},{0,3},{5,6},{7,4},{6,5},{4,7},{9,10},{11,8},{10,... | collective-permute-start | bytes 12296 | tf_op jit(solution)/shard_map/ppermute | solution.py:624
  69.6 2.2 %collective-permute-start.16 = (f32[8,64]{1,0:T(8,128)S(1)}, f32[8,64]{1,0:T(8,128)S(1)}, u32[]{:S(2)}, u32[]{:S(2)}) collective-permute-start(f32[8,64]{1,0:T(8,128)S(1)} %get-tuple-element.79), channel_id=1, source_target_pairs={{0,1},{1,0},{2,3},{3,2},{4,5},{5,4},{6,7},{7,6},{8,9},{9,8},{10,11... | collective-permute-start | bytes 6152 | tf_op jit(solution)/shard_map/ppermute | solution.py:633
  69.7 2.5 %collective-permute-start.17 = (f32[8,64]{1,0:T(8,128)S(1)}, f32[8,64]{1,0:T(8,128)S(1)}, u32[]{:S(2)}, u32[]{:S(2)}) collective-permute-start(f32[8,64]{1,0:T(8,128)S(1)} %get-tuple-element.79), channel_id=1, source_target_pairs={{0,2},{1,3},{2,0},{3,1},{4,6},{5,7},{6,4},{7,5},{8,10},{9,11},{10,... | collective-permute-start | bytes 6152 | tf_op jit(solution)/shard_map/ppermute | solution.py:633
  70.9 3.3 %collective-permute-start.18 = (f32[8,64]{1,0:T(8,128)S(1)}, f32[8,64]{1,0:T(8,128)S(1)}, u32[]{:S(2)}, u32[]{:S(2)}) collective-permute-start(f32[8,64]{1,0:T(8,128)S(1)} %get-tuple-element.79), channel_id=1, source_target_pairs={{0,3},{1,2},{2,1},{3,0},{4,7},{5,6},{6,5},{7,4},{8,11},{9,10},{10,... | collective-permute-start | bytes 6152 | tf_op jit(solution)/shard_map/ppermute | solution.py:633

commit v9 on v8

--- a/solution.py
+++ b/solution.py
@@ -221,16 +221,14 @@
 
 
 def send_joints(payload, near, far, corners):
-    devices = payload.shape[0] // 2
-    payload[pl.ds(0, devices, stride=2), :] = near
-    payload[pl.ds(1, devices, stride=2), :] = far
-    row = lax.broadcasted_iota(jnp.int32, (8, LANES), 0)
-    lane = lax.broadcasted_iota(jnp.int32, (8, LANES), 1)
+    payload[0] = near
+    payload[1] = far
+    row = lax.broadcasted_iota(jnp.int32, near.shape, 0)
+    lane = lax.broadcasted_iota(jnp.int32, near.shape, 1)
     free = jnp.logical_and(lane >= CORNER_LANE, lane < CORNER_LANE + FIELDS)
     for (device, _), corner in zip(corner_neighbours(), corners):
-        tile = lax.div(device, 4)
-        here = jnp.logical_and(free, row == 2 * lax.rem(device, 4))
-        set_tile(payload, tile, jnp.where(here, corner, tile_of(payload, tile)))
+        here = jnp.logical_and(free, row == device)
+        payload[0] = jnp.where(here, corner, payload[0])
 
 
 def in_order(axis, low, high):
@@ -255,9 +253,9 @@
 
 
 def corner_of(incoming, device):
-    row = lax.broadcasted_iota(jnp.int32, (8, LANES), 0)
-    tile = tile_of(incoming, lax.div(device, 4))
-    return jnp.sum(jnp.where(row == 2 * lax.rem(device, 4), tile, 0.0), axis=0, keepdims=True)
+    near = incoming[0]
+    row = lax.broadcasted_iota(jnp.int32, near.shape, 0)
+    return jnp.sum(jnp.where(row == device, near, 0.0), axis=0, keepdims=True)
 
 
 def fetch(done, pairs):
@@ -402,8 +400,9 @@
     else:
         plate_ext = refs[14]
         out = refs[15:]
-    (incoming, sec_first, sec_second, girth_first, girth_second,
-     column_marks, row_marks, picked, spring) = refs[5:14]
+    gathered = refs[5]
+    (sec_first, sec_second, girth_first, girth_second,
+     column_marks, row_marks, picked, spring) = refs[6:14]
     stress_out, velocity_out, disp_out = out[:3]
     out = out[3:]
     if first:
@@ -414,11 +413,11 @@
     if not last:
         picked_out, payload = out[:2]
         out = out[2:]
-    (stress_ext, res_ext, vel_ext, weld, velocity, disp, thickness, pressure,
+    (stress_ext, res_ext, vel_ext, weld, velocity, disp, thickness, pressure, gathered_tile,
      got, sent) = out
 
     _, rows, cols = velocity.shape
-    devices = incoming.shape[0] // 2
+    devices = gathered.shape[0]
     total = picked.shape[1]
     half = total // 2
     by_device, by_place = slot_marks(devices, half // devices)
@@ -435,7 +434,17 @@
             for part in pieces(rows + PAD_ROWS)
         ]
     pairs += [(disp_in, disp), (pressure_in, pressure)]
-    copies = fetch(got, pairs)
+    sec, girth, _, girths = place()
+    me = sec * girths + girth
+    tile = pl.ds(pl.multiple_of(lax.div(me, 8) * 8, 8), 8)
+    pairs = [(gathered.at[:, :, tile, :], gathered_tile)] + pairs
+    message, *copies = fetch(got, pairs)
+    message.wait()
+    row = lax.broadcasted_iota(jnp.int32, (devices, 8, LANES), 1)
+    incoming = [
+        jnp.sum(jnp.where(row == lax.rem(me, 8), gathered_tile[:, end], 0.0), axis=1)
+        for end in (0, 1)
+    ]
     sends = []
 
     def send(source, target):
@@ -445,7 +454,7 @@
 
     other = []
     for row in (1, 0):
-        high, low = split(incoming[pl.ds(row, devices, stride=2), :])
+        high, low = split(incoming[row])
         other.append(expand(high, by_device, by_place) + expand(low, by_device, by_place))
     if first:
         stiffness = jnp.concatenate([spring[0:1, :], other[1][5:6]], axis=1)
@@ -536,7 +545,7 @@
                 source = LANES - 1 if side else 0
                 target = CORNER_LANE + f
                 value = jnp.where(lane == target, pltpu.roll(part, (target - source) % LANES, 1), value)
-            corners.append(jnp.broadcast_to(value[row % 8 : row % 8 + 1], (8, LANES)))
+            corners.append(value[row % 8 : row % 8 + 1])
     send_sides(girth_pair, edge_rows(columns))
     send_joints(payload, near_out, far_out, corners)
     send_ends(
@@ -638,9 +647,7 @@
 
 
 def exchange(joints):
-    blocks = joints.reshape(joints.shape[0] // 2, 2, LANES)
-    blocks = lax.all_to_all(blocks, ("sec", "girth"), 0, 0, tiled=True)
-    return blocks.reshape(joints.shape)
+    return lax.all_gather(joints, ("sec", "girth"), axis=0)
 
 
 def local(displacement, velocity, stress, thickness, pressure, weld_from, weld_to, weld_stiff):
@@ -653,7 +660,7 @@
     height = jnp.broadcast_to(height[None, :], (8, cols))
 
     vmem_bytes = 8 * 1024 * 1024 + total * VMEM_PER_SLOT
-    message = (devices * 2, LANES)
+    message = (2, devices, LANES)
     edge = (8, LANES)
     strip = (16, cols)
     block = (FIELDS, rows, cols)
@@ -669,6 +676,7 @@
         (block, F32),
         ((rows, cols), jnp.int32),
         ((rows, cols), F32),
+        ((devices, 2, 8, LANES), F32),
     ]
 
     (payload, sec_first, sec_second, girth_first, girth_second,
@@ -712,9 +720,9 @@
             incoming, *ends, *sides,
             column_marks, row_marks, picked, spring,
             *([] if first else [plate]),
-            far=5,
+            far=6,
             far_out=3,
-            copies=(7, 3 + 2 * (rows // 32)),
+            copies=(8, 3 + 2 * (rows // 32)),
         )
         stress, velocity, displacement = results[:3]
         results = results[3:]

time: 75.2 us -> 211 us (2.81)
  the two profiles are of different devices: /device:TPU:5 before, /device:TPU:0 now
where the time goes in v9:
time: 211 us; the launch traced here: 210 us
  waiting for transfers between devices  156 us (74%)
  Pallas kernels  22.6 us (11%)
  starting transfers between devices  16.7 us (8%)
  between operations  13.9 us (7%)
    all_gather x3, waiting for transfers between devices, exchange(): return lax.all_gather(joints, ('sec', 'girth'), axis=0)  145 us
    pallas_call x5, Pallas kernels, call(): pl.pallas_call(kernel, out_shape=[pltpu.HBM(shape, dtype) if k < far_out...  22.6 us
    ppermute x16, starting transfers between devices, swap(): lax.ppermute(value, axis, couples + [(j, i) for i, j in couples])  14.6 us
    ppermute x16, waiting for transfers between devices, swap(): lax.ppermute(value, axis, couples + [(j, i) for i, j in couples])  8.28 us
  transfers between devices with their start and end apart: 22, of which 12 were waited for; matrix products, arithmetic and copies ran while one was open for 0% of the time, Pallas kernels for 0%

profile of v9, /device:TPU:0, one launch (start us, length us, event | category | flops | bytes accessed | tf_op | source)
XLA Modules:
  0.0 209.7 jit_solution(17645449288859476203)
XLA Ops:
  7.2 3.1 %shard_map.111 = (f32[2,32,128]{2,1,0:T(8,128)}, f32[16,512]{1,0:T(8,128)S(1)}, f32[16,512]{1,0:T(8,128)S(1)}, f32[8,128]{1,0:T(8,128)S(1)}, f32[8,128]{1,0:T(8,...) custom-call(f32[5,64,512]{2,1,0:T(8,128)} %refs_2_.1, ...), custom_call_target="tpu_custom_call" | custom-call | tf_op jit(solution)/shard_map/pallas_call | solution.py:614
  10.3 3.0 %collective-permute-start = (f32[16,512]{1,0:T(8,128)S(1)}, f32[16,512]{1,0:T(8,128)S(1)}, u32[]{:S(2)}, u32[]{:S(2)}) collective-permute-start(f32[16,512]{1,0:T(8,128)S(1)} %get-tuple-element.43), channel_id=1, source_target_pairs={{0,4},{8,12},{16,20},{24,28},{4,0},{12,8},{20,16},{28,24},{1,5},{9... | collective-permute-start | bytes 98312 | tf_op jit(solution)/shard_map/ppermute | solution.py:633
  13.4 0.7 collective-permute-start.1
  14.1 1.6 collective-permute-start.3
  15.7 1.5 collective-permute-done.3.refs_9_
  17.2 50.6 %all-gather.7.cloned.1.call-done = f32[64,32,128]{2,1,0:T(8,128)} async-done(((f32[2,32,128]{2,1,0:T(8,128)}), f32[64,32,128]{2,1,0:T(8,128)}) %all-gather.7.cloned.1.call-update) | async-done | bytes 1048592 | tf_op jit(solution)/shard_map/all_gather | solution.py:650
  67.8 5.5 %shard_map.112 = (f32[8,72,640]{2,1,0:T(8,128)}, f32[5,64,512]{2,1,0:T(8,128)}, f32[5,64,512]{2,1,0:T(8,128)}, f32[1,72,640]{2,1,0:T(8,128)S(1)}, f32[8,1024]{1,...) custom-call(f32[8,64,512]{2,1,0:T(8,128)} %refs_0_.1, ...), custom_call_target="tpu_custom_call" | custom-call | tf_op jit(solution)/shard_map/pallas_call | solution.py:614
  73.4 1.5 collective-permute-start.4
  75.7 0.8 collective-permute-start.7
  76.9 1.9 collective-permute-done.7.refs_9_
  78.8 47.3 %all-gather.9.cloned.1.call-done = f32[64,32,128]{2,1,0:T(8,128)} async-done(((f32[2,32,128]{2,1,0:T(8,128)}), f32[64,32,128]{2,1,0:T(8,128)}) %all-gather.9.cloned.1.call-update) | async-done | bytes 1048592 | tf_op jit(solution)/shard_map/all_gather | solution.py:650
  126.1 5.9 %shard_map.113 = (f32[8,72,640]{2,1,0:T(8,128)}, f32[5,64,512]{2,1,0:T(8,128)}, f32[5,64,512]{2,1,0:T(8,128)}, f32[8,128]{1,0:T(8,128)S(1)}, f32[8,128]{1,0:T(8,...) custom-call(f32[8,72,640]{2,1,0:T(8,128)} %get-tuple-element.51.refs_0_, ...), custom_call_target="tpu_custom_call" | custom-call | tf_op jit(solution)/shard_map/pallas_call | solution.py:614
  132.1 1.5 collective-permute-start.8
  134.3 0.8 collective-permute-start.11
  135.5 1.9 collective-permute-done.11.refs_9_
  137.4 47.4 %all-gather.11.cloned.1.call-done = f32[64,32,128]{2,1,0:T(8,128)} async-done(((f32[2,32,128]{2,1,0:T(8,128)}), f32[64,32,128]{2,1,0:T(8,128)}) %all-gather.11.cloned.1.call-update) | async-done | bytes 1048592 | tf_op jit(solution)/shard_map/all_gather | solution.py:650
  184.8 5.1 %shard_map.114 = (f32[8,72,640]{2,1,0:T(8,128)}, f32[5,64,512]{2,1,0:T(8,128)}, f32[5,64,512]{2,1,0:T(8,128)}, f32[8,128]{1,0:T(8,128)S(1)}, f32[8,128]{1,0:T(8,...) custom-call(f32[8,72,640]{2,1,0:T(8,128)} %get-tuple-element.62.refs_0_, f32[5,64,512]{2,1,0:T(8,128)} %get-tuple-element.63.refs_1_, ...), custom_call_target="tpu_custom_call" | custom-call | tf_op jit(solution)/shard_map/pallas_call | solution.py:614
  189.9 1.5 collective-permute-start.12
  192.2 0.8 collective-permute-start.15
  193.4 1.9 collective-permute-done.15.girth_second
  195.3 3.1 %shard_map.115 = (f32[8,64,512]{2,1,0:T(8,128)}, f32[8,64]{1,0:T(8,128)S(1)}) custom-call(f32[8,72,640]{2,1,0:T(8,128)} %get-tuple-element.73.stress_in, f32[5,64,512]{2,1,0:T(8,128)} %get-tuple-element.39.velocity_in, f32[8,512]{1,0:T(8,128)S(1)} %collective-permute-done.12.sec_first, f32[8,512]{1,0:T(8,128)S(1)} %collective-permute-done.13.sec_second, ...), custom_call_target="tpu_custom_call" | custom-call | tf_op jit(solution)/shard_map/pallas_call | solution.py:614
  198.9 0.7 collective-permute-start.17
  199.6 0.7 collective-permute-start.18
  200.3 2.2 %collective-permute-done.17 = f32[8,64]{1,0:T(8,128)S(1)} collective-permute-done((f32[8,64]{1,0:T(8,128)S(1)}, f32[8,64]{1,0:T(8,128)S(1)}, u32[]{:S(2)}, u32[]{:S(2)}) %collective-permute-start.17) | collective-permute-done | bytes 2080 | tf_op jit(solution)/shard_map/ppermute | solution.py:642
  (32 shorter events, 4.6 us)
Async XLA Ops:
  7.2 60.7 %all-gather.7.cloned.1.call-start = ((), (), s32[]{:S(2)}) async-start(), calls=%async_computation | async-start | bytes 1081344 | tf_op jit(solution)/shard_map/all_gather | solution.py:650
  10.3 115.8 %all-gather.9.cloned.1.call-start = ((), (), s32[]{:S(2)}) async-start(), calls=%async_computation.1 | async-start | bytes 1081344 | tf_op jit(solution)/shard_map/all_gather | solution.py:650
  10.3 6.9 %collective-permute-start = (f32[16,512]{1,0:T(8,128)S(1)}, f32[16,512]{1,0:T(8,128)S(1)}, u32[]{:S(2)}, u32[]{:S(2)}) collective-permute-start(f32[16,512]{1,0:T(8,128)S(1)} %get-tuple-element.43), channel_id=1, source_target_pairs={{0,4},{8,12},{16,20},{24,28},{4,0},{12,8},{20,16},{28,24},{1,5},{9... | collective-permute-start | bytes 98312 | tf_op jit(solution)/shard_map/ppermute | solution.py:633
  13.4 3.8 %collective-permute-start.1 = (f32[16,512]{1,0:T(8,128)S(1)}, f32[16,512]{1,0:T(8,128)S(1)}, u32[]{:S(2)}, u32[]{:S(2)}) collective-permute-start(f32[16,512]{1,0:T(8,128)S(1)} %get-tuple-element.44), channel_id=1, source_target_pairs={{4,8},{12,16},{20,24},{8,4},{16,12},{24,20},{5,9},{13,17},{21,25},... | collective-permute-start | bytes 98312 | tf_op jit(solution)/shard_map/ppermute | solution.py:633
  14.0 1.7 collective-permute-start.2
  14.1 3.1 %collective-permute-start.3 = (f32[8,128]{1,0:T(8,128)S(1)}, f32[8,128]{1,0:T(8,128)S(1)}, u32[]{:S(2)}, u32[]{:S(2)}) collective-permute-start(f32[8,128]{1,0:T(8,128)S(1)} %get-tuple-element.46), channel_id=1, source_target_pairs={{1,2},{3,0},{2,1},{0,3},{5,6},{7,4},{6,5},{4,7},{9,10},{11,8},{10,... | collective-permute-start | bytes 12296 | tf_op jit(solution)/shard_map/ppermute | solution.py:633
  73.4 111.5 %all-gather.11.cloned.1.call-start = ((), (), s32[]{:S(2)}) async-start(), calls=%async_computation.2 | async-start | bytes 1081344 | tf_op jit(solution)/shard_map/all_gather | solution.py:650
  73.4 5.4 %collective-permute-start.4 = (f32[16,512]{1,0:T(8,128)S(1)}, f32[16,512]{1,0:T(8,128)S(1)}, u32[]{:S(2)}, u32[]{:S(2)}) collective-permute-start(f32[16,512]{1,0:T(8,128)S(1)} %get-tuple-element.55), channel_id=1, source_target_pairs={{0,4},{8,12},{16,20},{24,28},{4,0},{12,8},{20,16},{28,24},{1,5},{9... | collective-permute-start | bytes 98312 | tf_op jit(solution)/shard_map/ppermute | solution.py:633
  75.0 3.8 %collective-permute-start.5 = (f32[16,512]{1,0:T(8,128)S(1)}, f32[16,512]{1,0:T(8,128)S(1)}, u32[]{:S(2)}, u32[]{:S(2)}) collective-permute-start(f32[16,512]{1,0:T(8,128)S(1)} %get-tuple-element.56), channel_id=1, source_target_pairs={{4,8},{12,16},{20,24},{8,4},{16,12},{24,20},{5,9},{13,17},{21,25},... | collective-permute-start | bytes 98312 | tf_op jit(solution)/shard_map/ppermute | solution.py:633
  75.6 1.2 collective-permute-start.6
  75.7 3.1 %collective-permute-start.7 = (f32[8,128]{1,0:T(8,128)S(1)}, f32[8,128]{1,0:T(8,128)S(1)}, u32[]{:S(2)}, u32[]{:S(2)}) collective-permute-start(f32[8,128]{1,0:T(8,128)S(1)} %get-tuple-element.58), channel_id=1, source_target_pairs={{1,2},{3,0},{2,1},{0,3},{5,6},{7,4},{6,5},{4,7},{9,10},{11,8},{10,... | collective-permute-start | bytes 12296 | tf_op jit(solution)/shard_map/ppermute | solution.py:633
  132.1 5.4 %collective-permute-start.8 = (f32[16,512]{1,0:T(8,128)S(1)}, f32[16,512]{1,0:T(8,128)S(1)}, u32[]{:S(2)}, u32[]{:S(2)}) collective-permute-start(f32[16,512]{1,0:T(8,128)S(1)} %get-tuple-element.66), channel_id=1, source_target_pairs={{0,4},{8,12},{16,20},{24,28},{4,0},{12,8},{20,16},{28,24},{1,5},{9... | collective-permute-start | bytes 98312 | tf_op jit(solution)/shard_map/ppermute | solution.py:633
  133.6 3.8 %collective-permute-start.9 = (f32[16,512]{1,0:T(8,128)S(1)}, f32[16,512]{1,0:T(8,128)S(1)}, u32[]{:S(2)}, u32[]{:S(2)}) collective-permute-start(f32[16,512]{1,0:T(8,128)S(1)} %get-tuple-element.67), channel_id=1, source_target_pairs={{4,8},{12,16},{20,24},{8,4},{16,12},{24,20},{5,9},{13,17},{21,25},... | collective-permute-start | bytes 98312 | tf_op jit(solution)/shard_map/ppermute | solution.py:633
  134.3 1.2 collective-permute-start.10
  134.3 3.1 %collective-permute-start.11 = (f32[8,128]{1,0:T(8,128)S(1)}, f32[8,128]{1,0:T(8,128)S(1)}, u32[]{:S(2)}, u32[]{:S(2)}) collective-permute-start(f32[8,128]{1,0:T(8,128)S(1)} %get-tuple-element.69), channel_id=1, source_target_pairs={{1,2},{3,0},{2,1},{0,3},{5,6},{7,4},{6,5},{4,7},{9,10},{11,8},{10,... | collective-permute-start | bytes 12296 | tf_op jit(solution)/shard_map/ppermute | solution.py:633
  189.9 5.4 %collective-permute-start.12 = (f32[8,512]{1,0:T(8,128)S(1)}, f32[8,512]{1,0:T(8,128)S(1)}, u32[]{:S(2)}, u32[]{:S(2)}) collective-permute-start(f32[8,512]{1,0:T(8,128)S(1)} %get-tuple-element.74), channel_id=1, source_target_pairs={{0,4},{8,12},{16,20},{24,28},{4,0},{12,8},{20,16},{28,24},{1,5},{9... | collective-permute-start | bytes 49160 | tf_op jit(solution)/shard_map/ppermute | solution.py:633
  191.5 3.8 %collective-permute-start.13 = (f32[8,512]{1,0:T(8,128)S(1)}, f32[8,512]{1,0:T(8,128)S(1)}, u32[]{:S(2)}, u32[]{:S(2)}) collective-permute-start(f32[8,512]{1,0:T(8,128)S(1)} %get-tuple-element.75), channel_id=1, source_target_pairs={{4,8},{12,16},{20,24},{8,4},{16,12},{24,20},{5,9},{13,17},{21,25},... | collective-permute-start | bytes 49160 | tf_op jit(solution)/shard_map/ppermute | solution.py:633
  192.1 1.2 collective-permute-start.14
  192.2 3.1 %collective-permute-start.15 = (f32[8,128]{1,0:T(8,128)S(1)}, f32[8,128]{1,0:T(8,128)S(1)}, u32[]{:S(2)}, u32[]{:S(2)}) collective-permute-start(f32[8,128]{1,0:T(8,128)S(1)} %get-tuple-element.77), channel_id=1, source_target_pairs={{1,2},{3,0},{2,1},{0,3},{5,6},{7,4},{6,5},{4,7},{9,10},{11,8},{10,... | collective-permute-start | bytes 12296 | tf_op jit(solution)/shard_map/ppermute | solution.py:633
  198.4 1.9 collective-permute-start.16
  198.9 3.6 %collective-permute-start.17 = (f32[8,64]{1,0:T(8,128)S(1)}, f32[8,64]{1,0:T(8,128)S(1)}, u32[]{:S(2)}, u32[]{:S(2)}) collective-permute-start(f32[8,64]{1,0:T(8,128)S(1)} %get-tuple-element.79), channel_id=1, source_target_pairs={{0,2},{1,3},{2,0},{3,1},{4,6},{5,7},{6,4},{7,5},{8,10},{9,11},{10,... | collective-permute-start | bytes 6152 | tf_op jit(solution)/shard_map/ppermute | solution.py:642
  199.6 3.1 %collective-permute-start.18 = (f32[8,64]{1,0:T(8,128)S(1)}, f32[8,64]{1,0:T(8,128)S(1)}, u32[]{:S(2)}, u32[]{:S(2)}) collective-permute-start(f32[8,64]{1,0:T(8,128)S(1)} %get-tuple-element.79), channel_id=1, source_target_pairs={{0,3},{1,2},{2,1},{3,0},{4,7},{5,6},{6,5},{7,4},{8,11},{9,10},{10,... | collective-permute-start | bytes 6152 | tf_op jit(solution)/shard_map/ppermute | solution.py:642
Sparse Core Ops, SparseCore 0:
  11.4 56.3 all-gather.6
  73.5 52.6 all-gather.8
  132.2 52.6 all-gather.10

commit v10 on v8

--- a/solution.py
+++ b/solution.py
@@ -171,28 +171,41 @@
     return xx * scale, yy * scale, xy * scale
 
 
-def stress_chunk(vel_ref, stress, plate, start):
-    current = [vel_ref[f, start : start + 8, :] for f in range(FIELDS)]
-    along_x = [difference_x(vel_ref, f, start) for f in range(FIELDS)]
-    along_y = [difference_y(value) for value in current]
+def membrane_chunk(along_x, along_y, stress):
     normal = 0.5 * time_step * plate_modulus
     skew = 0.5 * time_step * shear_modulus
-    arm = 0.5 * plate
-    membrane = radial_return(
+    return radial_return(
         stress[0] + normal * (along_x[0] + poisson_ratio * along_y[1]),
         stress[1] + normal * (along_y[1] + poisson_ratio * along_x[0]),
         stress[2] + skew * (along_y[0] + along_x[1]),
     )
+
+
+def plate_chunk(along_x, along_y, turns, stress, plate):
+    arm = 0.5 * plate
+    normal = 0.5 * time_step * plate_modulus * arm
+    skew = 0.5 * time_step * shear_modulus
     bending = radial_return(
-        stress[3] + (normal * arm) * (along_x[3] + poisson_ratio * along_y[4]),
-        stress[4] + (normal * arm) * (along_y[4] + poisson_ratio * along_x[3]),
-        stress[5] + (skew * arm) * (along_y[3] + along_x[4]),
-    )
-    shear = (
-        stress[6] + skew * (along_x[2] + 2.0 * current[3]),
-        stress[7] + skew * (along_y[2] + 2.0 * current[4]),
-    )
-    return membrane + bending + shear
+        stress[0] + normal * (along_x[1] + poisson_ratio * along_y[2]),
+        stress[1] + normal * (along_y[2] + poisson_ratio * along_x[1]),
+        stress[2] + (skew * arm) * (along_y[1] + along_x[2]),
+    )
+    return bending + (
+        stress[3] + skew * (along_x[0] + 2.0 * turns[0]),
+        stress[4] + skew * (along_y[0] + 2.0 * turns[1]),
+    )
+
+
+def differences(vel_ref, fields, start):
+    current = [vel_ref[f, start : start + 8, :] for f in fields]
+    along_x = [difference_x(vel_ref, f, start) for f in fields]
+    return current, along_x, [difference_y(value) for value in current]
+
+
+def stress_chunk(vel_ref, stress, plate, start):
+    current, along_x, along_y = differences(vel_ref, range(FIELDS), start)
+    membrane = membrane_chunk(along_x[:2], along_y[:2], stress[:3])
+    return membrane + plate_chunk(along_x[2:], along_y[2:], current[3:], stress[3:], plate)
 
 
 def resultants(stress, plate):
@@ -402,7 +415,7 @@
     else:
         plate_ext = refs[14]
         out = refs[15:]
-    (incoming, sec_first, sec_second, girth_first, girth_second,
+    (incoming, sec_second, sec_first, girth_second, girth_first,
      column_marks, row_marks, picked, spring) = refs[5:14]
     stress_out, velocity_out, disp_out = out[:3]
     out = out[3:]
@@ -548,52 +561,68 @@
         copy.wait()
 
 
-def final_kernel(
-    stress_in, velocity_in, sec_first, sec_second, girth_first, girth_second, plate_ext, height,
-    stress_out, moment, stress, vel_ext, got, sent,
-):
+def final_kernel(membrane, *refs):
+    (stress_in, velocity_in), refs = refs[:2], refs[2:]
+    if membrane:
+        sec_second, sec_first, girth_second, girth_first, plate_ext, height = refs[:6]
+        stress_out, moment = refs[6:8]
+        refs = refs[8:]
+    else:
+        sec_second, sec_first, girth_second, girth_first, plate_ext = refs[1:6]
+        stress_out = refs[6]
+        refs = refs[7:]
+    stress, made, vel_ext, got, sent = refs
     rows, cols = vel_ext.shape[1] - PAD_ROWS, vel_ext.shape[2] - LANES
-    pairs = [(velocity_in, vel_ext.at[:, 0:rows, 0:cols])]
-    pairs += [(stress_in.at[:, part, :], stress.at[:, part, :]) for part in pieces(rows)]
+    fields = range(0, 2) if membrane else range(2, FIELDS)
+    kinds = slice(0, 3) if membrane else slice(3, RESULTS)
+    pairs = [(velocity_in.at[fields.start : fields.stop], vel_ext.at[:, 0:rows, 0:cols])]
+    pairs += [(stress_in.at[kinds, part, 0:cols], stress.at[:, part, :]) for part in pieces(rows)]
     copies = fetch(got, pairs)
     above, below = in_order("sec", sec_first[...], sec_second[...])
     left, right = in_order("girth", girth_first[...], girth_second[...])
     first, _ = edge_columns(left, right)
     empty = jnp.zeros((PAD_ROWS, LANES), F32)
-    for f in range(FIELDS):
+    for k, f in enumerate(fields):
         sides = edge_block([(first, f, LANES - 1), (first, 8 + f, 0)])
-        fill_halo(vel_ext, f, above[f : f + 1, :], below[f : f + 1, :], sides, empty)
+        fill_halo(vel_ext, k, above[f : f + 1, :], below[f : f + 1, :], sides, empty)
     copies[0].wait()
-    weight = height[0:1, :]
     parts = []
     sends = []
     for start in range(0, rows, 8):
         if start in (0, PIECE, 2 * PIECE):
             copies[1 + start // PIECE].wait()
         part = slice(start, start + 8)
-        chunk = [stress[k, part, :] for k in range(RESULTS)]
-        plate = plate_ext[0, part, :]
-        chunk = stress_chunk(vel_ext, chunk, plate, start)
+        chunk = [stress[k, part, :] for k in range(stress.shape[0])]
+        plate = plate_ext[0, part, :cols]
+        current, along_x, along_y = [
+            [value[:, :cols] for value in values]
+            for values in differences(vel_ext, range(len(fields)), start)
+        ]
+        if membrane:
+            chunk = membrane_chunk(along_x, along_y, chunk)
+            weighted = plate * chunk[0] * height[0:1, :]
+            parts.append(jnp.sum(weighted, axis=1, keepdims=True))
+        else:
+            chunk = plate_chunk(along_x, along_y, current[1:], chunk, plate)
         for k, value in enumerate(chunk):
-            stress[k, part, :] = value
+            made[k, part, :] = value
         if start % 16 == 8:
             done = slice(start - 8, start + 8)
             copy = pltpu.make_async_copy(
-                stress.at[:, done, :cols], stress_out.at[:, done, :], sent.at[len(sends)]
+                made.at[:, done, :], stress_out.at[kinds, done, :], sent.at[len(sends)]
             )
             copy.start()
             sends.append(copy)
-        weighted = plate[:, :cols] * chunk[0][:, :cols] * weight
-        parts.append(jnp.sum(weighted, axis=1, keepdims=True))
-    column = jnp.broadcast_to(jnp.concatenate(parts, axis=0), (rows, LANES))
-    if rows < LANES:
-        column = jnp.concatenate([column, jnp.zeros((LANES - rows, LANES), F32)], axis=0)
-    moment[...] = column.T[0:8, :rows]
+    if membrane:
+        column = jnp.broadcast_to(jnp.concatenate(parts, axis=0), (rows, LANES))
+        if rows < LANES:
+            column = jnp.concatenate([column, jnp.zeros((LANES - rows, LANES), F32)], axis=0)
+        moment[...] = column.T[0:8, :rows]
     for copy in sends:
         copy.wait()
 
 
-def call(kernel, vmem_bytes, outs, scratch, *operands, far=0, far_out=0, copies=(1,)):
+def call(kernel, vmem_bytes, outs, scratch, *operands, far=0, far_out=0, copies=(1,), alias=None):
     operands = [
         pltpu.with_memory_space_constraint(value, pltpu.HBM) if k < far else value
         for k, value in enumerate(operands)
@@ -611,6 +640,7 @@
         in_specs=[away] * far + [whole] * (len(operands) - far),
         out_specs=[away] * far_out + [whole] * (len(outs) - far_out),
         scratch_shapes=scratch,
+        input_output_aliases=alias or {},
         compiler_params=pltpu.CompilerParams(vmem_limit_bytes=vmem_bytes),
     )(*operands)
 
@@ -618,7 +648,7 @@
 def swap(pair, axis, around):
     count = lax.axis_size(axis)
     out = []
-    for start, value in enumerate(pair):
+    for start, value in reversed(list(enumerate(pair))):
         couples = [(i, (i + 1) % count) for i in range(start, count, 2)]
         couples = [(i, j) for i, j in couples if j > i or around]
         out.append(lax.ppermute(value, axis, couples + [(j, i) for i, j in couples]))
@@ -629,9 +659,11 @@
     count = lax.axis_size(axis)
     if count & (count - 1):
         return lax.psum(value, axis)
-    parts = [value] + [
-        lax.ppermute(value, axis, [(i, i ^ step) for i in range(count)]) for step in range(1, count)
+    parts = [
+        lax.ppermute(value, axis, [(i, i ^ step) for i in range(count)])
+        for step in range(count - 1, 0, -1)
     ]
+    parts = [value] + parts[::-1]
     while len(parts) > 1:
         parts = [a + b for a, b in zip(parts[0::2], parts[1::2])]
     return parts[0]
@@ -727,15 +759,32 @@
 
     ends = swap((sec_first, sec_second), "sec", False)
     sides = swap((girth_first, girth_second), "girth", True)
-    stress, partial_moment = call(
-        final_kernel,
+    membrane, partial_moment = call(
+        functools.partial(final_kernel, True),
         vmem_bytes,
         [((RESULTS, rows, cols), F32), ((8, rows), F32)],
-        [(stress_shape, F32), ((FIELDS, rows + PAD_ROWS, cols + LANES), F32)],
+        [
+            ((3, rows, cols), F32), ((3, rows, cols), F32),
+            ((2, rows + PAD_ROWS, cols + LANES), F32),
+        ],
         stress, velocity, *ends, *sides, plate, height,
         far=2,
         far_out=1,
         copies=(4, rows // 16),
+    )
+    (stress,) = call(
+        functools.partial(final_kernel, False),
+        vmem_bytes,
+        [((RESULTS, rows, cols), F32)],
+        [
+            ((5, rows, cols), F32), ((5, rows, cols), F32),
+            ((3, rows + PAD_ROWS, cols + LANES), F32),
+        ],
+        stress, velocity, membrane, *ends, *sides, plate,
+        far=3,
+        far_out=1,
+        copies=(4, rows // 16),
+        alias={2: 0},
     )
     moment = sum_over(partial_moment, "girth")[0]
     return (displacement, velocity, stress, moment)

time: 75.2 us -> 74.4 us (0.989)
  the two profiles are of different devices: /device:TPU:5 before, /device:TPU:0 now
where the time goes in v10:
time: 74.4 us; the launch traced here: 74 us
  starting transfers between devices  45.1 us (61%)
  Pallas kernels  21.2 us (28%)
  waiting for transfers between devices  6.28 us (8%)
  between operations  0.81 us (1%)
    ppermute x16, starting transfers between devices, swap(): lax.ppermute(value, axis, couples + [(j, i) for i, j in couples])  26.8 us
    pallas_call x6, Pallas kernels, call(): pl.pallas_call(kernel, out_shape=[pltpu.HBM(shape, dtype) if k < far_out...  21.2 us
    all_to_all x3, starting transfers between devices, exchange(): blocks = lax.all_to_all(blocks, ('sec', 'girth'), 0, 0, tiled=True)  16.4 us
    ppermute x16, waiting for transfers between devices, swap(): lax.ppermute(value, axis, couples + [(j, i) for i, j in couples])  5.94 us
    ppermute x3, starting transfers between devices, sum_over(): lax.ppermute(value, axis, [(i, i ^ step) for i in range(count)])  1.94 us
  transfers between devices with their start and end apart: 22, of which 5 were waited for; matrix products, arithmetic and copies ran while one was open for 0% of the time, Pallas kernels for 3%

profile of v10, /device:TPU:0, one launch (start us, length us, event | category | flops | bytes accessed | tf_op | source)
XLA Modules:
  0.0 74.0 jit_solution(12837789098743619335)
XLA Ops:
  0.6 3.0 %shard_map.111 = (f32[64,128]{1,0:T(8,128)}, f32[16,512]{1,0:T(8,128)S(1)}, f32[16,512]{1,0:T(8,128)S(1)}, f32[8,128]{1,0:T(8,128)S(1)}, f32[8,128]{1,0:T(8,128)...) custom-call(f32[5,64,512]{2,1,0:T(8,128)} %refs_2_.1, ...), custom_call_target="tpu_custom_call" | custom-call | tf_op jit(solution)/shard_map/pallas_call | solution.py:634
  3.7 7.3 %all-to-all-start = ((f32[32,2,128]{2,1,0:T(2,128)}), f32[32,2,128]{2,1,0:T(2,128)S(1)}, u32[]{:S(2)}, u32[]{:S(2)}) async-start(f32[32,2,128]{2,1,0:T(2,128)} %bitcast.3), calls=%async_computation | async-start | bytes 65536 | tf_op jit(solution)/shard_map/all_to_all | solution.py:674
  11.0 0.7 collective-permute-start
  11.7 4.5 %collective-permute-start.1 = (f32[16,512]{1,0:T(8,128)S(1)}, f32[16,512]{1,0:T(8,128)S(1)}, u32[]{:S(2)}, u32[]{:S(2)}) collective-permute-start(f32[16,512]{1,0:T(8,128)S(1)} %get-tuple-element.44), channel_id=1, source_target_pairs={{0,4},{8,12},{16,20},{24,28},{4,0},{12,8},{20,16},{28,24},{1,5},{9... | collective-permute-start | bytes 98312 | tf_op jit(solution)/shard_map/ppermute | solution.py:654
  16.9 0.9 %collective-permute-start.3 = (f32[8,128]{1,0:T(8,128)S(1)}, f32[8,128]{1,0:T(8,128)S(1)}, u32[]{:S(2)}, u32[]{:S(2)}) collective-permute-start(f32[8,128]{1,0:T(8,128)S(1)} %get-tuple-element.46), channel_id=1, source_target_pairs={{0,1},{2,3},{1,0},{3,2},{4,5},{6,7},{5,4},{7,6},{8,9},{10,11},{9,8... | collective-permute-start | bytes 12296 | tf_op jit(solution)/shard_map/ppermute | solution.py:654
  17.8 1.5 %collective-permute-done.2.refs_8_ = f32[8,128]{1,0:T(8,128)S(1)} collective-permute-done((f32[8,128]{1,0:T(8,128)S(1)}, f32[8,128]{1,0:T(8,128)S(1)}, u32[]{:S(2)}, u32[]{:S(2)}) %collective-permute-start.2) | collective-permute-done | bytes 4128 | tf_op jit(solution)/shard_map/ppermute | solution.py:654
  19.3 4.2 %shard_map.112 = (f32[8,72,640]{2,1,0:T(8,128)}, f32[5,64,512]{2,1,0:T(8,128)}, f32[5,64,512]{2,1,0:T(8,128)}, f32[1,72,640]{2,1,0:T(8,128)S(1)}, f32[8,1024]{1,...) custom-call(f32[8,64,512]{2,1,0:T(8,128)} %refs_0_.1, ...), custom_call_target="tpu_custom_call" | custom-call | tf_op jit(solution)/shard_map/pallas_call | solution.py:634
  23.5 4.5 %all-to-all-start.1 = ((f32[32,2,128]{2,1,0:T(2,128)}), f32[32,2,128]{2,1,0:T(2,128)S(1)}, u32[]{:S(2)}, u32[]{:S(2)}) async-start(f32[32,2,128]{2,1,0:T(2,128)} %bitcast.5), calls=%async_computation.1 | async-start | bytes 65536 | tf_op jit(solution)/shard_map/all_to_all | solution.py:674
  28.1 0.7 collective-permute-start.4
  28.7 4.5 %collective-permute-start.5 = (f32[16,512]{1,0:T(8,128)S(1)}, f32[16,512]{1,0:T(8,128)S(1)}, u32[]{:S(2)}, u32[]{:S(2)}) collective-permute-start(f32[16,512]{1,0:T(8,128)S(1)} %get-tuple-element.56), channel_id=1, source_target_pairs={{0,4},{8,12},{16,20},{24,28},{4,0},{12,8},{20,16},{28,24},{1,5},{9... | collective-permute-start | bytes 98312 | tf_op jit(solution)/shard_map/ppermute | solution.py:654
  33.9 0.9 %collective-permute-start.7 = (f32[8,128]{1,0:T(8,128)S(1)}, f32[8,128]{1,0:T(8,128)S(1)}, u32[]{:S(2)}, u32[]{:S(2)}) collective-permute-start(f32[8,128]{1,0:T(8,128)S(1)} %get-tuple-element.58), channel_id=1, source_target_pairs={{0,1},{2,3},{1,0},{3,2},{4,5},{6,7},{5,4},{7,6},{8,9},{10,11},{9,8... | collective-permute-start | bytes 12296 | tf_op jit(solution)/shard_map/ppermute | solution.py:654
  34.8 1.5 %collective-permute-done.6.refs_8_ = f32[8,128]{1,0:T(8,128)S(1)} collective-permute-done((f32[8,128]{1,0:T(8,128)S(1)}, f32[8,128]{1,0:T(8,128)S(1)}, u32[]{:S(2)}, u32[]{:S(2)}) %collective-permute-start.6) | collective-permute-done | bytes 4128 | tf_op jit(solution)/shard_map/ppermute | solution.py:654
  36.4 5.1 %shard_map.113 = (f32[8,72,640]{2,1,0:T(8,128)}, f32[5,64,512]{2,1,0:T(8,128)}, f32[5,64,512]{2,1,0:T(8,128)}, f32[8,128]{1,0:T(8,128)S(1)}, f32[8,128]{1,0:T(8,...) custom-call(f32[8,72,640]{2,1,0:T(8,128)} %get-tuple-element.51.refs_0_, ...), custom_call_target="tpu_custom_call" | custom-call | tf_op jit(solution)/shard_map/pallas_call | solution.py:634
  41.5 4.5 %all-to-all-start.2 = ((f32[32,2,128]{2,1,0:T(2,128)}), f32[32,2,128]{2,1,0:T(2,128)S(1)}, u32[]{:S(2)}, u32[]{:S(2)}) async-start(f32[32,2,128]{2,1,0:T(2,128)} %bitcast.7), calls=%async_computation.2 | async-start | bytes 65536 | tf_op jit(solution)/shard_map/all_to_all | solution.py:674
  46.7 4.5 %collective-permute-start.9 = (f32[16,512]{1,0:T(8,128)S(1)}, f32[16,512]{1,0:T(8,128)S(1)}, u32[]{:S(2)}, u32[]{:S(2)}) collective-permute-start(f32[16,512]{1,0:T(8,128)S(1)} %get-tuple-element.67), channel_id=1, source_target_pairs={{0,4},{8,12},{16,20},{24,28},{4,0},{12,8},{20,16},{28,24},{1,5},{9... | collective-permute-start | bytes 98312 | tf_op jit(solution)/shard_map/ppermute | solution.py:654
  51.9 0.9 %collective-permute-start.11 = (f32[8,128]{1,0:T(8,128)S(1)}, f32[8,128]{1,0:T(8,128)S(1)}, u32[]{:S(2)}, u32[]{:S(2)}) collective-permute-start(f32[8,128]{1,0:T(8,128)S(1)} %get-tuple-element.69), channel_id=1, source_target_pairs={{0,1},{2,3},{1,0},{3,2},{4,5},{6,7},{5,4},{7,6},{8,9},{10,11},{9,8... | collective-permute-start | bytes 12296 | tf_op jit(solution)/shard_map/ppermute | solution.py:654
  52.8 1.5 %collective-permute-done.10.refs_8_ = f32[8,128]{1,0:T(8,128)S(1)} collective-permute-done((f32[8,128]{1,0:T(8,128)S(1)}, f32[8,128]{1,0:T(8,128)S(1)}, u32[]{:S(2)}, u32[]{:S(2)}) %collective-permute-start.10) | collective-permute-done | bytes 4128 | tf_op jit(solution)/shard_map/ppermute | solution.py:654
  54.3 4.3 %shard_map.114 = (f32[8,72,640]{2,1,0:T(8,128)}, f32[5,64,512]{2,1,0:T(8,128)}, f32[5,64,512]{2,1,0:T(8,128)}, f32[8,128]{1,0:T(8,128)S(1)}, f32[8,128]{1,0:T(8,...) custom-call(f32[8,72,640]{2,1,0:T(8,128)} %get-tuple-element.62.refs_0_, f32[5,64,512]{2,1,0:T(8,128)} %get-tuple-element.63.refs_1_, ...), custom_call_target="tpu_custom_call" | custom-call | tf_op jit(solution)/shard_map/pallas_call | solution.py:634
  59.2 4.2 %collective-permute-start.13 = (f32[8,512]{1,0:T(8,128)S(1)}, f32[8,512]{1,0:T(8,128)S(1)}, u32[]{:S(2)}, u32[]{:S(2)}) collective-permute-start(f32[8,512]{1,0:T(8,128)S(1)} %get-tuple-element.75), channel_id=1, source_target_pairs={{0,4},{8,12},{16,20},{24,28},{4,0},{12,8},{20,16},{28,24},{1,5},{9... | collective-permute-start | bytes 49160 | tf_op jit(solution)/shard_map/ppermute | solution.py:654
  63.6 1.5 %collective-permute-start.15 = (f32[8,128]{1,0:T(8,128)S(1)}, f32[8,128]{1,0:T(8,128)S(1)}, u32[]{:S(2)}, u32[]{:S(2)}) collective-permute-start(f32[8,128]{1,0:T(8,128)S(1)} %get-tuple-element.77), channel_id=1, source_target_pairs={{0,1},{2,3},{1,0},{3,2},{4,5},{6,7},{5,4},{7,6},{8,9},{10,11},{9,8... | collective-permute-start | bytes 12296 | tf_op jit(solution)/shard_map/ppermute | solution.py:654
  65.1 1.5 %collective-permute-done.14.refs_4_.refs_5_ = f32[8,128]{1,0:T(8,128)S(1)} collective-permute-done((f32[8,128]{1,0:T(8,128)S(1)}, f32[8,128]{1,0:T(8,128)S(1)}, u32[]{:S(2)}, u32[]{:S(2)}) %collective-permute-start.14) | collective-permute-done | bytes 4128 | tf_op jit(solution)/shard_map/ppermute | solution.py:654
  66.6 2.3 %shard_map.115 = (f32[8,64,512]{2,1,0:T(8,128)}, f32[8,64]{1,0:T(8,128)S(1)}) custom-call(f32[8,72,640]{2,1,0:T(8,128)} %get-tuple-element.73.refs_0_, f32[5,64,512]{2,1,0:T(8,128)} %get-tuple-element.39.refs_1_, f32[8,512]{1,0:T(8,128)S(1)} %collective-permute-done.12.refs_2_.refs_3_, f32[8,512]{1,0:T(8,128)S(1)} %collective-permute-done.13.refs_3_.refs_4_, ...), custom_call_target="tpu_custom_call" | custom-call | tf_op jit(solution)/shard_map/pallas_call | solution.py:634
  69.0 1.4 %collective-permute-start.17 = (f32[8,64]{1,0:T(8,128)S(1)}, f32[8,64]{1,0:T(8,128)S(1)}, u32[]{:S(2)}, u32[]{:S(2)}) collective-permute-start(f32[8,64]{1,0:T(8,128)S(1)} %get-tuple-element.79), channel_id=1, source_target_pairs={{0,2},{1,3},{2,0},{3,1},{4,6},{5,7},{6,4},{7,5},{8,10},{9,11},{10,... | collective-permute-start | bytes 6152 | tf_op jit(solution)/shard_map/ppermute | solution.py:663
  70.8 2.3 %shard_map.116 = f32[8,64,512]{2,1,0:T(8,128)} custom-call(f32[8,72,640]{2,1,0:T(8,128)} %get-tuple-element.73.refs_0_, f32[5,64,512]{2,1,0:T(8,128)} %get-tuple-element.39.refs_1_, f32[8,64,512]{2,1,0:T(8,128)} %get-tuple-element.78.refs_2_, f32[8,512]{1,0:T(8,128)S(1)} %collective-permute-done.12.refs_2_.refs_3_, ...), custom_call_target="tpu_custom_call", output_to_operand_aliasing={{}: (2, {})} | custom-call | tf_op jit(solution)/shard_map/pallas_call | solution.py:634
  (30 shorter events, 4.9 us)
Async XLA Ops:
  3.7 15.6 %all-to-all-start = ((f32[32,2,128]{2,1,0:T(2,128)}), f32[32,2,128]{2,1,0:T(2,128)S(1)}, u32[]{:S(2)}, u32[]{:S(2)}) async-start(f32[32,2,128]{2,1,0:T(2,128)} %bitcast.3), calls=%async_computation | async-start | bytes 65536 | tf_op jit(solution)/shard_map/all_to_all | solution.py:674
  11.0 8.3 %collective-permute-start = (f32[16,512]{1,0:T(8,128)S(1)}, f32[16,512]{1,0:T(8,128)S(1)}, u32[]{:S(2)}, u32[]{:S(2)}) collective-permute-start(f32[16,512]{1,0:T(8,128)S(1)} %get-tuple-element.43), channel_id=1, source_target_pairs={{4,8},{12,16},{20,24},{8,4},{16,12},{24,20},{5,9},{13,17},{21,25},... | collective-permute-start | bytes 98312 | tf_op jit(solution)/shard_map/ppermute | solution.py:654
  11.7 7.6 %collective-permute-start.1 = (f32[16,512]{1,0:T(8,128)S(1)}, f32[16,512]{1,0:T(8,128)S(1)}, u32[]{:S(2)}, u32[]{:S(2)}) collective-permute-start(f32[16,512]{1,0:T(8,128)S(1)} %get-tuple-element.44), channel_id=1, source_target_pairs={{0,4},{8,12},{16,20},{24,28},{4,0},{12,8},{20,16},{28,24},{1,5},{9... | collective-permute-start | bytes 98312 | tf_op jit(solution)/shard_map/ppermute | solution.py:654
  16.2 3.1 %collective-permute-start.2 = (f32[8,128]{1,0:T(8,128)S(1)}, f32[8,128]{1,0:T(8,128)S(1)}, u32[]{:S(2)}, u32[]{:S(2)}) collective-permute-start(f32[8,128]{1,0:T(8,128)S(1)} %get-tuple-element.45), channel_id=1, source_target_pairs={{1,2},{3,0},{2,1},{0,3},{5,6},{7,4},{6,5},{4,7},{9,10},{11,8},{10,... | collective-permute-start | bytes 12296 | tf_op jit(solution)/shard_map/ppermute | solution.py:654
  16.9 2.4 %collective-permute-start.3 = (f32[8,128]{1,0:T(8,128)S(1)}, f32[8,128]{1,0:T(8,128)S(1)}, u32[]{:S(2)}, u32[]{:S(2)}) collective-permute-start(f32[8,128]{1,0:T(8,128)S(1)} %get-tuple-element.46), channel_id=1, source_target_pairs={{0,1},{2,3},{1,0},{3,2},{4,5},{6,7},{5,4},{7,6},{8,9},{10,11},{9,8... | collective-permute-start | bytes 12296 | tf_op jit(solution)/shard_map/ppermute | solution.py:654
  23.5 12.8 %all-to-all-start.1 = ((f32[32,2,128]{2,1,0:T(2,128)}), f32[32,2,128]{2,1,0:T(2,128)S(1)}, u32[]{:S(2)}, u32[]{:S(2)}) async-start(f32[32,2,128]{2,1,0:T(2,128)} %bitcast.5), calls=%async_computation.1 | async-start | bytes 65536 | tf_op jit(solution)/shard_map/all_to_all | solution.py:674
  28.1 8.3 %collective-permute-start.4 = (f32[16,512]{1,0:T(8,128)S(1)}, f32[16,512]{1,0:T(8,128)S(1)}, u32[]{:S(2)}, u32[]{:S(2)}) collective-permute-start(f32[16,512]{1,0:T(8,128)S(1)} %get-tuple-element.55), channel_id=1, source_target_pairs={{4,8},{12,16},{20,24},{8,4},{16,12},{24,20},{5,9},{13,17},{21,25},... | collective-permute-start | bytes 98312 | tf_op jit(solution)/shard_map/ppermute | solution.py:654
  28.7 7.6 %collective-permute-start.5 = (f32[16,512]{1,0:T(8,128)S(1)}, f32[16,512]{1,0:T(8,128)S(1)}, u32[]{:S(2)}, u32[]{:S(2)}) collective-permute-start(f32[16,512]{1,0:T(8,128)S(1)} %get-tuple-element.56), channel_id=1, source_target_pairs={{0,4},{8,12},{16,20},{24,28},{4,0},{12,8},{20,16},{28,24},{1,5},{9... | collective-permute-start | bytes 98312 | tf_op jit(solution)/shard_map/ppermute | solution.py:654
  33.3 3.1 %collective-permute-start.6 = (f32[8,128]{1,0:T(8,128)S(1)}, f32[8,128]{1,0:T(8,128)S(1)}, u32[]{:S(2)}, u32[]{:S(2)}) collective-permute-start(f32[8,128]{1,0:T(8,128)S(1)} %get-tuple-element.57), channel_id=1, source_target_pairs={{1,2},{3,0},{2,1},{0,3},{5,6},{7,4},{6,5},{4,7},{9,10},{11,8},{10,... | collective-permute-start | bytes 12296 | tf_op jit(solution)/shard_map/ppermute | solution.py:654
  33.9 2.4 %collective-permute-start.7 = (f32[8,128]{1,0:T(8,128)S(1)}, f32[8,128]{1,0:T(8,128)S(1)}, u32[]{:S(2)}, u32[]{:S(2)}) collective-permute-start(f32[8,128]{1,0:T(8,128)S(1)} %get-tuple-element.58), channel_id=1, source_target_pairs={{0,1},{2,3},{1,0},{3,2},{4,5},{6,7},{5,4},{7,6},{8,9},{10,11},{9,8... | collective-permute-start | bytes 12296 | tf_op jit(solution)/shard_map/ppermute | solution.py:654
  41.5 12.8 %all-to-all-start.2 = ((f32[32,2,128]{2,1,0:T(2,128)}), f32[32,2,128]{2,1,0:T(2,128)S(1)}, u32[]{:S(2)}, u32[]{:S(2)}) async-start(f32[32,2,128]{2,1,0:T(2,128)} %bitcast.7), calls=%async_computation.2 | async-start | bytes 65536 | tf_op jit(solution)/shard_map/all_to_all | solution.py:674
  46.0 8.3 %collective-permute-start.8 = (f32[16,512]{1,0:T(8,128)S(1)}, f32[16,512]{1,0:T(8,128)S(1)}, u32[]{:S(2)}, u32[]{:S(2)}) collective-permute-start(f32[16,512]{1,0:T(8,128)S(1)} %get-tuple-element.66), channel_id=1, source_target_pairs={{4,8},{12,16},{20,24},{8,4},{16,12},{24,20},{5,9},{13,17},{21,25},... | collective-permute-start | bytes 98312 | tf_op jit(solution)/shard_map/ppermute | solution.py:654
  46.7 7.6 %collective-permute-start.9 = (f32[16,512]{1,0:T(8,128)S(1)}, f32[16,512]{1,0:T(8,128)S(1)}, u32[]{:S(2)}, u32[]{:S(2)}) collective-permute-start(f32[16,512]{1,0:T(8,128)S(1)} %get-tuple-element.67), channel_id=1, source_target_pairs={{0,4},{8,12},{16,20},{24,28},{4,0},{12,8},{20,16},{28,24},{1,5},{9... | collective-permute-start | bytes 98312 | tf_op jit(solution)/shard_map/ppermute | solution.py:654
  51.2 3.1 %collective-permute-start.10 = (f32[8,128]{1,0:T(8,128)S(1)}, f32[8,128]{1,0:T(8,128)S(1)}, u32[]{:S(2)}, u32[]{:S(2)}) collective-permute-start(f32[8,128]{1,0:T(8,128)S(1)} %get-tuple-element.68), channel_id=1, source_target_pairs={{1,2},{3,0},{2,1},{0,3},{5,6},{7,4},{6,5},{4,7},{9,10},{11,8},{10,... | collective-permute-start | bytes 12296 | tf_op jit(solution)/shard_map/ppermute | solution.py:654
  51.9 2.4 %collective-permute-start.11 = (f32[8,128]{1,0:T(8,128)S(1)}, f32[8,128]{1,0:T(8,128)S(1)}, u32[]{:S(2)}, u32[]{:S(2)}) collective-permute-start(f32[8,128]{1,0:T(8,128)S(1)} %get-tuple-element.69), channel_id=1, source_target_pairs={{0,1},{2,3},{1,0},{3,2},{4,5},{6,7},{5,4},{7,6},{8,9},{10,11},{9,8... | collective-permute-start | bytes 12296 | tf_op jit(solution)/shard_map/ppermute | solution.py:654
  58.6 8.0 %collective-permute-start.12 = (f32[8,512]{1,0:T(8,128)S(1)}, f32[8,512]{1,0:T(8,128)S(1)}, u32[]{:S(2)}, u32[]{:S(2)}) collective-permute-start(f32[8,512]{1,0:T(8,128)S(1)} %get-tuple-element.74), channel_id=1, source_target_pairs={{4,8},{12,16},{20,24},{8,4},{16,12},{24,20},{5,9},{13,17},{21,25},... | collective-permute-start | bytes 49160 | tf_op jit(solution)/shard_map/ppermute | solution.py:654
  59.2 7.3 %collective-permute-start.13 = (f32[8,512]{1,0:T(8,128)S(1)}, f32[8,512]{1,0:T(8,128)S(1)}, u32[]{:S(2)}, u32[]{:S(2)}) collective-permute-start(f32[8,512]{1,0:T(8,128)S(1)} %get-tuple-element.75), channel_id=1, source_target_pairs={{0,4},{8,12},{16,20},{24,28},{4,0},{12,8},{20,16},{28,24},{1,5},{9... | collective-permute-start | bytes 49160 | tf_op jit(solution)/shard_map/ppermute | solution.py:654
  63.5 3.1 %collective-permute-start.14 = (f32[8,128]{1,0:T(8,128)S(1)}, f32[8,128]{1,0:T(8,128)S(1)}, u32[]{:S(2)}, u32[]{:S(2)}) collective-permute-start(f32[8,128]{1,0:T(8,128)S(1)} %get-tuple-element.76), channel_id=1, source_target_pairs={{1,2},{3,0},{2,1},{0,3},{5,6},{7,4},{6,5},{4,7},{9,10},{11,8},{10,... | collective-permute-start | bytes 12296 | tf_op jit(solution)/shard_map/ppermute | solution.py:654
  63.6 3.0 %collective-permute-start.15 = (f32[8,128]{1,0:T(8,128)S(1)}, f32[8,128]{1,0:T(8,128)S(1)}, u32[]{:S(2)}, u32[]{:S(2)}) collective-permute-start(f32[8,128]{1,0:T(8,128)S(1)} %get-tuple-element.77), channel_id=1, source_target_pairs={{0,1},{2,3},{1,0},{3,2},{4,5},{6,7},{5,4},{7,6},{8,9},{10,11},{9,8... | collective-permute-start | bytes 12296 | tf_op jit(solution)/shard_map/ppermute | solution.py:654
  68.9 4.2 %collective-permute-start.16 = (f32[8,64]{1,0:T(8,128)S(1)}, f32[8,64]{1,0:T(8,128)S(1)}, u32[]{:S(2)}, u32[]{:S(2)}) collective-permute-start(f32[8,64]{1,0:T(8,128)S(1)} %get-tuple-element.79), channel_id=1, source_target_pairs={{0,1},{1,0},{2,3},{3,2},{4,5},{5,4},{6,7},{7,6},{8,9},{9,8},{10,11... | collective-permute-start | bytes 6152 | tf_op jit(solution)/shard_map/ppermute | solution.py:663
  69.0 4.1 %collective-permute-start.17 = (f32[8,64]{1,0:T(8,128)S(1)}, f32[8,64]{1,0:T(8,128)S(1)}, u32[]{:S(2)}, u32[]{:S(2)}) collective-permute-start(f32[8,64]{1,0:T(8,128)S(1)} %get-tuple-element.79), channel_id=1, source_target_pairs={{0,2},{1,3},{2,0},{3,1},{4,6},{5,7},{6,4},{7,5},{8,10},{9,11},{10,... | collective-permute-start | bytes 6152 | tf_op jit(solution)/shard_map/ppermute | solution.py:663
  70.4 3.0 %collective-permute-start.18 = (f32[8,64]{1,0:T(8,128)S(1)}, f32[8,64]{1,0:T(8,128)S(1)}, u32[]{:S(2)}, u32[]{:S(2)}) collective-permute-start(f32[8,64]{1,0:T(8,128)S(1)} %get-tuple-element.79), channel_id=1, source_target_pairs={{0,3},{1,2},{2,1},{3,0},{4,7},{5,6},{6,5},{7,4},{8,11},{9,10},{10,... | collective-permute-start | bytes 6152 | tf_op jit(solution)/shard_map/ppermute | solution.py:663

commit v11 on v10

--- a/solution.py
+++ b/solution.py
@@ -409,16 +409,16 @@
 
 
 def step_kernel(first, last, *refs):
-    (stress_in, velocity_in, disp_in, thickness_in, pressure_in) = refs[:5]
+    (stress_in, velocity_in, thickness_in, pressure_in) = refs[:4]
     if first:
+        out = refs[13:]
+    else:
+        plate_ext = refs[13]
         out = refs[14:]
-    else:
-        plate_ext = refs[14]
-        out = refs[15:]
-    (incoming, sec_second, sec_first, girth_second, girth_first,
-     column_marks, row_marks, picked, spring) = refs[5:14]
-    stress_out, velocity_out, disp_out = out[:3]
-    out = out[3:]
+    (incoming, girth_second, sec_first, sec_second, girth_first,
+     column_marks, row_marks, picked, spring) = refs[4:13]
+    stress_out, velocity_out = out[:2]
+    out = out[2:]
     if first:
         plate_ext, spring_out = out[:2]
         out = out[2:]
@@ -427,8 +427,7 @@
     if not last:
         picked_out, payload = out[:2]
         out = out[2:]
-    (stress_ext, res_ext, vel_ext, weld, velocity, disp, thickness, pressure,
-     got, sent) = out
+    (stress_ext, res_ext, vel_ext, weld, velocity, thickness, pressure, got, sent) = out
 
     _, rows, cols = velocity.shape
     devices = incoming.shape[0] // 2
@@ -447,7 +446,7 @@
             (stress_in.at[:, part, :], stress_ext.at[:, part, :])
             for part in pieces(rows + PAD_ROWS)
         ]
-    pairs += [(disp_in, disp), (pressure_in, pressure)]
+    pairs += [(pressure_in, pressure)]
     copies = fetch(got, pairs)
     sends = []
 
@@ -506,11 +505,9 @@
             before = velocity[f, part, :] if first else vel_ext[f, part, :cols]
             speed = before + (linear if f < 3 else angular) * joined
             velocity[f, part, :] = speed
-            disp[f, part, :] = disp[f, part, :] + time_step * speed
         if start % 32 == 24:
             done = slice(start - 24, start + 8)
-            for source, target in ((velocity, velocity_out), (disp, disp_out)):
-                send(source.at[:, done, :], target.at[:, done, :])
+            send(velocity.at[:, done, :], velocity_out.at[:, done, :])
 
     ends = (cols - LANES, cols)
     if last:
@@ -527,7 +524,8 @@
         for copy in sends:
             copy.wait()
         return
-    values = pick([disp[f] for f in range(FIELDS)], column_marks[...], row_marks[...])
+    moves = pick([velocity[f] for f in range(FIELDS)], column_marks[...], row_marks[...])
+    values = [picked[f : f + 1, :] + time_step * moves[f] for f in range(FIELDS)]
     picked_out[...] = jnp.concatenate(values + [values[0]] * 3, axis=0)
     near_out = collapse([value[:, :half] for value in values], by_device, by_place)
     far_out = collapse([value[:, half:] for value in values], by_device, by_place)
@@ -564,11 +562,11 @@
 def final_kernel(membrane, *refs):
     (stress_in, velocity_in), refs = refs[:2], refs[2:]
     if membrane:
-        sec_second, sec_first, girth_second, girth_first, plate_ext, height = refs[:6]
+        girth_second, sec_first, sec_second, girth_first, plate_ext, height = refs[:6]
         stress_out, moment = refs[6:8]
         refs = refs[8:]
     else:
-        sec_second, sec_first, girth_second, girth_first, plate_ext = refs[1:6]
+        girth_second, sec_first, sec_second, girth_first, plate_ext = refs[1:6]
         stress_out = refs[6]
         refs = refs[7:]
     stress, made, vel_ext, got, sent = refs
@@ -645,14 +643,20 @@
     )(*operands)
 
 
-def swap(pair, axis, around):
+def swap(value, axis, start, around):
     count = lax.axis_size(axis)
-    out = []
-    for start, value in reversed(list(enumerate(pair))):
-        couples = [(i, (i + 1) % count) for i in range(start, count, 2)]
-        couples = [(i, j) for i, j in couples if j > i or around]
-        out.append(lax.ppermute(value, axis, couples + [(j, i) for i, j in couples]))
-    return out
+    couples = [(i, (i + 1) % count) for i in range(start, count, 2)]
+    couples = [(i, j) for i, j in couples if j > i or around]
+    return lax.ppermute(value, axis, couples + [(j, i) for i, j in couples])
+
+
+def swap_halos(sec_first, sec_second, girth_first, girth_second):
+    return (
+        swap(girth_second, "girth", 1, True),
+        swap(sec_first, "sec", 0, False),
+        swap(sec_second, "sec", 1, False),
+        swap(girth_first, "girth", 0, True),
+    )
 
 
 def sum_over(value, axis):
@@ -697,7 +701,6 @@
         (stress_shape, F32),
         ((FIELDS, rows + PAD_ROWS, cols + LANES), F32),
         ((FIELDS * rows, cols), F32),
-        (block, F32),
         (block, F32),
         ((rows, cols), jnp.int32),
         ((rows, cols), F32),
@@ -723,12 +726,12 @@
         copies=(9,),
     )
     plate = None
+    moved = 0.0
     for step in range(STEPS):
         first, last = step == 0, step == STEPS - 1
         incoming = exchange(payload)
-        ends = swap((sec_first, sec_second), "sec", False)
-        sides = swap((girth_first, girth_second), "girth", True)
-        outs = [(stress_shape, F32), (block, F32), (block, F32)]
+        halos = swap_halos(sec_first, sec_second, girth_first, girth_second)
+        outs = [(stress_shape, F32), (block, F32)]
         if first:
             outs += [(plate_shape, F32), (slot_rows, F32)]
         halo = (8, cols) if last else strip
@@ -740,16 +743,17 @@
             vmem_bytes,
             outs,
             scratch,
-            stress, velocity, displacement, thickness, pressure,
-            incoming, *ends, *sides,
+            stress, velocity, thickness, pressure,
+            incoming, *halos,
             column_marks, row_marks, picked, spring,
             *([] if first else [plate]),
-            far=5,
-            far_out=3,
-            copies=(7, 3 + 2 * (rows // 32)),
+            far=4,
+            far_out=2,
+            copies=(6, 3 + rows // 32),
         )
-        stress, velocity, displacement = results[:3]
-        results = results[3:]
+        stress, velocity = results[:2]
+        results = results[2:]
+        moved = moved + velocity
         if first:
             plate, spring = results[:2]
             results = results[2:]
@@ -757,8 +761,9 @@
         if not last:
             picked, payload = results[4:]
 
-    ends = swap((sec_first, sec_second), "sec", False)
-    sides = swap((girth_first, girth_second), "girth", True)
+    halos = swap_halos(sec_first, sec_second, girth_first, girth_second)
+    moved = displacement + time_step * moved
+    velocity, moved = lax.optimization_barrier((velocity, moved))
     membrane, partial_moment = call(
         functools.partial(final_kernel, True),
         vmem_bytes,
@@ -767,7 +772,7 @@
             ((3, rows, cols), F32), ((3, rows, cols), F32),
             ((2, rows + PAD_ROWS, cols + LANES), F32),
         ],
-        stress, velocity, *ends, *sides, plate, height,
+        stress, velocity, *halos, plate, height,
         far=2,
         far_out=1,
         copies=(4, rows // 16),
@@ -780,14 +785,14 @@
             ((5, rows, cols), F32), ((5, rows, cols), F32),
             ((3, rows + PAD_ROWS, cols + LANES), F32),
         ],
-        stress, velocity, membrane, *ends, *sides, plate,
+        stress, velocity, membrane, *halos, plate,
         far=3,
         far_out=1,
         copies=(4, rows // 16),
         alias={2: 0},
     )
     moment = sum_over(partial_moment, "girth")[0]
-    return (displacement, velocity, stress, moment)
+    return (moved, velocity, stress, moment)
 
 
 def solution(mesh):

time: 74.4 us -> 77.2 us (1.038)
  the two profiles are of different devices: /device:TPU:0 before, /device:TPU:5 now
where the time goes in v11:
time: 77.2 us; the launch traced here: 76.7 us
  starting transfers between devices  42.8 us (55%)
  Pallas kernels  21.1 us (27%)
  waiting for transfers between devices  9.12 us (12%)
  other arithmetic  2.28 us (3%)
  between operations  0.87 us (1%)
    ppermute x16, starting transfers between devices, swap(): return lax.ppermute(value, axis, couples + [(j, i) for i, j in couples])  22.8 us
    pallas_call x6, Pallas kernels, call(): pl.pallas_call(kernel, out_shape=[pltpu.HBM(shape, dtype) if k < far_out...  21.1 us
    all_to_all x3, starting transfers between devices, exchange(): blocks = lax.all_to_all(blocks, ('sec', 'girth'), 0, 0, tiled=True)  16.9 us
    all_to_all x3, waiting for transfers between devices, exchange(): blocks = lax.all_to_all(blocks, ('sec', 'girth'), 0, 0, tiled=True)  5.9 us
    ppermute x16, waiting for transfers between devices, swap(): return lax.ppermute(value, axis, couples + [(j, i) for i, j in couples])  3.21 us
    ppermute x3, starting transfers between devices, sum_over(): lax.ppermute(value, axis, [(i, i ^ step) for i in range(count)])  3.2 us
    add x1, other arithmetic, local(): moved = displacement + time_step * moved  2.22 us
  transfers between devices with their start and end apart: 22, of which 3 were waited for; matrix products, arithmetic and copies ran while one was open for 3% of the time, Pallas kernels for 3%

profile of v11, /device:TPU:5, one launch (start us, length us, event | category | flops | bytes accessed | tf_op | source)
XLA Modules:
  0.0 76.7 jit_solution(18352429232523284650)
XLA Ops:
  0.6 3.0 %shard_map.111 = (f32[64,128]{1,0:T(8,128)}, f32[16,512]{1,0:T(8,128)S(1)}, f32[16,512]{1,0:T(8,128)S(1)}, f32[8,128]{1,0:T(8,128)S(1)}, f32[8,128]{1,0:T(8,128)...) custom-call(f32[5,64,512]{2,1,0:T(8,128)} %disp_in.1, ...), custom_call_target="tpu_custom_call" | custom-call | tf_op jit(solution)/shard_map/pallas_call | solution.py:632
  3.7 6.4 %all-to-all-start = ((f32[32,2,128]{2,1,0:T(2,128)}), f32[32,2,128]{2,1,0:T(2,128)S(1)}, u32[]{:S(2)}, u32[]{:S(2)}) async-start(f32[32,2,128]{2,1,0:T(2,128)} %bitcast.3), calls=%async_computation | async-start | bytes 65536 | tf_op jit(solution)/shard_map/all_to_all | solution.py:678
  10.3 4.2 %collective-permute-start.2 = (f32[16,512]{1,0:T(8,128)S(1)}, f32[16,512]{1,0:T(8,128)S(1)}, u32[]{:S(2)}, u32[]{:S(2)}) collective-permute-start(f32[16,512]{1,0:T(8,128)S(1)} %get-tuple-element.44), channel_id=1, source_target_pairs={{4,8},{12,16},{20,24},{8,4},{16,12},{24,20},{5,9},{13,17},{21,25},... | collective-permute-start | bytes 98312 | tf_op jit(solution)/shard_map/ppermute | solution.py:650
  14.4 2.1 %collective-permute-start = (f32[8,128]{1,0:T(8,128)S(1)}, f32[8,128]{1,0:T(8,128)S(1)}, u32[]{:S(2)}, u32[]{:S(2)}) collective-permute-start(f32[8,128]{1,0:T(8,128)S(1)} %get-tuple-element.42), channel_id=1, source_target_pairs={{1,2},{3,0},{2,1},{0,3},{5,6},{7,4},{6,5},{4,7},{9,10},{11,8},{10,... | collective-permute-start | bytes 12296 | tf_op jit(solution)/shard_map/ppermute | solution.py:650
  16.5 1.6 %collective-permute-done.refs_5_ = f32[8,128]{1,0:T(8,128)S(1)} collective-permute-done((f32[8,128]{1,0:T(8,128)S(1)}, f32[8,128]{1,0:T(8,128)S(1)}, u32[]{:S(2)}, u32[]{:S(2)}) %collective-permute-start) | collective-permute-done | bytes 4128 | tf_op jit(solution)/shard_map/ppermute | solution.py:650
  18.1 4.5 %shard_map.112 = (f32[8,72,640]{2,1,0:T(8,128)}, f32[5,64,512]{2,1,0:T(8,128)}, f32[1,72,640]{2,1,0:T(8,128)S(1)}, f32[8,1024]{1,0:T(8,128)S(1)}, f32[8,128]{1,0...) custom-call(f32[8,64,512]{2,1,0:T(8,128)} %refs_0_.1, ...), custom_call_target="tpu_custom_call" | custom-call | tf_op jit(solution)/shard_map/pallas_call | solution.py:632
  22.6 5.1 %all-to-all-start.1 = ((f32[32,2,128]{2,1,0:T(2,128)}), f32[32,2,128]{2,1,0:T(2,128)S(1)}, u32[]{:S(2)}, u32[]{:S(2)}) async-start(f32[32,2,128]{2,1,0:T(2,128)} %bitcast.5), calls=%async_computation.1 | async-start | bytes 65536 | tf_op jit(solution)/shard_map/all_to_all | solution.py:678
  27.9 4.2 %collective-permute-start.6 = (f32[16,512]{1,0:T(8,128)S(1)}, f32[16,512]{1,0:T(8,128)S(1)}, u32[]{:S(2)}, u32[]{:S(2)}) collective-permute-start(f32[16,512]{1,0:T(8,128)S(1)} %get-tuple-element.55), channel_id=1, source_target_pairs={{4,8},{12,16},{20,24},{8,4},{16,12},{24,20},{5,9},{13,17},{21,25},... | collective-permute-start | bytes 98312 | tf_op jit(solution)/shard_map/ppermute | solution.py:650
  32.1 2.1 %collective-permute-start.4 = (f32[8,128]{1,0:T(8,128)S(1)}, f32[8,128]{1,0:T(8,128)S(1)}, u32[]{:S(2)}, u32[]{:S(2)}) collective-permute-start(f32[8,128]{1,0:T(8,128)S(1)} %get-tuple-element.53), channel_id=1, source_target_pairs={{1,2},{3,0},{2,1},{0,3},{5,6},{7,4},{6,5},{4,7},{9,10},{11,8},{10,... | collective-permute-start | bytes 12296 | tf_op jit(solution)/shard_map/ppermute | solution.py:650
  34.1 1.6 %collective-permute-done.4.refs_5_ = f32[8,128]{1,0:T(8,128)S(1)} collective-permute-done((f32[8,128]{1,0:T(8,128)S(1)}, f32[8,128]{1,0:T(8,128)S(1)}, u32[]{:S(2)}, u32[]{:S(2)}) %collective-permute-start.4) | collective-permute-done | bytes 4128 | tf_op jit(solution)/shard_map/ppermute | solution.py:650
  35.7 4.8 %shard_map.113 = (f32[8,72,640]{2,1,0:T(8,128)}, f32[5,64,512]{2,1,0:T(8,128)}, f32[8,128]{1,0:T(8,128)S(1)}, f32[8,128]{1,0:T(8,128)S(1)}, f32[16,512]{1,0:T(8,...) custom-call(f32[8,72,640]{2,1,0:T(8,128)} %get-tuple-element.50.refs_0_, ...), custom_call_target="tpu_custom_call" | custom-call | tf_op jit(solution)/shard_map/pallas_call | solution.py:632
  40.6 1.9 %collective-permute-start.10 = (f32[16,512]{1,0:T(8,128)S(1)}, f32[16,512]{1,0:T(8,128)S(1)}, u32[]{:S(2)}, u32[]{:S(2)}) collective-permute-start(f32[16,512]{1,0:T(8,128)S(1)} %get-tuple-element.65), channel_id=1, source_target_pairs={{4,8},{12,16},{20,24},{8,4},{16,12},{24,20},{5,9},{13,17},{21,25},... | collective-permute-start | bytes 98312 | tf_op jit(solution)/shard_map/ppermute | solution.py:650
  42.6 2.1 %collective-permute-start.11 = (f32[8,128]{1,0:T(8,128)S(1)}, f32[8,128]{1,0:T(8,128)S(1)}, u32[]{:S(2)}, u32[]{:S(2)}) collective-permute-start(f32[8,128]{1,0:T(8,128)S(1)} %get-tuple-element.66), channel_id=1, source_target_pairs={{0,1},{2,3},{1,0},{3,2},{4,5},{6,7},{5,4},{7,6},{8,9},{10,11},{9,8... | collective-permute-start | bytes 12296 | tf_op jit(solution)/shard_map/ppermute | solution.py:650
  45.8 5.3 %all-to-all-start.2 = ((f32[32,2,128]{2,1,0:T(2,128)}), f32[32,2,128]{2,1,0:T(2,128)S(1)}, u32[]{:S(2)}, u32[]{:S(2)}) async-start(f32[32,2,128]{2,1,0:T(2,128)} %bitcast.7), calls=%async_computation.2 | async-start | bytes 65536 | tf_op jit(solution)/shard_map/all_to_all | solution.py:678
  51.2 5.9 %all-to-all-done.2 = f32[32,2,128]{2,1,0:T(2,128)S(1)} async-done(((f32[32,2,128]{2,1,0:T(2,128)}), f32[32,2,128]{2,1,0:T(2,128)S(1)}, u32[]{:S(2)}, u32[]{:S(2)}) %all-to-all-start.2) | async-done | bytes 32800 | tf_op jit(solution)/shard_map/all_to_all | solution.py:678
  57.1 4.2 %shard_map.114 = (f32[8,72,640]{2,1,0:T(8,128)}, f32[5,64,512]{2,1,0:T(8,128)}, f32[8,128]{1,0:T(8,128)S(1)}, f32[8,128]{1,0:T(8,128)S(1)}, f32[8,512]{1,0:T(8,128)S(1)}, /*index=5*/f32[8,512]{1,0:T(8,128)S(1)}) custom-call(f32[8,72,640]{2,1,0:T(8,128)} %get-tuple-element.60.refs_0_, f32[5,64,512]{2,1,0:T(8,128)} %get-tuple-element.61.refs_1_, ...), custom_call_target="tpu_custom_call" | custom-call | tf_op jit(solution)/shard_map/pallas_call | solution.py:632
  61.4 1.3 %collective-permute-start.13 = (f32[8,512]{1,0:T(8,128)S(1)}, f32[8,512]{1,0:T(8,128)S(1)}, u32[]{:S(2)}, u32[]{:S(2)}) collective-permute-start(f32[8,512]{1,0:T(8,128)S(1)} %get-tuple-element.73), channel_id=1, source_target_pairs={{0,4},{8,12},{16,20},{24,28},{4,0},{12,8},{20,16},{28,24},{1,5},{9... | collective-permute-start | bytes 49160 | tf_op jit(solution)/shard_map/ppermute | solution.py:650
  62.6 2.2 %collective-permute-start.14 = (f32[8,512]{1,0:T(8,128)S(1)}, f32[8,512]{1,0:T(8,128)S(1)}, u32[]{:S(2)}, u32[]{:S(2)}) collective-permute-start(f32[8,512]{1,0:T(8,128)S(1)} %get-tuple-element.74), channel_id=1, source_target_pairs={{4,8},{12,16},{20,24},{8,4},{16,12},{24,20},{5,9},{13,17},{21,25},... | collective-permute-start | bytes 49160 | tf_op jit(solution)/shard_map/ppermute | solution.py:650
  64.8 1.3 %collective-permute-start.12 = (f32[8,128]{1,0:T(8,128)S(1)}, f32[8,128]{1,0:T(8,128)S(1)}, u32[]{:S(2)}, u32[]{:S(2)}) collective-permute-start(f32[8,128]{1,0:T(8,128)S(1)} %get-tuple-element.72), channel_id=1, source_target_pairs={{1,2},{3,0},{2,1},{0,3},{5,6},{7,4},{6,5},{4,7},{9,10},{11,8},{10,... | collective-permute-start | bytes 12296 | tf_op jit(solution)/shard_map/ppermute | solution.py:650
  66.1 2.2 %multiply_add_fusion = f32[5,64,512]{2,1,0:T(8,128)} fusion(f32[5,64,512]{2,1,0:T(8,128)S(1)} %copy-done, f32[5,64,512]{2,1,0:T(8,128)} %get-tuple-element.38.refs_1_, f32[5,64,512]{2,1,0:T(8,128)S(1)} %copy-done.1, f32[5,64,512]{2,1,0:T(8,128)S(1)} %copy-done.2), kind=kLoop, calls=%fused_computation | loop fusion | flops 655360 | bytes 3276800 | tf_op jit(solution)/shard_map/add | solution.py:765
  68.4 2.3 %shard_map.115 = (f32[8,64,512]{2,1,0:T(8,128)}, f32[8,64]{1,0:T(8,128)S(1)}) custom-call(f32[8,72,640]{2,1,0:T(8,128)} %get-tuple-element.71.refs_0_, f32[5,64,512]{2,1,0:T(8,128)} %get-tuple-element.38.refs_1_, f32[8,128]{1,0:T(8,128)S(1)} %collective-permute-done.12.refs_2_.refs_3_, f32[8,512]{1,0:T(8,128)S(1)} %collective-permute-done.13.refs_3_.refs_4_, ...), custom_call_target="tpu_custom_call" | custom-call | tf_op jit(solution)/shard_map/pallas_call | solution.py:632
  70.7 1.5 %collective-permute-start.16 = (f32[8,64]{1,0:T(8,128)S(1)}, f32[8,64]{1,0:T(8,128)S(1)}, u32[]{:S(2)}, u32[]{:S(2)}) collective-permute-start(f32[8,64]{1,0:T(8,128)S(1)} %get-tuple-element.77), channel_id=1, source_target_pairs={{0,1},{1,0},{2,3},{3,2},{4,5},{5,4},{6,7},{7,6},{8,9},{9,8},{10,11... | collective-permute-start | bytes 6152 | tf_op jit(solution)/shard_map/ppermute | solution.py:667
  72.4 1.5 %collective-permute-start.18 = (f32[8,64]{1,0:T(8,128)S(1)}, f32[8,64]{1,0:T(8,128)S(1)}, u32[]{:S(2)}, u32[]{:S(2)}) collective-permute-start(f32[8,64]{1,0:T(8,128)S(1)} %get-tuple-element.77), channel_id=1, source_target_pairs={{0,3},{1,2},{2,1},{3,0},{4,7},{5,6},{6,5},{7,4},{8,11},{9,10},{10,... | collective-permute-start | bytes 6152 | tf_op jit(solution)/shard_map/ppermute | solution.py:667
  73.9 2.3 %shard_map.116 = f32[8,64,512]{2,1,0:T(8,128)} custom-call(f32[8,72,640]{2,1,0:T(8,128)} %get-tuple-element.71.refs_0_, f32[5,64,512]{2,1,0:T(8,128)} %get-tuple-element.38.refs_1_, f32[8,64,512]{2,1,0:T(8,128)} %get-tuple-element.76.refs_2_, f32[8,128]{1,0:T(8,128)S(1)} %collective-permute-done.12.refs_2_.refs_3_, ...), custom_call_target="tpu_custom_call", output_to_operand_aliasing={{}: (2, {})} | custom-call | tf_op jit(solution)/shard_map/pallas_call | solution.py:632
  (37 shorter events, 2.4 us)
Async XLA Ops:
  3.7 14.4 %all-to-all-start = ((f32[32,2,128]{2,1,0:T(2,128)}), f32[32,2,128]{2,1,0:T(2,128)S(1)}, u32[]{:S(2)}, u32[]{:S(2)}) async-start(f32[32,2,128]{2,1,0:T(2,128)} %bitcast.3), calls=%async_computation | async-start | bytes 65536 | tf_op jit(solution)/shard_map/all_to_all | solution.py:678
  10.1 8.0 %collective-permute-start.1 = (f32[16,512]{1,0:T(8,128)S(1)}, f32[16,512]{1,0:T(8,128)S(1)}, u32[]{:S(2)}, u32[]{:S(2)}) collective-permute-start(f32[16,512]{1,0:T(8,128)S(1)} %get-tuple-element.43), channel_id=1, source_target_pairs={{0,4},{8,12},{16,20},{24,28},{4,0},{12,8},{20,16},{28,24},{1,5},{9... | collective-permute-start | bytes 98312 | tf_op jit(solution)/shard_map/ppermute | solution.py:650
  10.3 7.8 %collective-permute-start.2 = (f32[16,512]{1,0:T(8,128)S(1)}, f32[16,512]{1,0:T(8,128)S(1)}, u32[]{:S(2)}, u32[]{:S(2)}) collective-permute-start(f32[16,512]{1,0:T(8,128)S(1)} %get-tuple-element.44), channel_id=1, source_target_pairs={{4,8},{12,16},{20,24},{8,4},{16,12},{24,20},{5,9},{13,17},{21,25},... | collective-permute-start | bytes 98312 | tf_op jit(solution)/shard_map/ppermute | solution.py:650
  14.4 3.6 %collective-permute-start = (f32[8,128]{1,0:T(8,128)S(1)}, f32[8,128]{1,0:T(8,128)S(1)}, u32[]{:S(2)}, u32[]{:S(2)}) collective-permute-start(f32[8,128]{1,0:T(8,128)S(1)} %get-tuple-element.42), channel_id=1, source_target_pairs={{1,2},{3,0},{2,1},{0,3},{5,6},{7,4},{6,5},{4,7},{9,10},{11,8},{10,... | collective-permute-start | bytes 12296 | tf_op jit(solution)/shard_map/ppermute | solution.py:650
  16.5 1.6 %collective-permute-start.3 = (f32[8,128]{1,0:T(8,128)S(1)}, f32[8,128]{1,0:T(8,128)S(1)}, u32[]{:S(2)}, u32[]{:S(2)}) collective-permute-start(f32[8,128]{1,0:T(8,128)S(1)} %get-tuple-element.45), channel_id=1, source_target_pairs={{0,1},{2,3},{1,0},{3,2},{4,5},{6,7},{5,4},{7,6},{8,9},{10,11},{9,8... | collective-permute-start | bytes 12296 | tf_op jit(solution)/shard_map/ppermute | solution.py:650
  22.6 13.2 %all-to-all-start.1 = ((f32[32,2,128]{2,1,0:T(2,128)}), f32[32,2,128]{2,1,0:T(2,128)S(1)}, u32[]{:S(2)}, u32[]{:S(2)}) async-start(f32[32,2,128]{2,1,0:T(2,128)} %bitcast.5), calls=%async_computation.1 | async-start | bytes 65536 | tf_op jit(solution)/shard_map/all_to_all | solution.py:678
  27.7 8.0 %collective-permute-start.5 = (f32[16,512]{1,0:T(8,128)S(1)}, f32[16,512]{1,0:T(8,128)S(1)}, u32[]{:S(2)}, u32[]{:S(2)}) collective-permute-start(f32[16,512]{1,0:T(8,128)S(1)} %get-tuple-element.54), channel_id=1, source_target_pairs={{0,4},{8,12},{16,20},{24,28},{4,0},{12,8},{20,16},{28,24},{1,5},{9... | collective-permute-start | bytes 98312 | tf_op jit(solution)/shard_map/ppermute | solution.py:650
  27.9 7.8 %collective-permute-start.6 = (f32[16,512]{1,0:T(8,128)S(1)}, f32[16,512]{1,0:T(8,128)S(1)}, u32[]{:S(2)}, u32[]{:S(2)}) collective-permute-start(f32[16,512]{1,0:T(8,128)S(1)} %get-tuple-element.55), channel_id=1, source_target_pairs={{4,8},{12,16},{20,24},{8,4},{16,12},{24,20},{5,9},{13,17},{21,25},... | collective-permute-start | bytes 98312 | tf_op jit(solution)/shard_map/ppermute | solution.py:650
  32.1 3.6 %collective-permute-start.4 = (f32[8,128]{1,0:T(8,128)S(1)}, f32[8,128]{1,0:T(8,128)S(1)}, u32[]{:S(2)}, u32[]{:S(2)}) collective-permute-start(f32[8,128]{1,0:T(8,128)S(1)} %get-tuple-element.53), channel_id=1, source_target_pairs={{1,2},{3,0},{2,1},{0,3},{5,6},{7,4},{6,5},{4,7},{9,10},{11,8},{10,... | collective-permute-start | bytes 12296 | tf_op jit(solution)/shard_map/ppermute | solution.py:650
  34.1 1.6 %collective-permute-start.7 = (f32[8,128]{1,0:T(8,128)S(1)}, f32[8,128]{1,0:T(8,128)S(1)}, u32[]{:S(2)}, u32[]{:S(2)}) collective-permute-start(f32[8,128]{1,0:T(8,128)S(1)} %get-tuple-element.56), channel_id=1, source_target_pairs={{0,1},{2,3},{1,0},{3,2},{4,5},{6,7},{5,4},{7,6},{8,9},{10,11},{9,8... | collective-permute-start | bytes 12296 | tf_op jit(solution)/shard_map/ppermute | solution.py:650
  40.6 10.6 %collective-permute-start.10 = (f32[16,512]{1,0:T(8,128)S(1)}, f32[16,512]{1,0:T(8,128)S(1)}, u32[]{:S(2)}, u32[]{:S(2)}) collective-permute-start(f32[16,512]{1,0:T(8,128)S(1)} %get-tuple-element.65), channel_id=1, source_target_pairs={{4,8},{12,16},{20,24},{8,4},{16,12},{24,20},{5,9},{13,17},{21,25},... | collective-permute-start | bytes 98312 | tf_op jit(solution)/shard_map/ppermute | solution.py:650
  42.5 8.7 %collective-permute-start.9 = (f32[16,512]{1,0:T(8,128)S(1)}, f32[16,512]{1,0:T(8,128)S(1)}, u32[]{:S(2)}, u32[]{:S(2)}) collective-permute-start(f32[16,512]{1,0:T(8,128)S(1)} %get-tuple-element.64), channel_id=1, source_target_pairs={{0,4},{8,12},{16,20},{24,28},{4,0},{12,8},{20,16},{28,24},{1,5},{9... | collective-permute-start | bytes 98312 | tf_op jit(solution)/shard_map/ppermute | solution.py:650
  42.6 8.6 %collective-permute-start.11 = (f32[8,128]{1,0:T(8,128)S(1)}, f32[8,128]{1,0:T(8,128)S(1)}, u32[]{:S(2)}, u32[]{:S(2)}) collective-permute-start(f32[8,128]{1,0:T(8,128)S(1)} %get-tuple-element.66), channel_id=1, source_target_pairs={{0,1},{2,3},{1,0},{3,2},{4,5},{6,7},{5,4},{7,6},{8,9},{10,11},{9,8... | collective-permute-start | bytes 12296 | tf_op jit(solution)/shard_map/ppermute | solution.py:650
  44.7 6.5 %collective-permute-start.8 = (f32[8,128]{1,0:T(8,128)S(1)}, f32[8,128]{1,0:T(8,128)S(1)}, u32[]{:S(2)}, u32[]{:S(2)}) collective-permute-start(f32[8,128]{1,0:T(8,128)S(1)} %get-tuple-element.63), channel_id=1, source_target_pairs={{1,2},{3,0},{2,1},{0,3},{5,6},{7,4},{6,5},{4,7},{9,10},{11,8},{10,... | collective-permute-start | bytes 12296 | tf_op jit(solution)/shard_map/ppermute | solution.py:650
  45.8 11.3 %all-to-all-start.2 = ((f32[32,2,128]{2,1,0:T(2,128)}), f32[32,2,128]{2,1,0:T(2,128)S(1)}, u32[]{:S(2)}, u32[]{:S(2)}) async-start(f32[32,2,128]{2,1,0:T(2,128)} %bitcast.7), calls=%async_computation.2 | async-start | bytes 65536 | tf_op jit(solution)/shard_map/all_to_all | solution.py:678
  57.1 9.0 %copy-start.1 = (f32[5,64,512]{2,1,0:T(8,128)S(1)}, f32[5,64,512]{2,1,0:T(8,128)}, u32[]{:S(2)}) copy-start(f32[5,64,512]{2,1,0:T(8,128)} %get-tuple-element.51.refs_1_) | copy-start | bytes 1966084
  57.1 9.0 %copy-start.2 = (f32[5,64,512]{2,1,0:T(8,128)S(1)}, f32[5,64,512]{2,1,0:T(8,128)}, u32[]{:S(2)}) copy-start(f32[5,64,512]{2,1,0:T(8,128)} %get-tuple-element.61.refs_1_) | copy-start | bytes 1966084
  61.4 7.0 %collective-permute-start.13 = (f32[8,512]{1,0:T(8,128)S(1)}, f32[8,512]{1,0:T(8,128)S(1)}, u32[]{:S(2)}, u32[]{:S(2)}) collective-permute-start(f32[8,512]{1,0:T(8,128)S(1)} %get-tuple-element.73), channel_id=1, source_target_pairs={{0,4},{8,12},{16,20},{24,28},{4,0},{12,8},{20,16},{28,24},{1,5},{9... | collective-permute-start | bytes 49160 | tf_op jit(solution)/shard_map/ppermute | solution.py:650
  62.6 5.7 %collective-permute-start.14 = (f32[8,512]{1,0:T(8,128)S(1)}, f32[8,512]{1,0:T(8,128)S(1)}, u32[]{:S(2)}, u32[]{:S(2)}) collective-permute-start(f32[8,512]{1,0:T(8,128)S(1)} %get-tuple-element.74), channel_id=1, source_target_pairs={{4,8},{12,16},{20,24},{8,4},{16,12},{24,20},{5,9},{13,17},{21,25},... | collective-permute-start | bytes 49160 | tf_op jit(solution)/shard_map/ppermute | solution.py:650
  64.8 3.5 %collective-permute-start.12 = (f32[8,128]{1,0:T(8,128)S(1)}, f32[8,128]{1,0:T(8,128)S(1)}, u32[]{:S(2)}, u32[]{:S(2)}) collective-permute-start(f32[8,128]{1,0:T(8,128)S(1)} %get-tuple-element.72), channel_id=1, source_target_pairs={{1,2},{3,0},{2,1},{0,3},{5,6},{7,4},{6,5},{4,7},{9,10},{11,8},{10,... | collective-permute-start | bytes 12296 | tf_op jit(solution)/shard_map/ppermute | solution.py:650
  66.1 2.2 %collective-permute-start.15 = (f32[8,128]{1,0:T(8,128)S(1)}, f32[8,128]{1,0:T(8,128)S(1)}, u32[]{:S(2)}, u32[]{:S(2)}) collective-permute-start(f32[8,128]{1,0:T(8,128)S(1)} %get-tuple-element.75), channel_id=1, source_target_pairs={{0,1},{2,3},{1,0},{3,2},{4,5},{6,7},{5,4},{7,6},{8,9},{10,11},{9,8... | collective-permute-start | bytes 12296 | tf_op jit(solution)/shard_map/ppermute | solution.py:650
  70.7 5.5 %collective-permute-start.16 = (f32[8,64]{1,0:T(8,128)S(1)}, f32[8,64]{1,0:T(8,128)S(1)}, u32[]{:S(2)}, u32[]{:S(2)}) collective-permute-start(f32[8,64]{1,0:T(8,128)S(1)} %get-tuple-element.77), channel_id=1, source_target_pairs={{0,1},{1,0},{2,3},{3,2},{4,5},{5,4},{6,7},{7,6},{8,9},{9,8},{10,11... | collective-permute-start | bytes 6152 | tf_op jit(solution)/shard_map/ppermute | solution.py:667
  72.2 4.0 %collective-permute-start.17 = (f32[8,64]{1,0:T(8,128)S(1)}, f32[8,64]{1,0:T(8,128)S(1)}, u32[]{:S(2)}, u32[]{:S(2)}) collective-permute-start(f32[8,64]{1,0:T(8,128)S(1)} %get-tuple-element.77), channel_id=1, source_target_pairs={{0,2},{1,3},{2,0},{3,1},{4,6},{5,7},{6,4},{7,5},{8,10},{9,11},{10,... | collective-permute-start | bytes 6152 | tf_op jit(solution)/shard_map/ppermute | solution.py:667
  72.4 3.8 %collective-permute-start.18 = (f32[8,64]{1,0:T(8,128)S(1)}, f32[8,64]{1,0:T(8,128)S(1)}, u32[]{:S(2)}, u32[]{:S(2)}) collective-permute-start(f32[8,64]{1,0:T(8,128)S(1)} %get-tuple-element.77), channel_id=1, source_target_pairs={{0,3},{1,2},{2,1},{3,0},{4,7},{5,6},{6,5},{7,4},{8,11},{9,10},{10,... | collective-permute-start | bytes 6152 | tf_op jit(solution)/shard_map/ppermute | solution.py:667
  (1 other events, 9.0 us)

commit v12 on v10

--- a/solution.py
+++ b/solution.py
@@ -427,8 +427,14 @@
     if not last:
         picked_out, payload = out[:2]
         out = out[2:]
-    (stress_ext, res_ext, vel_ext, weld, velocity, disp, thickness, pressure,
-     got, sent) = out
+    res_ext, vel_ext, weld, thickness, pressure = out[:5]
+    out = out[5:]
+    if last:
+        stress_ext, velocity, disp = stress_out, velocity_out, disp_out
+    else:
+        stress_ext, velocity, disp = out[:3]
+        out = out[3:]
+    got, sent = out
 
     _, rows, cols = velocity.shape
     devices = incoming.shape[0] // 2
@@ -452,6 +458,8 @@
     sends = []
 
     def send(source, target):
+        if last:
+            return
         copy = pltpu.make_async_copy(source, target, sent.at[len(sends)])
         copy.start()
         sends.append(copy)
@@ -562,37 +570,42 @@
 
 
 def final_kernel(membrane, *refs):
-    (stress_in, velocity_in), refs = refs[:2], refs[2:]
     if membrane:
-        sec_second, sec_first, girth_second, girth_first, plate_ext, height = refs[:6]
-        stress_out, moment = refs[6:8]
-        refs = refs[8:]
+        stress, velocity = refs[:2]
+        sec_second, sec_first, girth_second, girth_first, plate_ext, height = refs[2:8]
+        stress_out, moment = refs[8:10]
+        refs = refs[10:]
     else:
-        sec_second, sec_first, girth_second, girth_first, plate_ext = refs[1:6]
-        stress_out = refs[6]
-        refs = refs[7:]
-    stress, made, vel_ext, got, sent = refs
-    rows, cols = vel_ext.shape[1] - PAD_ROWS, vel_ext.shape[2] - LANES
+        stress, velocity, disp = refs[1:4]
+        sec_second, sec_first, girth_second, girth_first, plate_ext = refs[4:9]
+        stress_out, velocity_out, disp_out = refs[9:12]
+        refs = refs[12:]
+    made, vel_ext, sent = refs
+    _, rows, cols = velocity.shape
     fields = range(0, 2) if membrane else range(2, FIELDS)
-    kinds = slice(0, 3) if membrane else slice(3, RESULTS)
-    pairs = [(velocity_in.at[fields.start : fields.stop], vel_ext.at[:, 0:rows, 0:cols])]
-    pairs += [(stress_in.at[kinds, part, 0:cols], stress.at[:, part, :]) for part in pieces(rows)]
-    copies = fetch(got, pairs)
+    kinds = range(0, 3) if membrane else range(3, RESULTS)
+    sends = []
+
+    def send(source, target):
+        copy = pltpu.make_async_copy(source, target, sent.at[len(sends)])
+        copy.start()
+        sends.append(copy)
+
+    if not membrane:
+        send(velocity, velocity_out)
+        send(disp, disp_out)
     above, below = in_order("sec", sec_first[...], sec_second[...])
     left, right = in_order("girth", girth_first[...], girth_second[...])
     first, _ = edge_columns(left, right)
     empty = jnp.zeros((PAD_ROWS, LANES), F32)
     for k, f in enumerate(fields):
+        vel_ext[k, :rows, :cols] = velocity[f]
         sides = edge_block([(first, f, LANES - 1), (first, 8 + f, 0)])
         fill_halo(vel_ext, k, above[f : f + 1, :], below[f : f + 1, :], sides, empty)
-    copies[0].wait()
     parts = []
-    sends = []
     for start in range(0, rows, 8):
-        if start in (0, PIECE, 2 * PIECE):
-            copies[1 + start // PIECE].wait()
         part = slice(start, start + 8)
-        chunk = [stress[k, part, :] for k in range(stress.shape[0])]
+        chunk = [stress[k, part, :cols] for k in kinds]
         plate = plate_ext[0, part, :cols]
         current, along_x, along_y = [
             [value[:, :cols] for value in values]
@@ -608,24 +621,31 @@
             made[k, part, :] = value
         if start % 16 == 8:
             done = slice(start - 8, start + 8)
-            copy = pltpu.make_async_copy(
-                made.at[:, done, :], stress_out.at[kinds, done, :], sent.at[len(sends)]
-            )
-            copy.start()
-            sends.append(copy)
+            send(made.at[:, done, :], stress_out.at[kinds.start : kinds.stop, done, :])
     if membrane:
         column = jnp.broadcast_to(jnp.concatenate(parts, axis=0), (rows, LANES))
         if rows < LANES:
             column = jnp.concatenate([column, jnp.zeros((LANES - rows, LANES), F32)], axis=0)
-        moment[...] = column.T[0:8, :rows]
+        moment[...] = column.T[0:1, :rows]
     for copy in sends:
         copy.wait()
 
 
-def call(kernel, vmem_bytes, outs, scratch, *operands, far=0, far_out=0, copies=(1,), alias=None):
+def call(
+    kernel, vmem_bytes, outs, scratch, *operands, far=0, kept=0, far_out=0, kept_out=0,
+    copies=(1,), alias=None,
+):
+    def placed(k, away, here):
+        return pltpu.HBM if k < away else pltpu.VMEM if k < away + here else None
+
     operands = [
-        pltpu.with_memory_space_constraint(value, pltpu.HBM) if k < far else value
+        value if placed(k, far, kept) is None
+        else pltpu.with_memory_space_constraint(value, placed(k, far, kept))
         for k, value in enumerate(operands)
+    ]
+    results = [
+        (placed(k, far_out, kept_out) or jax.ShapeDtypeStruct)(shape, dtype)
+        for k, (shape, dtype) in enumerate(outs)
     ]
     whole = pl.BlockSpec(memory_space=pltpu.VMEM)
     away = pl.BlockSpec(memory_space=pltpu.HBM)
@@ -633,10 +653,7 @@
     scratch += [pltpu.SemaphoreType.DMA((count,)) for count in copies]
     return pl.pallas_call(
         kernel,
-        out_shape=[
-            pltpu.HBM(shape, dtype) if k < far_out else jax.ShapeDtypeStruct(shape, dtype)
-            for k, (shape, dtype) in enumerate(outs)
-        ],
+        out_shape=results,
         in_specs=[away] * far + [whole] * (len(operands) - far),
         out_specs=[away] * far_out + [whole] * (len(outs) - far_out),
         scratch_shapes=scratch,
@@ -694,11 +711,8 @@
     slot_rows = (8, total)
     scratch = [
         (stress_shape, F32),
-        (stress_shape, F32),
         ((FIELDS, rows + PAD_ROWS, cols + LANES), F32),
         ((FIELDS * rows, cols), F32),
-        (block, F32),
-        (block, F32),
         ((rows, cols), jnp.int32),
         ((rows, cols), F32),
     ]
@@ -739,13 +753,14 @@
             functools.partial(step_kernel, first, last),
             vmem_bytes,
             outs,
-            scratch,
+            scratch + ([] if last else outs[:3]),
             stress, velocity, displacement, thickness, pressure,
             incoming, *ends, *sides,
             column_marks, row_marks, picked, spring,
             *([] if first else [plate]),
             far=5,
-            far_out=3,
+            far_out=0 if last else 3,
+            kept_out=3 if last else 0,
             copies=(7, 3 + 2 * (rows // 32)),
         )
         stress, velocity, displacement = results[:3]
@@ -762,29 +777,24 @@
     membrane, partial_moment = call(
         functools.partial(final_kernel, True),
         vmem_bytes,
-        [((RESULTS, rows, cols), F32), ((8, rows), F32)],
-        [
-            ((3, rows, cols), F32), ((3, rows, cols), F32),
-            ((2, rows + PAD_ROWS, cols + LANES), F32),
-        ],
+        [((RESULTS, rows, cols), F32), ((1, rows), F32)],
+        [((3, rows, cols), F32), ((2, rows + PAD_ROWS, cols + LANES), F32)],
         stress, velocity, *ends, *sides, plate, height,
-        far=2,
+        kept=2,
         far_out=1,
-        copies=(4, rows // 16),
-    )
-    (stress,) = call(
+        copies=(rows // 16,),
+    )
+    stress, velocity, displacement = call(
         functools.partial(final_kernel, False),
         vmem_bytes,
-        [((RESULTS, rows, cols), F32)],
-        [
-            ((5, rows, cols), F32), ((5, rows, cols), F32),
-            ((3, rows + PAD_ROWS, cols + LANES), F32),
-        ],
-        stress, velocity, membrane, *ends, *sides, plate,
-        far=3,
-        far_out=1,
-        copies=(4, rows // 16),
-        alias={2: 0},
+        [((RESULTS, rows, cols), F32), (block, F32), (block, F32)],
+        [((5, rows, cols), F32), ((3, rows + PAD_ROWS, cols + LANES), F32)],
+        membrane, stress, velocity, displacement, *ends, *sides, plate,
+        far=1,
+        kept=3,
+        far_out=3,
+        copies=(2 + rows // 16,),
+        alias={0: 0},
     )
     moment = sum_over(partial_moment, "girth")[0]
     return (displacement, velocity, stress, moment)

time: 74.4 us -> 72.4 us (0.973)
  Pallas kernels: 21.2 us -> 18.3 us
  waiting for transfers between devices: 6.28 us -> 7.16 us
    pallas_call x6, Pallas kernels: 21.2 us -> 18.3 us  [call(): pl.pallas_call(kernel, out_shape=results, in_specs=[away] * far + [whole]...]
    ppermute x3, waiting for transfers between devices: 0.33 us -> 1.22 us  [sum_over(): lax.ppermute(value, axis, [(i, i ^ step) for i in range(count)])]
  transfers between devices with their start and end apart: 22 -> 22, of which waited for: 5 -> 6; matrix products, arithmetic and copies ran while one was open for 0% -> 0% of each run, Pallas kernels for 3% -> 2%
where the time goes in v12:
time: 72.4 us; the launch traced here: 72 us
  starting transfers between devices  45.2 us (62%)
  Pallas kernels  18.3 us (25%)
  waiting for transfers between devices  7.16 us (10%)
  between operations  0.8 us (1%)
    ppermute x16, starting transfers between devices, swap(): lax.ppermute(value, axis, couples + [(j, i) for i, j in couples])  26.8 us
    pallas_call x6, Pallas kernels, call(): pl.pallas_call(kernel, out_shape=results, in_specs=[away] * far + [whole]...  18.3 us
    all_to_all x3, starting transfers between devices, exchange(): blocks = lax.all_to_all(blocks, ('sec', 'girth'), 0, 0, tiled=True)  16.4 us
    ppermute x16, waiting for transfers between devices, swap(): lax.ppermute(value, axis, couples + [(j, i) for i, j in couples])  5.94 us
    ppermute x3, starting transfers between devices, sum_over(): lax.ppermute(value, axis, [(i, i ^ step) for i in range(count)])  1.95 us
  transfers between devices with their start and end apart: 22, of which 6 were waited for; matrix products, arithmetic and copies ran while one was open for 0% of the time, Pallas kernels for 2%

profile of v12, /device:TPU:0, one launch (start us, length us, event | category | flops | bytes accessed | tf_op | source)
XLA Modules:
  0.0 72.0 jit_solution(1967690101323381843)
XLA Ops:
  0.6 3.0 %shard_map.111 = (f32[64,128]{1,0:T(8,128)}, f32[16,512]{1,0:T(8,128)S(1)}, f32[16,512]{1,0:T(8,128)S(1)}, f32[8,128]{1,0:T(8,128)S(1)}, f32[8,128]{1,0:T(8,128)...) custom-call(f32[5,64,512]{2,1,0:T(8,128)} %refs_2_.1, ...), custom_call_target="tpu_custom_call" | custom-call | tf_op jit(solution)/shard_map/pallas_call | solution.py:654
  3.7 7.3 %all-to-all-start = ((f32[32,2,128]{2,1,0:T(2,128)}), f32[32,2,128]{2,1,0:T(2,128)S(1)}, u32[]{:S(2)}, u32[]{:S(2)}) async-start(f32[32,2,128]{2,1,0:T(2,128)} %bitcast.3), calls=%async_computation | async-start | bytes 65536 | tf_op jit(solution)/shard_map/all_to_all | solution.py:691
  11.0 0.7 collective-permute-start
  11.7 4.5 %collective-permute-start.1 = (f32[16,512]{1,0:T(8,128)S(1)}, f32[16,512]{1,0:T(8,128)S(1)}, u32[]{:S(2)}, u32[]{:S(2)}) collective-permute-start(f32[16,512]{1,0:T(8,128)S(1)} %get-tuple-element.47), channel_id=1, source_target_pairs={{0,4},{8,12},{16,20},{24,28},{4,0},{12,8},{20,16},{28,24},{1,5},{9... | collective-permute-start | bytes 98312 | tf_op jit(solution)/shard_map/ppermute | solution.py:671
  16.9 0.9 %collective-permute-start.3 = (f32[8,128]{1,0:T(8,128)S(1)}, f32[8,128]{1,0:T(8,128)S(1)}, u32[]{:S(2)}, u32[]{:S(2)}) collective-permute-start(f32[8,128]{1,0:T(8,128)S(1)} %get-tuple-element.49), channel_id=1, source_target_pairs={{0,1},{2,3},{1,0},{3,2},{4,5},{6,7},{5,4},{7,6},{8,9},{10,11},{9,8... | collective-permute-start | bytes 12296 | tf_op jit(solution)/shard_map/ppermute | solution.py:671
  17.8 1.5 %collective-permute-done.2.refs_8_ = f32[8,128]{1,0:T(8,128)S(1)} collective-permute-done((f32[8,128]{1,0:T(8,128)S(1)}, f32[8,128]{1,0:T(8,128)S(1)}, u32[]{:S(2)}, u32[]{:S(2)}) %collective-permute-start.2) | collective-permute-done | bytes 4128 | tf_op jit(solution)/shard_map/ppermute | solution.py:671
  19.3 4.2 %shard_map.112 = (f32[8,72,640]{2,1,0:T(8,128)}, f32[5,64,512]{2,1,0:T(8,128)}, f32[5,64,512]{2,1,0:T(8,128)}, f32[1,72,640]{2,1,0:T(8,128)S(1)}, f32[8,1024]{1,...) custom-call(f32[8,64,512]{2,1,0:T(8,128)} %refs_0_.1, ...), custom_call_target="tpu_custom_call" | custom-call | tf_op jit(solution)/shard_map/pallas_call | solution.py:654
  23.5 4.5 %all-to-all-start.1 = ((f32[32,2,128]{2,1,0:T(2,128)}), f32[32,2,128]{2,1,0:T(2,128)S(1)}, u32[]{:S(2)}, u32[]{:S(2)}) async-start(f32[32,2,128]{2,1,0:T(2,128)} %bitcast.5), calls=%async_computation.1 | async-start | bytes 65536 | tf_op jit(solution)/shard_map/all_to_all | solution.py:691
  28.7 4.5 %collective-permute-start.5 = (f32[16,512]{1,0:T(8,128)S(1)}, f32[16,512]{1,0:T(8,128)S(1)}, u32[]{:S(2)}, u32[]{:S(2)}) collective-permute-start(f32[16,512]{1,0:T(8,128)S(1)} %get-tuple-element.59), channel_id=1, source_target_pairs={{0,4},{8,12},{16,20},{24,28},{4,0},{12,8},{20,16},{28,24},{1,5},{9... | collective-permute-start | bytes 98312 | tf_op jit(solution)/shard_map/ppermute | solution.py:671
  33.9 0.9 %collective-permute-start.7 = (f32[8,128]{1,0:T(8,128)S(1)}, f32[8,128]{1,0:T(8,128)S(1)}, u32[]{:S(2)}, u32[]{:S(2)}) collective-permute-start(f32[8,128]{1,0:T(8,128)S(1)} %get-tuple-element.61), channel_id=1, source_target_pairs={{0,1},{2,3},{1,0},{3,2},{4,5},{6,7},{5,4},{7,6},{8,9},{10,11},{9,8... | collective-permute-start | bytes 12296 | tf_op jit(solution)/shard_map/ppermute | solution.py:671
  34.8 1.5 %collective-permute-done.6.refs_8_ = f32[8,128]{1,0:T(8,128)S(1)} collective-permute-done((f32[8,128]{1,0:T(8,128)S(1)}, f32[8,128]{1,0:T(8,128)S(1)}, u32[]{:S(2)}, u32[]{:S(2)}) %collective-permute-start.6) | collective-permute-done | bytes 4128 | tf_op jit(solution)/shard_map/ppermute | solution.py:671
  36.4 5.1 %shard_map.113 = (f32[8,72,640]{2,1,0:T(8,128)}, f32[5,64,512]{2,1,0:T(8,128)}, f32[5,64,512]{2,1,0:T(8,128)}, f32[8,128]{1,0:T(8,128)S(1)}, f32[8,128]{1,0:T(8,...) custom-call(f32[8,72,640]{2,1,0:T(8,128)} %get-tuple-element.54.refs_0_, ...), custom_call_target="tpu_custom_call" | custom-call | tf_op jit(solution)/shard_map/pallas_call | solution.py:654
  41.5 4.5 %all-to-all-start.2 = ((f32[32,2,128]{2,1,0:T(2,128)}), f32[32,2,128]{2,1,0:T(2,128)S(1)}, u32[]{:S(2)}, u32[]{:S(2)}) async-start(f32[32,2,128]{2,1,0:T(2,128)} %bitcast.7), calls=%async_computation.2 | async-start | bytes 65536 | tf_op jit(solution)/shard_map/all_to_all | solution.py:691
  46.7 4.5 %collective-permute-start.9 = (f32[16,512]{1,0:T(8,128)S(1)}, f32[16,512]{1,0:T(8,128)S(1)}, u32[]{:S(2)}, u32[]{:S(2)}) collective-permute-start(f32[16,512]{1,0:T(8,128)S(1)} %get-tuple-element.70), channel_id=1, source_target_pairs={{0,4},{8,12},{16,20},{24,28},{4,0},{12,8},{20,16},{28,24},{1,5},{9... | collective-permute-start | bytes 98312 | tf_op jit(solution)/shard_map/ppermute | solution.py:671
  51.9 0.9 %collective-permute-start.11 = (f32[8,128]{1,0:T(8,128)S(1)}, f32[8,128]{1,0:T(8,128)S(1)}, u32[]{:S(2)}, u32[]{:S(2)}) collective-permute-start(f32[8,128]{1,0:T(8,128)S(1)} %get-tuple-element.72), channel_id=1, source_target_pairs={{0,1},{2,3},{1,0},{3,2},{4,5},{6,7},{5,4},{7,6},{8,9},{10,11},{9,8... | collective-permute-start | bytes 12296 | tf_op jit(solution)/shard_map/ppermute | solution.py:671
  52.8 1.5 %collective-permute-done.10.refs_8_ = f32[8,128]{1,0:T(8,128)S(1)} collective-permute-done((f32[8,128]{1,0:T(8,128)S(1)}, f32[8,128]{1,0:T(8,128)S(1)}, u32[]{:S(2)}, u32[]{:S(2)}) %collective-permute-start.10) | collective-permute-done | bytes 4128 | tf_op jit(solution)/shard_map/ppermute | solution.py:671
  54.3 3.4 %shard_map.114 = (f32[8,72,640]{2,1,0:T(8,128)S(1)}, f32[5,64,512]{2,1,0:T(8,128)S(1)}, f32[5,64,512]{2,1,0:T(8,128)S(1)}, f32[8,128]{1,0:T(8,128)S(1)}, f32[8,1...) custom-call(f32[8,72,640]{2,1,0:T(8,128)} %get-tuple-element.65.refs_0_, ...), custom_call_target="tpu_custom_call" | custom-call | tf_op jit(solution)/shard_map/pallas_call | solution.py:654
  58.4 4.2 %collective-permute-start.13 = (f32[8,512]{1,0:T(8,128)S(1)}, f32[8,512]{1,0:T(8,128)S(1)}, u32[]{:S(2)}, u32[]{:S(2)}) collective-permute-start(f32[8,512]{1,0:T(8,128)S(1)} %get-tuple-element.77), channel_id=1, source_target_pairs={{0,4},{8,12},{16,20},{24,28},{4,0},{12,8},{20,16},{28,24},{1,5},{9... | collective-permute-start | bytes 49160 | tf_op jit(solution)/shard_map/ppermute | solution.py:671
  62.7 1.5 %collective-permute-start.15 = (f32[8,128]{1,0:T(8,128)S(1)}, f32[8,128]{1,0:T(8,128)S(1)}, u32[]{:S(2)}, u32[]{:S(2)}) collective-permute-start(f32[8,128]{1,0:T(8,128)S(1)} %get-tuple-element.79), channel_id=1, source_target_pairs={{0,1},{2,3},{1,0},{3,2},{4,5},{6,7},{5,4},{7,6},{8,9},{10,11},{9,8... | collective-permute-start | bytes 12296 | tf_op jit(solution)/shard_map/ppermute | solution.py:671
  64.3 1.5 %collective-permute-done.14.refs_4_.refs_6_ = f32[8,128]{1,0:T(8,128)S(1)} collective-permute-done((f32[8,128]{1,0:T(8,128)S(1)}, f32[8,128]{1,0:T(8,128)S(1)}, u32[]{:S(2)}, u32[]{:S(2)}) %collective-permute-start.14) | collective-permute-done | bytes 4128 | tf_op jit(solution)/shard_map/ppermute | solution.py:671
  65.8 1.2 %shard_map.115 = (f32[8,64,512]{2,1,0:T(8,128)}, f32[1,64]{1,0:T(1,128)S(1)}) custom-call(f32[8,72,640]{2,1,0:T(8,128)S(1)} %get-tuple-element.74.refs_0_.refs_1_, f32[5,64,512]{2,1,0:T(8,128)S(1)} %get-tuple-element.75.refs_1_.refs_2_, f32[8,512]{1,0:T(8,128)S(1)} %collective-permute-done.12.refs_2_.refs_4_, ...), custom_call_target="tpu_custom_call" | custom-call | tf_op jit(solution)/shard_map/pallas_call | solution.py:654
  67.1 1.4 %collective-permute-start.17 = (f32[1,64]{1,0:T(1,128)S(1)}, f32[1,64]{1,0:T(1,128)S(1)}, u32[]{:S(2)}, u32[]{:S(2)}) collective-permute-start(f32[1,64]{1,0:T(1,128)S(1)} %get-tuple-element.85), channel_id=1, source_target_pairs={{0,2},{1,3},{2,0},{3,1},{4,6},{5,7},{6,4},{7,5},{8,10},{9,11},{10,... | collective-permute-start | bytes 776 | tf_op jit(solution)/shard_map/ppermute | solution.py:680
  68.9 1.3 %shard_map.116 = (f32[8,64,512]{2,1,0:T(8,128)}, f32[5,64,512]{2,1,0:T(8,128)}, f32[5,64,512]{2,1,0:T(8,128)}) custom-call(f32[8,64,512]{2,1,0:T(8,128)} %get-tuple-element.80.refs_0_, f32[8,72,640]{2,1,0:T(8,128)S(1)} %get-tuple-element.74.refs_0_.refs_1_, f32[5,64,512]{2,1,0:T(8,128)S(1)} %get-tuple-element.75.refs_1_.refs_2_, ...), custom_call_target="tpu_custom_call", output_to_operand_aliasing={{0}: (0, {})} | custom-call | tf_op jit(solution)/shard_map/pallas_call | solution.py:654
  70.7 0.8 %collective-permute-done.18 = f32[1,64]{1,0:T(1,128)S(1)} collective-permute-done((f32[1,64]{1,0:T(1,128)S(1)}, f32[1,64]{1,0:T(1,128)S(1)}, u32[]{:S(2)}, u32[]{:S(2)}) %collective-permute-start.18) | collective-permute-done | bytes 288 | tf_op jit(solution)/shard_map/ppermute | solution.py:680
  (29 shorter events, 5.6 us)
Async XLA Ops:
  3.7 15.6 %all-to-all-start = ((f32[32,2,128]{2,1,0:T(2,128)}), f32[32,2,128]{2,1,0:T(2,128)S(1)}, u32[]{:S(2)}, u32[]{:S(2)}) async-start(f32[32,2,128]{2,1,0:T(2,128)} %bitcast.3), calls=%async_computation | async-start | bytes 65536 | tf_op jit(solution)/shard_map/all_to_all | solution.py:691
  11.0 8.3 %collective-permute-start = (f32[16,512]{1,0:T(8,128)S(1)}, f32[16,512]{1,0:T(8,128)S(1)}, u32[]{:S(2)}, u32[]{:S(2)}) collective-permute-start(f32[16,512]{1,0:T(8,128)S(1)} %get-tuple-element.46), channel_id=1, source_target_pairs={{4,8},{12,16},{20,24},{8,4},{16,12},{24,20},{5,9},{13,17},{21,25},... | collective-permute-start | bytes 98312 | tf_op jit(solution)/shard_map/ppermute | solution.py:671
  11.7 7.6 %collective-permute-start.1 = (f32[16,512]{1,0:T(8,128)S(1)}, f32[16,512]{1,0:T(8,128)S(1)}, u32[]{:S(2)}, u32[]{:S(2)}) collective-permute-start(f32[16,512]{1,0:T(8,128)S(1)} %get-tuple-element.47), channel_id=1, source_target_pairs={{0,4},{8,12},{16,20},{24,28},{4,0},{12,8},{20,16},{28,24},{1,5},{9... | collective-permute-start | bytes 98312 | tf_op jit(solution)/shard_map/ppermute | solution.py:671
  16.2 3.1 %collective-permute-start.2 = (f32[8,128]{1,0:T(8,128)S(1)}, f32[8,128]{1,0:T(8,128)S(1)}, u32[]{:S(2)}, u32[]{:S(2)}) collective-permute-start(f32[8,128]{1,0:T(8,128)S(1)} %get-tuple-element.48), channel_id=1, source_target_pairs={{1,2},{3,0},{2,1},{0,3},{5,6},{7,4},{6,5},{4,7},{9,10},{11,8},{10,... | collective-permute-start | bytes 12296 | tf_op jit(solution)/shard_map/ppermute | solution.py:671
  16.9 2.4 %collective-permute-start.3 = (f32[8,128]{1,0:T(8,128)S(1)}, f32[8,128]{1,0:T(8,128)S(1)}, u32[]{:S(2)}, u32[]{:S(2)}) collective-permute-start(f32[8,128]{1,0:T(8,128)S(1)} %get-tuple-element.49), channel_id=1, source_target_pairs={{0,1},{2,3},{1,0},{3,2},{4,5},{6,7},{5,4},{7,6},{8,9},{10,11},{9,8... | collective-permute-start | bytes 12296 | tf_op jit(solution)/shard_map/ppermute | solution.py:671
  23.5 12.8 %all-to-all-start.1 = ((f32[32,2,128]{2,1,0:T(2,128)}), f32[32,2,128]{2,1,0:T(2,128)S(1)}, u32[]{:S(2)}, u32[]{:S(2)}) async-start(f32[32,2,128]{2,1,0:T(2,128)} %bitcast.5), calls=%async_computation.1 | async-start | bytes 65536 | tf_op jit(solution)/shard_map/all_to_all | solution.py:691
  28.1 8.3 %collective-permute-start.4 = (f32[16,512]{1,0:T(8,128)S(1)}, f32[16,512]{1,0:T(8,128)S(1)}, u32[]{:S(2)}, u32[]{:S(2)}) collective-permute-start(f32[16,512]{1,0:T(8,128)S(1)} %get-tuple-element.58), channel_id=1, source_target_pairs={{4,8},{12,16},{20,24},{8,4},{16,12},{24,20},{5,9},{13,17},{21,25},... | collective-permute-start | bytes 98312 | tf_op jit(solution)/shard_map/ppermute | solution.py:671
  28.7 7.6 %collective-permute-start.5 = (f32[16,512]{1,0:T(8,128)S(1)}, f32[16,512]{1,0:T(8,128)S(1)}, u32[]{:S(2)}, u32[]{:S(2)}) collective-permute-start(f32[16,512]{1,0:T(8,128)S(1)} %get-tuple-element.59), channel_id=1, source_target_pairs={{0,4},{8,12},{16,20},{24,28},{4,0},{12,8},{20,16},{28,24},{1,5},{9... | collective-permute-start | bytes 98312 | tf_op jit(solution)/shard_map/ppermute | solution.py:671
  33.3 3.1 %collective-permute-start.6 = (f32[8,128]{1,0:T(8,128)S(1)}, f32[8,128]{1,0:T(8,128)S(1)}, u32[]{:S(2)}, u32[]{:S(2)}) collective-permute-start(f32[8,128]{1,0:T(8,128)S(1)} %get-tuple-element.60), channel_id=1, source_target_pairs={{1,2},{3,0},{2,1},{0,3},{5,6},{7,4},{6,5},{4,7},{9,10},{11,8},{10,... | collective-permute-start | bytes 12296 | tf_op jit(solution)/shard_map/ppermute | solution.py:671
  33.9 2.4 %collective-permute-start.7 = (f32[8,128]{1,0:T(8,128)S(1)}, f32[8,128]{1,0:T(8,128)S(1)}, u32[]{:S(2)}, u32[]{:S(2)}) collective-permute-start(f32[8,128]{1,0:T(8,128)S(1)} %get-tuple-element.61), channel_id=1, source_target_pairs={{0,1},{2,3},{1,0},{3,2},{4,5},{6,7},{5,4},{7,6},{8,9},{10,11},{9,8... | collective-permute-start | bytes 12296 | tf_op jit(solution)/shard_map/ppermute | solution.py:671
  41.5 12.8 %all-to-all-start.2 = ((f32[32,2,128]{2,1,0:T(2,128)}), f32[32,2,128]{2,1,0:T(2,128)S(1)}, u32[]{:S(2)}, u32[]{:S(2)}) async-start(f32[32,2,128]{2,1,0:T(2,128)} %bitcast.7), calls=%async_computation.2 | async-start | bytes 65536 | tf_op jit(solution)/shard_map/all_to_all | solution.py:691
  46.0 8.3 %collective-permute-start.8 = (f32[16,512]{1,0:T(8,128)S(1)}, f32[16,512]{1,0:T(8,128)S(1)}, u32[]{:S(2)}, u32[]{:S(2)}) collective-permute-start(f32[16,512]{1,0:T(8,128)S(1)} %get-tuple-element.69), channel_id=1, source_target_pairs={{4,8},{12,16},{20,24},{8,4},{16,12},{24,20},{5,9},{13,17},{21,25},... | collective-permute-start | bytes 98312 | tf_op jit(solution)/shard_map/ppermute | solution.py:671
  46.7 7.6 %collective-permute-start.9 = (f32[16,512]{1,0:T(8,128)S(1)}, f32[16,512]{1,0:T(8,128)S(1)}, u32[]{:S(2)}, u32[]{:S(2)}) collective-permute-start(f32[16,512]{1,0:T(8,128)S(1)} %get-tuple-element.70), channel_id=1, source_target_pairs={{0,4},{8,12},{16,20},{24,28},{4,0},{12,8},{20,16},{28,24},{1,5},{9... | collective-permute-start | bytes 98312 | tf_op jit(solution)/shard_map/ppermute | solution.py:671
  51.2 3.1 %collective-permute-start.10 = (f32[8,128]{1,0:T(8,128)S(1)}, f32[8,128]{1,0:T(8,128)S(1)}, u32[]{:S(2)}, u32[]{:S(2)}) collective-permute-start(f32[8,128]{1,0:T(8,128)S(1)} %get-tuple-element.71), channel_id=1, source_target_pairs={{1,2},{3,0},{2,1},{0,3},{5,6},{7,4},{6,5},{4,7},{9,10},{11,8},{10,... | collective-permute-start | bytes 12296 | tf_op jit(solution)/shard_map/ppermute | solution.py:671
  51.9 2.4 %collective-permute-start.11 = (f32[8,128]{1,0:T(8,128)S(1)}, f32[8,128]{1,0:T(8,128)S(1)}, u32[]{:S(2)}, u32[]{:S(2)}) collective-permute-start(f32[8,128]{1,0:T(8,128)S(1)} %get-tuple-element.72), channel_id=1, source_target_pairs={{0,1},{2,3},{1,0},{3,2},{4,5},{6,7},{5,4},{7,6},{8,9},{10,11},{9,8... | collective-permute-start | bytes 12296 | tf_op jit(solution)/shard_map/ppermute | solution.py:671
  57.8 8.0 %collective-permute-start.12 = (f32[8,512]{1,0:T(8,128)S(1)}, f32[8,512]{1,0:T(8,128)S(1)}, u32[]{:S(2)}, u32[]{:S(2)}) collective-permute-start(f32[8,512]{1,0:T(8,128)S(1)} %get-tuple-element.76), channel_id=1, source_target_pairs={{4,8},{12,16},{20,24},{8,4},{16,12},{24,20},{5,9},{13,17},{21,25},... | collective-permute-start | bytes 49160 | tf_op jit(solution)/shard_map/ppermute | solution.py:671
  58.4 7.3 %collective-permute-start.13 = (f32[8,512]{1,0:T(8,128)S(1)}, f32[8,512]{1,0:T(8,128)S(1)}, u32[]{:S(2)}, u32[]{:S(2)}) collective-permute-start(f32[8,512]{1,0:T(8,128)S(1)} %get-tuple-element.77), channel_id=1, source_target_pairs={{0,4},{8,12},{16,20},{24,28},{4,0},{12,8},{20,16},{28,24},{1,5},{9... | collective-permute-start | bytes 49160 | tf_op jit(solution)/shard_map/ppermute | solution.py:671
  62.7 3.1 %collective-permute-start.14 = (f32[8,128]{1,0:T(8,128)S(1)}, f32[8,128]{1,0:T(8,128)S(1)}, u32[]{:S(2)}, u32[]{:S(2)}) collective-permute-start(f32[8,128]{1,0:T(8,128)S(1)} %get-tuple-element.78), channel_id=1, source_target_pairs={{1,2},{3,0},{2,1},{0,3},{5,6},{7,4},{6,5},{4,7},{9,10},{11,8},{10,... | collective-permute-start | bytes 12296 | tf_op jit(solution)/shard_map/ppermute | solution.py:671
  62.7 3.0 %collective-permute-start.15 = (f32[8,128]{1,0:T(8,128)S(1)}, f32[8,128]{1,0:T(8,128)S(1)}, u32[]{:S(2)}, u32[]{:S(2)}) collective-permute-start(f32[8,128]{1,0:T(8,128)S(1)} %get-tuple-element.79), channel_id=1, source_target_pairs={{0,1},{2,3},{1,0},{3,2},{4,5},{6,7},{5,4},{7,6},{8,9},{10,11},{9,8... | collective-permute-start | bytes 12296 | tf_op jit(solution)/shard_map/ppermute | solution.py:671
  67.0 3.3 %collective-permute-start.16 = (f32[1,64]{1,0:T(1,128)S(1)}, f32[1,64]{1,0:T(1,128)S(1)}, u32[]{:S(2)}, u32[]{:S(2)}) collective-permute-start(f32[1,64]{1,0:T(1,128)S(1)} %get-tuple-element.85), channel_id=1, source_target_pairs={{0,1},{1,0},{2,3},{3,2},{4,5},{5,4},{6,7},{7,6},{8,9},{9,8},{10,11... | collective-permute-start | bytes 776 | tf_op jit(solution)/shard_map/ppermute | solution.py:680
  67.1 3.5 %collective-permute-start.17 = (f32[1,64]{1,0:T(1,128)S(1)}, f32[1,64]{1,0:T(1,128)S(1)}, u32[]{:S(2)}, u32[]{:S(2)}) collective-permute-start(f32[1,64]{1,0:T(1,128)S(1)} %get-tuple-element.85), channel_id=1, source_target_pairs={{0,2},{1,3},{2,0},{3,1},{4,6},{5,7},{6,4},{7,5},{8,10},{9,11},{10,... | collective-permute-start | bytes 776 | tf_op jit(solution)/shard_map/ppermute | solution.py:680
  68.5 3.0 %collective-permute-start.18 = (f32[1,64]{1,0:T(1,128)S(1)}, f32[1,64]{1,0:T(1,128)S(1)}, u32[]{:S(2)}, u32[]{:S(2)}) collective-permute-start(f32[1,64]{1,0:T(1,128)S(1)} %get-tuple-element.85), channel_id=1, source_target_pairs={{0,3},{1,2},{2,1},{3,0},{4,7},{5,6},{6,5},{7,4},{8,11},{9,10},{10,... | collective-permute-start | bytes 776 | tf_op jit(solution)/shard_map/ppermute | solution.py:680

commit v13 on v12

--- a/solution.py
+++ b/solution.py
@@ -371,7 +371,7 @@
     ref[f, rows:, cols:] = corner
 
 
-def load_velocity(vel_ext, incoming, above, below, left, right):
+def load_velocity(vel_ext, velocity, incoming, above, below, left, right):
     first, second = edge_columns(left, right)
     row = lax.broadcasted_iota(jnp.int32, (8, LANES), 0)
     corner_tiles = [
@@ -379,6 +379,7 @@
         for device, inside in corner_neighbours()
     ]
     for f in range(FIELDS):
+        vel_ext[f, : velocity.shape[1], : velocity.shape[2]] = velocity[f]
         sides = edge_block(
             [
                 (first, 2 + f, LANES - 2),
@@ -408,68 +409,23 @@
         fill_halo(ref, k, above[f : f + 1, :], below[f : f + 1, :], sides, empty)
 
 
-def step_kernel(first, last, *refs):
-    (stress_in, velocity_in, disp_in, thickness_in, pressure_in) = refs[:5]
-    if first:
-        out = refs[14:]
-    else:
-        plate_ext = refs[14]
-        out = refs[15:]
-    (incoming, sec_second, sec_first, girth_second, girth_first,
-     column_marks, row_marks, picked, spring) = refs[5:14]
-    stress_out, velocity_out, disp_out = out[:3]
-    out = out[3:]
-    if first:
-        plate_ext, spring_out = out[:2]
-        out = out[2:]
-    girth_pair, sec_pair = out[0:2], out[2:4]
-    out = out[4:]
-    if not last:
-        picked_out, payload = out[:2]
-        out = out[2:]
-    res_ext, vel_ext, weld, thickness, pressure = out[:5]
-    out = out[5:]
-    if last:
-        stress_ext, velocity, disp = stress_out, velocity_out, disp_out
-    else:
-        stress_ext, velocity, disp = out[:3]
-        out = out[3:]
-    got, sent = out
-
-    _, rows, cols = velocity.shape
+def joint_kernel(first, *refs):
+    far = refs[: 4 + first]
+    incoming, column_marks, row_marks, picked, spring = refs[4 + first : 9 + first]
+    refs = refs[9 + first :]
+    near = refs[: 4 + first]
+    weld = refs[4 + first]
+    copies = fetch(refs[-1], list(zip(far, near)))
     devices = incoming.shape[0] // 2
     total = picked.shape[1]
-    half = total // 2
-    by_device, by_place = slot_marks(devices, half // devices)
-    if first:
-        pairs = [(thickness_in, thickness)]
-        pairs += [
-            (stress_in.at[:, part, :], stress_ext.at[:, part, 0:cols]) for part in pieces(rows)
-        ]
-        pairs += [(velocity_in, velocity)]
-    else:
-        pairs = [(velocity_in, vel_ext.at[:, 0:rows, 0:cols])]
-        pairs += [
-            (stress_in.at[:, part, :], stress_ext.at[:, part, :])
-            for part in pieces(rows + PAD_ROWS)
-        ]
-    pairs += [(disp_in, disp), (pressure_in, pressure)]
-    copies = fetch(got, pairs)
-    sends = []
-
-    def send(source, target):
-        if last:
-            return
-        copy = pltpu.make_async_copy(source, target, sent.at[len(sends)])
-        copy.start()
-        sends.append(copy)
-
+    by_device, by_place = slot_marks(devices, total // 2 // devices)
     other = []
     for row in (1, 0):
         high, low = split(incoming[pl.ds(row, devices, stride=2), :])
         other.append(expand(high, by_device, by_place) + expand(low, by_device, by_place))
     if first:
         stiffness = jnp.concatenate([spring[0:1, :], other[1][5:6]], axis=1)
+        spring_out = refs[5 + first]
         spring_out[...] = jnp.broadcast_to(stiffness, spring_out.shape)
     else:
         stiffness = spring[0:1, :]
@@ -477,19 +433,63 @@
     scale = jnp.where(field < 3, 1.0, rotary_share) * stiffness
     pulls = scale * (jnp.concatenate(other, axis=1) - picked[...])
     weld[...] = spread(pulls, column_marks[...], row_marks[...])
+    for copy in copies:
+        copy.wait()
+
+
+def step_kernel(first, last, *refs):
+    stress_in, velocity_in, disp_in, pressure = refs[:4]
+    if first:
+        thickness, refs = refs[4], refs[5:]
+    else:
+        refs = refs[4:]
+    (weld, incoming, sec_second, sec_first, girth_second, girth_first,
+     column_marks, row_marks, picked) = refs[:9]
+    out = refs[9:]
+    if not first:
+        plate_ext, out = out[0], out[1:]
+    stress_out, velocity_out, disp_out = out[:3]
+    out = out[3:]
+    if first:
+        plate_ext, out = out[0], out[1:]
+    girth_pair, sec_pair = out[0:2], out[2:4]
+    out = out[4:]
+    if not last:
+        picked_out, payload = out[:2]
+        out = out[2:]
+    res_ext, vel_ext = out[:2]
+    if last:
+        stress_ext, velocity, disp = stress_out, velocity_out, disp_out
+    else:
+        stress_ext, velocity, disp = out[2:5]
+    sent = out[-1]
+
+    _, rows, cols = velocity.shape
+    devices = incoming.shape[0] // 2
+    total = picked.shape[1]
+    half = total // 2
+    by_device, by_place = slot_marks(devices, half // devices)
+    sends = []
+
+    def send(source, target):
+        if last:
+            return
+        copy = pltpu.make_async_copy(source, target, sent.at[len(sends)])
+        copy.start()
+        sends.append(copy)
 
     above, below = in_order("sec", sec_first[...], sec_second[...])
     left, right = in_order("girth", girth_first[...], girth_second[...])
-    copies[0].wait()
     if first:
+        for k in range(RESULTS):
+            stress_ext[k, :rows, :cols] = stress_in[k]
         load_stress(stress_ext, plate_ext, thickness, above, below, left, right)
     else:
-        load_velocity(vel_ext, incoming, above, below, left, right)
+        load_velocity(vel_ext, velocity_in, incoming, above, below, left, right)
     for start in range(0, rows + PAD_ROWS, 8):
-        if start in (0, PIECE, 2 * PIECE):
-            copies[1 + start // PIECE].wait()
         plate = plate_ext[0, start : start + 8, :]
-        chunk = [stress_ext[k, start : start + 8, :] for k in range(RESULTS)]
+        source = stress_ext if first else stress_in
+        chunk = [source[k, start : start + 8, :] for k in range(RESULTS)]
         if not first:
             chunk = stress_chunk(vel_ext, chunk, plate, start)
             for k, value in enumerate(chunk):
@@ -499,8 +499,6 @@
         for part in pieces(rows + PAD_ROWS):
             if part.stop == start + 8:
                 send(stress_ext.at[:, part, :], stress_out.at[:, part, :])
-    for copy in copies[4:]:
-        copy.wait()
 
     for start in range(0, rows, 8):
         part = slice(start, start + 8)
@@ -511,10 +509,9 @@
         force[2] = force[2] + pressure[part, :]
         for f in range(FIELDS):
             joined = force[f] + weld[f * rows + start : f * rows + start + 8, :]
-            before = velocity[f, part, :] if first else vel_ext[f, part, :cols]
-            speed = before + (linear if f < 3 else angular) * joined
+            speed = velocity_in[f, part, :] + (linear if f < 3 else angular) * joined
             velocity[f, part, :] = speed
-            disp[f, part, :] = disp[f, part, :] + time_step * speed
+            disp[f, part, :] = disp_in[f, part, :] + time_step * speed
         if start % 32 == 24:
             done = slice(start - 24, start + 8)
             for source, target in ((velocity, velocity_out), (disp, disp_out)):
@@ -709,13 +706,7 @@
     stress_shape = (RESULTS, rows + PAD_ROWS, cols + LANES)
     plate_shape = (1, rows + PAD_ROWS, cols + LANES)
     slot_rows = (8, total)
-    scratch = [
-        (stress_shape, F32),
-        ((FIELDS, rows + PAD_ROWS, cols + LANES), F32),
-        ((FIELDS * rows, cols), F32),
-        ((rows, cols), jnp.int32),
-        ((rows, cols), F32),
-    ]
+    scratch = [(stress_shape, F32), ((FIELDS, rows + PAD_ROWS, cols + LANES), F32)]
 
     (payload, sec_first, sec_second, girth_first, girth_second,
      column_marks, row_marks, picked, spring) = call(
@@ -742,10 +733,23 @@
         incoming = exchange(payload)
         ends = swap((sec_first, sec_second), "sec", False)
         sides = swap((girth_first, girth_second), "girth", True)
-        outs = [(stress_shape, F32), (block, F32), (block, F32)]
+        state = [stress, velocity, displacement, pressure] + [thickness] * first
+        *state, weld = call(
+            functools.partial(joint_kernel, first),
+            vmem_bytes,
+            [(value.shape, value.dtype) for value in state]
+            + [((FIELDS * rows, cols), F32)]
+            + [(slot_rows, F32)] * first,
+            [],
+            *state, incoming, column_marks, row_marks, picked, spring,
+            far=len(state),
+            kept_out=len(state) + 1,
+            copies=(len(state),),
+        )
         if first:
-            outs += [(plate_shape, F32), (slot_rows, F32)]
+            spring, weld, state = weld, state[-1], state[:-1]
         halo = (8, cols) if last else strip
+        outs = [(stress_shape, F32), (block, F32), (block, F32)] + [(plate_shape, F32)] * first
         outs += [(edge, F32), (edge, F32), (halo, F32), (halo, F32)]
         if not last:
             outs += [(slot_rows, F32), (message, F32)]
@@ -754,20 +758,17 @@
             vmem_bytes,
             outs,
             scratch + ([] if last else outs[:3]),
-            stress, velocity, displacement, thickness, pressure,
-            incoming, *ends, *sides,
-            column_marks, row_marks, picked, spring,
+            *state, weld, incoming, *ends, *sides, column_marks, row_marks, picked,
             *([] if first else [plate]),
-            far=5,
+            kept=len(state) + 1,
             far_out=0 if last else 3,
             kept_out=3 if last else 0,
-            copies=(7, 3 + 2 * (rows // 32)),
+            copies=(3 + 2 * (rows // 32),),
         )
         stress, velocity, displacement = results[:3]
         results = results[3:]
         if first:
-            plate, spring = results[:2]
-            results = results[2:]
+            plate, results = results[0], results[1:]
         girth_first, girth_second, sec_first, sec_second = results[:4]
         if not last:
             picked, payload = results[4:]

time: 72.4 us -> 68.4 us (0.945)
  waiting for transfers between devices: 7.16 us -> 4.1 us
  starting transfers between devices: 45.2 us -> 42.6 us
  Pallas kernels: 18.3 us -> 19.8 us
    ppermute x16, waiting for transfers between devices: 5.94 us -> 1.87 us  [swap(): lax.ppermute(value, axis, couples + [(j, i) for i, j in couples])]
    all_to_all x3, starting transfers between devices: 16.4 us -> 14.7 us  [exchange(): blocks = lax.all_to_all(blocks, ('sec', 'girth'), 0, 0, tiled=True)]
    pallas_call x6 -> x9, Pallas kernels: 18.3 us -> 19.8 us  [call(): pl.pallas_call(kernel, out_shape=results, in_specs=[away] * far + [whole]...]
    all_to_all x3, waiting for transfers between devices: 0.01 us -> 1.36 us  [exchange(): blocks = lax.all_to_all(blocks, ('sec', 'girth'), 0, 0, tiled=True)]
    ppermute x16, starting transfers between devices: 26.8 us -> 26 us  [swap(): lax.ppermute(value, axis, couples + [(j, i) for i, j in couples])]
  transfers between devices with their start and end apart: 22 -> 22, of which waited for: 6 -> 6; matrix products, arithmetic and copies ran while one was open for 0% -> 0% of each run, Pallas kernels for 2% -> 10%
where the time goes in v13:
time: 68.4 us; the launch traced here: 68 us
  starting transfers between devices  42.6 us (62%)
  Pallas kernels  19.8 us (29%)
  waiting for transfers between devices  4.1 us (6%)
  between operations  0.89 us (1%)
    ppermute x16, starting transfers between devices, swap(): lax.ppermute(value, axis, couples + [(j, i) for i, j in couples])  26 us
    pallas_call x9, Pallas kernels, call(): pl.pallas_call(kernel, out_shape=results, in_specs=[away] * far + [whole]...  19.8 us
    all_to_all x3, starting transfers between devices, exchange(): blocks = lax.all_to_all(blocks, ('sec', 'girth'), 0, 0, tiled=True)  14.7 us
    ppermute x3, starting transfers between devices, sum_over(): lax.ppermute(value, axis, [(i, i ^ step) for i in range(count)])  1.93 us
    ppermute x16, waiting for transfers between devices, swap(): lax.ppermute(value, axis, couples + [(j, i) for i, j in couples])  1.87 us
  transfers between devices with their start and end apart: 22, of which 6 were waited for; matrix products, arithmetic and copies ran while one was open for 0% of the time, Pallas kernels for 10%

profile of v13, /device:TPU:0, one launch (start us, length us, event | category | flops | bytes accessed | tf_op | source)
XLA Modules:
  0.0 68.0 jit_solution(17171220332259163045)
XLA Ops:
  0.6 3.0 %shard_map.111 = (f32[64,128]{1,0:T(8,128)}, f32[16,512]{1,0:T(8,128)S(1)}, f32[16,512]{1,0:T(8,128)S(1)}, f32[8,128]{1,0:T(8,128)S(1)}, f32[8,128]{1,0:T(8,128)...) custom-call(f32[5,64,512]{2,1,0:T(8,128)} %refs_2_.1, ...), custom_call_target="tpu_custom_call" | custom-call | tf_op jit(solution)/shard_map/pallas_call | solution.py:651
  3.7 7.3 %all-to-all-start = ((f32[32,2,128]{2,1,0:T(2,128)}), f32[32,2,128]{2,1,0:T(2,128)S(1)}, u32[]{:S(2)}, u32[]{:S(2)}) async-start(f32[32,2,128]{2,1,0:T(2,128)} %bitcast.3), calls=%async_computation | async-start | bytes 65536 | tf_op jit(solution)/shard_map/all_to_all | solution.py:688
  11.0 0.7 collective-permute-start
  11.7 4.5 %collective-permute-start.1 = (f32[16,512]{1,0:T(8,128)S(1)}, f32[16,512]{1,0:T(8,128)S(1)}, u32[]{:S(2)}, u32[]{:S(2)}) collective-permute-start(f32[16,512]{1,0:T(8,128)S(1)} %get-tuple-element.73), channel_id=1, source_target_pairs={{0,4},{8,12},{16,20},{24,28},{4,0},{12,8},{20,16},{28,24},{1,5},{9... | collective-permute-start | bytes 98312 | tf_op jit(solution)/shard_map/ppermute | solution.py:668
  16.9 0.9 %collective-permute-start.3 = (f32[8,128]{1,0:T(8,128)S(1)}, f32[8,128]{1,0:T(8,128)S(1)}, u32[]{:S(2)}, u32[]{:S(2)}) collective-permute-start(f32[8,128]{1,0:T(8,128)S(1)} %get-tuple-element.75), channel_id=1, source_target_pairs={{0,1},{2,3},{1,0},{3,2},{4,5},{6,7},{5,4},{7,6},{8,9},{10,11},{9,8... | collective-permute-start | bytes 12296 | tf_op jit(solution)/shard_map/ppermute | solution.py:668
  18.2 1.8 %shard_map.112 = (f32[8,64,512]{2,1,0:T(8,128)S(1)}, f32[5,64,512]{2,1,0:T(8,128)S(1)}, f32[5,64,512]{2,1,0:T(8,128)S(1)}, f32[64,512]{1,0:T(8,128)S(1)}, s32[64...) custom-call(f32[8,64,512]{2,1,0:T(8,128)} %refs_0_.1, f32[5,64,512]{2,1,0:T(8,128)} %refs_1_.1, ...), custom_call_target="tpu_custom_call" | custom-call | tf_op jit(solution)/shard_map/pallas_call | solution.py:651
  20.1 3.0 %shard_map.113 = (f32[8,72,640]{2,1,0:T(8,128)}, f32[5,64,512]{2,1,0:T(8,128)}, f32[5,64,512]{2,1,0:T(8,128)}, f32[1,72,640]{2,1,0:T(8,128)S(1)}, f32[8,128]{1,0...) custom-call(f32[8,64,512]{2,1,0:T(8,128)S(1)} %get-tuple-element.66., ...), custom_call_target="tpu_custom_call" | custom-call | tf_op jit(solution)/shard_map/pallas_call | solution.py:651
  23.1 3.7 %all-to-all-start.1 = ((f32[32,2,128]{2,1,0:T(2,128)}), f32[32,2,128]{2,1,0:T(2,128)S(1)}, u32[]{:S(2)}, u32[]{:S(2)}) async-start(f32[32,2,128]{2,1,0:T(2,128)} %bitcast.5), calls=%async_computation.1 | async-start | bytes 65536 | tf_op jit(solution)/shard_map/all_to_all | solution.py:688
  27.5 4.5 %collective-permute-start.5 = (f32[16,512]{1,0:T(8,128)S(1)}, f32[16,512]{1,0:T(8,128)S(1)}, u32[]{:S(2)}, u32[]{:S(2)}) collective-permute-start(f32[16,512]{1,0:T(8,128)S(1)} %get-tuple-element.88), channel_id=1, source_target_pairs={{0,4},{8,12},{16,20},{24,28},{4,0},{12,8},{20,16},{28,24},{1,5},{9... | collective-permute-start | bytes 98312 | tf_op jit(solution)/shard_map/ppermute | solution.py:668
  32.7 0.9 %collective-permute-start.7 = (f32[8,128]{1,0:T(8,128)S(1)}, f32[8,128]{1,0:T(8,128)S(1)}, u32[]{:S(2)}, u32[]{:S(2)}) collective-permute-start(f32[8,128]{1,0:T(8,128)S(1)} %get-tuple-element.90), channel_id=1, source_target_pairs={{0,1},{2,3},{1,0},{3,2},{4,5},{6,7},{5,4},{7,6},{8,9},{10,11},{9,8... | collective-permute-start | bytes 12296 | tf_op jit(solution)/shard_map/ppermute | solution.py:668
  34.1 1.8 %shard_map.114 = (f32[8,72,640]{2,1,0:T(8,128)S(1)}, f32[5,64,512]{2,1,0:T(8,128)S(1)}, f32[5,64,512]{2,1,0:T(8,128)S(1)}, f32[64,512]{1,0:T(8,128)S(1)}, f32[320,512]{1,0:T(8,128)S(1)}) custom-call(f32[8,72,640]{2,1,0:T(8,128)} %get-tuple-element.76.refs_0_, f32[5,64,512]{2,1,0:T(8,128)} %get-tuple-element.77.refs_1_, ...), custom_call_target="tpu_custom_call" | custom-call | tf_op jit(solution)/shard_map/pallas_call | solution.py:651
  36.0 3.7 %shard_map.115 = (f32[8,72,640]{2,1,0:T(8,128)}, f32[5,64,512]{2,1,0:T(8,128)}, f32[5,64,512]{2,1,0:T(8,128)}, f32[8,128]{1,0:T(8,128)S(1)}, f32[8,128]{1,0:T(8,...) custom-call(f32[8,72,640]{2,1,0:T(8,128)S(1)} %get-tuple-element.82.refs_0_, ...), custom_call_target="tpu_custom_call" | custom-call | tf_op jit(solution)/shard_map/pallas_call | solution.py:651
  39.6 3.7 %all-to-all-start.2 = ((f32[32,2,128]{2,1,0:T(2,128)}), f32[32,2,128]{2,1,0:T(2,128)S(1)}, u32[]{:S(2)}, u32[]{:S(2)}) async-start(f32[32,2,128]{2,1,0:T(2,128)} %bitcast.7), calls=%async_computation.2 | async-start | bytes 65536 | tf_op jit(solution)/shard_map/all_to_all | solution.py:688
  44.0 4.5 %collective-permute-start.9 = (f32[16,512]{1,0:T(8,128)S(1)}, f32[16,512]{1,0:T(8,128)S(1)}, u32[]{:S(2)}, u32[]{:S(2)}) collective-permute-start(f32[16,512]{1,0:T(8,128)S(1)} %get-tuple-element.103), channel_id=1, source_target_pairs={{0,4},{8,12},{16,20},{24,28},{4,0},{12,8},{20,16},{28,24},{1,5},{9... | collective-permute-start | bytes 98312 | tf_op jit(solution)/shard_map/ppermute | solution.py:668
  49.2 0.9 %collective-permute-start.11 = (f32[8,128]{1,0:T(8,128)S(1)}, f32[8,128]{1,0:T(8,128)S(1)}, u32[]{:S(2)}, u32[]{:S(2)}) collective-permute-start(f32[8,128]{1,0:T(8,128)S(1)} %get-tuple-element.105), channel_id=1, source_target_pairs={{0,1},{2,3},{1,0},{3,2},{4,5},{6,7},{5,4},{7,6},{8,9},{10,11},{9,8... | collective-permute-start | bytes 12296 | tf_op jit(solution)/shard_map/ppermute | solution.py:668
  50.6 1.8 %shard_map.116 = (f32[8,72,640]{2,1,0:T(8,128)S(1)}, f32[5,64,512]{2,1,0:T(8,128)S(1)}, f32[5,64,512]{2,1,0:T(8,128)S(1)}, f32[64,512]{1,0:T(8,128)S(1)}, f32[320,512]{1,0:T(8,128)S(1)}) custom-call(f32[8,72,640]{2,1,0:T(8,128)} %get-tuple-element.92.refs_0_, f32[5,64,512]{2,1,0:T(8,128)} %get-tuple-element.93.refs_1_, ...), custom_call_target="tpu_custom_call" | custom-call | tf_op jit(solution)/shard_map/pallas_call | solution.py:651
  52.5 2.1 %shard_map.117 = (f32[8,72,640]{2,1,0:T(8,128)S(1)}, f32[5,64,512]{2,1,0:T(8,128)S(1)}, f32[5,64,512]{2,1,0:T(8,128)S(1)}, f32[8,128]{1,0:T(8,128)S(1)}, f32[8,1...) custom-call(f32[8,72,640]{2,1,0:T(8,128)S(1)} %get-tuple-element.97.refs_0_, ...), custom_call_target="tpu_custom_call" | custom-call | tf_op jit(solution)/shard_map/pallas_call | solution.py:651
  55.2 3.8 %collective-permute-start.13 = (f32[8,512]{1,0:T(8,128)S(1)}, f32[8,512]{1,0:T(8,128)S(1)}, u32[]{:S(2)}, u32[]{:S(2)}) collective-permute-start(f32[8,512]{1,0:T(8,128)S(1)} %get-tuple-element.109), channel_id=1, source_target_pairs={{0,4},{8,12},{16,20},{24,28},{4,0},{12,8},{20,16},{28,24},{1,5},{9... | collective-permute-start | bytes 49160 | tf_op jit(solution)/shard_map/ppermute | solution.py:668
  59.0 1.2 %collective-permute-start.15 = (f32[8,128]{1,0:T(8,128)S(1)}, f32[8,128]{1,0:T(8,128)S(1)}, u32[]{:S(2)}, u32[]{:S(2)}) collective-permute-start(f32[8,128]{1,0:T(8,128)S(1)} %get-tuple-element.111), channel_id=1, source_target_pairs={{0,1},{2,3},{1,0},{3,2},{4,5},{6,7},{5,4},{7,6},{8,9},{10,11},{9,8... | collective-permute-start | bytes 12296 | tf_op jit(solution)/shard_map/ppermute | solution.py:668
  60.2 1.8 %collective-permute-done.14.refs_4_.refs_6_ = f32[8,128]{1,0:T(8,128)S(1)} collective-permute-done((f32[8,128]{1,0:T(8,128)S(1)}, f32[8,128]{1,0:T(8,128)S(1)}, u32[]{:S(2)}, u32[]{:S(2)}) %collective-permute-start.14) | collective-permute-done | bytes 4128 | tf_op jit(solution)/shard_map/ppermute | solution.py:668
  62.1 1.2 %shard_map.118 = (f32[8,64,512]{2,1,0:T(8,128)}, f32[1,64]{1,0:T(1,128)S(1)}) custom-call(f32[8,72,640]{2,1,0:T(8,128)S(1)} %get-tuple-element.106.refs_0_.refs_1_, f32[5,64,512]{2,1,0:T(8,128)S(1)} %get-tuple-element.107.refs_1_.refs_2_, f32[8,512]{1,0:T(8,128)S(1)} %collective-permute-done.12.refs_2_.refs_4_, ...), custom_call_target="tpu_custom_call" | custom-call | tf_op jit(solution)/shard_map/pallas_call | solution.py:651
  63.4 1.1 %collective-permute-start.17 = (f32[1,64]{1,0:T(1,128)S(1)}, f32[1,64]{1,0:T(1,128)S(1)}, u32[]{:S(2)}, u32[]{:S(2)}) collective-permute-start(f32[1,64]{1,0:T(1,128)S(1)} %get-tuple-element.117), channel_id=1, source_target_pairs={{0,2},{1,3},{2,0},{3,1},{4,6},{5,7},{6,4},{7,5},{8,10},{9,11},{10,... | collective-permute-start | bytes 776 | tf_op jit(solution)/shard_map/ppermute | solution.py:677
  64.5 0.8 %collective-permute-start.18 = (f32[1,64]{1,0:T(1,128)S(1)}, f32[1,64]{1,0:T(1,128)S(1)}, u32[]{:S(2)}, u32[]{:S(2)}) collective-permute-start(f32[1,64]{1,0:T(1,128)S(1)} %get-tuple-element.117), channel_id=1, source_target_pairs={{0,3},{1,2},{2,1},{3,0},{4,7},{5,6},{6,5},{7,4},{8,11},{9,10},{10,... | collective-permute-start | bytes 776 | tf_op jit(solution)/shard_map/ppermute | solution.py:677
  65.2 1.3 %shard_map.119 = (f32[8,64,512]{2,1,0:T(8,128)}, f32[5,64,512]{2,1,0:T(8,128)}, f32[5,64,512]{2,1,0:T(8,128)}) custom-call(f32[8,64,512]{2,1,0:T(8,128)} %get-tuple-element.112.refs_0_, f32[8,72,640]{2,1,0:T(8,128)S(1)} %get-tuple-element.106.refs_0_.refs_1_, f32[5,64,512]{2,1,0:T(8,128)S(1)} %get-tuple-element.107.refs_1_.refs_2_, ...), custom_call_target="tpu_custom_call", output_to_operand_aliasing={{0}: (0, {})} | custom-call | tf_op jit(solution)/shard_map/pallas_call | solution.py:651
  (32 shorter events, 6.9 us)
Async XLA Ops:
  3.7 14.6 %all-to-all-start = ((f32[32,2,128]{2,1,0:T(2,128)}), f32[32,2,128]{2,1,0:T(2,128)S(1)}, u32[]{:S(2)}, u32[]{:S(2)}) async-start(f32[32,2,128]{2,1,0:T(2,128)} %bitcast.3), calls=%async_computation | async-start | bytes 65536 | tf_op jit(solution)/shard_map/all_to_all | solution.py:688
  11.0 9.1 %collective-permute-start = (f32[16,512]{1,0:T(8,128)S(1)}, f32[16,512]{1,0:T(8,128)S(1)}, u32[]{:S(2)}, u32[]{:S(2)}) collective-permute-start(f32[16,512]{1,0:T(8,128)S(1)} %get-tuple-element.72), channel_id=1, source_target_pairs={{4,8},{12,16},{20,24},{8,4},{16,12},{24,20},{5,9},{13,17},{21,25},... | collective-permute-start | bytes 98312 | tf_op jit(solution)/shard_map/ppermute | solution.py:668
  11.7 8.4 %collective-permute-start.1 = (f32[16,512]{1,0:T(8,128)S(1)}, f32[16,512]{1,0:T(8,128)S(1)}, u32[]{:S(2)}, u32[]{:S(2)}) collective-permute-start(f32[16,512]{1,0:T(8,128)S(1)} %get-tuple-element.73), channel_id=1, source_target_pairs={{0,4},{8,12},{16,20},{24,28},{4,0},{12,8},{20,16},{28,24},{1,5},{9... | collective-permute-start | bytes 98312 | tf_op jit(solution)/shard_map/ppermute | solution.py:668
  16.2 3.8 %collective-permute-start.2 = (f32[8,128]{1,0:T(8,128)S(1)}, f32[8,128]{1,0:T(8,128)S(1)}, u32[]{:S(2)}, u32[]{:S(2)}) collective-permute-start(f32[8,128]{1,0:T(8,128)S(1)} %get-tuple-element.74), channel_id=1, source_target_pairs={{1,2},{3,0},{2,1},{0,3},{5,6},{7,4},{6,5},{4,7},{9,10},{11,8},{10,... | collective-permute-start | bytes 12296 | tf_op jit(solution)/shard_map/ppermute | solution.py:668
  16.9 3.2 %collective-permute-start.3 = (f32[8,128]{1,0:T(8,128)S(1)}, f32[8,128]{1,0:T(8,128)S(1)}, u32[]{:S(2)}, u32[]{:S(2)}) collective-permute-start(f32[8,128]{1,0:T(8,128)S(1)} %get-tuple-element.75), channel_id=1, source_target_pairs={{0,1},{2,3},{1,0},{3,2},{4,5},{6,7},{5,4},{7,6},{8,9},{10,11},{9,8... | collective-permute-start | bytes 12296 | tf_op jit(solution)/shard_map/ppermute | solution.py:668
  23.1 11.0 %all-to-all-start.1 = ((f32[32,2,128]{2,1,0:T(2,128)}), f32[32,2,128]{2,1,0:T(2,128)S(1)}, u32[]{:S(2)}, u32[]{:S(2)}) async-start(f32[32,2,128]{2,1,0:T(2,128)} %bitcast.5), calls=%async_computation.1 | async-start | bytes 65536 | tf_op jit(solution)/shard_map/all_to_all | solution.py:688
  26.8 9.1 %collective-permute-start.4 = (f32[16,512]{1,0:T(8,128)S(1)}, f32[16,512]{1,0:T(8,128)S(1)}, u32[]{:S(2)}, u32[]{:S(2)}) collective-permute-start(f32[16,512]{1,0:T(8,128)S(1)} %get-tuple-element.87), channel_id=1, source_target_pairs={{4,8},{12,16},{20,24},{8,4},{16,12},{24,20},{5,9},{13,17},{21,25},... | collective-permute-start | bytes 98312 | tf_op jit(solution)/shard_map/ppermute | solution.py:668
  27.5 8.5 %collective-permute-start.5 = (f32[16,512]{1,0:T(8,128)S(1)}, f32[16,512]{1,0:T(8,128)S(1)}, u32[]{:S(2)}, u32[]{:S(2)}) collective-permute-start(f32[16,512]{1,0:T(8,128)S(1)} %get-tuple-element.88), channel_id=1, source_target_pairs={{0,4},{8,12},{16,20},{24,28},{4,0},{12,8},{20,16},{28,24},{1,5},{9... | collective-permute-start | bytes 98312 | tf_op jit(solution)/shard_map/ppermute | solution.py:668
  32.0 3.9 %collective-permute-start.6 = (f32[8,128]{1,0:T(8,128)S(1)}, f32[8,128]{1,0:T(8,128)S(1)}, u32[]{:S(2)}, u32[]{:S(2)}) collective-permute-start(f32[8,128]{1,0:T(8,128)S(1)} %get-tuple-element.89), channel_id=1, source_target_pairs={{1,2},{3,0},{2,1},{0,3},{5,6},{7,4},{6,5},{4,7},{9,10},{11,8},{10,... | collective-permute-start | bytes 12296 | tf_op jit(solution)/shard_map/ppermute | solution.py:668
  32.7 3.2 %collective-permute-start.7 = (f32[8,128]{1,0:T(8,128)S(1)}, f32[8,128]{1,0:T(8,128)S(1)}, u32[]{:S(2)}, u32[]{:S(2)}) collective-permute-start(f32[8,128]{1,0:T(8,128)S(1)} %get-tuple-element.90), channel_id=1, source_target_pairs={{0,1},{2,3},{1,0},{3,2},{4,5},{6,7},{5,4},{7,6},{8,9},{10,11},{9,8... | collective-permute-start | bytes 12296 | tf_op jit(solution)/shard_map/ppermute | solution.py:668
  39.6 11.0 %all-to-all-start.2 = ((f32[32,2,128]{2,1,0:T(2,128)}), f32[32,2,128]{2,1,0:T(2,128)S(1)}, u32[]{:S(2)}, u32[]{:S(2)}) async-start(f32[32,2,128]{2,1,0:T(2,128)} %bitcast.7), calls=%async_computation.2 | async-start | bytes 65536 | tf_op jit(solution)/shard_map/all_to_all | solution.py:688
  43.3 9.1 %collective-permute-start.8 = (f32[16,512]{1,0:T(8,128)S(1)}, f32[16,512]{1,0:T(8,128)S(1)}, u32[]{:S(2)}, u32[]{:S(2)}) collective-permute-start(f32[16,512]{1,0:T(8,128)S(1)} %get-tuple-element.102), channel_id=1, source_target_pairs={{4,8},{12,16},{20,24},{8,4},{16,12},{24,20},{5,9},{13,17},{21,25},... | collective-permute-start | bytes 98312 | tf_op jit(solution)/shard_map/ppermute | solution.py:668
  44.0 8.5 %collective-permute-start.9 = (f32[16,512]{1,0:T(8,128)S(1)}, f32[16,512]{1,0:T(8,128)S(1)}, u32[]{:S(2)}, u32[]{:S(2)}) collective-permute-start(f32[16,512]{1,0:T(8,128)S(1)} %get-tuple-element.103), channel_id=1, source_target_pairs={{0,4},{8,12},{16,20},{24,28},{4,0},{12,8},{20,16},{28,24},{1,5},{9... | collective-permute-start | bytes 98312 | tf_op jit(solution)/shard_map/ppermute | solution.py:668
  48.5 3.9 %collective-permute-start.10 = (f32[8,128]{1,0:T(8,128)S(1)}, f32[8,128]{1,0:T(8,128)S(1)}, u32[]{:S(2)}, u32[]{:S(2)}) collective-permute-start(f32[8,128]{1,0:T(8,128)S(1)} %get-tuple-element.104), channel_id=1, source_target_pairs={{1,2},{3,0},{2,1},{0,3},{5,6},{7,4},{6,5},{4,7},{9,10},{11,8},{10,... | collective-permute-start | bytes 12296 | tf_op jit(solution)/shard_map/ppermute | solution.py:668
  49.2 3.2 %collective-permute-start.11 = (f32[8,128]{1,0:T(8,128)S(1)}, f32[8,128]{1,0:T(8,128)S(1)}, u32[]{:S(2)}, u32[]{:S(2)}) collective-permute-start(f32[8,128]{1,0:T(8,128)S(1)} %get-tuple-element.105), channel_id=1, source_target_pairs={{0,1},{2,3},{1,0},{3,2},{4,5},{6,7},{5,4},{7,6},{8,9},{10,11},{9,8... | collective-permute-start | bytes 12296 | tf_op jit(solution)/shard_map/ppermute | solution.py:668
  54.6 7.5 %collective-permute-start.12 = (f32[8,512]{1,0:T(8,128)S(1)}, f32[8,512]{1,0:T(8,128)S(1)}, u32[]{:S(2)}, u32[]{:S(2)}) collective-permute-start(f32[8,512]{1,0:T(8,128)S(1)} %get-tuple-element.108), channel_id=1, source_target_pairs={{4,8},{12,16},{20,24},{8,4},{16,12},{24,20},{5,9},{13,17},{21,25},... | collective-permute-start | bytes 49160 | tf_op jit(solution)/shard_map/ppermute | solution.py:668
  55.2 6.8 %collective-permute-start.13 = (f32[8,512]{1,0:T(8,128)S(1)}, f32[8,512]{1,0:T(8,128)S(1)}, u32[]{:S(2)}, u32[]{:S(2)}) collective-permute-start(f32[8,512]{1,0:T(8,128)S(1)} %get-tuple-element.109), channel_id=1, source_target_pairs={{0,4},{8,12},{16,20},{24,28},{4,0},{12,8},{20,16},{28,24},{1,5},{9... | collective-permute-start | bytes 49160 | tf_op jit(solution)/shard_map/ppermute | solution.py:668
  59.0 3.0 %collective-permute-start.14 = (f32[8,128]{1,0:T(8,128)S(1)}, f32[8,128]{1,0:T(8,128)S(1)}, u32[]{:S(2)}, u32[]{:S(2)}) collective-permute-start(f32[8,128]{1,0:T(8,128)S(1)} %get-tuple-element.110), channel_id=1, source_target_pairs={{1,2},{3,0},{2,1},{0,3},{5,6},{7,4},{6,5},{4,7},{9,10},{11,8},{10,... | collective-permute-start | bytes 12296 | tf_op jit(solution)/shard_map/ppermute | solution.py:668
  59.0 3.0 %collective-permute-start.15 = (f32[8,128]{1,0:T(8,128)S(1)}, f32[8,128]{1,0:T(8,128)S(1)}, u32[]{:S(2)}, u32[]{:S(2)}) collective-permute-start(f32[8,128]{1,0:T(8,128)S(1)} %get-tuple-element.111), channel_id=1, source_target_pairs={{0,1},{2,3},{1,0},{3,2},{4,5},{6,7},{5,4},{7,6},{8,9},{10,11},{9,8... | collective-permute-start | bytes 12296 | tf_op jit(solution)/shard_map/ppermute | solution.py:668
  63.3 3.3 %collective-permute-start.16 = (f32[1,64]{1,0:T(1,128)S(1)}, f32[1,64]{1,0:T(1,128)S(1)}, u32[]{:S(2)}, u32[]{:S(2)}) collective-permute-start(f32[1,64]{1,0:T(1,128)S(1)} %get-tuple-element.117), channel_id=1, source_target_pairs={{0,1},{1,0},{2,3},{3,2},{4,5},{5,4},{6,7},{7,6},{8,9},{9,8},{10,11... | collective-permute-start | bytes 776 | tf_op jit(solution)/shard_map/ppermute | solution.py:677
  63.4 3.6 %collective-permute-start.17 = (f32[1,64]{1,0:T(1,128)S(1)}, f32[1,64]{1,0:T(1,128)S(1)}, u32[]{:S(2)}, u32[]{:S(2)}) collective-permute-start(f32[1,64]{1,0:T(1,128)S(1)} %get-tuple-element.117), channel_id=1, source_target_pairs={{0,2},{1,3},{2,0},{3,1},{4,6},{5,7},{6,4},{7,5},{8,10},{9,11},{10,... | collective-permute-start | bytes 776 | tf_op jit(solution)/shard_map/ppermute | solution.py:677
  64.5 3.0 %collective-permute-start.18 = (f32[1,64]{1,0:T(1,128)S(1)}, f32[1,64]{1,0:T(1,128)S(1)}, u32[]{:S(2)}, u32[]{:S(2)}) collective-permute-start(f32[1,64]{1,0:T(1,128)S(1)} %get-tuple-element.117), channel_id=1, source_target_pairs={{0,3},{1,2},{2,1},{3,0},{4,7},{5,6},{6,5},{7,4},{8,11},{9,10},{10,... | collective-permute-start | bytes 776 | tf_op jit(solution)/shard_map/ppermute | solution.py:677

commit v14 on v13

--- a/solution.py
+++ b/solution.py
@@ -478,7 +478,7 @@
         copy.start()
         sends.append(copy)
 
-    above, below = in_order("sec", sec_first[...], sec_second[...])
+    above, below = in_order("sec", sec_first[...], second_of(sec_second))
     left, right = in_order("girth", girth_first[...], girth_second[...])
     if first:
         for k in range(RESULTS):
@@ -669,6 +669,18 @@
     return out
 
 
+def gather_second(value, axis):
+    count = lax.axis_size(axis)
+    pairs = [[i, (i + 1) % count] for i in range(1, count, 2)]
+    return lax.all_gather(value, axis, axis_index_groups=pairs)
+
+
+def second_of(gathered):
+    sec, _, secs, _ = place()
+    value = jnp.where(lax.rem(sec, 2) == 0, gathered[0], gathered[1])
+    return jnp.where(jnp.logical_or(sec == 0, sec == secs - 1), 0.0, value)
+
+
 def sum_over(value, axis):
     count = lax.axis_size(axis)
     if count & (count - 1):
@@ -731,7 +743,7 @@
     for step in range(STEPS):
         first, last = step == 0, step == STEPS - 1
         incoming = exchange(payload)
-        ends = swap((sec_first, sec_second), "sec", False)
+        ends = (gather_second(sec_second, "sec"), swap((sec_first,), "sec", False)[0])
         sides = swap((girth_first, girth_second), "girth", True)
         state = [stress, velocity, displacement, pressure] + [thickness] * first
         *state, weld = call(

time: 68.4 us -> 76.6 us (1.12)
  the two profiles are of different devices: /device:TPU:0 before, /device:TPU:5 now
where the time goes in v14:
time: 76.6 us; the launch traced here: 76.2 us
  starting transfers between devices  40.6 us (53%)
  Pallas kernels  19.8 us (26%)
  blocking collectives  13 us (17%)
  waiting for transfers between devices  1.49 us (2%)
  between operations  0.85 us (1%)
    all_to_all x3, starting transfers between devices, exchange(): blocks = lax.all_to_all(blocks, ('sec', 'girth'), 0, 0, tiled=True)  22.4 us
    pallas_call x9, Pallas kernels, call(): pl.pallas_call(kernel, out_shape=results, in_specs=[away] * far + [whole]...  19.8 us
    ppermute x13, starting transfers between devices, swap(): lax.ppermute(value, axis, couples + [(j, i) for i, j in couples])  13.3 us
    all_gather x3, blocking collectives, gather_second(): return lax.all_gather(value, axis, axis_index_groups=pairs)  13 us
    ppermute x3, starting transfers between devices, sum_over(): lax.ppermute(value, axis, [(i, i ^ step) for i in range(count)])  4.83 us
  transfers between devices with their start and end apart: 19, of which 2 were waited for; matrix products, arithmetic and copies ran while one was open for 0% of the time, Pallas kernels for 9%

profile of v14, /device:TPU:5, one launch (start us, length us, event | category | flops | bytes accessed | tf_op | source)
XLA Modules:
  0.0 76.2 jit_solution(10965727949312388262)
XLA Ops:
  0.6 3.0 %shard_map.111 = (f32[64,128]{1,0:T(8,128)}, f32[16,512]{1,0:T(8,128)S(1)}, f32[16,512]{1,0:T(8,128)S(1)}, f32[8,128]{1,0:T(8,128)S(1)}, f32[8,128]{1,0:T(8,128)...) custom-call(f32[5,64,512]{2,1,0:T(8,128)} %refs_2_.1, ...), custom_call_target="tpu_custom_call" | custom-call | tf_op jit(solution)/shard_map/pallas_call | solution.py:651
  3.7 6.4 %all-to-all-start = ((f32[32,2,128]{2,1,0:T(2,128)}), f32[32,2,128]{2,1,0:T(2,128)S(1)}, u32[]{:S(2)}, u32[]{:S(2)}) async-start(f32[32,2,128]{2,1,0:T(2,128)} %bitcast.3), calls=%async_computation | async-start | bytes 65536 | tf_op jit(solution)/shard_map/all_to_all | solution.py:700
  10.3 1.9 %collective-permute-start.1 = (f32[8,128]{1,0:T(8,128)S(1)}, f32[8,128]{1,0:T(8,128)S(1)}, u32[]{:S(2)}, u32[]{:S(2)}) collective-permute-start(f32[8,128]{1,0:T(8,128)S(1)} %get-tuple-element.74), channel_id=1, source_target_pairs={{1,2},{3,0},{2,1},{0,3},{5,6},{7,4},{6,5},{4,7},{9,10},{11,8},{10,... | collective-permute-start | bytes 12296 | tf_op jit(solution)/shard_map/ppermute | solution.py:668
  12.2 4.3 %all-gather = f32[32,512]{1,0:T(8,128)S(1)} all-gather(f32[16,512]{1,0:T(8,128)S(1)} %get-tuple-element.72), channel_id=2, replica_groups={{4,8},{12,16},{20,24},{28,0},{5,9},{13,17},{21,25},{29,1},{6,10},{14,18..., dimensions={0}, use_global_device_ids=true | all-gather | bytes 98304 | tf_op jit(solution)/shard_map/all_gather | solution.py:675
  16.5 1.8 %shard_map.112 = (f32[8,64,512]{2,1,0:T(8,128)S(1)}, f32[5,64,512]{2,1,0:T(8,128)S(1)}, f32[5,64,512]{2,1,0:T(8,128)S(1)}, f32[64,512]{1,0:T(8,128)S(1)}, s32[64...) custom-call(f32[8,64,512]{2,1,0:T(8,128)} %refs_0_.1, f32[5,64,512]{2,1,0:T(8,128)} %refs_1_.1, ...), custom_call_target="tpu_custom_call" | custom-call | tf_op jit(solution)/shard_map/pallas_call | solution.py:651
  18.3 3.0 %shard_map.113 = (f32[8,72,640]{2,1,0:T(8,128)}, f32[5,64,512]{2,1,0:T(8,128)}, f32[5,64,512]{2,1,0:T(8,128)}, f32[1,72,640]{2,1,0:T(8,128)S(1)}, f32[8,128]{1,0...) custom-call(f32[8,64,512]{2,1,0:T(8,128)S(1)} %get-tuple-element.66., ...), custom_call_target="tpu_custom_call" | custom-call | tf_op jit(solution)/shard_map/pallas_call | solution.py:651
  21.3 8.0 %all-to-all-start.1 = ((f32[32,2,128]{2,1,0:T(2,128)}), f32[32,2,128]{2,1,0:T(2,128)S(1)}, u32[]{:S(2)}, u32[]{:S(2)}) async-start(f32[32,2,128]{2,1,0:T(2,128)} %bitcast.6), calls=%async_computation.1 | async-start | bytes 65536 | tf_op jit(solution)/shard_map/all_to_all | solution.py:700
  29.5 1.9 %collective-permute-start.4 = (f32[8,128]{1,0:T(8,128)S(1)}, f32[8,128]{1,0:T(8,128)S(1)}, u32[]{:S(2)}, u32[]{:S(2)}) collective-permute-start(f32[8,128]{1,0:T(8,128)S(1)} %get-tuple-element.89), channel_id=1, source_target_pairs={{1,2},{3,0},{2,1},{0,3},{5,6},{7,4},{6,5},{4,7},{9,10},{11,8},{10,... | collective-permute-start | bytes 12296 | tf_op jit(solution)/shard_map/ppermute | solution.py:668
  31.4 4.3 %all-gather.1 = f32[32,512]{1,0:T(8,128)S(1)} all-gather(f32[16,512]{1,0:T(8,128)S(1)} %get-tuple-element.87), channel_id=3, replica_groups={{4,8},{12,16},{20,24},{28,0},{5,9},{13,17},{21,25},{29,1},{6,10},{14,18..., dimensions={0}, use_global_device_ids=true | all-gather | bytes 98304 | tf_op jit(solution)/shard_map/all_gather | solution.py:675
  35.7 1.8 %shard_map.114 = (f32[8,72,640]{2,1,0:T(8,128)S(1)}, f32[5,64,512]{2,1,0:T(8,128)S(1)}, f32[5,64,512]{2,1,0:T(8,128)S(1)}, f32[64,512]{1,0:T(8,128)S(1)}, f32[320,512]{1,0:T(8,128)S(1)}) custom-call(f32[8,72,640]{2,1,0:T(8,128)} %get-tuple-element.76.refs_0_, f32[5,64,512]{2,1,0:T(8,128)} %get-tuple-element.77.refs_1_, ...), custom_call_target="tpu_custom_call" | custom-call | tf_op jit(solution)/shard_map/pallas_call | solution.py:651
  37.6 3.7 %shard_map.115 = (f32[8,72,640]{2,1,0:T(8,128)}, f32[5,64,512]{2,1,0:T(8,128)}, f32[5,64,512]{2,1,0:T(8,128)}, f32[8,128]{1,0:T(8,128)S(1)}, f32[8,128]{1,0:T(8,...) custom-call(f32[8,72,640]{2,1,0:T(8,128)S(1)} %get-tuple-element.82.refs_0_, ...), custom_call_target="tpu_custom_call" | custom-call | tf_op jit(solution)/shard_map/pallas_call | solution.py:651
  41.3 8.0 %all-to-all-start.2 = ((f32[32,2,128]{2,1,0:T(2,128)}), f32[32,2,128]{2,1,0:T(2,128)S(1)}, u32[]{:S(2)}, u32[]{:S(2)}) async-start(f32[32,2,128]{2,1,0:T(2,128)} %bitcast.9), calls=%async_computation.2 | async-start | bytes 65536 | tf_op jit(solution)/shard_map/all_to_all | solution.py:700
  49.4 1.9 %collective-permute-start.7 = (f32[8,128]{1,0:T(8,128)S(1)}, f32[8,128]{1,0:T(8,128)S(1)}, u32[]{:S(2)}, u32[]{:S(2)}) collective-permute-start(f32[8,128]{1,0:T(8,128)S(1)} %get-tuple-element.104), channel_id=1, source_target_pairs={{1,2},{3,0},{2,1},{0,3},{5,6},{7,4},{6,5},{4,7},{9,10},{11,8},{10,... | collective-permute-start | bytes 12296 | tf_op jit(solution)/shard_map/ppermute | solution.py:668
  51.4 4.3 %all-gather.2 = f32[32,512]{1,0:T(8,128)S(1)} all-gather(f32[16,512]{1,0:T(8,128)S(1)} %get-tuple-element.102), channel_id=4, replica_groups={{4,8},{12,16},{20,24},{28,0},{5,9},{13,17},{21,25},{29,1},{6,10},{14,18..., dimensions={0}, use_global_device_ids=true | all-gather | bytes 98304 | tf_op jit(solution)/shard_map/all_gather | solution.py:675
  55.7 1.8 %shard_map.116 = (f32[8,72,640]{2,1,0:T(8,128)S(1)}, f32[5,64,512]{2,1,0:T(8,128)S(1)}, f32[5,64,512]{2,1,0:T(8,128)S(1)}, f32[64,512]{1,0:T(8,128)S(1)}, f32[320,512]{1,0:T(8,128)S(1)}) custom-call(f32[8,72,640]{2,1,0:T(8,128)} %get-tuple-element.92.refs_0_, f32[5,64,512]{2,1,0:T(8,128)} %get-tuple-element.93.refs_1_, ...), custom_call_target="tpu_custom_call" | custom-call | tf_op jit(solution)/shard_map/pallas_call | solution.py:651
  57.6 2.1 %shard_map.117 = (f32[8,72,640]{2,1,0:T(8,128)S(1)}, f32[5,64,512]{2,1,0:T(8,128)S(1)}, f32[5,64,512]{2,1,0:T(8,128)S(1)}, f32[8,128]{1,0:T(8,128)S(1)}, f32[8,1...) custom-call(f32[8,72,640]{2,1,0:T(8,128)S(1)} %get-tuple-element.97.refs_0_, ...), custom_call_target="tpu_custom_call" | custom-call | tf_op jit(solution)/shard_map/pallas_call | solution.py:651
  59.7 3.0 %collective-permute-start.10 = (f32[8,512]{1,0:T(8,128)S(1)}, f32[8,512]{1,0:T(8,128)S(1)}, u32[]{:S(2)}, u32[]{:S(2)}) collective-permute-start(f32[8,512]{1,0:T(8,128)S(1)} %get-tuple-element.109), channel_id=1, source_target_pairs={{0,4},{8,12},{16,20},{24,28},{4,0},{12,8},{20,16},{28,24},{1,5},{9... | collective-permute-start | bytes 49160 | tf_op jit(solution)/shard_map/ppermute | solution.py:668
  62.7 1.9 %collective-permute-start.9 = (f32[8,512]{1,0:T(8,128)S(1)}, f32[8,512]{1,0:T(8,128)S(1)}, u32[]{:S(2)}, u32[]{:S(2)}) collective-permute-start(f32[8,512]{1,0:T(8,128)S(1)} %get-tuple-element.108), channel_id=1, source_target_pairs={{4,8},{12,16},{20,24},{8,4},{16,12},{24,20},{5,9},{13,17},{21,25},... | collective-permute-start | bytes 49160 | tf_op jit(solution)/shard_map/ppermute | solution.py:668
  64.6 2.2 %collective-permute-start.11 = (f32[8,128]{1,0:T(8,128)S(1)}, f32[8,128]{1,0:T(8,128)S(1)}, u32[]{:S(2)}, u32[]{:S(2)}) collective-permute-start(f32[8,128]{1,0:T(8,128)S(1)} %get-tuple-element.110), channel_id=1, source_target_pairs={{1,2},{3,0},{2,1},{0,3},{5,6},{7,4},{6,5},{4,7},{9,10},{11,8},{10,... | collective-permute-start | bytes 12296 | tf_op jit(solution)/shard_map/ppermute | solution.py:668
  66.9 1.2 %collective-permute-done.11.refs_4_.refs_6_ = f32[8,128]{1,0:T(8,128)S(1)} collective-permute-done((f32[8,128]{1,0:T(8,128)S(1)}, f32[8,128]{1,0:T(8,128)S(1)}, u32[]{:S(2)}, u32[]{:S(2)}) %collective-permute-start.11) | collective-permute-done | bytes 4128 | tf_op jit(solution)/shard_map/ppermute | solution.py:668
  68.1 1.2 %shard_map.118 = (f32[8,64,512]{2,1,0:T(8,128)}, f32[1,64]{1,0:T(1,128)S(1)}) custom-call(f32[8,72,640]{2,1,0:T(8,128)S(1)} %get-tuple-element.106.refs_0_.refs_1_, f32[5,64,512]{2,1,0:T(8,128)S(1)} %get-tuple-element.107.refs_1_.refs_2_, f32[8,512]{1,0:T(8,128)S(1)} %collective-permute-done.9.refs_2_.refs_4_, ...), custom_call_target="tpu_custom_call" | custom-call | tf_op jit(solution)/shard_map/pallas_call | solution.py:651
  69.3 3.1 %collective-permute-start.13 = (f32[1,64]{1,0:T(1,128)S(1)}, f32[1,64]{1,0:T(1,128)S(1)}, u32[]{:S(2)}, u32[]{:S(2)}) collective-permute-start(f32[1,64]{1,0:T(1,128)S(1)} %get-tuple-element.117), channel_id=1, source_target_pairs={{0,1},{1,0},{2,3},{3,2},{4,5},{5,4},{6,7},{7,6},{8,9},{9,8},{10,11... | collective-permute-start | bytes 776 | tf_op jit(solution)/shard_map/ppermute | solution.py:689
  72.7 1.4 %collective-permute-start.15 = (f32[1,64]{1,0:T(1,128)S(1)}, f32[1,64]{1,0:T(1,128)S(1)}, u32[]{:S(2)}, u32[]{:S(2)}) collective-permute-start(f32[1,64]{1,0:T(1,128)S(1)} %get-tuple-element.117), channel_id=1, source_target_pairs={{0,3},{1,2},{2,1},{3,0},{4,7},{5,6},{6,5},{7,4},{8,11},{9,10},{10,... | collective-permute-start | bytes 776 | tf_op jit(solution)/shard_map/ppermute | solution.py:689
  74.2 1.3 %shard_map.119 = (f32[8,64,512]{2,1,0:T(8,128)}, f32[5,64,512]{2,1,0:T(8,128)}, f32[5,64,512]{2,1,0:T(8,128)}) custom-call(f32[8,64,512]{2,1,0:T(8,128)} %get-tuple-element.112.refs_0_, f32[8,72,640]{2,1,0:T(8,128)S(1)} %get-tuple-element.106.refs_0_.refs_1_, f32[5,64,512]{2,1,0:T(8,128)S(1)} %get-tuple-element.107.refs_1_.refs_2_, ...), custom_call_target="tpu_custom_call", output_to_operand_aliasing={{0}: (0, {})} | custom-call | tf_op jit(solution)/shard_map/pallas_call | solution.py:651
  (29 shorter events, 1.5 us)
Async XLA Ops:
  3.7 12.8 %all-to-all-start = ((f32[32,2,128]{2,1,0:T(2,128)}), f32[32,2,128]{2,1,0:T(2,128)S(1)}, u32[]{:S(2)}, u32[]{:S(2)}) async-start(f32[32,2,128]{2,1,0:T(2,128)} %bitcast.3), calls=%async_computation | async-start | bytes 65536 | tf_op jit(solution)/shard_map/all_to_all | solution.py:700
  10.1 8.2 %collective-permute-start = (f32[16,512]{1,0:T(8,128)S(1)}, f32[16,512]{1,0:T(8,128)S(1)}, u32[]{:S(2)}, u32[]{:S(2)}) collective-permute-start(f32[16,512]{1,0:T(8,128)S(1)} %get-tuple-element.73), channel_id=1, source_target_pairs={{0,4},{8,12},{16,20},{24,28},{4,0},{12,8},{20,16},{28,24},{1,5},{9... | collective-permute-start | bytes 98312 | tf_op jit(solution)/shard_map/ppermute | solution.py:668
  10.3 8.1 %collective-permute-start.1 = (f32[8,128]{1,0:T(8,128)S(1)}, f32[8,128]{1,0:T(8,128)S(1)}, u32[]{:S(2)}, u32[]{:S(2)}) collective-permute-start(f32[8,128]{1,0:T(8,128)S(1)} %get-tuple-element.74), channel_id=1, source_target_pairs={{1,2},{3,0},{2,1},{0,3},{5,6},{7,4},{6,5},{4,7},{9,10},{11,8},{10,... | collective-permute-start | bytes 12296 | tf_op jit(solution)/shard_map/ppermute | solution.py:668
  12.2 6.2 %collective-permute-start.2 = (f32[8,128]{1,0:T(8,128)S(1)}, f32[8,128]{1,0:T(8,128)S(1)}, u32[]{:S(2)}, u32[]{:S(2)}) collective-permute-start(f32[8,128]{1,0:T(8,128)S(1)} %get-tuple-element.75), channel_id=1, source_target_pairs={{0,1},{2,3},{1,0},{3,2},{4,5},{6,7},{5,4},{7,6},{8,9},{10,11},{9,8... | collective-permute-start | bytes 12296 | tf_op jit(solution)/shard_map/ppermute | solution.py:668
  21.3 14.4 %all-to-all-start.1 = ((f32[32,2,128]{2,1,0:T(2,128)}), f32[32,2,128]{2,1,0:T(2,128)S(1)}, u32[]{:S(2)}, u32[]{:S(2)}) async-start(f32[32,2,128]{2,1,0:T(2,128)} %bitcast.6), calls=%async_computation.1 | async-start | bytes 65536 | tf_op jit(solution)/shard_map/all_to_all | solution.py:700
  29.3 8.3 %collective-permute-start.3 = (f32[16,512]{1,0:T(8,128)S(1)}, f32[16,512]{1,0:T(8,128)S(1)}, u32[]{:S(2)}, u32[]{:S(2)}) collective-permute-start(f32[16,512]{1,0:T(8,128)S(1)} %get-tuple-element.88), channel_id=1, source_target_pairs={{0,4},{8,12},{16,20},{24,28},{4,0},{12,8},{20,16},{28,24},{1,5},{9... | collective-permute-start | bytes 98312 | tf_op jit(solution)/shard_map/ppermute | solution.py:668
  29.5 8.1 %collective-permute-start.4 = (f32[8,128]{1,0:T(8,128)S(1)}, f32[8,128]{1,0:T(8,128)S(1)}, u32[]{:S(2)}, u32[]{:S(2)}) collective-permute-start(f32[8,128]{1,0:T(8,128)S(1)} %get-tuple-element.89), channel_id=1, source_target_pairs={{1,2},{3,0},{2,1},{0,3},{5,6},{7,4},{6,5},{4,7},{9,10},{11,8},{10,... | collective-permute-start | bytes 12296 | tf_op jit(solution)/shard_map/ppermute | solution.py:668
  31.4 6.2 %collective-permute-start.5 = (f32[8,128]{1,0:T(8,128)S(1)}, f32[8,128]{1,0:T(8,128)S(1)}, u32[]{:S(2)}, u32[]{:S(2)}) collective-permute-start(f32[8,128]{1,0:T(8,128)S(1)} %get-tuple-element.90), channel_id=1, source_target_pairs={{0,1},{2,3},{1,0},{3,2},{4,5},{6,7},{5,4},{7,6},{8,9},{10,11},{9,8... | collective-permute-start | bytes 12296 | tf_op jit(solution)/shard_map/ppermute | solution.py:668
  41.3 14.4 %all-to-all-start.2 = ((f32[32,2,128]{2,1,0:T(2,128)}), f32[32,2,128]{2,1,0:T(2,128)S(1)}, u32[]{:S(2)}, u32[]{:S(2)}) async-start(f32[32,2,128]{2,1,0:T(2,128)} %bitcast.9), calls=%async_computation.2 | async-start | bytes 65536 | tf_op jit(solution)/shard_map/all_to_all | solution.py:700
  49.3 8.3 %collective-permute-start.6 = (f32[16,512]{1,0:T(8,128)S(1)}, f32[16,512]{1,0:T(8,128)S(1)}, u32[]{:S(2)}, u32[]{:S(2)}) collective-permute-start(f32[16,512]{1,0:T(8,128)S(1)} %get-tuple-element.103), channel_id=1, source_target_pairs={{0,4},{8,12},{16,20},{24,28},{4,0},{12,8},{20,16},{28,24},{1,5},{9... | collective-permute-start | bytes 98312 | tf_op jit(solution)/shard_map/ppermute | solution.py:668
  49.4 8.1 %collective-permute-start.7 = (f32[8,128]{1,0:T(8,128)S(1)}, f32[8,128]{1,0:T(8,128)S(1)}, u32[]{:S(2)}, u32[]{:S(2)}) collective-permute-start(f32[8,128]{1,0:T(8,128)S(1)} %get-tuple-element.104), channel_id=1, source_target_pairs={{1,2},{3,0},{2,1},{0,3},{5,6},{7,4},{6,5},{4,7},{9,10},{11,8},{10,... | collective-permute-start | bytes 12296 | tf_op jit(solution)/shard_map/ppermute | solution.py:668
  51.3 6.2 %collective-permute-start.8 = (f32[8,128]{1,0:T(8,128)S(1)}, f32[8,128]{1,0:T(8,128)S(1)}, u32[]{:S(2)}, u32[]{:S(2)}) collective-permute-start(f32[8,128]{1,0:T(8,128)S(1)} %get-tuple-element.105), channel_id=1, source_target_pairs={{0,1},{2,3},{1,0},{3,2},{4,5},{6,7},{5,4},{7,6},{8,9},{10,11},{9,8... | collective-permute-start | bytes 12296 | tf_op jit(solution)/shard_map/ppermute | solution.py:668
  59.7 8.4 %collective-permute-start.10 = (f32[8,512]{1,0:T(8,128)S(1)}, f32[8,512]{1,0:T(8,128)S(1)}, u32[]{:S(2)}, u32[]{:S(2)}) collective-permute-start(f32[8,512]{1,0:T(8,128)S(1)} %get-tuple-element.109), channel_id=1, source_target_pairs={{0,4},{8,12},{16,20},{24,28},{4,0},{12,8},{20,16},{28,24},{1,5},{9... | collective-permute-start | bytes 49160 | tf_op jit(solution)/shard_map/ppermute | solution.py:668
  62.7 5.4 %collective-permute-start.9 = (f32[8,512]{1,0:T(8,128)S(1)}, f32[8,512]{1,0:T(8,128)S(1)}, u32[]{:S(2)}, u32[]{:S(2)}) collective-permute-start(f32[8,512]{1,0:T(8,128)S(1)} %get-tuple-element.108), channel_id=1, source_target_pairs={{4,8},{12,16},{20,24},{8,4},{16,12},{24,20},{5,9},{13,17},{21,25},... | collective-permute-start | bytes 49160 | tf_op jit(solution)/shard_map/ppermute | solution.py:668
  64.6 3.5 %collective-permute-start.11 = (f32[8,128]{1,0:T(8,128)S(1)}, f32[8,128]{1,0:T(8,128)S(1)}, u32[]{:S(2)}, u32[]{:S(2)}) collective-permute-start(f32[8,128]{1,0:T(8,128)S(1)} %get-tuple-element.110), channel_id=1, source_target_pairs={{1,2},{3,0},{2,1},{0,3},{5,6},{7,4},{6,5},{4,7},{9,10},{11,8},{10,... | collective-permute-start | bytes 12296 | tf_op jit(solution)/shard_map/ppermute | solution.py:668
  66.8 1.3 %collective-permute-start.12 = (f32[8,128]{1,0:T(8,128)S(1)}, f32[8,128]{1,0:T(8,128)S(1)}, u32[]{:S(2)}, u32[]{:S(2)}) collective-permute-start(f32[8,128]{1,0:T(8,128)S(1)} %get-tuple-element.111), channel_id=1, source_target_pairs={{0,1},{2,3},{1,0},{3,2},{4,5},{6,7},{5,4},{7,6},{8,9},{10,11},{9,8... | collective-permute-start | bytes 12296 | tf_op jit(solution)/shard_map/ppermute | solution.py:668
  69.3 6.2 %collective-permute-start.13 = (f32[1,64]{1,0:T(1,128)S(1)}, f32[1,64]{1,0:T(1,128)S(1)}, u32[]{:S(2)}, u32[]{:S(2)}) collective-permute-start(f32[1,64]{1,0:T(1,128)S(1)} %get-tuple-element.117), channel_id=1, source_target_pairs={{0,1},{1,0},{2,3},{3,2},{4,5},{5,4},{6,7},{7,6},{8,9},{9,8},{10,11... | collective-permute-start | bytes 776 | tf_op jit(solution)/shard_map/ppermute | solution.py:689
  72.4 3.1 %collective-permute-start.14 = (f32[1,64]{1,0:T(1,128)S(1)}, f32[1,64]{1,0:T(1,128)S(1)}, u32[]{:S(2)}, u32[]{:S(2)}) collective-permute-start(f32[1,64]{1,0:T(1,128)S(1)} %get-tuple-element.117), channel_id=1, source_target_pairs={{0,2},{1,3},{2,0},{3,1},{4,6},{5,7},{6,4},{7,5},{8,10},{9,11},{10,... | collective-permute-start | bytes 776 | tf_op jit(solution)/shard_map/ppermute | solution.py:689
  72.7 3.0 %collective-permute-start.15 = (f32[1,64]{1,0:T(1,128)S(1)}, f32[1,64]{1,0:T(1,128)S(1)}, u32[]{:S(2)}, u32[]{:S(2)}) collective-permute-start(f32[1,64]{1,0:T(1,128)S(1)} %get-tuple-element.117), channel_id=1, source_target_pairs={{0,3},{1,2},{2,1},{3,0},{4,7},{5,6},{6,5},{7,4},{8,11},{9,10},{10,... | collective-permute-start | bytes 776 | tf_op jit(solution)/shard_map/ppermute | solution.py:689

commit v15 on v13

--- a/solution.py
+++ b/solution.py
@@ -9,6 +9,7 @@
 
 STEPS = 3
 CORNER_LANE = 112
+SIDE_ROWS = 24
 PIECE = 24
 FIELDS = 5
 RESULTS = 8
@@ -119,31 +120,40 @@
     return out
 
 
-def edge_rows(columns):
-    rows = columns[0][0].shape[0]
-    lane = lax.broadcasted_iota(jnp.int32, (rows, LANES), 1)
-    halves = [jnp.zeros((rows, LANES), F32), jnp.zeros((rows, LANES), F32)]
-    for value, source, half, row in columns:
-        moved = pltpu.roll(value, (row - source) % LANES, 1)
-        halves[half] = jnp.where(lane == row, moved, halves[half])
-    return jnp.concatenate(halves, axis=0).T
-
-
-def edge_columns(left_tile, right_tile):
-    stacked = jnp.concatenate(
-        [left_tile, right_tile, jnp.zeros((LANES - 16, LANES), F32)], axis=0
-    )
-    turned = stacked.T
-    return turned[: LANES // 2], turned[LANES // 2 :]
-
-
-def edge_block(pieces):
-    rows = pieces[0][0].shape[0]
-    lane = lax.broadcasted_iota(jnp.int32, (rows, LANES), 1)
-    block = jnp.zeros((rows, LANES), F32)
-    for value, source, target in pieces:
-        block = jnp.where(lane == target, pltpu.roll(value, (target - source) % LANES, 1), block)
+def place_lanes(pieces):
+    shape = pieces[0][0].shape
+    lane = lax.broadcasted_iota(jnp.int32, shape, 1)
+    block = jnp.zeros(shape, F32)
+    for value, source, target, count in pieces:
+        moved = value if source == target else pltpu.roll(value, (target - source) % LANES, 1)
+        inside = jnp.logical_and(lane >= target, lane < target + count)
+        if target + count > LANES:
+            inside = jnp.logical_or(inside, lane < target + count - LANES)
+        block = jnp.where(inside, moved, block)
     return block
+
+
+def edge_rows(left, right, depth):
+    pieces = []
+    for k, (low, high) in enumerate(zip(left, right)):
+        pieces.append((high, LANES - depth, 2 * depth * k, depth))
+        pieces.append((low, 0, 2 * depth * k + depth, depth))
+    block = place_lanes(pieces)
+    rows = block.shape[0]
+    if rows < LANES:
+        block = jnp.concatenate([block, jnp.zeros((LANES - rows, LANES), F32)], axis=0)
+    return block.T[:SIDE_ROWS]
+
+
+def edge_columns(left, right, depth, rows):
+    row = lax.broadcasted_iota(jnp.int32, left.shape, 0)
+    both = jnp.where(lax.rem(row, 2 * depth) < depth, left, right)
+    both = jnp.concatenate([both, jnp.zeros((LANES - SIDE_ROWS, LANES), F32)], axis=0)
+    return both.T[:rows]
+
+
+def side_block(columns, k, depth):
+    return place_lanes([(columns, 2 * depth * k, LANES - depth, 2 * depth)])
 
 
 def row_chunk(ref, f, start):
@@ -251,11 +261,6 @@
     return jnp.where(even, high, low), jnp.where(even, low, high)
 
 
-def send_sides(pair, halo_rows):
-    for ref, value in zip(pair, in_order("girth", halo_rows[0:8], halo_rows[8:16])):
-        ref[...] = value
-
-
 def send_ends(pair, low, high):
     for ref in pair:
         ref[...] = jnp.zeros(ref.shape, F32)
@@ -289,14 +294,14 @@
 
 def start_kernel(
     disp_in, stress_in, thickness_in, from_in, to_in, stiff_in,
-    payload, sec_first, sec_second, girth_first, girth_second,
+    payload, sec_first, sec_second, sides,
     column_marks, row_marks, picked, spring,
     disp, stress_left, stress_right, stress_top, stress_bottom, thickness,
     weld_from, weld_to, weld_stiff, done,
 ):
     rows, cols = thickness.shape
     _, slots, devices = weld_from.shape
-    sec_pair, girth_pair = (sec_first, sec_second), (girth_first, girth_second)
+    sec_pair = (sec_first, sec_second)
     copies = fetch(
         done,
         [
@@ -346,13 +351,11 @@
     for copy in copies[4:]:
         copy.wait()
     plate = thickness[...].astype(F32) * (1.0 / spacing_mm)
-    columns = []
-    for f in range(RESULTS + 1):
-        left = stress_left[f] if f < RESULTS else plate[:, 0:LANES]
-        right = stress_right[f] if f < RESULTS else plate[:, cols - LANES :]
-        columns.append((left, 0, f // 5, 2 + f % 5))
-        columns.append((right, LANES - 1, f // 5, 10 + f % 5))
-    send_sides(girth_pair, edge_rows(columns))
+    sides[...] = edge_rows(
+        [stress_left[f] for f in range(RESULTS)] + [plate[:, 0:LANES]],
+        [stress_right[f] for f in range(RESULTS)] + [plate[:, cols - LANES :]],
+        1,
+    )
     send_joints(payload, near_out, far_out, [])
     send_ends(
         sec_pair,
@@ -372,7 +375,7 @@
 
 
 def load_velocity(vel_ext, velocity, incoming, above, below, left, right):
-    first, second = edge_columns(left, right)
+    columns = edge_columns(left, right, 2, velocity.shape[1])
     row = lax.broadcasted_iota(jnp.int32, (8, LANES), 0)
     corner_tiles = [
         jnp.broadcast_to(jnp.where(inside, corner_of(incoming, device), 0.0), (8, LANES))
@@ -380,16 +383,12 @@
     ]
     for f in range(FIELDS):
         vel_ext[f, : velocity.shape[1], : velocity.shape[2]] = velocity[f]
-        sides = edge_block(
-            [
-                (first, 2 + f, LANES - 2),
-                (second, 2 + f, LANES - 1),
-                (first, 10 + f, 0),
-                (second, 10 + f, 1),
-            ]
-        )
-        upper = edge_block([(corner_tiles[0], CORNER_LANE + f, LANES - 1), (corner_tiles[1], CORNER_LANE + f, 0)])
-        lower = edge_block([(corner_tiles[2], CORNER_LANE + f, LANES - 1), (corner_tiles[3], CORNER_LANE + f, 0)])
+        sides = side_block(columns, f, 2)
+        corner_lane = CORNER_LANE + f
+        upper, lower = [
+            place_lanes([(low, corner_lane, LANES - 1, 1), (high, corner_lane, 0, 1)])
+            for low, high in (corner_tiles[0:2], corner_tiles[2:4])
+        ]
         corner = jnp.where(row == 0, lower, jnp.where(row == 7, upper, 0.0))
         fill_halo(
             vel_ext, f, above[2 * f : 2 * f + 2, :], below[2 * f : 2 * f + 2, :], sides, corner
@@ -398,23 +397,29 @@
 
 def load_stress(stress_ext, plate_ext, thickness, above, below, left, right):
     rows, cols = thickness.shape
-    halves = edge_columns(left, right)
+    columns = edge_columns(left, right, 1, rows)
     plate_ext[0, :rows, :cols] = thickness[...].astype(F32) * (1.0 / spacing_mm)
     empty = jnp.zeros((PAD_ROWS, LANES), F32)
     for f in range(RESULTS + 1):
-        lane = 2 + f % 5
-        half = halves[f // 5]
-        sides = edge_block([(half, lane, LANES - 1), (half, 8 + lane, 0)])
+        sides = side_block(columns, f, 1)
         ref, k = (stress_ext, f) if f < RESULTS else (plate_ext, 0)
         fill_halo(ref, k, above[f : f + 1, :], below[f : f + 1, :], sides, empty)
+
+
+def set_rates(linear, angular, plate):
+    rate = time_step / plate
+    linear[...] = rate
+    angular[...] = (12.0 * rate) / (1.0 + plate * plate)
 
 
 def joint_kernel(first, *refs):
     far = refs[: 4 + first]
     incoming, column_marks, row_marks, picked, spring = refs[4 + first : 9 + first]
     refs = refs[9 + first :]
+    if not first:
+        plate_ext, refs = refs[0], refs[1:]
     near = refs[: 4 + first]
-    weld = refs[4 + first]
+    weld, linear, angular = refs[4 + first : 7 + first]
     copies = fetch(refs[-1], list(zip(far, near)))
     devices = incoming.shape[0] // 2
     total = picked.shape[1]
@@ -425,7 +430,7 @@
         other.append(expand(high, by_device, by_place) + expand(low, by_device, by_place))
     if first:
         stiffness = jnp.concatenate([spring[0:1, :], other[1][5:6]], axis=1)
-        spring_out = refs[5 + first]
+        spring_out = refs[8]
         spring_out[...] = jnp.broadcast_to(stiffness, spring_out.shape)
     else:
         stiffness = spring[0:1, :]
@@ -433,8 +438,13 @@
     scale = jnp.where(field < 3, 1.0, rotary_share) * stiffness
     pulls = scale * (jnp.concatenate(other, axis=1) - picked[...])
     weld[...] = spread(pulls, column_marks[...], row_marks[...])
+    rows, cols = linear.shape
+    if not first:
+        set_rates(linear, angular, plate_ext[0, :rows, :cols])
     for copy in copies:
         copy.wait()
+    if first:
+        set_rates(linear, angular, near[-1][...].astype(F32) * (1.0 / spacing_mm))
 
 
 def step_kernel(first, last, *refs):
@@ -443,17 +453,17 @@
         thickness, refs = refs[4], refs[5:]
     else:
         refs = refs[4:]
-    (weld, incoming, sec_second, sec_first, girth_second, girth_first,
-     column_marks, row_marks, picked) = refs[:9]
-    out = refs[9:]
+    (weld, linear, angular, incoming, sec_second, sec_first, girth_second, girth_first,
+     column_marks, row_marks, picked) = refs[:11]
+    out = refs[11:]
     if not first:
         plate_ext, out = out[0], out[1:]
     stress_out, velocity_out, disp_out = out[:3]
     out = out[3:]
     if first:
         plate_ext, out = out[0], out[1:]
-    girth_pair, sec_pair = out[0:2], out[2:4]
-    out = out[4:]
+    sides, sec_pair = out[0], out[1:3]
+    out = out[3:]
     if not last:
         picked_out, payload = out[:2]
         out = out[2:]
@@ -502,14 +512,12 @@
 
     for start in range(0, rows, 8):
         part = slice(start, start + 8)
-        plate = plate_ext[0, part, :cols]
-        linear = time_step / plate
-        angular = (12.0 * linear) / (1.0 + plate * plate)
+        rates = [linear[part, :]] * 3 + [angular[part, :]] * 2
         force = force_chunk(res_ext, start, cols)
         force[2] = force[2] + pressure[part, :]
         for f in range(FIELDS):
             joined = force[f] + weld[f * rows + start : f * rows + start + 8, :]
-            speed = velocity_in[f, part, :] + (linear if f < 3 else angular) * joined
+            speed = velocity_in[f, part, :] + rates[f] * joined
             velocity[f, part, :] = speed
             disp[f, part, :] = disp_in[f, part, :] + time_step * speed
         if start % 32 == 24:
@@ -518,12 +526,10 @@
                 send(source.at[:, done, :], target.at[:, done, :])
 
     ends = (cols - LANES, cols)
+    left_lanes = [velocity[f, :, 0:LANES] for f in range(FIELDS)]
+    right_lanes = [velocity[f, :, ends[0] : ends[1]] for f in range(FIELDS)]
+    sides[...] = edge_rows(left_lanes, right_lanes, 1 if last else 2)
     if last:
-        columns = []
-        for f in range(FIELDS):
-            columns.append((velocity[f, :, 0:LANES], 0, 0, f))
-            columns.append((velocity[f, :, ends[0] : ends[1]], LANES - 1, 0, 8 + f))
-        send_sides(girth_pair, edge_rows(columns))
         send_ends(
             sec_pair,
             [velocity[f, 0:1, :] for f in range(FIELDS)],
@@ -536,13 +542,6 @@
     picked_out[...] = jnp.concatenate(values + [values[0]] * 3, axis=0)
     near_out = collapse([value[:, :half] for value in values], by_device, by_place)
     far_out = collapse([value[:, half:] for value in values], by_device, by_place)
-    columns = []
-    for f in range(FIELDS):
-        left_lanes = velocity[f, :, 0:LANES]
-        right_lanes = velocity[f, :, ends[0] : ends[1]]
-        for depth in (0, 1):
-            columns.append((left_lanes, depth, depth, 2 + f))
-            columns.append((right_lanes, LANES - 2 + depth, depth, 10 + f))
     corners = []
     lane = lax.broadcasted_iota(jnp.int32, (8, LANES), 1)
     for row in (0, rows - 1):
@@ -555,7 +554,6 @@
                 target = CORNER_LANE + f
                 value = jnp.where(lane == target, pltpu.roll(part, (target - source) % LANES, 1), value)
             corners.append(jnp.broadcast_to(value[row % 8 : row % 8 + 1], (8, LANES)))
-    send_sides(girth_pair, edge_rows(columns))
     send_joints(payload, near_out, far_out, corners)
     send_ends(
         sec_pair,
@@ -593,11 +591,11 @@
         send(disp, disp_out)
     above, below = in_order("sec", sec_first[...], sec_second[...])
     left, right = in_order("girth", girth_first[...], girth_second[...])
-    first, _ = edge_columns(left, right)
+    columns = edge_columns(left, right, 1, rows)
     empty = jnp.zeros((PAD_ROWS, LANES), F32)
     for k, f in enumerate(fields):
         vel_ext[k, :rows, :cols] = velocity[f]
-        sides = edge_block([(first, f, LANES - 1), (first, 8 + f, 0)])
+        sides = side_block(columns, f, 1)
         fill_halo(vel_ext, k, above[f : f + 1, :], below[f : f + 1, :], sides, empty)
     parts = []
     for start in range(0, rows, 8):
@@ -677,7 +675,7 @@
         lax.ppermute(value, axis, [(i, i ^ step) for i in range(count)])
         for step in range(count - 1, 0, -1)
     ]
-    parts = [value] + parts[::-1]
+    parts = parts + [value]
     while len(parts) > 1:
         parts = [a + b for a, b in zip(parts[0::2], parts[1::2])]
     return parts[0]
@@ -700,7 +698,7 @@
 
     vmem_bytes = 8 * 1024 * 1024 + total * VMEM_PER_SLOT
     message = (devices * 2, LANES)
-    edge = (8, LANES)
+    edge = (SIDE_ROWS, LANES)
     strip = (16, cols)
     block = (FIELDS, rows, cols)
     stress_shape = (RESULTS, rows + PAD_ROWS, cols + LANES)
@@ -708,12 +706,12 @@
     slot_rows = (8, total)
     scratch = [(stress_shape, F32), ((FIELDS, rows + PAD_ROWS, cols + LANES), F32)]
 
-    (payload, sec_first, sec_second, girth_first, girth_second,
+    (payload, sec_first, sec_second, sides,
      column_marks, row_marks, picked, spring) = call(
         start_kernel,
         vmem_bytes,
         [
-            (message, F32), (strip, F32), (strip, F32), (edge, F32), (edge, F32),
+            (message, F32), (strip, F32), (strip, F32), (edge, F32),
             ((cols, total), BF16), ((rows, total), BF16), (slot_rows, F32), ((8, total // 2), F32),
         ],
         [
@@ -732,25 +730,26 @@
         first, last = step == 0, step == STEPS - 1
         incoming = exchange(payload)
         ends = swap((sec_first, sec_second), "sec", False)
-        sides = swap((girth_first, girth_second), "girth", True)
+        sides = swap((sides, sides), "girth", True)
         state = [stress, velocity, displacement, pressure] + [thickness] * first
-        *state, weld = call(
+        *state, weld, linear, angular = call(
             functools.partial(joint_kernel, first),
             vmem_bytes,
             [(value.shape, value.dtype) for value in state]
-            + [((FIELDS * rows, cols), F32)]
+            + [((FIELDS * rows, cols), F32), ((rows, cols), F32), ((rows, cols), F32)]
             + [(slot_rows, F32)] * first,
             [],
             *state, incoming, column_marks, row_marks, picked, spring,
+            *([] if first else [plate]),
             far=len(state),
-            kept_out=len(state) + 1,
+            kept_out=len(state) + 3,
             copies=(len(state),),
         )
         if first:
-            spring, weld, state = weld, state[-1], state[:-1]
+            *state, weld, linear, angular, spring = *state, weld, linear, angular
         halo = (8, cols) if last else strip
         outs = [(stress_shape, F32), (block, F32), (block, F32)] + [(plate_shape, F32)] * first
-        outs += [(edge, F32), (edge, F32), (halo, F32), (halo, F32)]
+        outs += [(edge, F32), (halo, F32), (halo, F32)]
         if not last:
             outs += [(slot_rows, F32), (message, F32)]
         results = call(
@@ -758,9 +757,9 @@
             vmem_bytes,
             outs,
             scratch + ([] if last else outs[:3]),
-            *state, weld, incoming, *ends, *sides, column_marks, row_marks, picked,
+            *state, weld, linear, angular, incoming, *ends, *sides, column_marks, row_marks, picked,
             *([] if first else [plate]),
-            kept=len(state) + 1,
+            kept=len(state) + 3,
             far_out=0 if last else 3,
             kept_out=3 if last else 0,
             copies=(3 + 2 * (rows // 32),),
@@ -769,12 +768,12 @@
         results = results[3:]
         if first:
             plate, results = results[0], results[1:]
-        girth_first, girth_second, sec_first, sec_second = results[:4]
+        sides, sec_first, sec_second = results[:3]
         if not last:
-            picked, payload = results[4:]
+            picked, payload = results[3:]
 
     ends = swap((sec_first, sec_second), "sec", False)
-    sides = swap((girth_first, girth_second), "girth", True)
+    sides = swap((sides, sides), "girth", True)
     membrane, partial_moment = call(
         functools.partial(final_kernel, True),
         vmem_bytes,

time: 68.4 us -> 67.6 us (0.988)
  transfers between devices with their start and end apart: 22 -> 22, of which waited for: 6 -> 5; matrix products, arithmetic and copies ran while one was open for 0% -> 0% of each run, Pallas kernels for 10% -> 11%
where the time goes in v15:
time: 67.6 us; the launch traced here: 67.1 us
  starting transfers between devices  42.5 us (63%)
  Pallas kernels  19.7 us (29%)
  waiting for transfers between devices  3.47 us (5%)
  between operations  0.9 us (1%)
    ppermute x16, starting transfers between devices, swap(): lax.ppermute(value, axis, couples + [(j, i) for i, j in couples])  25.9 us
    pallas_call x9, Pallas kernels, call(): pl.pallas_call(kernel, out_shape=results, in_specs=[away] * far + [whole]...  19.7 us
    all_to_all x3, starting transfers between devices, exchange(): blocks = lax.all_to_all(blocks, ('sec', 'girth'), 0, 0, tiled=True)  14.7 us
    ppermute x3, starting transfers between devices, sum_over(): lax.ppermute(value, axis, [(i, i ^ step) for i in range(count)])  1.92 us
    ppermute x16, waiting for transfers between devices, swap(): lax.ppermute(value, axis, couples + [(j, i) for i, j in couples])  1.68 us
    all_to_all x3, waiting for transfers between devices, exchange(): blocks = lax.all_to_all(blocks, ('sec', 'girth'), 0, 0, tiled=True)  1.36 us
  transfers between devices with their start and end apart: 22, of which 5 were waited for; matrix products, arithmetic and copies ran while one was open for 0% of the time, Pallas kernels for 11%

profile of v15, /device:TPU:0, one launch (start us, length us, event | category | flops | bytes accessed | tf_op | source)
XLA Modules:
  0.0 67.1 jit_solution(7696437672314415892)
XLA Ops:
  0.6 3.0 %shard_map.111 = (f32[64,128]{1,0:T(8,128)}, f32[16,512]{1,0:T(8,128)S(1)}, f32[16,512]{1,0:T(8,128)S(1)}, f32[24,128]{1,0:T(8,128)S(1)}, bf16[512,1024]{1,0:T(8...) custom-call(f32[5,64,512]{2,1,0:T(8,128)} %refs_2_.1, ...), custom_call_target="tpu_custom_call" | custom-call | tf_op jit(solution)/shard_map/pallas_call | solution.py:649
  3.7 7.3 %all-to-all-start = ((f32[32,2,128]{2,1,0:T(2,128)}), f32[32,2,128]{2,1,0:T(2,128)S(1)}, u32[]{:S(2)}, u32[]{:S(2)}) async-start(f32[32,2,128]{2,1,0:T(2,128)} %bitcast.3), calls=%async_computation | async-start | bytes 65536 | tf_op jit(solution)/shard_map/all_to_all | solution.py:686
  11.0 0.7 collective-permute-start
  11.7 4.5 %collective-permute-start.1 = (f32[16,512]{1,0:T(8,128)S(1)}, f32[16,512]{1,0:T(8,128)S(1)}, u32[]{:S(2)}, u32[]{:S(2)}) collective-permute-start(f32[16,512]{1,0:T(8,128)S(1)} %get-tuple-element.77), channel_id=1, source_target_pairs={{0,4},{8,12},{16,20},{24,28},{4,0},{12,8},{20,16},{28,24},{1,5},{9... | collective-permute-start | bytes 98312 | tf_op jit(solution)/shard_map/ppermute | solution.py:666
  16.9 0.9 %collective-permute-start.3 = (f32[24,128]{1,0:T(8,128)S(1)}, f32[24,128]{1,0:T(8,128)S(1)}, u32[]{:S(2)}, u32[]{:S(2)}) collective-permute-start(f32[24,128]{1,0:T(8,128)S(1)} %get-tuple-element.78), channel_id=1, source_target_pairs={{0,1},{2,3},{1,0},{3,2},{4,5},{6,7},{5,4},{7,6},{8,9},{10,11},{9,8... | collective-permute-start | bytes 36872 | tf_op jit(solution)/shard_map/ppermute | solution.py:666
  18.2 1.7 %shard_map.112 = (f32[8,64,512]{2,1,0:T(8,128)S(1)}, f32[5,64,512]{2,1,0:T(8,128)S(1)}, f32[5,64,512]{2,1,0:T(8,128)S(1)}, f32[64,512]{1,0:T(8,128)S(1)}, s32[64...) custom-call(f32[8,64,512]{2,1,0:T(8,128)} %refs_0_.1, ...), custom_call_target="tpu_custom_call" | custom-call | tf_op jit(solution)/shard_map/pallas_call | solution.py:649
  20.0 2.9 %shard_map.113 = (f32[8,72,640]{2,1,0:T(8,128)}, f32[5,64,512]{2,1,0:T(8,128)}, f32[5,64,512]{2,1,0:T(8,128)}, f32[1,72,640]{2,1,0:T(8,128)S(1)}, f32[24,128]{1,...) custom-call(f32[8,64,512]{2,1,0:T(8,128)S(1)} %get-tuple-element.68.r, ...), custom_call_target="tpu_custom_call" | custom-call | tf_op jit(solution)/shard_map/pallas_call | solution.py:649
  22.9 3.9 %all-to-all-start.1 = ((f32[32,2,128]{2,1,0:T(2,128)}), f32[32,2,128]{2,1,0:T(2,128)S(1)}, u32[]{:S(2)}, u32[]{:S(2)}) async-start(f32[32,2,128]{2,1,0:T(2,128)} %bitcast.5), calls=%async_computation.1 | async-start | bytes 65536 | tf_op jit(solution)/shard_map/all_to_all | solution.py:686
  26.8 0.7 collective-permute-start.4
  27.5 4.5 %collective-permute-start.5 = (f32[16,512]{1,0:T(8,128)S(1)}, f32[16,512]{1,0:T(8,128)S(1)}, u32[]{:S(2)}, u32[]{:S(2)}) collective-permute-start(f32[16,512]{1,0:T(8,128)S(1)} %get-tuple-element.94), channel_id=1, source_target_pairs={{0,4},{8,12},{16,20},{24,28},{4,0},{12,8},{20,16},{28,24},{1,5},{9... | collective-permute-start | bytes 98312 | tf_op jit(solution)/shard_map/ppermute | solution.py:666
  32.7 0.9 %collective-permute-start.7 = (f32[24,128]{1,0:T(8,128)S(1)}, f32[24,128]{1,0:T(8,128)S(1)}, u32[]{:S(2)}, u32[]{:S(2)}) collective-permute-start(f32[24,128]{1,0:T(8,128)S(1)} %get-tuple-element.95), channel_id=1, source_target_pairs={{0,1},{2,3},{1,0},{3,2},{4,5},{6,7},{5,4},{7,6},{8,9},{10,11},{9,8... | collective-permute-start | bytes 36872 | tf_op jit(solution)/shard_map/ppermute | solution.py:666
  34.0 2.1 %shard_map.114 = (f32[8,72,640]{2,1,0:T(8,128)S(1)}, f32[5,64,512]{2,1,0:T(8,128)S(1)}, f32[5,64,512]{2,1,0:T(8,128)S(1)}, f32[64,512]{1,0:T(8,128)S(1)}, f32[32...) custom-call(f32[8,72,640]{2,1,0:T(8,128)} %get-tuple-element.79.refs_0_, ...), custom_call_target="tpu_custom_call" | custom-call | tf_op jit(solution)/shard_map/pallas_call | solution.py:649
  36.1 3.5 %shard_map.115 = (f32[8,72,640]{2,1,0:T(8,128)}, f32[5,64,512]{2,1,0:T(8,128)}, f32[5,64,512]{2,1,0:T(8,128)}, f32[24,128]{1,0:T(8,128)S(1)}, f32[16,512]{1,0:T(...) custom-call(f32[8,72,640]{2,1,0:T(8,128)S(1)} %get-tuple-element.86.refs_0_, ...), custom_call_target="tpu_custom_call" | custom-call | tf_op jit(solution)/shard_map/pallas_call | solution.py:649
  39.7 3.6 %all-to-all-start.2 = ((f32[32,2,128]{2,1,0:T(2,128)}), f32[32,2,128]{2,1,0:T(2,128)S(1)}, u32[]{:S(2)}, u32[]{:S(2)}) async-start(f32[32,2,128]{2,1,0:T(2,128)} %bitcast.7), calls=%async_computation.2 | async-start | bytes 65536 | tf_op jit(solution)/shard_map/all_to_all | solution.py:686
  43.9 4.5 %collective-permute-start.9 = (f32[16,512]{1,0:T(8,128)S(1)}, f32[16,512]{1,0:T(8,128)S(1)}, u32[]{:S(2)}, u32[]{:S(2)}) collective-permute-start(f32[16,512]{1,0:T(8,128)S(1)} %get-tuple-element.109), channel_id=1, source_target_pairs={{0,4},{8,12},{16,20},{24,28},{4,0},{12,8},{20,16},{28,24},{1,5},{9... | collective-permute-start | bytes 98312 | tf_op jit(solution)/shard_map/ppermute | solution.py:666
  49.1 0.9 %collective-permute-start.11 = (f32[24,128]{1,0:T(8,128)S(1)}, f32[24,128]{1,0:T(8,128)S(1)}, u32[]{:S(2)}, u32[]{:S(2)}) collective-permute-start(f32[24,128]{1,0:T(8,128)S(1)} %get-tuple-element.110), channel_id=1, source_target_pairs={{0,1},{2,3},{1,0},{3,2},{4,5},{6,7},{5,4},{7,6},{8,9},{10,11},{9,8... | collective-permute-start | bytes 36872 | tf_op jit(solution)/shard_map/ppermute | solution.py:666
  50.5 2.0 %shard_map.116 = (f32[8,72,640]{2,1,0:T(8,128)S(1)}, f32[5,64,512]{2,1,0:T(8,128)S(1)}, f32[5,64,512]{2,1,0:T(8,128)S(1)}, f32[64,512]{1,0:T(8,128)S(1)}, f32[32...) custom-call(f32[8,72,640]{2,1,0:T(8,128)} %get-tuple-element.96.refs_0_, ...), custom_call_target="tpu_custom_call" | custom-call | tf_op jit(solution)/shard_map/pallas_call | solution.py:649
  52.6 1.9 %shard_map.117 = (f32[8,72,640]{2,1,0:T(8,128)S(1)}, f32[5,64,512]{2,1,0:T(8,128)S(1)}, f32[5,64,512]{2,1,0:T(8,128)S(1)}, f32[24,128]{1,0:T(8,128)S(1)}, f32[8,512]{1,0:T(8,128)S(1)}, /*index=5*/f32[8,512]{1,0:T(8,128)S(1)}) custom-call(f32[8,72,640]{2,1,0:T(8,128)S(1)} %get-tuple-element.101.refs_0_, f32[5,64,512]{2,1,0:T(8,128)S(1)} %get-tuple-element.102.refs_1_, ...), custom_call_target="tpu_custom_call" | custom-call | tf_op jit(solution)/shard_map/pallas_call | solution.py:649
  55.9 4.2 %collective-permute-start.13 = (f32[8,512]{1,0:T(8,128)S(1)}, f32[8,512]{1,0:T(8,128)S(1)}, u32[]{:S(2)}, u32[]{:S(2)}) collective-permute-start(f32[8,512]{1,0:T(8,128)S(1)} %get-tuple-element.114), channel_id=1, source_target_pairs={{0,4},{8,12},{16,20},{24,28},{4,0},{12,8},{20,16},{28,24},{1,5},{9... | collective-permute-start | bytes 49160 | tf_op jit(solution)/shard_map/ppermute | solution.py:666
  60.1 1.6 %collective-permute-done.13.refs_3_.refs_5_ = f32[8,512]{1,0:T(8,128)S(1)} collective-permute-done((f32[8,512]{1,0:T(8,128)S(1)}, f32[8,512]{1,0:T(8,128)S(1)}, u32[]{:S(2)}, u32[]{:S(2)}) %collective-permute-start.13) | collective-permute-done | bytes 16416 | tf_op jit(solution)/shard_map/ppermute | solution.py:666
  61.8 1.1 %shard_map.118 = (f32[8,64,512]{2,1,0:T(8,128)}, f32[1,64]{1,0:T(1,128)S(1)}) custom-call(f32[8,72,640]{2,1,0:T(8,128)S(1)} %get-tuple-element.111.refs_0_.refs_1_, f32[5,64,512]{2,1,0:T(8,128)S(1)} %get-tuple-element.112.refs_1_.refs_2_, f32[8,512]{1,0:T(8,128)S(1)} %collective-permute-done.12.refs_2_.refs_4_, ...), custom_call_target="tpu_custom_call" | custom-call | tf_op jit(solution)/shard_map/pallas_call | solution.py:649
  63.0 1.2 %collective-permute-start.17 = (f32[1,64]{1,0:T(1,128)S(1)}, f32[1,64]{1,0:T(1,128)S(1)}, u32[]{:S(2)}, u32[]{:S(2)}) collective-permute-start(f32[1,64]{1,0:T(1,128)S(1)} %get-tuple-element.121), channel_id=1, source_target_pairs={{0,2},{1,3},{2,0},{3,1},{4,6},{5,7},{6,4},{7,5},{8,10},{9,11},{10,... | collective-permute-start | bytes 776 | tf_op jit(solution)/shard_map/ppermute | solution.py:675
  64.2 0.7 collective-permute-start.18
  64.9 1.3 %shard_map.119 = (f32[8,64,512]{2,1,0:T(8,128)}, f32[5,64,512]{2,1,0:T(8,128)}, f32[5,64,512]{2,1,0:T(8,128)}) custom-call(f32[8,64,512]{2,1,0:T(8,128)} %get-tuple-element.116.refs_0_, f32[8,72,640]{2,1,0:T(8,128)S(1)} %get-tuple-element.111.refs_0_.refs_1_, f32[5,64,512]{2,1,0:T(8,128)S(1)} %get-tuple-element.112.refs_1_.refs_2_, ...), custom_call_target="tpu_custom_call", output_to_operand_aliasing={{0}: (0, {})} | custom-call | tf_op jit(solution)/shard_map/pallas_call | solution.py:649
  (32 shorter events, 6.4 us)
Async XLA Ops:
  3.7 14.6 %all-to-all-start = ((f32[32,2,128]{2,1,0:T(2,128)}), f32[32,2,128]{2,1,0:T(2,128)S(1)}, u32[]{:S(2)}, u32[]{:S(2)}) async-start(f32[32,2,128]{2,1,0:T(2,128)} %bitcast.3), calls=%async_computation | async-start | bytes 65536 | tf_op jit(solution)/shard_map/all_to_all | solution.py:686
  11.0 9.0 %collective-permute-start = (f32[16,512]{1,0:T(8,128)S(1)}, f32[16,512]{1,0:T(8,128)S(1)}, u32[]{:S(2)}, u32[]{:S(2)}) collective-permute-start(f32[16,512]{1,0:T(8,128)S(1)} %get-tuple-element.76), channel_id=1, source_target_pairs={{4,8},{12,16},{20,24},{8,4},{16,12},{24,20},{5,9},{13,17},{21,25},... | collective-permute-start | bytes 98312 | tf_op jit(solution)/shard_map/ppermute | solution.py:666
  11.7 8.4 %collective-permute-start.1 = (f32[16,512]{1,0:T(8,128)S(1)}, f32[16,512]{1,0:T(8,128)S(1)}, u32[]{:S(2)}, u32[]{:S(2)}) collective-permute-start(f32[16,512]{1,0:T(8,128)S(1)} %get-tuple-element.77), channel_id=1, source_target_pairs={{0,4},{8,12},{16,20},{24,28},{4,0},{12,8},{20,16},{28,24},{1,5},{9... | collective-permute-start | bytes 98312 | tf_op jit(solution)/shard_map/ppermute | solution.py:666
  16.2 3.8 %collective-permute-start.2 = (f32[24,128]{1,0:T(8,128)S(1)}, f32[24,128]{1,0:T(8,128)S(1)}, u32[]{:S(2)}, u32[]{:S(2)}) collective-permute-start(f32[24,128]{1,0:T(8,128)S(1)} %get-tuple-element.78), channel_id=1, source_target_pairs={{1,2},{3,0},{2,1},{0,3},{5,6},{7,4},{6,5},{4,7},{9,10},{11,8},{10,... | collective-permute-start | bytes 36872 | tf_op jit(solution)/shard_map/ppermute | solution.py:666
  16.9 3.1 %collective-permute-start.3 = (f32[24,128]{1,0:T(8,128)S(1)}, f32[24,128]{1,0:T(8,128)S(1)}, u32[]{:S(2)}, u32[]{:S(2)}) collective-permute-start(f32[24,128]{1,0:T(8,128)S(1)} %get-tuple-element.78), channel_id=1, source_target_pairs={{0,1},{2,3},{1,0},{3,2},{4,5},{6,7},{5,4},{7,6},{8,9},{10,11},{9,8... | collective-permute-start | bytes 36872 | tf_op jit(solution)/shard_map/ppermute | solution.py:666
  22.9 11.1 %all-to-all-start.1 = ((f32[32,2,128]{2,1,0:T(2,128)}), f32[32,2,128]{2,1,0:T(2,128)S(1)}, u32[]{:S(2)}, u32[]{:S(2)}) async-start(f32[32,2,128]{2,1,0:T(2,128)} %bitcast.5), calls=%async_computation.1 | async-start | bytes 65536 | tf_op jit(solution)/shard_map/all_to_all | solution.py:686
  26.8 9.3 %collective-permute-start.4 = (f32[16,512]{1,0:T(8,128)S(1)}, f32[16,512]{1,0:T(8,128)S(1)}, u32[]{:S(2)}, u32[]{:S(2)}) collective-permute-start(f32[16,512]{1,0:T(8,128)S(1)} %get-tuple-element.93), channel_id=1, source_target_pairs={{4,8},{12,16},{20,24},{8,4},{16,12},{24,20},{5,9},{13,17},{21,25},... | collective-permute-start | bytes 98312 | tf_op jit(solution)/shard_map/ppermute | solution.py:666
  27.5 8.7 %collective-permute-start.5 = (f32[16,512]{1,0:T(8,128)S(1)}, f32[16,512]{1,0:T(8,128)S(1)}, u32[]{:S(2)}, u32[]{:S(2)}) collective-permute-start(f32[16,512]{1,0:T(8,128)S(1)} %get-tuple-element.94), channel_id=1, source_target_pairs={{0,4},{8,12},{16,20},{24,28},{4,0},{12,8},{20,16},{28,24},{1,5},{9... | collective-permute-start | bytes 98312 | tf_op jit(solution)/shard_map/ppermute | solution.py:666
  32.0 4.1 %collective-permute-start.6 = (f32[24,128]{1,0:T(8,128)S(1)}, f32[24,128]{1,0:T(8,128)S(1)}, u32[]{:S(2)}, u32[]{:S(2)}) collective-permute-start(f32[24,128]{1,0:T(8,128)S(1)} %get-tuple-element.95), channel_id=1, source_target_pairs={{1,2},{3,0},{2,1},{0,3},{5,6},{7,4},{6,5},{4,7},{9,10},{11,8},{10,... | collective-permute-start | bytes 36872 | tf_op jit(solution)/shard_map/ppermute | solution.py:666
  32.7 3.5 %collective-permute-start.7 = (f32[24,128]{1,0:T(8,128)S(1)}, f32[24,128]{1,0:T(8,128)S(1)}, u32[]{:S(2)}, u32[]{:S(2)}) collective-permute-start(f32[24,128]{1,0:T(8,128)S(1)} %get-tuple-element.95), channel_id=1, source_target_pairs={{0,1},{2,3},{1,0},{3,2},{4,5},{6,7},{5,4},{7,6},{8,9},{10,11},{9,8... | collective-permute-start | bytes 36872 | tf_op jit(solution)/shard_map/ppermute | solution.py:666
  39.7 10.8 %all-to-all-start.2 = ((f32[32,2,128]{2,1,0:T(2,128)}), f32[32,2,128]{2,1,0:T(2,128)S(1)}, u32[]{:S(2)}, u32[]{:S(2)}) async-start(f32[32,2,128]{2,1,0:T(2,128)} %bitcast.7), calls=%async_computation.2 | async-start | bytes 65536 | tf_op jit(solution)/shard_map/all_to_all | solution.py:686
  43.2 9.3 %collective-permute-start.8 = (f32[16,512]{1,0:T(8,128)S(1)}, f32[16,512]{1,0:T(8,128)S(1)}, u32[]{:S(2)}, u32[]{:S(2)}) collective-permute-start(f32[16,512]{1,0:T(8,128)S(1)} %get-tuple-element.108), channel_id=1, source_target_pairs={{4,8},{12,16},{20,24},{8,4},{16,12},{24,20},{5,9},{13,17},{21,25},... | collective-permute-start | bytes 98312 | tf_op jit(solution)/shard_map/ppermute | solution.py:666
  43.9 8.7 %collective-permute-start.9 = (f32[16,512]{1,0:T(8,128)S(1)}, f32[16,512]{1,0:T(8,128)S(1)}, u32[]{:S(2)}, u32[]{:S(2)}) collective-permute-start(f32[16,512]{1,0:T(8,128)S(1)} %get-tuple-element.109), channel_id=1, source_target_pairs={{0,4},{8,12},{16,20},{24,28},{4,0},{12,8},{20,16},{28,24},{1,5},{9... | collective-permute-start | bytes 98312 | tf_op jit(solution)/shard_map/ppermute | solution.py:666
  48.5 4.1 %collective-permute-start.10 = (f32[24,128]{1,0:T(8,128)S(1)}, f32[24,128]{1,0:T(8,128)S(1)}, u32[]{:S(2)}, u32[]{:S(2)}) collective-permute-start(f32[24,128]{1,0:T(8,128)S(1)} %get-tuple-element.110), channel_id=1, source_target_pairs={{1,2},{3,0},{2,1},{0,3},{5,6},{7,4},{6,5},{4,7},{9,10},{11,8},{10,... | collective-permute-start | bytes 36872 | tf_op jit(solution)/shard_map/ppermute | solution.py:666
  49.1 3.4 %collective-permute-start.11 = (f32[24,128]{1,0:T(8,128)S(1)}, f32[24,128]{1,0:T(8,128)S(1)}, u32[]{:S(2)}, u32[]{:S(2)}) collective-permute-start(f32[24,128]{1,0:T(8,128)S(1)} %get-tuple-element.110), channel_id=1, source_target_pairs={{0,1},{2,3},{1,0},{3,2},{4,5},{6,7},{5,4},{7,6},{8,9},{10,11},{9,8... | collective-permute-start | bytes 36872 | tf_op jit(solution)/shard_map/ppermute | solution.py:666
  54.5 5.6 %collective-permute-start.14 = (f32[24,128]{1,0:T(8,128)S(1)}, f32[24,128]{1,0:T(8,128)S(1)}, u32[]{:S(2)}, u32[]{:S(2)}) collective-permute-start(f32[24,128]{1,0:T(8,128)S(1)} %get-tuple-element.115), channel_id=1, source_target_pairs={{1,2},{3,0},{2,1},{0,3},{5,6},{7,4},{6,5},{4,7},{9,10},{11,8},{10,... | collective-permute-start | bytes 36872 | tf_op jit(solution)/shard_map/ppermute | solution.py:666
  54.8 5.3 %collective-permute-start.15 = (f32[24,128]{1,0:T(8,128)S(1)}, f32[24,128]{1,0:T(8,128)S(1)}, u32[]{:S(2)}, u32[]{:S(2)}) collective-permute-start(f32[24,128]{1,0:T(8,128)S(1)} %get-tuple-element.115), channel_id=1, source_target_pairs={{0,1},{2,3},{1,0},{3,2},{4,5},{6,7},{5,4},{7,6},{8,9},{10,11},{9,8... | collective-permute-start | bytes 36872 | tf_op jit(solution)/shard_map/ppermute | solution.py:666
  55.2 4.9 %collective-permute-start.12 = (f32[8,512]{1,0:T(8,128)S(1)}, f32[8,512]{1,0:T(8,128)S(1)}, u32[]{:S(2)}, u32[]{:S(2)}) collective-permute-start(f32[8,512]{1,0:T(8,128)S(1)} %get-tuple-element.113), channel_id=1, source_target_pairs={{4,8},{12,16},{20,24},{8,4},{16,12},{24,20},{5,9},{13,17},{21,25},... | collective-permute-start | bytes 49160 | tf_op jit(solution)/shard_map/ppermute | solution.py:666
  55.9 5.9 %collective-permute-start.13 = (f32[8,512]{1,0:T(8,128)S(1)}, f32[8,512]{1,0:T(8,128)S(1)}, u32[]{:S(2)}, u32[]{:S(2)}) collective-permute-start(f32[8,512]{1,0:T(8,128)S(1)} %get-tuple-element.114), channel_id=1, source_target_pairs={{0,4},{8,12},{16,20},{24,28},{4,0},{12,8},{20,16},{28,24},{1,5},{9... | collective-permute-start | bytes 49160 | tf_op jit(solution)/shard_map/ppermute | solution.py:666
  62.9 3.3 %collective-permute-start.16 = (f32[1,64]{1,0:T(1,128)S(1)}, f32[1,64]{1,0:T(1,128)S(1)}, u32[]{:S(2)}, u32[]{:S(2)}) collective-permute-start(f32[1,64]{1,0:T(1,128)S(1)} %get-tuple-element.121), channel_id=1, source_target_pairs={{0,3},{1,2},{2,1},{3,0},{4,7},{5,6},{6,5},{7,4},{8,11},{9,10},{10,... | collective-permute-start | bytes 776 | tf_op jit(solution)/shard_map/ppermute | solution.py:675
  63.0 3.6 %collective-permute-start.17 = (f32[1,64]{1,0:T(1,128)S(1)}, f32[1,64]{1,0:T(1,128)S(1)}, u32[]{:S(2)}, u32[]{:S(2)}) collective-permute-start(f32[1,64]{1,0:T(1,128)S(1)} %get-tuple-element.121), channel_id=1, source_target_pairs={{0,2},{1,3},{2,0},{3,1},{4,6},{5,7},{6,4},{7,5},{8,10},{9,11},{10,... | collective-permute-start | bytes 776 | tf_op jit(solution)/shard_map/ppermute | solution.py:675
  64.2 2.4 %collective-permute-start.18 = (f32[1,64]{1,0:T(1,128)S(1)}, f32[1,64]{1,0:T(1,128)S(1)}, u32[]{:S(2)}, u32[]{:S(2)}) collective-permute-start(f32[1,64]{1,0:T(1,128)S(1)} %get-tuple-element.121), channel_id=1, source_target_pairs={{0,1},{1,0},{2,3},{3,2},{4,5},{5,4},{6,7},{7,6},{8,9},{9,8},{10,11... | collective-permute-start | bytes 776 | tf_op jit(solution)/shard_map/ppermute | solution.py:675

commit v16 on v15

--- a/solution.py
+++ b/solution.py
@@ -294,10 +294,10 @@
 
 def start_kernel(
     disp_in, stress_in, thickness_in, from_in, to_in, stiff_in,
-    payload, sec_first, sec_second, sides,
+    payload_out, sec_first, sec_second, sides,
     column_marks, row_marks, picked, spring,
     disp, stress_left, stress_right, stress_top, stress_bottom, thickness,
-    weld_from, weld_to, weld_stiff, done,
+    weld_from, weld_to, weld_stiff, payload, done,
 ):
     rows, cols = thickness.shape
     _, slots, devices = weld_from.shape
@@ -348,6 +348,9 @@
     near_out = collapse([value[:, :half] for value in values] + [stiff_row], by_device, by_place)
     far_out = collapse([value[:, half:] for value in values], by_device, by_place)
 
+    send_joints(payload, near_out, far_out, [])
+    message = pltpu.make_async_copy(payload, payload_out, done.at[len(copies)])
+    message.start()
     for copy in copies[4:]:
         copy.wait()
     plate = thickness[...].astype(F32) * (1.0 / spacing_mm)
@@ -356,12 +359,12 @@
         [stress_right[f] for f in range(RESULTS)] + [plate[:, cols - LANES :]],
         1,
     )
-    send_joints(payload, near_out, far_out, [])
     send_ends(
         sec_pair,
         [stress_top[f, 0:1, :] for f in range(RESULTS)] + [plate[0:1, :]],
         [stress_bottom[f, 7:8, :] for f in range(RESULTS)] + [plate[rows - 1 : rows, :]],
     )
+    message.wait()
 
 
 def fill_halo(ref, f, above, below, sides, corner):
@@ -460,18 +463,19 @@
         plate_ext, out = out[0], out[1:]
     stress_out, velocity_out, disp_out = out[:3]
     out = out[3:]
+    if not last:
+        payload_out, out = out[0], out[1:]
     if first:
         plate_ext, out = out[0], out[1:]
     sides, sec_pair = out[0], out[1:3]
     out = out[3:]
     if not last:
-        picked_out, payload = out[:2]
-        out = out[2:]
+        picked_out, out = out[0], out[1:]
     res_ext, vel_ext = out[:2]
     if last:
         stress_ext, velocity, disp = stress_out, velocity_out, disp_out
     else:
-        stress_ext, velocity, disp = out[2:5]
+        stress_ext, velocity, disp, payload = out[2:6]
     sent = out[-1]
 
     _, rows, cols = velocity.shape
@@ -528,8 +532,8 @@
     ends = (cols - LANES, cols)
     left_lanes = [velocity[f, :, 0:LANES] for f in range(FIELDS)]
     right_lanes = [velocity[f, :, ends[0] : ends[1]] for f in range(FIELDS)]
-    sides[...] = edge_rows(left_lanes, right_lanes, 1 if last else 2)
     if last:
+        sides[...] = edge_rows(left_lanes, right_lanes, 1)
         send_ends(
             sec_pair,
             [velocity[f, 0:1, :] for f in range(FIELDS)],
@@ -555,6 +559,8 @@
                 value = jnp.where(lane == target, pltpu.roll(part, (target - source) % LANES, 1), value)
             corners.append(jnp.broadcast_to(value[row % 8 : row % 8 + 1], (8, LANES)))
     send_joints(payload, near_out, far_out, corners)
+    send(payload, payload_out)
+    sides[...] = edge_rows(left_lanes, right_lanes, 2)
     send_ends(
         sec_pair,
         [velocity[f, 0:2, :] for f in range(FIELDS)],
@@ -568,14 +574,12 @@
     if membrane:
         stress, velocity = refs[:2]
         sec_second, sec_first, girth_second, girth_first, plate_ext, height = refs[2:8]
-        stress_out, moment = refs[8:10]
-        refs = refs[10:]
+        made, moment, vel_ext = refs[8:11]
     else:
-        stress, velocity, disp = refs[1:4]
+        stress, velocity, disp, ready = refs[:4]
         sec_second, sec_first, girth_second, girth_first, plate_ext = refs[4:9]
         stress_out, velocity_out, disp_out = refs[9:12]
-        refs = refs[12:]
-    made, vel_ext, sent = refs
+        made, vel_ext, sent = refs[12:]
     _, rows, cols = velocity.shape
     fields = range(0, 2) if membrane else range(2, FIELDS)
     kinds = range(0, 3) if membrane else range(3, RESULTS)
@@ -587,6 +591,7 @@
         sends.append(copy)
 
     if not membrane:
+        send(ready, stress_out.at[0:3])
         send(velocity, velocity_out)
         send(disp, disp_out)
     above, below = in_order("sec", sec_first[...], sec_second[...])
@@ -614,7 +619,7 @@
             chunk = plate_chunk(along_x, along_y, current[1:], chunk, plate)
         for k, value in enumerate(chunk):
             made[k, part, :] = value
-        if start % 16 == 8:
+        if not membrane and start % 16 == 8:
             done = slice(start - 8, start + 8)
             send(made.at[:, done, :], stress_out.at[kinds.start : kinds.stop, done, :])
     if membrane:
@@ -628,7 +633,7 @@
 
 def call(
     kernel, vmem_bytes, outs, scratch, *operands, far=0, kept=0, far_out=0, kept_out=0,
-    copies=(1,), alias=None,
+    copies=(1,),
 ):
     def placed(k, away, here):
         return pltpu.HBM if k < away else pltpu.VMEM if k < away + here else None
@@ -652,7 +657,6 @@
         in_specs=[away] * far + [whole] * (len(operands) - far),
         out_specs=[away] * far_out + [whole] * (len(outs) - far_out),
         scratch_shapes=scratch,
-        input_output_aliases=alias or {},
         compiler_params=pltpu.CompilerParams(vmem_limit_bytes=vmem_bytes),
     )(*operands)
 
@@ -718,12 +722,13 @@
             (block, F32), ((RESULTS, rows, LANES), F32), ((RESULTS, rows, LANES), F32),
             ((RESULTS, 8, cols), F32), ((RESULTS, 8, cols), F32), ((rows, cols), jnp.int32),
             ((1, slots, devices), jnp.int32), ((1, slots, devices), jnp.int32),
-            ((1, slots, devices), F32),
+            ((1, slots, devices), F32), (message, F32),
         ],
         displacement, stress, thickness,
         *[jnp.swapaxes(array, 1, 2) for array in (weld_from, weld_to, weld_stiff)],
         far=6,
-        copies=(9,),
+        far_out=1,
+        copies=(10,),
     )
     plate = None
     for step in range(STEPS):
@@ -747,54 +752,53 @@
         )
         if first:
             *state, weld, linear, angular, spring = *state, weld, linear, angular
-        halo = (8, cols) if last else strip
-        outs = [(stress_shape, F32), (block, F32), (block, F32)] + [(plate_shape, F32)] * first
-        outs += [(edge, F32), (halo, F32), (halo, F32)]
-        if not last:
-            outs += [(slot_rows, F32), (message, F32)]
+        outs = [(stress_shape, F32), (block, F32), (block, F32)] + [(message, F32)] * (not last)
+        own = [] if last else outs
+        outs = outs + [(plate_shape, F32)] * first
+        outs += [(edge, F32), (strip, F32), (strip, F32)] + [(slot_rows, F32)] * (not last)
         results = call(
             functools.partial(step_kernel, first, last),
             vmem_bytes,
             outs,
-            scratch + ([] if last else outs[:3]),
+            scratch + own,
             *state, weld, linear, angular, incoming, *ends, *sides, column_marks, row_marks, picked,
             *([] if first else [plate]),
             kept=len(state) + 3,
-            far_out=0 if last else 3,
+            far_out=0 if last else 4,
             kept_out=3 if last else 0,
-            copies=(3 + 2 * (rows // 32),),
+            copies=(4 + 2 * (rows // 32),),
         )
         stress, velocity, displacement = results[:3]
         results = results[3:]
+        if not last:
+            payload, results = results[0], results[1:]
         if first:
             plate, results = results[0], results[1:]
         sides, sec_first, sec_second = results[:3]
         if not last:
-            picked, payload = results[3:]
+            picked = results[3]
 
     ends = swap((sec_first, sec_second), "sec", False)
     sides = swap((sides, sides), "girth", True)
     membrane, partial_moment = call(
         functools.partial(final_kernel, True),
         vmem_bytes,
-        [((RESULTS, rows, cols), F32), ((1, rows), F32)],
-        [((3, rows, cols), F32), ((2, rows + PAD_ROWS, cols + LANES), F32)],
+        [((3, rows, cols), F32), ((1, rows), F32)],
+        [((2, rows + PAD_ROWS, cols + LANES), F32)],
         stress, velocity, *ends, *sides, plate, height,
         kept=2,
-        far_out=1,
-        copies=(rows // 16,),
+        kept_out=1,
+        copies=(),
     )
     stress, velocity, displacement = call(
         functools.partial(final_kernel, False),
         vmem_bytes,
         [((RESULTS, rows, cols), F32), (block, F32), (block, F32)],
         [((5, rows, cols), F32), ((3, rows + PAD_ROWS, cols + LANES), F32)],
-        membrane, stress, velocity, displacement, *ends, *sides, plate,
-        far=1,
-        kept=3,
+        stress, velocity, displacement, membrane, *ends, *sides, plate,
+        kept=4,
         far_out=3,
-        copies=(2 + rows // 16,),
-        alias={0: 0},
+        copies=(3 + rows // 16,),
     )
     moment = sum_over(partial_moment, "girth")[0]
     return (displacement, velocity, stress, moment)

time: 67.6 us -> 66.6 us (0.985)
  Pallas kernels: 19.7 us -> 18.7 us
    pallas_call x9, Pallas kernels: 19.7 us -> 18.7 us  [call(): pl.pallas_call(kernel, out_shape=results, in_specs=[away] * far + [whole]...]
where the time goes in v16:
time: 66.6 us; the launch traced here: 66.2 us
  starting transfers between devices  42.5 us (64%)
  Pallas kernels  18.7 us (28%)
  waiting for transfers between devices  3.46 us (5%)
  between operations  0.89 us (1%)
    ppermute x16, starting transfers between devices, swap(): lax.ppermute(value, axis, couples + [(j, i) for i, j in couples])  25.9 us
    pallas_call x9, Pallas kernels, call(): pl.pallas_call(kernel, out_shape=results, in_specs=[away] * far + [whole]...  18.7 us
    all_to_all x3, starting transfers between devices, exchange(): blocks = lax.all_to_all(blocks, ('sec', 'girth'), 0, 0, tiled=True)  14.7 us
    ppermute x3, starting transfers between devices, sum_over(): lax.ppermute(value, axis, [(i, i ^ step) for i in range(count)])  1.9 us
    ppermute x16, waiting for transfers between devices, swap(): lax.ppermute(value, axis, couples + [(j, i) for i, j in couples])  1.86 us
    all_to_all x3, waiting for transfers between devices, exchange(): blocks = lax.all_to_all(blocks, ('sec', 'girth'), 0, 0, tiled=True)  1.36 us
  transfers between devices with their start and end apart: 22, of which 5 were waited for; matrix products, arithmetic and copies ran while one was open for 0% of the time, Pallas kernels for 11%

profile of v16, /device:TPU:0, one launch (start us, length us, event | category | flops | bytes accessed | tf_op | source)
XLA Modules:
  0.0 66.2 jit_solution(17089308634209978233)
XLA Ops:
  0.6 2.9 %shard_map.111 = (f32[64,128]{1,0:T(8,128)}, f32[16,512]{1,0:T(8,128)S(1)}, f32[16,512]{1,0:T(8,128)S(1)}, f32[24,128]{1,0:T(8,128)S(1)}, bf16[512,1024]{1,0:T(8...) custom-call(f32[5,64,512]{2,1,0:T(8,128)} %refs_2_.1, ...), custom_call_target="tpu_custom_call" | custom-call | tf_op jit(solution)/shard_map/pallas_call | solution.py:654
  3.6 7.3 %all-to-all-start = ((f32[32,2,128]{2,1,0:T(2,128)}), f32[32,2,128]{2,1,0:T(2,128)S(1)}, u32[]{:S(2)}, u32[]{:S(2)}) async-start(f32[32,2,128]{2,1,0:T(2,128)} %bitcast.19), calls=%async_computation | async-start | bytes 65536 | tf_op jit(solution)/shard_map/all_to_all | solution.py:690
  10.9 0.7 %collective-permute-start = (f32[16,512]{1,0:T(8,128)S(1)}, f32[16,512]{1,0:T(8,128)S(1)}, u32[]{:S(2)}, u32[]{:S(2)}) collective-permute-start(f32[16,512]{1,0:T(8,128)S(1)} %get-tuple-element.76), channel_id=1, source_target_pairs={{4,8},{12,16},{20,24},{8,4},{16,12},{24,20},{5,9},{13,17},{21,25},... | collective-permute-start | bytes 98312 | tf_op jit(solution)/shard_map/ppermute | solution.py:670
  11.6 4.5 %collective-permute-start.1 = (f32[16,512]{1,0:T(8,128)S(1)}, f32[16,512]{1,0:T(8,128)S(1)}, u32[]{:S(2)}, u32[]{:S(2)}) collective-permute-start(f32[16,512]{1,0:T(8,128)S(1)} %get-tuple-element.77), channel_id=1, source_target_pairs={{0,4},{8,12},{16,20},{24,28},{4,0},{12,8},{20,16},{28,24},{1,5},{9... | collective-permute-start | bytes 98312 | tf_op jit(solution)/shard_map/ppermute | solution.py:670
  16.8 0.9 %collective-permute-start.3 = (f32[24,128]{1,0:T(8,128)S(1)}, f32[24,128]{1,0:T(8,128)S(1)}, u32[]{:S(2)}, u32[]{:S(2)}) collective-permute-start(f32[24,128]{1,0:T(8,128)S(1)} %get-tuple-element.78), channel_id=1, source_target_pairs={{0,1},{2,3},{1,0},{3,2},{4,5},{6,7},{5,4},{7,6},{8,9},{10,11},{9,8... | collective-permute-start | bytes 36872 | tf_op jit(solution)/shard_map/ppermute | solution.py:670
  18.1 1.7 %shard_map.112 = (f32[8,64,512]{2,1,0:T(8,128)S(1)}, f32[5,64,512]{2,1,0:T(8,128)S(1)}, f32[5,64,512]{2,1,0:T(8,128)S(1)}, f32[64,512]{1,0:T(8,128)S(1)}, s32[64...) custom-call(f32[8,64,512]{2,1,0:T(8,128)} %refs_0_.1, ...), custom_call_target="tpu_custom_call" | custom-call | tf_op jit(solution)/shard_map/pallas_call | solution.py:654
  19.9 2.7 %shard_map.113 = (f32[8,72,640]{2,1,0:T(8,128)}, f32[5,64,512]{2,1,0:T(8,128)}, f32[5,64,512]{2,1,0:T(8,128)}, f32[64,128]{1,0:T(8,128)}, f32[1,72,640]{2,1,0:T(...) custom-call(f32[8,64,512]{2,1,0:T(8,128)S(1)} %get-tuple-element.68.r, ...), custom_call_target="tpu_custom_call" | custom-call | tf_op jit(solution)/shard_map/pallas_call | solution.py:654
  22.6 3.9 %all-to-all-start.1 = ((f32[32,2,128]{2,1,0:T(2,128)}), f32[32,2,128]{2,1,0:T(2,128)S(1)}, u32[]{:S(2)}, u32[]{:S(2)}) async-start(f32[32,2,128]{2,1,0:T(2,128)} %bitcast.18), calls=%async_computation.1 | async-start | bytes 65536 | tf_op jit(solution)/shard_map/all_to_all | solution.py:690
  26.5 0.7 %collective-permute-start.4 = (f32[16,512]{1,0:T(8,128)S(1)}, f32[16,512]{1,0:T(8,128)S(1)}, u32[]{:S(2)}, u32[]{:S(2)}) collective-permute-start(f32[16,512]{1,0:T(8,128)S(1)} %get-tuple-element.93), channel_id=1, source_target_pairs={{4,8},{12,16},{20,24},{8,4},{16,12},{24,20},{5,9},{13,17},{21,25},... | collective-permute-start | bytes 98312 | tf_op jit(solution)/shard_map/ppermute | solution.py:670
  27.1 4.5 %collective-permute-start.5 = (f32[16,512]{1,0:T(8,128)S(1)}, f32[16,512]{1,0:T(8,128)S(1)}, u32[]{:S(2)}, u32[]{:S(2)}) collective-permute-start(f32[16,512]{1,0:T(8,128)S(1)} %get-tuple-element.94), channel_id=1, source_target_pairs={{0,4},{8,12},{16,20},{24,28},{4,0},{12,8},{20,16},{28,24},{1,5},{9... | collective-permute-start | bytes 98312 | tf_op jit(solution)/shard_map/ppermute | solution.py:670
  32.4 0.9 %collective-permute-start.7 = (f32[24,128]{1,0:T(8,128)S(1)}, f32[24,128]{1,0:T(8,128)S(1)}, u32[]{:S(2)}, u32[]{:S(2)}) collective-permute-start(f32[24,128]{1,0:T(8,128)S(1)} %get-tuple-element.95), channel_id=1, source_target_pairs={{0,1},{2,3},{1,0},{3,2},{4,5},{6,7},{5,4},{7,6},{8,9},{10,11},{9,8... | collective-permute-start | bytes 36872 | tf_op jit(solution)/shard_map/ppermute | solution.py:670
  33.7 2.1 %shard_map.114 = (f32[8,72,640]{2,1,0:T(8,128)S(1)}, f32[5,64,512]{2,1,0:T(8,128)S(1)}, f32[5,64,512]{2,1,0:T(8,128)S(1)}, f32[64,512]{1,0:T(8,128)S(1)}, f32[32...) custom-call(f32[8,72,640]{2,1,0:T(8,128)} %get-tuple-element.79.refs_0_, ...), custom_call_target="tpu_custom_call" | custom-call | tf_op jit(solution)/shard_map/pallas_call | solution.py:654
  35.8 3.4 %shard_map.115 = (f32[8,72,640]{2,1,0:T(8,128)}, f32[5,64,512]{2,1,0:T(8,128)}, f32[5,64,512]{2,1,0:T(8,128)}, f32[64,128]{1,0:T(8,128)}, f32[24,128]{1,0:T(8,12...) custom-call(f32[8,72,640]{2,1,0:T(8,128)S(1)} %get-tuple-element.86.refs_0_, ...), custom_call_target="tpu_custom_call" | custom-call | tf_op jit(solution)/shard_map/pallas_call | solution.py:654
  39.2 3.6 %all-to-all-start.2 = ((f32[32,2,128]{2,1,0:T(2,128)}), f32[32,2,128]{2,1,0:T(2,128)S(1)}, u32[]{:S(2)}, u32[]{:S(2)}) async-start(f32[32,2,128]{2,1,0:T(2,128)} %bitcast.17), calls=%async_computation.2 | async-start | bytes 65536 | tf_op jit(solution)/shard_map/all_to_all | solution.py:690
  42.8 0.7 %collective-permute-start.8 = (f32[16,512]{1,0:T(8,128)S(1)}, f32[16,512]{1,0:T(8,128)S(1)}, u32[]{:S(2)}, u32[]{:S(2)}) collective-permute-start(f32[16,512]{1,0:T(8,128)S(1)} %get-tuple-element.108), channel_id=1, source_target_pairs={{4,8},{12,16},{20,24},{8,4},{16,12},{24,20},{5,9},{13,17},{21,25},... | collective-permute-start | bytes 98312 | tf_op jit(solution)/shard_map/ppermute | solution.py:670
  43.5 4.5 %collective-permute-start.9 = (f32[16,512]{1,0:T(8,128)S(1)}, f32[16,512]{1,0:T(8,128)S(1)}, u32[]{:S(2)}, u32[]{:S(2)}) collective-permute-start(f32[16,512]{1,0:T(8,128)S(1)} %get-tuple-element.109), channel_id=1, source_target_pairs={{0,4},{8,12},{16,20},{24,28},{4,0},{12,8},{20,16},{28,24},{1,5},{9... | collective-permute-start | bytes 98312 | tf_op jit(solution)/shard_map/ppermute | solution.py:670
  48.7 0.9 %collective-permute-start.11 = (f32[24,128]{1,0:T(8,128)S(1)}, f32[24,128]{1,0:T(8,128)S(1)}, u32[]{:S(2)}, u32[]{:S(2)}) collective-permute-start(f32[24,128]{1,0:T(8,128)S(1)} %get-tuple-element.110), channel_id=1, source_target_pairs={{0,1},{2,3},{1,0},{3,2},{4,5},{6,7},{5,4},{7,6},{8,9},{10,11},{9,8... | collective-permute-start | bytes 36872 | tf_op jit(solution)/shard_map/ppermute | solution.py:670
  50.1 2.1 %shard_map.116 = (f32[8,72,640]{2,1,0:T(8,128)S(1)}, f32[5,64,512]{2,1,0:T(8,128)S(1)}, f32[5,64,512]{2,1,0:T(8,128)S(1)}, f32[64,512]{1,0:T(8,128)S(1)}, f32[32...) custom-call(f32[8,72,640]{2,1,0:T(8,128)} %get-tuple-element.96.refs_0_, ...), custom_call_target="tpu_custom_call" | custom-call | tf_op jit(solution)/shard_map/pallas_call | solution.py:654
  52.2 1.8 %shard_map.117 = (f32[8,72,640]{2,1,0:T(8,128)S(1)}, f32[5,64,512]{2,1,0:T(8,128)S(1)}, f32[5,64,512]{2,1,0:T(8,128)S(1)}, f32[24,128]{1,0:T(8,128)S(1)}, f32[16,512]{1,0:T(8,128)S(1)}, /*index=5*/f32[16,512]{1,0:T(8,128)S(1)}) custom-call(f32[8,72,640]{2,1,0:T(8,128)S(1)} %get-tuple-element.101.refs_0_, f32[5,64,512]{2,1,0:T(8,128)S(1)} %get-tuple-element.102.refs_1_, ...), custom_call_target="tpu_custom_call" | custom-call | tf_op jit(solution)/shard_map/pallas_call | solution.py:654
  55.3 4.2 %collective-permute-start.13 = (f32[16,512]{1,0:T(8,128)S(1)}, f32[16,512]{1,0:T(8,128)S(1)}, u32[]{:S(2)}, u32[]{:S(2)}) collective-permute-start(f32[16,512]{1,0:T(8,128)S(1)} %get-tuple-element.115), channel_id=1, source_target_pairs={{0,4},{8,12},{16,20},{24,28},{4,0},{12,8},{20,16},{28,24},{1,5},{9... | collective-permute-start | bytes 98312 | tf_op jit(solution)/shard_map/ppermute | solution.py:670
  59.6 1.8 %collective-permute-done.13.refs_3_.refs_5_ = f32[16,512]{1,0:T(8,128)S(1)} collective-permute-done((f32[16,512]{1,0:T(8,128)S(1)}, f32[16,512]{1,0:T(8,128)S(1)}, u32[]{:S(2)}, u32[]{:S(2)}) %collective-permute-start.13) | collective-permute-done | bytes 32800 | tf_op jit(solution)/shard_map/ppermute | solution.py:670
  62.0 1.2 %collective-permute-start.17 = (f32[1,64]{1,0:T(1,128)S(1)}, f32[1,64]{1,0:T(1,128)S(1)}, u32[]{:S(2)}, u32[]{:S(2)}) collective-permute-start(f32[1,64]{1,0:T(1,128)S(1)} %get-tuple-element.121), channel_id=1, source_target_pairs={{0,2},{1,3},{2,0},{3,1},{4,6},{5,7},{6,4},{7,5},{8,10},{9,11},{10,... | collective-permute-start | bytes 776 | tf_op jit(solution)/shard_map/ppermute | solution.py:679
  63.2 0.7 %collective-permute-start.18 = (f32[1,64]{1,0:T(1,128)S(1)}, f32[1,64]{1,0:T(1,128)S(1)}, u32[]{:S(2)}, u32[]{:S(2)}) collective-permute-start(f32[1,64]{1,0:T(1,128)S(1)} %get-tuple-element.121), channel_id=1, source_target_pairs={{0,1},{1,0},{2,3},{3,2},{4,5},{5,4},{6,7},{7,6},{8,9},{9,8},{10,11... | collective-permute-start | bytes 776 | tf_op jit(solution)/shard_map/ppermute | solution.py:679
  63.9 1.5 %shard_map.119 = (f32[8,64,512]{2,1,0:T(8,128)}, f32[5,64,512]{2,1,0:T(8,128)}, f32[5,64,512]{2,1,0:T(8,128)}) custom-call(f32[8,72,640]{2,1,0:T(8,128)S(1)} %get-tuple-element.111.refs_0_, f32[5,64,512]{2,1,0:T(8,128)S(1)} %get-tuple-element.112.refs_1_, f32[5,64,512]{2,1,0:T(8,128)S(1)} %get-tuple-element.113.refs_2_, ...), custom_call_target="tpu_custom_call" | custom-call | tf_op jit(solution)/shard_map/pallas_call | solution.py:654
  (32 shorter events, 6.1 us)
Async XLA Ops:
  3.6 14.6 %all-to-all-start = ((f32[32,2,128]{2,1,0:T(2,128)}), f32[32,2,128]{2,1,0:T(2,128)S(1)}, u32[]{:S(2)}, u32[]{:S(2)}) async-start(f32[32,2,128]{2,1,0:T(2,128)} %bitcast.19), calls=%async_computation | async-start | bytes 65536 | tf_op jit(solution)/shard_map/all_to_all | solution.py:690
  10.9 9.0 %collective-permute-start = (f32[16,512]{1,0:T(8,128)S(1)}, f32[16,512]{1,0:T(8,128)S(1)}, u32[]{:S(2)}, u32[]{:S(2)}) collective-permute-start(f32[16,512]{1,0:T(8,128)S(1)} %get-tuple-element.76), channel_id=1, source_target_pairs={{4,8},{12,16},{20,24},{8,4},{16,12},{24,20},{5,9},{13,17},{21,25},... | collective-permute-start | bytes 98312 | tf_op jit(solution)/shard_map/ppermute | solution.py:670
  11.6 8.4 %collective-permute-start.1 = (f32[16,512]{1,0:T(8,128)S(1)}, f32[16,512]{1,0:T(8,128)S(1)}, u32[]{:S(2)}, u32[]{:S(2)}) collective-permute-start(f32[16,512]{1,0:T(8,128)S(1)} %get-tuple-element.77), channel_id=1, source_target_pairs={{0,4},{8,12},{16,20},{24,28},{4,0},{12,8},{20,16},{28,24},{1,5},{9... | collective-permute-start | bytes 98312 | tf_op jit(solution)/shard_map/ppermute | solution.py:670
  16.1 3.8 %collective-permute-start.2 = (f32[24,128]{1,0:T(8,128)S(1)}, f32[24,128]{1,0:T(8,128)S(1)}, u32[]{:S(2)}, u32[]{:S(2)}) collective-permute-start(f32[24,128]{1,0:T(8,128)S(1)} %get-tuple-element.78), channel_id=1, source_target_pairs={{1,2},{3,0},{2,1},{0,3},{5,6},{7,4},{6,5},{4,7},{9,10},{11,8},{10,... | collective-permute-start | bytes 36872 | tf_op jit(solution)/shard_map/ppermute | solution.py:670
  16.8 3.1 %collective-permute-start.3 = (f32[24,128]{1,0:T(8,128)S(1)}, f32[24,128]{1,0:T(8,128)S(1)}, u32[]{:S(2)}, u32[]{:S(2)}) collective-permute-start(f32[24,128]{1,0:T(8,128)S(1)} %get-tuple-element.78), channel_id=1, source_target_pairs={{0,1},{2,3},{1,0},{3,2},{4,5},{6,7},{5,4},{7,6},{8,9},{10,11},{9,8... | collective-permute-start | bytes 36872 | tf_op jit(solution)/shard_map/ppermute | solution.py:670
  22.6 11.1 %all-to-all-start.1 = ((f32[32,2,128]{2,1,0:T(2,128)}), f32[32,2,128]{2,1,0:T(2,128)S(1)}, u32[]{:S(2)}, u32[]{:S(2)}) async-start(f32[32,2,128]{2,1,0:T(2,128)} %bitcast.18), calls=%async_computation.1 | async-start | bytes 65536 | tf_op jit(solution)/shard_map/all_to_all | solution.py:690
  26.5 9.3 %collective-permute-start.4 = (f32[16,512]{1,0:T(8,128)S(1)}, f32[16,512]{1,0:T(8,128)S(1)}, u32[]{:S(2)}, u32[]{:S(2)}) collective-permute-start(f32[16,512]{1,0:T(8,128)S(1)} %get-tuple-element.93), channel_id=1, source_target_pairs={{4,8},{12,16},{20,24},{8,4},{16,12},{24,20},{5,9},{13,17},{21,25},... | collective-permute-start | bytes 98312 | tf_op jit(solution)/shard_map/ppermute | solution.py:670
  27.1 8.7 %collective-permute-start.5 = (f32[16,512]{1,0:T(8,128)S(1)}, f32[16,512]{1,0:T(8,128)S(1)}, u32[]{:S(2)}, u32[]{:S(2)}) collective-permute-start(f32[16,512]{1,0:T(8,128)S(1)} %get-tuple-element.94), channel_id=1, source_target_pairs={{0,4},{8,12},{16,20},{24,28},{4,0},{12,8},{20,16},{28,24},{1,5},{9... | collective-permute-start | bytes 98312 | tf_op jit(solution)/shard_map/ppermute | solution.py:670
  31.7 4.1 %collective-permute-start.6 = (f32[24,128]{1,0:T(8,128)S(1)}, f32[24,128]{1,0:T(8,128)S(1)}, u32[]{:S(2)}, u32[]{:S(2)}) collective-permute-start(f32[24,128]{1,0:T(8,128)S(1)} %get-tuple-element.95), channel_id=1, source_target_pairs={{1,2},{3,0},{2,1},{0,3},{5,6},{7,4},{6,5},{4,7},{9,10},{11,8},{10,... | collective-permute-start | bytes 36872 | tf_op jit(solution)/shard_map/ppermute | solution.py:670
  32.4 3.5 %collective-permute-start.7 = (f32[24,128]{1,0:T(8,128)S(1)}, f32[24,128]{1,0:T(8,128)S(1)}, u32[]{:S(2)}, u32[]{:S(2)}) collective-permute-start(f32[24,128]{1,0:T(8,128)S(1)} %get-tuple-element.95), channel_id=1, source_target_pairs={{0,1},{2,3},{1,0},{3,2},{4,5},{6,7},{5,4},{7,6},{8,9},{10,11},{9,8... | collective-permute-start | bytes 36872 | tf_op jit(solution)/shard_map/ppermute | solution.py:670
  39.2 10.8 %all-to-all-start.2 = ((f32[32,2,128]{2,1,0:T(2,128)}), f32[32,2,128]{2,1,0:T(2,128)S(1)}, u32[]{:S(2)}, u32[]{:S(2)}) async-start(f32[32,2,128]{2,1,0:T(2,128)} %bitcast.17), calls=%async_computation.2 | async-start | bytes 65536 | tf_op jit(solution)/shard_map/all_to_all | solution.py:690
  42.8 9.3 %collective-permute-start.8 = (f32[16,512]{1,0:T(8,128)S(1)}, f32[16,512]{1,0:T(8,128)S(1)}, u32[]{:S(2)}, u32[]{:S(2)}) collective-permute-start(f32[16,512]{1,0:T(8,128)S(1)} %get-tuple-element.108), channel_id=1, source_target_pairs={{4,8},{12,16},{20,24},{8,4},{16,12},{24,20},{5,9},{13,17},{21,25},... | collective-permute-start | bytes 98312 | tf_op jit(solution)/shard_map/ppermute | solution.py:670
  43.5 8.7 %collective-permute-start.9 = (f32[16,512]{1,0:T(8,128)S(1)}, f32[16,512]{1,0:T(8,128)S(1)}, u32[]{:S(2)}, u32[]{:S(2)}) collective-permute-start(f32[16,512]{1,0:T(8,128)S(1)} %get-tuple-element.109), channel_id=1, source_target_pairs={{0,4},{8,12},{16,20},{24,28},{4,0},{12,8},{20,16},{28,24},{1,5},{9... | collective-permute-start | bytes 98312 | tf_op jit(solution)/shard_map/ppermute | solution.py:670
  48.0 4.1 %collective-permute-start.10 = (f32[24,128]{1,0:T(8,128)S(1)}, f32[24,128]{1,0:T(8,128)S(1)}, u32[]{:S(2)}, u32[]{:S(2)}) collective-permute-start(f32[24,128]{1,0:T(8,128)S(1)} %get-tuple-element.110), channel_id=1, source_target_pairs={{1,2},{3,0},{2,1},{0,3},{5,6},{7,4},{6,5},{4,7},{9,10},{11,8},{10,... | collective-permute-start | bytes 36872 | tf_op jit(solution)/shard_map/ppermute | solution.py:670
  48.7 3.5 %collective-permute-start.11 = (f32[24,128]{1,0:T(8,128)S(1)}, f32[24,128]{1,0:T(8,128)S(1)}, u32[]{:S(2)}, u32[]{:S(2)}) collective-permute-start(f32[24,128]{1,0:T(8,128)S(1)} %get-tuple-element.110), channel_id=1, source_target_pairs={{0,1},{2,3},{1,0},{3,2},{4,5},{6,7},{5,4},{7,6},{8,9},{10,11},{9,8... | collective-permute-start | bytes 36872 | tf_op jit(solution)/shard_map/ppermute | solution.py:670
  54.0 5.6 %collective-permute-start.14 = (f32[24,128]{1,0:T(8,128)S(1)}, f32[24,128]{1,0:T(8,128)S(1)}, u32[]{:S(2)}, u32[]{:S(2)}) collective-permute-start(f32[24,128]{1,0:T(8,128)S(1)} %get-tuple-element.116), channel_id=1, source_target_pairs={{1,2},{3,0},{2,1},{0,3},{5,6},{7,4},{6,5},{4,7},{9,10},{11,8},{10,... | collective-permute-start | bytes 36872 | tf_op jit(solution)/shard_map/ppermute | solution.py:670
  54.3 5.3 %collective-permute-start.15 = (f32[24,128]{1,0:T(8,128)S(1)}, f32[24,128]{1,0:T(8,128)S(1)}, u32[]{:S(2)}, u32[]{:S(2)}) collective-permute-start(f32[24,128]{1,0:T(8,128)S(1)} %get-tuple-element.116), channel_id=1, source_target_pairs={{0,1},{2,3},{1,0},{3,2},{4,5},{6,7},{5,4},{7,6},{8,9},{10,11},{9,8... | collective-permute-start | bytes 36872 | tf_op jit(solution)/shard_map/ppermute | solution.py:670
  54.7 4.9 %collective-permute-start.12 = (f32[16,512]{1,0:T(8,128)S(1)}, f32[16,512]{1,0:T(8,128)S(1)}, u32[]{:S(2)}, u32[]{:S(2)}) collective-permute-start(f32[16,512]{1,0:T(8,128)S(1)} %get-tuple-element.114), channel_id=1, source_target_pairs={{4,8},{12,16},{20,24},{8,4},{16,12},{24,20},{5,9},{13,17},{21,25},... | collective-permute-start | bytes 98312 | tf_op jit(solution)/shard_map/ppermute | solution.py:670
  55.3 6.1 %collective-permute-start.13 = (f32[16,512]{1,0:T(8,128)S(1)}, f32[16,512]{1,0:T(8,128)S(1)}, u32[]{:S(2)}, u32[]{:S(2)}) collective-permute-start(f32[16,512]{1,0:T(8,128)S(1)} %get-tuple-element.115), channel_id=1, source_target_pairs={{0,4},{8,12},{16,20},{24,28},{4,0},{12,8},{20,16},{28,24},{1,5},{9... | collective-permute-start | bytes 98312 | tf_op jit(solution)/shard_map/ppermute | solution.py:670
  62.0 3.4 %collective-permute-start.16 = (f32[1,64]{1,0:T(1,128)S(1)}, f32[1,64]{1,0:T(1,128)S(1)}, u32[]{:S(2)}, u32[]{:S(2)}) collective-permute-start(f32[1,64]{1,0:T(1,128)S(1)} %get-tuple-element.121), channel_id=1, source_target_pairs={{0,3},{1,2},{2,1},{3,0},{4,7},{5,6},{6,5},{7,4},{8,11},{9,10},{10,... | collective-permute-start | bytes 776 | tf_op jit(solution)/shard_map/ppermute | solution.py:679
  62.0 3.6 %collective-permute-start.17 = (f32[1,64]{1,0:T(1,128)S(1)}, f32[1,64]{1,0:T(1,128)S(1)}, u32[]{:S(2)}, u32[]{:S(2)}) collective-permute-start(f32[1,64]{1,0:T(1,128)S(1)} %get-tuple-element.121), channel_id=1, source_target_pairs={{0,2},{1,3},{2,0},{3,1},{4,6},{5,7},{6,4},{7,5},{8,10},{9,11},{10,... | collective-permute-start | bytes 776 | tf_op jit(solution)/shard_map/ppermute | solution.py:679
  63.2 2.4 %collective-permute-start.18 = (f32[1,64]{1,0:T(1,128)S(1)}, f32[1,64]{1,0:T(1,128)S(1)}, u32[]{:S(2)}, u32[]{:S(2)}) collective-permute-start(f32[1,64]{1,0:T(1,128)S(1)} %get-tuple-element.121), channel_id=1, source_target_pairs={{0,1},{1,0},{2,3},{3,2},{4,5},{5,4},{6,7},{7,6},{8,9},{9,8},{10,11... | collective-permute-start | bytes 776 | tf_op jit(solution)/shard_map/ppermute | solution.py:679

commit v17 on v16

--- a/solution.py
+++ b/solution.py
@@ -410,9 +410,10 @@
 
 
 def set_rates(linear, angular, plate):
-    rate = time_step / plate
-    linear[...] = rate
-    angular[...] = (12.0 * rate) / (1.0 + plate * plate)
+    square = 1.0 + plate * plate
+    inverse = time_step / (plate * square)
+    linear[...] = square * inverse
+    angular[...] = 12.0 * inverse
 
 
 def joint_kernel(first, *refs):
@@ -469,7 +470,9 @@
         plate_ext, out = out[0], out[1:]
     sides, sec_pair = out[0], out[1:3]
     out = out[3:]
-    if not last:
+    if last:
+        sides_again, out = out[0], out[1:]
+    else:
         picked_out, out = out[0], out[1:]
     res_ext, vel_ext = out[:2]
     if last:
@@ -534,6 +537,7 @@
     right_lanes = [velocity[f, :, ends[0] : ends[1]] for f in range(FIELDS)]
     if last:
         sides[...] = edge_rows(left_lanes, right_lanes, 1)
+        sides_again[...] = sides[...]
         send_ends(
             sec_pair,
             [velocity[f, 0:1, :] for f in range(FIELDS)],
@@ -755,7 +759,7 @@
         outs = [(stress_shape, F32), (block, F32), (block, F32)] + [(message, F32)] * (not last)
         own = [] if last else outs
         outs = outs + [(plate_shape, F32)] * first
-        outs += [(edge, F32), (strip, F32), (strip, F32)] + [(slot_rows, F32)] * (not last)
+        outs += [(edge, F32), (strip, F32), (strip, F32), (edge if last else slot_rows, F32)]
         results = call(
             functools.partial(step_kernel, first, last),
             vmem_bytes,
@@ -775,11 +779,13 @@
         if first:
             plate, results = results[0], results[1:]
         sides, sec_first, sec_second = results[:3]
-        if not last:
+        if last:
+            sides_again = results[3]
+        else:
             picked = results[3]
 
     ends = swap((sec_first, sec_second), "sec", False)
-    sides = swap((sides, sides), "girth", True)
+    sides = swap((sides, sides_again), "girth", True)
     membrane, partial_moment = call(
         functools.partial(final_kernel, True),
         vmem_bytes,

time: 66.6 us -> 66.7 us (level)
  no operation moved by 1% of the time
where the time goes in v17:
time: 66.7 us; the launch traced here: 66.3 us
  starting transfers between devices  42.5 us (64%)
  Pallas kernels  18.7 us (28%)
  waiting for transfers between devices  3.69 us (6%)
  between operations  0.88 us (1%)
    ppermute x16, starting transfers between devices, swap(): lax.ppermute(value, axis, couples + [(j, i) for i, j in couples])  25.8 us
    pallas_call x9, Pallas kernels, call(): pl.pallas_call(kernel, out_shape=results, in_specs=[away] * far + [whole]...  18.7 us
    all_to_all x3, starting transfers between devices, exchange(): blocks = lax.all_to_all(blocks, ('sec', 'girth'), 0, 0, tiled=True)  14.7 us
    ppermute x16, waiting for transfers between devices, swap(): lax.ppermute(value, axis, couples + [(j, i) for i, j in couples])  2.09 us
    ppermute x3, starting transfers between devices, sum_over(): lax.ppermute(value, axis, [(i, i ^ step) for i in range(count)])  1.9 us
    all_to_all x3, waiting for transfers between devices, exchange(): blocks = lax.all_to_all(blocks, ('sec', 'girth'), 0, 0, tiled=True)  1.36 us
  transfers between devices with their start and end apart: 22, of which 5 were waited for; matrix products, arithmetic and copies ran while one was open for 0% of the time, Pallas kernels for 11%

profile of v17, /device:TPU:0, one launch (start us, length us, event | category | flops | bytes accessed | tf_op | source)
XLA Modules:
  0.0 66.3 jit_solution(6015215037997409658)
XLA Ops:
  0.6 2.9 %shard_map.111 = (f32[64,128]{1,0:T(8,128)}, f32[16,512]{1,0:T(8,128)S(1)}, f32[16,512]{1,0:T(8,128)S(1)}, f32[24,128]{1,0:T(8,128)S(1)}, bf16[512,1024]{1,0:T(8...) custom-call(f32[5,64,512]{2,1,0:T(8,128)} %refs_2_.1, ...), custom_call_target="tpu_custom_call" | custom-call | tf_op jit(solution)/shard_map/pallas_call | solution.py:658
  3.6 7.3 %all-to-all-start = ((f32[32,2,128]{2,1,0:T(2,128)}), f32[32,2,128]{2,1,0:T(2,128)S(1)}, u32[]{:S(2)}, u32[]{:S(2)}) async-start(f32[32,2,128]{2,1,0:T(2,128)} %bitcast.19), calls=%async_computation | async-start | bytes 65536 | tf_op jit(solution)/shard_map/all_to_all | solution.py:694
  10.9 0.7 collective-permute-start
  11.6 4.5 %collective-permute-start.1 = (f32[16,512]{1,0:T(8,128)S(1)}, f32[16,512]{1,0:T(8,128)S(1)}, u32[]{:S(2)}, u32[]{:S(2)}) collective-permute-start(f32[16,512]{1,0:T(8,128)S(1)} %get-tuple-element.78), channel_id=1, source_target_pairs={{0,4},{8,12},{16,20},{24,28},{4,0},{12,8},{20,16},{28,24},{1,5},{9... | collective-permute-start | bytes 98312 | tf_op jit(solution)/shard_map/ppermute | solution.py:674
  16.8 0.9 %collective-permute-start.3 = (f32[24,128]{1,0:T(8,128)S(1)}, f32[24,128]{1,0:T(8,128)S(1)}, u32[]{:S(2)}, u32[]{:S(2)}) collective-permute-start(f32[24,128]{1,0:T(8,128)S(1)} %get-tuple-element.79), channel_id=1, source_target_pairs={{0,1},{2,3},{1,0},{3,2},{4,5},{6,7},{5,4},{7,6},{8,9},{10,11},{9,8... | collective-permute-start | bytes 36872 | tf_op jit(solution)/shard_map/ppermute | solution.py:674
  18.1 1.7 %shard_map.112 = (f32[8,64,512]{2,1,0:T(8,128)S(1)}, f32[5,64,512]{2,1,0:T(8,128)S(1)}, f32[5,64,512]{2,1,0:T(8,128)S(1)}, f32[64,512]{1,0:T(8,128)S(1)}, s32[64...) custom-call(f32[8,64,512]{2,1,0:T(8,128)} %refs_0_.1, ...), custom_call_target="tpu_custom_call" | custom-call | tf_op jit(solution)/shard_map/pallas_call | solution.py:658
  19.9 2.7 %shard_map.113 = (f32[8,72,640]{2,1,0:T(8,128)}, f32[5,64,512]{2,1,0:T(8,128)}, f32[5,64,512]{2,1,0:T(8,128)}, f32[64,128]{1,0:T(8,128)}, f32[1,72,640]{2,1,0:T(...) custom-call(f32[8,64,512]{2,1,0:T(8,128)S(1)} %get-tuple-element.69.r, ...), custom_call_target="tpu_custom_call" | custom-call | tf_op jit(solution)/shard_map/pallas_call | solution.py:658
  22.6 3.9 %all-to-all-start.1 = ((f32[32,2,128]{2,1,0:T(2,128)}), f32[32,2,128]{2,1,0:T(2,128)S(1)}, u32[]{:S(2)}, u32[]{:S(2)}) async-start(f32[32,2,128]{2,1,0:T(2,128)} %bitcast.18), calls=%async_computation.1 | async-start | bytes 65536 | tf_op jit(solution)/shard_map/all_to_all | solution.py:694
  27.1 4.5 %collective-permute-start.5 = (f32[16,512]{1,0:T(8,128)S(1)}, f32[16,512]{1,0:T(8,128)S(1)}, u32[]{:S(2)}, u32[]{:S(2)}) collective-permute-start(f32[16,512]{1,0:T(8,128)S(1)} %get-tuple-element.95), channel_id=1, source_target_pairs={{0,4},{8,12},{16,20},{24,28},{4,0},{12,8},{20,16},{28,24},{1,5},{9... | collective-permute-start | bytes 98312 | tf_op jit(solution)/shard_map/ppermute | solution.py:674
  32.4 0.9 %collective-permute-start.7 = (f32[24,128]{1,0:T(8,128)S(1)}, f32[24,128]{1,0:T(8,128)S(1)}, u32[]{:S(2)}, u32[]{:S(2)}) collective-permute-start(f32[24,128]{1,0:T(8,128)S(1)} %get-tuple-element.96), channel_id=1, source_target_pairs={{0,1},{2,3},{1,0},{3,2},{4,5},{6,7},{5,4},{7,6},{8,9},{10,11},{9,8... | collective-permute-start | bytes 36872 | tf_op jit(solution)/shard_map/ppermute | solution.py:674
  33.7 2.1 %shard_map.114 = (f32[8,72,640]{2,1,0:T(8,128)S(1)}, f32[5,64,512]{2,1,0:T(8,128)S(1)}, f32[5,64,512]{2,1,0:T(8,128)S(1)}, f32[64,512]{1,0:T(8,128)S(1)}, f32[32...) custom-call(f32[8,72,640]{2,1,0:T(8,128)} %get-tuple-element.80.refs_0_, ...), custom_call_target="tpu_custom_call" | custom-call | tf_op jit(solution)/shard_map/pallas_call | solution.py:658
  35.8 3.4 %shard_map.115 = (f32[8,72,640]{2,1,0:T(8,128)}, f32[5,64,512]{2,1,0:T(8,128)}, f32[5,64,512]{2,1,0:T(8,128)}, f32[64,128]{1,0:T(8,128)}, f32[24,128]{1,0:T(8,12...) custom-call(f32[8,72,640]{2,1,0:T(8,128)S(1)} %get-tuple-element.87.refs_0_, ...), custom_call_target="tpu_custom_call" | custom-call | tf_op jit(solution)/shard_map/pallas_call | solution.py:658
  39.2 3.6 %all-to-all-start.2 = ((f32[32,2,128]{2,1,0:T(2,128)}), f32[32,2,128]{2,1,0:T(2,128)S(1)}, u32[]{:S(2)}, u32[]{:S(2)}) async-start(f32[32,2,128]{2,1,0:T(2,128)} %bitcast.17), calls=%async_computation.2 | async-start | bytes 65536 | tf_op jit(solution)/shard_map/all_to_all | solution.py:694
  42.8 0.7 collective-permute-start.8
  43.5 4.5 %collective-permute-start.9 = (f32[16,512]{1,0:T(8,128)S(1)}, f32[16,512]{1,0:T(8,128)S(1)}, u32[]{:S(2)}, u32[]{:S(2)}) collective-permute-start(f32[16,512]{1,0:T(8,128)S(1)} %get-tuple-element.110), channel_id=1, source_target_pairs={{0,4},{8,12},{16,20},{24,28},{4,0},{12,8},{20,16},{28,24},{1,5},{9... | collective-permute-start | bytes 98312 | tf_op jit(solution)/shard_map/ppermute | solution.py:674
  48.7 0.9 %collective-permute-start.11 = (f32[24,128]{1,0:T(8,128)S(1)}, f32[24,128]{1,0:T(8,128)S(1)}, u32[]{:S(2)}, u32[]{:S(2)}) collective-permute-start(f32[24,128]{1,0:T(8,128)S(1)} %get-tuple-element.111), channel_id=1, source_target_pairs={{0,1},{2,3},{1,0},{3,2},{4,5},{6,7},{5,4},{7,6},{8,9},{10,11},{9,8... | collective-permute-start | bytes 36872 | tf_op jit(solution)/shard_map/ppermute | solution.py:674
  50.1 2.1 %shard_map.116 = (f32[8,72,640]{2,1,0:T(8,128)S(1)}, f32[5,64,512]{2,1,0:T(8,128)S(1)}, f32[5,64,512]{2,1,0:T(8,128)S(1)}, f32[64,512]{1,0:T(8,128)S(1)}, f32[32...) custom-call(f32[8,72,640]{2,1,0:T(8,128)} %get-tuple-element.97.refs_0_, ...), custom_call_target="tpu_custom_call" | custom-call | tf_op jit(solution)/shard_map/pallas_call | solution.py:658
  52.2 1.8 %shard_map.117 = (f32[8,72,640]{2,1,0:T(8,128)S(1)}, f32[5,64,512]{2,1,0:T(8,128)S(1)}, f32[5,64,512]{2,1,0:T(8,128)S(1)}, f32[24,128]{1,0:T(8,128)S(1)}, f32[16...) custom-call(f32[8,72,640]{2,1,0:T(8,128)S(1)} %get-tuple-element.102.refs_0_, ...), custom_call_target="tpu_custom_call" | custom-call | tf_op jit(solution)/shard_map/pallas_call | solution.py:658
  54.7 3.8 %collective-permute-start.13 = (f32[16,512]{1,0:T(8,128)S(1)}, f32[16,512]{1,0:T(8,128)S(1)}, u32[]{:S(2)}, u32[]{:S(2)}) collective-permute-start(f32[16,512]{1,0:T(8,128)S(1)} %get-tuple-element.116), channel_id=1, source_target_pairs={{0,4},{8,12},{16,20},{24,28},{4,0},{12,8},{20,16},{28,24},{1,5},{9... | collective-permute-start | bytes 98312 | tf_op jit(solution)/shard_map/ppermute | solution.py:674
  58.5 1.0 %collective-permute-start.15 = (f32[24,128]{1,0:T(8,128)S(1)}, f32[24,128]{1,0:T(8,128)S(1)}, u32[]{:S(2)}, u32[]{:S(2)}) collective-permute-start(f32[24,128]{1,0:T(8,128)S(1)} %get-tuple-element.118), channel_id=1, source_target_pairs={{0,1},{2,3},{1,0},{3,2},{4,5},{6,7},{5,4},{7,6},{8,9},{10,11},{9,8... | collective-permute-start | bytes 36872 | tf_op jit(solution)/shard_map/ppermute | solution.py:674
  59.5 2.0 %collective-permute-done.14.refs_4_.refs_6_ = f32[24,128]{1,0:T(8,128)S(1)} collective-permute-done((f32[24,128]{1,0:T(8,128)S(1)}, f32[24,128]{1,0:T(8,128)S(1)}, u32[]{:S(2)}, u32[]{:S(2)}) %collective-permute-start.14) | collective-permute-done | bytes 12320 | tf_op jit(solution)/shard_map/ppermute | solution.py:674
  62.2 1.1 %collective-permute-start.17 = (f32[1,64]{1,0:T(1,128)S(1)}, f32[1,64]{1,0:T(1,128)S(1)}, u32[]{:S(2)}, u32[]{:S(2)}) collective-permute-start(f32[1,64]{1,0:T(1,128)S(1)} %get-tuple-element.123), channel_id=1, source_target_pairs={{0,2},{1,3},{2,0},{3,1},{4,6},{5,7},{6,4},{7,5},{8,10},{9,11},{10,... | collective-permute-start | bytes 776 | tf_op jit(solution)/shard_map/ppermute | solution.py:683
  63.3 0.8 %collective-permute-start.18 = (f32[1,64]{1,0:T(1,128)S(1)}, f32[1,64]{1,0:T(1,128)S(1)}, u32[]{:S(2)}, u32[]{:S(2)}) collective-permute-start(f32[1,64]{1,0:T(1,128)S(1)} %get-tuple-element.123), channel_id=1, source_target_pairs={{0,1},{1,0},{2,3},{3,2},{4,5},{5,4},{6,7},{7,6},{8,9},{9,8},{10,11... | collective-permute-start | bytes 776 | tf_op jit(solution)/shard_map/ppermute | solution.py:683
  64.1 1.5 %shard_map.119 = (f32[8,64,512]{2,1,0:T(8,128)}, f32[5,64,512]{2,1,0:T(8,128)}, f32[5,64,512]{2,1,0:T(8,128)}) custom-call(f32[8,72,640]{2,1,0:T(8,128)S(1)} %get-tuple-element.112.refs_0_, f32[5,64,512]{2,1,0:T(8,128)S(1)} %get-tuple-element.113.refs_1_, f32[5,64,512]{2,1,0:T(8,128)S(1)} %get-tuple-element.114.refs_2_, ...), custom_call_target="tpu_custom_call" | custom-call | tf_op jit(solution)/shard_map/pallas_call | solution.py:658
  (32 shorter events, 6.2 us)
Async XLA Ops:
  3.6 14.6 %all-to-all-start = ((f32[32,2,128]{2,1,0:T(2,128)}), f32[32,2,128]{2,1,0:T(2,128)S(1)}, u32[]{:S(2)}, u32[]{:S(2)}) async-start(f32[32,2,128]{2,1,0:T(2,128)} %bitcast.19), calls=%async_computation | async-start | bytes 65536 | tf_op jit(solution)/shard_map/all_to_all | solution.py:694
  10.9 9.0 %collective-permute-start = (f32[16,512]{1,0:T(8,128)S(1)}, f32[16,512]{1,0:T(8,128)S(1)}, u32[]{:S(2)}, u32[]{:S(2)}) collective-permute-start(f32[16,512]{1,0:T(8,128)S(1)} %get-tuple-element.77), channel_id=1, source_target_pairs={{4,8},{12,16},{20,24},{8,4},{16,12},{24,20},{5,9},{13,17},{21,25},... | collective-permute-start | bytes 98312 | tf_op jit(solution)/shard_map/ppermute | solution.py:674
  11.6 8.4 %collective-permute-start.1 = (f32[16,512]{1,0:T(8,128)S(1)}, f32[16,512]{1,0:T(8,128)S(1)}, u32[]{:S(2)}, u32[]{:S(2)}) collective-permute-start(f32[16,512]{1,0:T(8,128)S(1)} %get-tuple-element.78), channel_id=1, source_target_pairs={{0,4},{8,12},{16,20},{24,28},{4,0},{12,8},{20,16},{28,24},{1,5},{9... | collective-permute-start | bytes 98312 | tf_op jit(solution)/shard_map/ppermute | solution.py:674
  16.1 3.8 %collective-permute-start.2 = (f32[24,128]{1,0:T(8,128)S(1)}, f32[24,128]{1,0:T(8,128)S(1)}, u32[]{:S(2)}, u32[]{:S(2)}) collective-permute-start(f32[24,128]{1,0:T(8,128)S(1)} %get-tuple-element.79), channel_id=1, source_target_pairs={{1,2},{3,0},{2,1},{0,3},{5,6},{7,4},{6,5},{4,7},{9,10},{11,8},{10,... | collective-permute-start | bytes 36872 | tf_op jit(solution)/shard_map/ppermute | solution.py:674
  16.8 3.1 %collective-permute-start.3 = (f32[24,128]{1,0:T(8,128)S(1)}, f32[24,128]{1,0:T(8,128)S(1)}, u32[]{:S(2)}, u32[]{:S(2)}) collective-permute-start(f32[24,128]{1,0:T(8,128)S(1)} %get-tuple-element.79), channel_id=1, source_target_pairs={{0,1},{2,3},{1,0},{3,2},{4,5},{6,7},{5,4},{7,6},{8,9},{10,11},{9,8... | collective-permute-start | bytes 36872 | tf_op jit(solution)/shard_map/ppermute | solution.py:674
  22.6 11.1 %all-to-all-start.1 = ((f32[32,2,128]{2,1,0:T(2,128)}), f32[32,2,128]{2,1,0:T(2,128)S(1)}, u32[]{:S(2)}, u32[]{:S(2)}) async-start(f32[32,2,128]{2,1,0:T(2,128)} %bitcast.18), calls=%async_computation.1 | async-start | bytes 65536 | tf_op jit(solution)/shard_map/all_to_all | solution.py:694
  26.5 9.3 %collective-permute-start.4 = (f32[16,512]{1,0:T(8,128)S(1)}, f32[16,512]{1,0:T(8,128)S(1)}, u32[]{:S(2)}, u32[]{:S(2)}) collective-permute-start(f32[16,512]{1,0:T(8,128)S(1)} %get-tuple-element.94), channel_id=1, source_target_pairs={{4,8},{12,16},{20,24},{8,4},{16,12},{24,20},{5,9},{13,17},{21,25},... | collective-permute-start | bytes 98312 | tf_op jit(solution)/shard_map/ppermute | solution.py:674
  27.1 8.7 %collective-permute-start.5 = (f32[16,512]{1,0:T(8,128)S(1)}, f32[16,512]{1,0:T(8,128)S(1)}, u32[]{:S(2)}, u32[]{:S(2)}) collective-permute-start(f32[16,512]{1,0:T(8,128)S(1)} %get-tuple-element.95), channel_id=1, source_target_pairs={{0,4},{8,12},{16,20},{24,28},{4,0},{12,8},{20,16},{28,24},{1,5},{9... | collective-permute-start | bytes 98312 | tf_op jit(solution)/shard_map/ppermute | solution.py:674
  31.7 4.1 %collective-permute-start.6 = (f32[24,128]{1,0:T(8,128)S(1)}, f32[24,128]{1,0:T(8,128)S(1)}, u32[]{:S(2)}, u32[]{:S(2)}) collective-permute-start(f32[24,128]{1,0:T(8,128)S(1)} %get-tuple-element.96), channel_id=1, source_target_pairs={{1,2},{3,0},{2,1},{0,3},{5,6},{7,4},{6,5},{4,7},{9,10},{11,8},{10,... | collective-permute-start | bytes 36872 | tf_op jit(solution)/shard_map/ppermute | solution.py:674
  32.4 3.5 %collective-permute-start.7 = (f32[24,128]{1,0:T(8,128)S(1)}, f32[24,128]{1,0:T(8,128)S(1)}, u32[]{:S(2)}, u32[]{:S(2)}) collective-permute-start(f32[24,128]{1,0:T(8,128)S(1)} %get-tuple-element.96), channel_id=1, source_target_pairs={{0,1},{2,3},{1,0},{3,2},{4,5},{6,7},{5,4},{7,6},{8,9},{10,11},{9,8... | collective-permute-start | bytes 36872 | tf_op jit(solution)/shard_map/ppermute | solution.py:674
  39.2 10.8 %all-to-all-start.2 = ((f32[32,2,128]{2,1,0:T(2,128)}), f32[32,2,128]{2,1,0:T(2,128)S(1)}, u32[]{:S(2)}, u32[]{:S(2)}) async-start(f32[32,2,128]{2,1,0:T(2,128)} %bitcast.17), calls=%async_computation.2 | async-start | bytes 65536 | tf_op jit(solution)/shard_map/all_to_all | solution.py:694
  42.8 9.3 %collective-permute-start.8 = (f32[16,512]{1,0:T(8,128)S(1)}, f32[16,512]{1,0:T(8,128)S(1)}, u32[]{:S(2)}, u32[]{:S(2)}) collective-permute-start(f32[16,512]{1,0:T(8,128)S(1)} %get-tuple-element.109), channel_id=1, source_target_pairs={{4,8},{12,16},{20,24},{8,4},{16,12},{24,20},{5,9},{13,17},{21,25},... | collective-permute-start | bytes 98312 | tf_op jit(solution)/shard_map/ppermute | solution.py:674
  43.5 8.7 %collective-permute-start.9 = (f32[16,512]{1,0:T(8,128)S(1)}, f32[16,512]{1,0:T(8,128)S(1)}, u32[]{:S(2)}, u32[]{:S(2)}) collective-permute-start(f32[16,512]{1,0:T(8,128)S(1)} %get-tuple-element.110), channel_id=1, source_target_pairs={{0,4},{8,12},{16,20},{24,28},{4,0},{12,8},{20,16},{28,24},{1,5},{9... | collective-permute-start | bytes 98312 | tf_op jit(solution)/shard_map/ppermute | solution.py:674
  48.0 4.1 %collective-permute-start.10 = (f32[24,128]{1,0:T(8,128)S(1)}, f32[24,128]{1,0:T(8,128)S(1)}, u32[]{:S(2)}, u32[]{:S(2)}) collective-permute-start(f32[24,128]{1,0:T(8,128)S(1)} %get-tuple-element.111), channel_id=1, source_target_pairs={{1,2},{3,0},{2,1},{0,3},{5,6},{7,4},{6,5},{4,7},{9,10},{11,8},{10,... | collective-permute-start | bytes 36872 | tf_op jit(solution)/shard_map/ppermute | solution.py:674
  48.7 3.5 %collective-permute-start.11 = (f32[24,128]{1,0:T(8,128)S(1)}, f32[24,128]{1,0:T(8,128)S(1)}, u32[]{:S(2)}, u32[]{:S(2)}) collective-permute-start(f32[24,128]{1,0:T(8,128)S(1)} %get-tuple-element.111), channel_id=1, source_target_pairs={{0,1},{2,3},{1,0},{3,2},{4,5},{6,7},{5,4},{7,6},{8,9},{10,11},{9,8... | collective-permute-start | bytes 36872 | tf_op jit(solution)/shard_map/ppermute | solution.py:674
  54.0 7.6 %collective-permute-start.12 = (f32[16,512]{1,0:T(8,128)S(1)}, f32[16,512]{1,0:T(8,128)S(1)}, u32[]{:S(2)}, u32[]{:S(2)}) collective-permute-start(f32[16,512]{1,0:T(8,128)S(1)} %get-tuple-element.115), channel_id=1, source_target_pairs={{4,8},{12,16},{20,24},{8,4},{16,12},{24,20},{5,9},{13,17},{21,25},... | collective-permute-start | bytes 98312 | tf_op jit(solution)/shard_map/ppermute | solution.py:674
  54.7 6.9 %collective-permute-start.13 = (f32[16,512]{1,0:T(8,128)S(1)}, f32[16,512]{1,0:T(8,128)S(1)}, u32[]{:S(2)}, u32[]{:S(2)}) collective-permute-start(f32[16,512]{1,0:T(8,128)S(1)} %get-tuple-element.116), channel_id=1, source_target_pairs={{0,4},{8,12},{16,20},{24,28},{4,0},{12,8},{20,16},{28,24},{1,5},{9... | collective-permute-start | bytes 98312 | tf_op jit(solution)/shard_map/ppermute | solution.py:674
  58.4 3.1 %collective-permute-start.14 = (f32[24,128]{1,0:T(8,128)S(1)}, f32[24,128]{1,0:T(8,128)S(1)}, u32[]{:S(2)}, u32[]{:S(2)}) collective-permute-start(f32[24,128]{1,0:T(8,128)S(1)} %get-tuple-element.117), channel_id=1, source_target_pairs={{1,2},{3,0},{2,1},{0,3},{5,6},{7,4},{6,5},{4,7},{9,10},{11,8},{10,... | collective-permute-start | bytes 36872 | tf_op jit(solution)/shard_map/ppermute | solution.py:674
  58.5 3.1 %collective-permute-start.15 = (f32[24,128]{1,0:T(8,128)S(1)}, f32[24,128]{1,0:T(8,128)S(1)}, u32[]{:S(2)}, u32[]{:S(2)}) collective-permute-start(f32[24,128]{1,0:T(8,128)S(1)} %get-tuple-element.118), channel_id=1, source_target_pairs={{0,1},{2,3},{1,0},{3,2},{4,5},{6,7},{5,4},{7,6},{8,9},{10,11},{9,8... | collective-permute-start | bytes 36872 | tf_op jit(solution)/shard_map/ppermute | solution.py:674
  62.2 3.4 %collective-permute-start.16 = (f32[1,64]{1,0:T(1,128)S(1)}, f32[1,64]{1,0:T(1,128)S(1)}, u32[]{:S(2)}, u32[]{:S(2)}) collective-permute-start(f32[1,64]{1,0:T(1,128)S(1)} %get-tuple-element.123), channel_id=1, source_target_pairs={{0,3},{1,2},{2,1},{3,0},{4,7},{5,6},{6,5},{7,4},{8,11},{9,10},{10,... | collective-permute-start | bytes 776 | tf_op jit(solution)/shard_map/ppermute | solution.py:683
  62.2 3.6 %collective-permute-start.17 = (f32[1,64]{1,0:T(1,128)S(1)}, f32[1,64]{1,0:T(1,128)S(1)}, u32[]{:S(2)}, u32[]{:S(2)}) collective-permute-start(f32[1,64]{1,0:T(1,128)S(1)} %get-tuple-element.123), channel_id=1, source_target_pairs={{0,2},{1,3},{2,0},{3,1},{4,6},{5,7},{6,4},{7,5},{8,10},{9,11},{10,... | collective-permute-start | bytes 776 | tf_op jit(solution)/shard_map/ppermute | solution.py:683
  63.3 2.5 %collective-permute-start.18 = (f32[1,64]{1,0:T(1,128)S(1)}, f32[1,64]{1,0:T(1,128)S(1)}, u32[]{:S(2)}, u32[]{:S(2)}) collective-permute-start(f32[1,64]{1,0:T(1,128)S(1)} %get-tuple-element.123), channel_id=1, source_target_pairs={{0,1},{1,0},{2,3},{3,2},{4,5},{5,4},{6,7},{7,6},{8,9},{9,8},{10,11... | collective-permute-start | bytes 776 | tf_op jit(solution)/shard_map/ppermute | solution.py:683

commit v18 on v17

--- a/solution.py
+++ b/solution.py
@@ -72,9 +72,9 @@
 def pick(fields, column_marks, row_marks):
     rows = fields[0].shape[0]
     parts = [split(field) for field in fields]
-    high = jnp.concatenate([part[0] for part in parts], axis=0)
-    low = jnp.concatenate([part[1] for part in parts], axis=0)
-    by_column = dot(high, column_marks, ((1,), (0,))) + dot(low, column_marks, ((1,), (0,)))
+    both = jnp.concatenate([part[0] for part in parts] + [part[1] for part in parts], axis=0)
+    by_column = dot(both, column_marks, ((1,), (0,)))
+    by_column = by_column[: rows * len(fields)] + by_column[rows * len(fields) :]
     marks = row_marks.astype(F32)
     return [
         jnp.sum(by_column[rows * f : rows * (f + 1)] * marks, axis=0, keepdims=True)
@@ -83,15 +83,12 @@
 
 
 def spread(pulls, column_marks, row_marks):
-    high, low = split(pulls)
-    total = None
-    for part in (high, low):
-        marked = jnp.concatenate(
-            [part[f : f + 1] * row_marks for f in range(FIELDS)], axis=0
-        )
-        summed = dot(marked, column_marks, ((1,), (1,)))
-        total = summed if total is None else total + summed
-    return total
+    marked = [
+        part[f : f + 1] * row_marks for part in split(pulls) for f in range(FIELDS)
+    ]
+    summed = dot(jnp.concatenate(marked, axis=0), column_marks, ((1,), (1,)))
+    half = summed.shape[0] // 2
+    return summed[:half] + summed[half:]
 
 
 def place():

time: 66.7 us -> 66.4 us (level)
  transfers between devices with their start and end apart: 22 -> 22, of which waited for: 5 -> 5; matrix products, arithmetic and copies ran while one was open for 0% -> 0% of each run, Pallas kernels for 11% -> 10%
where the time goes in v18:
time: 66.4 us; the launch traced here: 66 us
  starting transfers between devices  43 us (65%)
  Pallas kernels  18.1 us (27%)
  waiting for transfers between devices  3.42 us (5%)
  between operations  0.88 us (1%)
    ppermute x16, starting transfers between devices, swap(): lax.ppermute(value, axis, couples + [(j, i) for i, j in couples])  26.1 us
    pallas_call x9, Pallas kernels, call(): pl.pallas_call(kernel, out_shape=results, in_specs=[away] * far + [whole]...  18.1 us
    all_to_all x3, starting transfers between devices, exchange(): blocks = lax.all_to_all(blocks, ('sec', 'girth'), 0, 0, tiled=True)  15 us
    ppermute x3, starting transfers between devices, sum_over(): lax.ppermute(value, axis, [(i, i ^ step) for i in range(count)])  1.9 us
    ppermute x16, waiting for transfers between devices, swap(): lax.ppermute(value, axis, couples + [(j, i) for i, j in couples])  1.81 us
    all_to_all x3, waiting for transfers between devices, exchange(): blocks = lax.all_to_all(blocks, ('sec', 'girth'), 0, 0, tiled=True)  1.36 us
  transfers between devices with their start and end apart: 22, of which 5 were waited for; matrix products, arithmetic and copies ran while one was open for 0% of the time, Pallas kernels for 10%

profile of v18, /device:TPU:0, one launch (start us, length us, event | category | flops | bytes accessed | tf_op | source)
XLA Modules:
  0.0 66.0 jit_solution(16297208709481274693)
XLA Ops:
  0.6 2.9 %shard_map.111 = (f32[64,128]{1,0:T(8,128)}, f32[16,512]{1,0:T(8,128)S(1)}, f32[16,512]{1,0:T(8,128)S(1)}, f32[24,128]{1,0:T(8,128)S(1)}, bf16[512,1024]{1,0:T(8...) custom-call(f32[5,64,512]{2,1,0:T(8,128)} %refs_2_.1, ...), custom_call_target="tpu_custom_call" | custom-call | tf_op jit(solution)/shard_map/pallas_call | solution.py:655
  3.6 7.3 %all-to-all-start = ((f32[32,2,128]{2,1,0:T(2,128)}), f32[32,2,128]{2,1,0:T(2,128)S(1)}, u32[]{:S(2)}, u32[]{:S(2)}) async-start(f32[32,2,128]{2,1,0:T(2,128)} %bitcast.19), calls=%async_computation | async-start | bytes 65536 | tf_op jit(solution)/shard_map/all_to_all | solution.py:691
  10.9 0.7 %collective-permute-start = (f32[16,512]{1,0:T(8,128)S(1)}, f32[16,512]{1,0:T(8,128)S(1)}, u32[]{:S(2)}, u32[]{:S(2)}) collective-permute-start(f32[16,512]{1,0:T(8,128)S(1)} %get-tuple-element.77), channel_id=1, source_target_pairs={{4,8},{12,16},{20,24},{8,4},{16,12},{24,20},{5,9},{13,17},{21,25},... | collective-permute-start | bytes 98312 | tf_op jit(solution)/shard_map/ppermute | solution.py:671
  11.5 4.5 %collective-permute-start.1 = (f32[16,512]{1,0:T(8,128)S(1)}, f32[16,512]{1,0:T(8,128)S(1)}, u32[]{:S(2)}, u32[]{:S(2)}) collective-permute-start(f32[16,512]{1,0:T(8,128)S(1)} %get-tuple-element.78), channel_id=1, source_target_pairs={{0,4},{8,12},{16,20},{24,28},{4,0},{12,8},{20,16},{28,24},{1,5},{9... | collective-permute-start | bytes 98312 | tf_op jit(solution)/shard_map/ppermute | solution.py:671
  16.7 0.9 %collective-permute-start.3 = (f32[24,128]{1,0:T(8,128)S(1)}, f32[24,128]{1,0:T(8,128)S(1)}, u32[]{:S(2)}, u32[]{:S(2)}) collective-permute-start(f32[24,128]{1,0:T(8,128)S(1)} %get-tuple-element.79), channel_id=1, source_target_pairs={{0,1},{2,3},{1,0},{3,2},{4,5},{6,7},{5,4},{7,6},{8,9},{10,11},{9,8... | collective-permute-start | bytes 36872 | tf_op jit(solution)/shard_map/ppermute | solution.py:671
  18.1 1.7 %shard_map.112 = (f32[8,64,512]{2,1,0:T(8,128)S(1)}, f32[5,64,512]{2,1,0:T(8,128)S(1)}, f32[5,64,512]{2,1,0:T(8,128)S(1)}, f32[64,512]{1,0:T(8,128)S(1)}, s32[64...) custom-call(f32[8,64,512]{2,1,0:T(8,128)} %refs_0_.1, ...), custom_call_target="tpu_custom_call" | custom-call | tf_op jit(solution)/shard_map/pallas_call | solution.py:655
  19.9 2.6 %shard_map.113 = (f32[8,72,640]{2,1,0:T(8,128)}, f32[5,64,512]{2,1,0:T(8,128)}, f32[5,64,512]{2,1,0:T(8,128)}, f32[64,128]{1,0:T(8,128)}, f32[1,72,640]{2,1,0:T(...) custom-call(f32[8,64,512]{2,1,0:T(8,128)S(1)} %get-tuple-element.69.r, ...), custom_call_target="tpu_custom_call" | custom-call | tf_op jit(solution)/shard_map/pallas_call | solution.py:655
  22.6 3.9 %all-to-all-start.1 = ((f32[32,2,128]{2,1,0:T(2,128)}), f32[32,2,128]{2,1,0:T(2,128)S(1)}, u32[]{:S(2)}, u32[]{:S(2)}) async-start(f32[32,2,128]{2,1,0:T(2,128)} %bitcast.18), calls=%async_computation.1 | async-start | bytes 65536 | tf_op jit(solution)/shard_map/all_to_all | solution.py:691
  26.4 0.7 %collective-permute-start.4 = (f32[16,512]{1,0:T(8,128)S(1)}, f32[16,512]{1,0:T(8,128)S(1)}, u32[]{:S(2)}, u32[]{:S(2)}) collective-permute-start(f32[16,512]{1,0:T(8,128)S(1)} %get-tuple-element.94), channel_id=1, source_target_pairs={{4,8},{12,16},{20,24},{8,4},{16,12},{24,20},{5,9},{13,17},{21,25},... | collective-permute-start | bytes 98312 | tf_op jit(solution)/shard_map/ppermute | solution.py:671
  27.1 4.5 %collective-permute-start.5 = (f32[16,512]{1,0:T(8,128)S(1)}, f32[16,512]{1,0:T(8,128)S(1)}, u32[]{:S(2)}, u32[]{:S(2)}) collective-permute-start(f32[16,512]{1,0:T(8,128)S(1)} %get-tuple-element.95), channel_id=1, source_target_pairs={{0,4},{8,12},{16,20},{24,28},{4,0},{12,8},{20,16},{28,24},{1,5},{9... | collective-permute-start | bytes 98312 | tf_op jit(solution)/shard_map/ppermute | solution.py:671
  32.3 0.9 %collective-permute-start.7 = (f32[24,128]{1,0:T(8,128)S(1)}, f32[24,128]{1,0:T(8,128)S(1)}, u32[]{:S(2)}, u32[]{:S(2)}) collective-permute-start(f32[24,128]{1,0:T(8,128)S(1)} %get-tuple-element.96), channel_id=1, source_target_pairs={{0,1},{2,3},{1,0},{3,2},{4,5},{6,7},{5,4},{7,6},{8,9},{10,11},{9,8... | collective-permute-start | bytes 36872 | tf_op jit(solution)/shard_map/ppermute | solution.py:671
  33.7 1.8 %shard_map.114 = (f32[8,72,640]{2,1,0:T(8,128)S(1)}, f32[5,64,512]{2,1,0:T(8,128)S(1)}, f32[5,64,512]{2,1,0:T(8,128)S(1)}, f32[64,512]{1,0:T(8,128)S(1)}, f32[32...) custom-call(f32[8,72,640]{2,1,0:T(8,128)} %get-tuple-element.80.refs_0_, ...), custom_call_target="tpu_custom_call" | custom-call | tf_op jit(solution)/shard_map/pallas_call | solution.py:655
  35.5 3.4 %shard_map.115 = (f32[8,72,640]{2,1,0:T(8,128)}, f32[5,64,512]{2,1,0:T(8,128)}, f32[5,64,512]{2,1,0:T(8,128)}, f32[64,128]{1,0:T(8,128)}, f32[24,128]{1,0:T(8,12...) custom-call(f32[8,72,640]{2,1,0:T(8,128)S(1)} %get-tuple-element.87.refs_0_, ...), custom_call_target="tpu_custom_call" | custom-call | tf_op jit(solution)/shard_map/pallas_call | solution.py:655
  38.9 3.8 %all-to-all-start.2 = ((f32[32,2,128]{2,1,0:T(2,128)}), f32[32,2,128]{2,1,0:T(2,128)S(1)}, u32[]{:S(2)}, u32[]{:S(2)}) async-start(f32[32,2,128]{2,1,0:T(2,128)} %bitcast.17), calls=%async_computation.2 | async-start | bytes 65536 | tf_op jit(solution)/shard_map/all_to_all | solution.py:691
  42.7 0.7 %collective-permute-start.8 = (f32[16,512]{1,0:T(8,128)S(1)}, f32[16,512]{1,0:T(8,128)S(1)}, u32[]{:S(2)}, u32[]{:S(2)}) collective-permute-start(f32[16,512]{1,0:T(8,128)S(1)} %get-tuple-element.109), channel_id=1, source_target_pairs={{4,8},{12,16},{20,24},{8,4},{16,12},{24,20},{5,9},{13,17},{21,25},... | collective-permute-start | bytes 98312 | tf_op jit(solution)/shard_map/ppermute | solution.py:671
  43.4 4.5 %collective-permute-start.9 = (f32[16,512]{1,0:T(8,128)S(1)}, f32[16,512]{1,0:T(8,128)S(1)}, u32[]{:S(2)}, u32[]{:S(2)}) collective-permute-start(f32[16,512]{1,0:T(8,128)S(1)} %get-tuple-element.110), channel_id=1, source_target_pairs={{0,4},{8,12},{16,20},{24,28},{4,0},{12,8},{20,16},{28,24},{1,5},{9... | collective-permute-start | bytes 98312 | tf_op jit(solution)/shard_map/ppermute | solution.py:671
  48.6 0.9 %collective-permute-start.11 = (f32[24,128]{1,0:T(8,128)S(1)}, f32[24,128]{1,0:T(8,128)S(1)}, u32[]{:S(2)}, u32[]{:S(2)}) collective-permute-start(f32[24,128]{1,0:T(8,128)S(1)} %get-tuple-element.111), channel_id=1, source_target_pairs={{0,1},{2,3},{1,0},{3,2},{4,5},{6,7},{5,4},{7,6},{8,9},{10,11},{9,8... | collective-permute-start | bytes 36872 | tf_op jit(solution)/shard_map/ppermute | solution.py:671
  50.0 1.8 %shard_map.116 = (f32[8,72,640]{2,1,0:T(8,128)S(1)}, f32[5,64,512]{2,1,0:T(8,128)S(1)}, f32[5,64,512]{2,1,0:T(8,128)S(1)}, f32[64,512]{1,0:T(8,128)S(1)}, f32[32...) custom-call(f32[8,72,640]{2,1,0:T(8,128)} %get-tuple-element.97.refs_0_, ...), custom_call_target="tpu_custom_call" | custom-call | tf_op jit(solution)/shard_map/pallas_call | solution.py:655
  51.8 1.8 %shard_map.117 = (f32[8,72,640]{2,1,0:T(8,128)S(1)}, f32[5,64,512]{2,1,0:T(8,128)S(1)}, f32[5,64,512]{2,1,0:T(8,128)S(1)}, f32[24,128]{1,0:T(8,128)S(1)}, f32[16...) custom-call(f32[8,72,640]{2,1,0:T(8,128)S(1)} %get-tuple-element.102.refs_0_, ...), custom_call_target="tpu_custom_call" | custom-call | tf_op jit(solution)/shard_map/pallas_call | solution.py:655
  54.3 3.8 %collective-permute-start.13 = (f32[16,512]{1,0:T(8,128)S(1)}, f32[16,512]{1,0:T(8,128)S(1)}, u32[]{:S(2)}, u32[]{:S(2)}) collective-permute-start(f32[16,512]{1,0:T(8,128)S(1)} %get-tuple-element.116), channel_id=1, source_target_pairs={{0,4},{8,12},{16,20},{24,28},{4,0},{12,8},{20,16},{28,24},{1,5},{9... | collective-permute-start | bytes 98312 | tf_op jit(solution)/shard_map/ppermute | solution.py:671
  58.1 1.3 %collective-permute-start.15 = (f32[24,128]{1,0:T(8,128)S(1)}, f32[24,128]{1,0:T(8,128)S(1)}, u32[]{:S(2)}, u32[]{:S(2)}) collective-permute-start(f32[24,128]{1,0:T(8,128)S(1)} %get-tuple-element.118), channel_id=1, source_target_pairs={{0,1},{2,3},{1,0},{3,2},{4,5},{6,7},{5,4},{7,6},{8,9},{10,11},{9,8... | collective-permute-start | bytes 36872 | tf_op jit(solution)/shard_map/ppermute | solution.py:671
  59.4 1.8 %collective-permute-done.14.refs_4_.refs_6_ = f32[24,128]{1,0:T(8,128)S(1)} collective-permute-done((f32[24,128]{1,0:T(8,128)S(1)}, f32[24,128]{1,0:T(8,128)S(1)}, u32[]{:S(2)}, u32[]{:S(2)}) %collective-permute-start.14) | collective-permute-done | bytes 12320 | tf_op jit(solution)/shard_map/ppermute | solution.py:671
  61.9 1.2 %collective-permute-start.17 = (f32[1,64]{1,0:T(1,128)S(1)}, f32[1,64]{1,0:T(1,128)S(1)}, u32[]{:S(2)}, u32[]{:S(2)}) collective-permute-start(f32[1,64]{1,0:T(1,128)S(1)} %get-tuple-element.123), channel_id=1, source_target_pairs={{0,2},{1,3},{2,0},{3,1},{4,6},{5,7},{6,4},{7,5},{8,10},{9,11},{10,... | collective-permute-start | bytes 776 | tf_op jit(solution)/shard_map/ppermute | solution.py:680
  63.7 1.5 %shard_map.119 = (f32[8,64,512]{2,1,0:T(8,128)}, f32[5,64,512]{2,1,0:T(8,128)}, f32[5,64,512]{2,1,0:T(8,128)}) custom-call(f32[8,72,640]{2,1,0:T(8,128)S(1)} %get-tuple-element.112.refs_0_, f32[5,64,512]{2,1,0:T(8,128)S(1)} %get-tuple-element.113.refs_1_, f32[5,64,512]{2,1,0:T(8,128)S(1)} %get-tuple-element.114.refs_2_, ...), custom_call_target="tpu_custom_call" | custom-call | tf_op jit(solution)/shard_map/pallas_call | solution.py:655
  (32 shorter events, 6.1 us)
Async XLA Ops:
  3.6 14.6 %all-to-all-start = ((f32[32,2,128]{2,1,0:T(2,128)}), f32[32,2,128]{2,1,0:T(2,128)S(1)}, u32[]{:S(2)}, u32[]{:S(2)}) async-start(f32[32,2,128]{2,1,0:T(2,128)} %bitcast.19), calls=%async_computation | async-start | bytes 65536 | tf_op jit(solution)/shard_map/all_to_all | solution.py:691
  10.9 9.0 %collective-permute-start = (f32[16,512]{1,0:T(8,128)S(1)}, f32[16,512]{1,0:T(8,128)S(1)}, u32[]{:S(2)}, u32[]{:S(2)}) collective-permute-start(f32[16,512]{1,0:T(8,128)S(1)} %get-tuple-element.77), channel_id=1, source_target_pairs={{4,8},{12,16},{20,24},{8,4},{16,12},{24,20},{5,9},{13,17},{21,25},... | collective-permute-start | bytes 98312 | tf_op jit(solution)/shard_map/ppermute | solution.py:671
  11.5 8.4 %collective-permute-start.1 = (f32[16,512]{1,0:T(8,128)S(1)}, f32[16,512]{1,0:T(8,128)S(1)}, u32[]{:S(2)}, u32[]{:S(2)}) collective-permute-start(f32[16,512]{1,0:T(8,128)S(1)} %get-tuple-element.78), channel_id=1, source_target_pairs={{0,4},{8,12},{16,20},{24,28},{4,0},{12,8},{20,16},{28,24},{1,5},{9... | collective-permute-start | bytes 98312 | tf_op jit(solution)/shard_map/ppermute | solution.py:671
  16.1 3.8 %collective-permute-start.2 = (f32[24,128]{1,0:T(8,128)S(1)}, f32[24,128]{1,0:T(8,128)S(1)}, u32[]{:S(2)}, u32[]{:S(2)}) collective-permute-start(f32[24,128]{1,0:T(8,128)S(1)} %get-tuple-element.79), channel_id=1, source_target_pairs={{1,2},{3,0},{2,1},{0,3},{5,6},{7,4},{6,5},{4,7},{9,10},{11,8},{10,... | collective-permute-start | bytes 36872 | tf_op jit(solution)/shard_map/ppermute | solution.py:671
  16.7 3.1 %collective-permute-start.3 = (f32[24,128]{1,0:T(8,128)S(1)}, f32[24,128]{1,0:T(8,128)S(1)}, u32[]{:S(2)}, u32[]{:S(2)}) collective-permute-start(f32[24,128]{1,0:T(8,128)S(1)} %get-tuple-element.79), channel_id=1, source_target_pairs={{0,1},{2,3},{1,0},{3,2},{4,5},{6,7},{5,4},{7,6},{8,9},{10,11},{9,8... | collective-permute-start | bytes 36872 | tf_op jit(solution)/shard_map/ppermute | solution.py:671
  22.6 11.1 %all-to-all-start.1 = ((f32[32,2,128]{2,1,0:T(2,128)}), f32[32,2,128]{2,1,0:T(2,128)S(1)}, u32[]{:S(2)}, u32[]{:S(2)}) async-start(f32[32,2,128]{2,1,0:T(2,128)} %bitcast.18), calls=%async_computation.1 | async-start | bytes 65536 | tf_op jit(solution)/shard_map/all_to_all | solution.py:691
  26.4 9.1 %collective-permute-start.4 = (f32[16,512]{1,0:T(8,128)S(1)}, f32[16,512]{1,0:T(8,128)S(1)}, u32[]{:S(2)}, u32[]{:S(2)}) collective-permute-start(f32[16,512]{1,0:T(8,128)S(1)} %get-tuple-element.94), channel_id=1, source_target_pairs={{4,8},{12,16},{20,24},{8,4},{16,12},{24,20},{5,9},{13,17},{21,25},... | collective-permute-start | bytes 98312 | tf_op jit(solution)/shard_map/ppermute | solution.py:671
  27.1 8.4 %collective-permute-start.5 = (f32[16,512]{1,0:T(8,128)S(1)}, f32[16,512]{1,0:T(8,128)S(1)}, u32[]{:S(2)}, u32[]{:S(2)}) collective-permute-start(f32[16,512]{1,0:T(8,128)S(1)} %get-tuple-element.95), channel_id=1, source_target_pairs={{0,4},{8,12},{16,20},{24,28},{4,0},{12,8},{20,16},{28,24},{1,5},{9... | collective-permute-start | bytes 98312 | tf_op jit(solution)/shard_map/ppermute | solution.py:671
  31.7 3.8 %collective-permute-start.6 = (f32[24,128]{1,0:T(8,128)S(1)}, f32[24,128]{1,0:T(8,128)S(1)}, u32[]{:S(2)}, u32[]{:S(2)}) collective-permute-start(f32[24,128]{1,0:T(8,128)S(1)} %get-tuple-element.96), channel_id=1, source_target_pairs={{1,2},{3,0},{2,1},{0,3},{5,6},{7,4},{6,5},{4,7},{9,10},{11,8},{10,... | collective-permute-start | bytes 36872 | tf_op jit(solution)/shard_map/ppermute | solution.py:671
  32.3 3.2 %collective-permute-start.7 = (f32[24,128]{1,0:T(8,128)S(1)}, f32[24,128]{1,0:T(8,128)S(1)}, u32[]{:S(2)}, u32[]{:S(2)}) collective-permute-start(f32[24,128]{1,0:T(8,128)S(1)} %get-tuple-element.96), channel_id=1, source_target_pairs={{0,1},{2,3},{1,0},{3,2},{4,5},{6,7},{5,4},{7,6},{8,9},{10,11},{9,8... | collective-permute-start | bytes 36872 | tf_op jit(solution)/shard_map/ppermute | solution.py:671
  38.9 11.1 %all-to-all-start.2 = ((f32[32,2,128]{2,1,0:T(2,128)}), f32[32,2,128]{2,1,0:T(2,128)S(1)}, u32[]{:S(2)}, u32[]{:S(2)}) async-start(f32[32,2,128]{2,1,0:T(2,128)} %bitcast.17), calls=%async_computation.2 | async-start | bytes 65536 | tf_op jit(solution)/shard_map/all_to_all | solution.py:691
  42.7 9.1 %collective-permute-start.8 = (f32[16,512]{1,0:T(8,128)S(1)}, f32[16,512]{1,0:T(8,128)S(1)}, u32[]{:S(2)}, u32[]{:S(2)}) collective-permute-start(f32[16,512]{1,0:T(8,128)S(1)} %get-tuple-element.109), channel_id=1, source_target_pairs={{4,8},{12,16},{20,24},{8,4},{16,12},{24,20},{5,9},{13,17},{21,25},... | collective-permute-start | bytes 98312 | tf_op jit(solution)/shard_map/ppermute | solution.py:671
  43.4 8.4 %collective-permute-start.9 = (f32[16,512]{1,0:T(8,128)S(1)}, f32[16,512]{1,0:T(8,128)S(1)}, u32[]{:S(2)}, u32[]{:S(2)}) collective-permute-start(f32[16,512]{1,0:T(8,128)S(1)} %get-tuple-element.110), channel_id=1, source_target_pairs={{0,4},{8,12},{16,20},{24,28},{4,0},{12,8},{20,16},{28,24},{1,5},{9... | collective-permute-start | bytes 98312 | tf_op jit(solution)/shard_map/ppermute | solution.py:671
  47.9 3.8 %collective-permute-start.10 = (f32[24,128]{1,0:T(8,128)S(1)}, f32[24,128]{1,0:T(8,128)S(1)}, u32[]{:S(2)}, u32[]{:S(2)}) collective-permute-start(f32[24,128]{1,0:T(8,128)S(1)} %get-tuple-element.111), channel_id=1, source_target_pairs={{1,2},{3,0},{2,1},{0,3},{5,6},{7,4},{6,5},{4,7},{9,10},{11,8},{10,... | collective-permute-start | bytes 36872 | tf_op jit(solution)/shard_map/ppermute | solution.py:671
  48.6 3.2 %collective-permute-start.11 = (f32[24,128]{1,0:T(8,128)S(1)}, f32[24,128]{1,0:T(8,128)S(1)}, u32[]{:S(2)}, u32[]{:S(2)}) collective-permute-start(f32[24,128]{1,0:T(8,128)S(1)} %get-tuple-element.111), channel_id=1, source_target_pairs={{0,1},{2,3},{1,0},{3,2},{4,5},{6,7},{5,4},{7,6},{8,9},{10,11},{9,8... | collective-permute-start | bytes 36872 | tf_op jit(solution)/shard_map/ppermute | solution.py:671
  53.6 7.6 %collective-permute-start.12 = (f32[16,512]{1,0:T(8,128)S(1)}, f32[16,512]{1,0:T(8,128)S(1)}, u32[]{:S(2)}, u32[]{:S(2)}) collective-permute-start(f32[16,512]{1,0:T(8,128)S(1)} %get-tuple-element.115), channel_id=1, source_target_pairs={{4,8},{12,16},{20,24},{8,4},{16,12},{24,20},{5,9},{13,17},{21,25},... | collective-permute-start | bytes 98312 | tf_op jit(solution)/shard_map/ppermute | solution.py:671
  54.3 6.9 %collective-permute-start.13 = (f32[16,512]{1,0:T(8,128)S(1)}, f32[16,512]{1,0:T(8,128)S(1)}, u32[]{:S(2)}, u32[]{:S(2)}) collective-permute-start(f32[16,512]{1,0:T(8,128)S(1)} %get-tuple-element.116), channel_id=1, source_target_pairs={{0,4},{8,12},{16,20},{24,28},{4,0},{12,8},{20,16},{28,24},{1,5},{9... | collective-permute-start | bytes 98312 | tf_op jit(solution)/shard_map/ppermute | solution.py:671
  58.1 3.1 %collective-permute-start.14 = (f32[24,128]{1,0:T(8,128)S(1)}, f32[24,128]{1,0:T(8,128)S(1)}, u32[]{:S(2)}, u32[]{:S(2)}) collective-permute-start(f32[24,128]{1,0:T(8,128)S(1)} %get-tuple-element.117), channel_id=1, source_target_pairs={{1,2},{3,0},{2,1},{0,3},{5,6},{7,4},{6,5},{4,7},{9,10},{11,8},{10,... | collective-permute-start | bytes 36872 | tf_op jit(solution)/shard_map/ppermute | solution.py:671
  58.1 3.1 %collective-permute-start.15 = (f32[24,128]{1,0:T(8,128)S(1)}, f32[24,128]{1,0:T(8,128)S(1)}, u32[]{:S(2)}, u32[]{:S(2)}) collective-permute-start(f32[24,128]{1,0:T(8,128)S(1)} %get-tuple-element.118), channel_id=1, source_target_pairs={{0,1},{2,3},{1,0},{3,2},{4,5},{6,7},{5,4},{7,6},{8,9},{10,11},{9,8... | collective-permute-start | bytes 36872 | tf_op jit(solution)/shard_map/ppermute | solution.py:671
  61.8 3.4 %collective-permute-start.16 = (f32[1,64]{1,0:T(1,128)S(1)}, f32[1,64]{1,0:T(1,128)S(1)}, u32[]{:S(2)}, u32[]{:S(2)}) collective-permute-start(f32[1,64]{1,0:T(1,128)S(1)} %get-tuple-element.123), channel_id=1, source_target_pairs={{0,3},{1,2},{2,1},{3,0},{4,7},{5,6},{6,5},{7,4},{8,11},{9,10},{10,... | collective-permute-start | bytes 776 | tf_op jit(solution)/shard_map/ppermute | solution.py:680
  61.9 3.6 %collective-permute-start.17 = (f32[1,64]{1,0:T(1,128)S(1)}, f32[1,64]{1,0:T(1,128)S(1)}, u32[]{:S(2)}, u32[]{:S(2)}) collective-permute-start(f32[1,64]{1,0:T(1,128)S(1)} %get-tuple-element.123), channel_id=1, source_target_pairs={{0,2},{1,3},{2,0},{3,1},{4,6},{5,7},{6,4},{7,5},{8,10},{9,11},{10,... | collective-permute-start | bytes 776 | tf_op jit(solution)/shard_map/ppermute | solution.py:680
  63.1 2.4 %collective-permute-start.18 = (f32[1,64]{1,0:T(1,128)S(1)}, f32[1,64]{1,0:T(1,128)S(1)}, u32[]{:S(2)}, u32[]{:S(2)}) collective-permute-start(f32[1,64]{1,0:T(1,128)S(1)} %get-tuple-element.123), channel_id=1, source_target_pairs={{0,1},{1,0},{2,3},{3,2},{4,5},{5,4},{6,7},{7,6},{8,9},{9,8},{10,11... | collective-permute-start | bytes 776 | tf_op jit(solution)/shard_map/ppermute | solution.py:680
